TPU v7x, 32 devices: a whole 2x2x4 slice. The times are simulated.
32 devices in a mesh: ulysses: 4 (over y, x), blk: 8 (over z, core).
Axes of the slice: x: 2, y: 2, z: 4, core: 2. Of those that a mesh axis runs over, the one named last changes fastest.
Arguments:
- inputs: bfloat16 [4096, 2048], P(('ulysses', 'blk')), may hold values from -6 to 6
- cotangent: bfloat16 [4096, 2048], P(('ulysses', 'blk')), may hold values from -6 to 6
- segments: int32 [4096], replicated, may hold values from 0 to 7, as said below
- expert_ids: int32 [4096, 8], P(('ulysses', 'blk')), may hold values from 0 to 15, all different within a row; in each aligned block of 128 rows (0 to 127, 128 to 255, ...) at most 128 rows name the same one
- gate_weights: float32 [4096, 8], P(('ulysses', 'blk')), as said below
- fill_order: int32 [4096], P(('ulysses', 'blk')), may hold values from 0 to 127, as said below
- norm1_gain: bfloat16 [2048], P(('ulysses', 'blk')), may hold values from 0.099609375 to 1.8984375
- w_query: bfloat16 [2048, 2048], P(('ulysses', 'blk')), may hold values from -0.125 to 0.125
- w_key: bfloat16 [2048, 2048], P(('ulysses', 'blk')), may hold values from -0.125 to 0.125
- w_value: bfloat16 [2048, 2048], P(('ulysses', 'blk')), may hold values from -0.125 to 0.125
- w_output: bfloat16 [2048, 2048], P(('ulysses', 'blk')), may hold values from -0.5 to 0.5
- query_gain: bfloat16 [2048], P(('ulysses', 'blk')), may hold values from 0.099609375 to 1.8984375
- key_gain: bfloat16 [2048], P(('ulysses', 'blk')), may hold values from 0.099609375 to 1.8984375
- norm2_gain: bfloat16 [2048], P(('ulysses', 'blk')), may hold values from 0.099609375 to 1.8984375
- expert_gate: bfloat16 [32768, 1024], P(('ulysses', 'blk')), may hold values from -0.125 to 0.125
- expert_up: bfloat16 [32768, 1024], P(('ulysses', 'blk')), may hold values from -0.125 to 0.125
- expert_down: bfloat16 [16384, 2048], P(('ulysses', 'blk')), may hold values from -0.5 to 0.5
Outputs:
- output: float32 [4096, 2048], P(('ulysses', 'blk'))
- d_inputs: float32 [4096, 2048], P(('ulysses', 'blk'))
- d_norm1_gain: float32 [2048], P(('ulysses', 'blk'))
- d_w_query: float32 [2048, 2048], P(('ulysses', 'blk'))
- d_w_key: float32 [2048, 2048], P(('ulysses', 'blk'))
- d_w_value: float32 [2048, 2048], P(('ulysses', 'blk'))
- d_w_output: float32 [2048, 2048], P(('ulysses', 'blk'))
- d_query_gain: float32 [2048], P(('ulysses', 'blk'))
- d_key_gain: float32 [2048], P(('ulysses', 'blk'))
- d_norm2_gain: float32 [2048], P(('ulysses', 'blk'))
- d_expert_gate: float32 [32768, 1024], P(('ulysses', 'blk'))
- d_expert_up: float32 [32768, 1024], P(('ulysses', 'blk'))
- d_expert_down: float32 [16384, 2048], P(('ulysses', 'blk'))
Inputs may be any that keep to these rules, and one draw needn't show every extreme that they name: `segments`: document ids along the positions: they start at 0, never fall and rise by one where a new document begins; each document has 1 to 1024 positions, and one document has exactly 1024. `expert_ids`: each row names 8 different experts; in each aligned block of 128 rows (the rows of one device) no expert is named by more than 128 rows, a bound that some block reaches. `gate_weights`: Positive; each row sums to one. `fill_order`: within each aligned block of 128 positions, a permutation of 0 to 127.
All inputs are finite; a program needn't handle non-finite values.
Results may differ from a plain program's by a relative error of at most 0.025.
Values may be sent and summed in bfloat16 or wider, within the bound.
A program may use at most 256 MiB of HBM per device.

v0:
```python
import math

import jax
import jax.numpy as jnp
from jax import lax
from jax.sharding import PartitionSpec as P

HEAD_DIM = 128


EPS = 1e-05
ROPE_BASE = 10000.0
NEG = -1e30


def as_sent(value):

    def short(part):
        return part.astype(jnp.bfloat16) if part.dtype == jnp.float32 else part

    return jax.tree.map(short, value)


def passed_along(block, axis, distance):
    devices = range(lax.axis_size(axis))
    route = [((i - distance) % len(devices), i) for i in devices]
    return lax.ppermute(block, axis, route)


def prefix(value, axis, join, neutral):
    count, mine = (lax.axis_size(axis), lax.axis_index(axis))
    pieces = lax.all_gather(value, axis)
    subtotal = jnp.full_like(value, 0) + jnp.asarray(neutral, value.dtype)

    def hop(position, subtotal):
        longer = join(subtotal, pieces[position])
        return jnp.where(position < mine, longer, subtotal)

    return lax.fori_loop(0, count - 1, hop, subtotal)


def partner_2(block, axis, bit):
    count = lax.axis_size(axis)
    route = []
    for low in range(count):
        high = low | 1 << bit
        if high != low and high < count:
            route += [(low, high), (high, low)]
    return lax.ppermute(block, axis, route)


def norm_rows(values, gain_vec):
    return values * lax.rsqrt(jnp.mean(values * values, axis=-1, keepdims=True) + EPS) * gain_vec


def rotate(values, positions):
    half_dim = HEAD_DIM // 2
    heads_here = values.shape[1] // HEAD_DIM
    inv_freq = jnp.exp(
        jnp.arange(half_dim, dtype=jnp.float32) * (-2.0 * math.log(ROPE_BASE) / HEAD_DIM)
    )
    angles = positions.astype(jnp.float32)[:, None] * inv_freq[None, :]
    cosine = jnp.cos(angles)[:, None, :]
    sin_t = jnp.sin(angles)[:, None, :]
    shaped = values.reshape(values.shape[0], heads_here, HEAD_DIM)
    lower_half = shaped[..., :half_dim]
    upper_half = shaped[..., half_dim:]
    turned = jnp.concatenate(
        [lower_half * cosine - upper_half * sin_t, upper_half * cosine + lower_half * sin_t],
        axis=-1,
    )
    return turned.reshape(values.shape)


def attn_inputs(q_lin, k_lin, gain_q, gain_k, positions):
    return (
        rotate(norm_rows(q_lin, gain_q), positions),
        rotate(norm_rows(k_lin, gain_k), positions),
    )


def banded(shaped, fill_value):
    earlier = jnp.concatenate([jnp.full_like(shaped[:1], fill_value), shaped[:-1]], axis=0)
    return jnp.concatenate([earlier, shaped], axis=1)


def unbanded(band, local_rows):
    earlier = band[:, :local_rows]
    own_part = band[:, local_rows:]
    moved_up = jnp.concatenate([earlier[1:], jnp.zeros_like(earlier[:1])], axis=0)
    return own_part + moved_up


def add_counts(earlier, later):
    return earlier + later


def expert_move(buffer):
    return lax.all_to_all(buffer, ("ulysses", "blk"), split_axis=0, concat_axis=0, tiled=True)


def to_head_layout(values):
    return jax.tree.map(
        lambda part, own: part.astype(own.dtype),
        lax.all_to_all(as_sent(values), "ulysses", split_axis=1, concat_axis=0, tiled=True),
        values,
    )


def to_token_layout(values):
    return jax.tree.map(
        lambda part, own: part.astype(own.dtype),
        lax.all_to_all(as_sent(values), "ulysses", split_axis=0, concat_axis=1, tiled=True),
        values,
    )


def local(
    inputs,
    cotangent,
    segments,
    expert_ids,
    gate_weights,
    fill_order,
    norm1_gain,
    w_query,
    w_key,
    w_value,
    w_output,
    query_gain,
    key_gain,
    norm2_gain,
    expert_gate,
    expert_up,
    expert_down,
):
    blk_size = lax.axis_size("blk")
    groups = lax.axis_size("ulysses")
    devices = blk_size * groups
    local_rows = inputs.shape[0]
    model_width = inputs.shape[1]
    blk_index = lax.axis_index("blk")
    group_index = lax.axis_index("ulysses")
    device_index = group_index * blk_size + blk_index
    positions = device_index * local_rows + jnp.arange(local_rows, dtype=jnp.int32)
    heads_dev = model_width // groups // HEAD_DIM
    score_scale = 1.0 / math.sqrt(HEAD_DIM)
    layer_in = inputs.astype(jnp.float32)
    dense = (w_query, w_key, w_value, w_output, norm1_gain, query_gain, key_gain, norm2_gain)
    gathered = (
        lax.all_gather(dense[0], ("ulysses", "blk"), axis=0, tiled=True),
        lax.all_gather(dense[1], ("ulysses", "blk"), axis=0, tiled=True),
        lax.all_gather(dense[2], ("ulysses", "blk"), axis=0, tiled=True),
        lax.all_gather(dense[3], ("ulysses", "blk"), axis=0, tiled=True),
        lax.all_gather(dense[4], ("ulysses", "blk"), axis=0, tiled=True),
        lax.all_gather(dense[5], ("ulysses", "blk"), axis=0, tiled=True),
        lax.all_gather(dense[6], ("ulysses", "blk"), axis=0, tiled=True),
        lax.all_gather(dense[7], ("ulysses", "blk"), axis=0, tiled=True),
    )
    w_q, w_k, w_v, w_o = (gathered[0], gathered[1], gathered[2], gathered[3])
    gain_one = gathered[4].astype(jnp.float32)
    gain_q = gathered[5].astype(jnp.float32)
    gain_k = gathered[6].astype(jnp.float32)
    gain_two = gathered[7].astype(jnp.float32)
    normed_one = norm_rows(layer_in, gain_one).astype(jnp.bfloat16)
    q_lin = jnp.dot(normed_one, w_q, preferred_element_type=jnp.float32)
    k_lin = jnp.dot(normed_one, w_k, preferred_element_type=jnp.float32)
    v_lin = jnp.dot(normed_one, w_v, preferred_element_type=jnp.float32)
    (q_rot, k_rot), pre_back = jax.vjp(
        lambda q_in, k_in, gq_in, gk_in: attn_inputs(q_in, k_in, gq_in, gk_in, positions),
        q_lin,
        k_lin,
        gain_q,
        gain_k,
    )
    q_heads, k_heads, v_heads = to_head_layout(
        (q_rot.astype(jnp.bfloat16), k_rot.astype(jnp.bfloat16), v_lin.astype(jnp.bfloat16))
    )
    group_ids = jnp.arange(groups, dtype=jnp.int32)[:, None]
    row_ids = jnp.arange(local_rows, dtype=jnp.int32)[None, :]
    q_pos = (group_ids * blk_size + blk_index) * local_rows + row_ids
    q_seg = segments[q_pos]
    four_shape = (groups, local_rows, heads_dev, HEAD_DIM)
    q_four = q_heads.reshape(four_shape)

    def score_block(k_now, source):
        k_pos = (group_ids * blk_size + source) * local_rows + row_ids
        k_seg = banded(segments[k_pos], -1)
        k_pos = banded(k_pos, 0)
        k_band = banded(k_now.reshape(four_shape), 0)
        raw_scores = (
            jnp.einsum("gqhd,gkhd->gqhk", q_four, k_band, preferred_element_type=jnp.float32)
            * score_scale
        )
        allowed = (k_seg[:, None, :] == q_seg[:, :, None]) & (
            k_pos[:, None, :] <= q_pos[:, :, None]
        )
        return (raw_scores, allowed[:, :, None, :], k_band)

    def forward_step(flash_state, kv_stack, step_id):
        run_max, run_sum, run_out = flash_state
        source = jnp.mod(blk_index - step_id, blk_size)
        raw_scores, allowed, k_band = score_block(kv_stack[0], source)
        raw_scores = jnp.where(allowed, raw_scores, NEG)
        new_max = jnp.maximum(run_max, jnp.max(raw_scores, axis=-1))
        shrink = jnp.exp(run_max - new_max)
        weights = jnp.where(allowed, jnp.exp(raw_scores - new_max[..., None]), 0.0)
        run_sum = run_sum * shrink + jnp.sum(weights, axis=-1)
        v_band = banded(kv_stack[1].reshape(four_shape), 0)
        run_out = run_out * shrink[..., None] + jnp.einsum(
            "gqhk,gkhd->gqhd",
            weights.astype(jnp.bfloat16),
            v_band,
            preferred_element_type=jnp.float32,
        )
        return (new_max, run_sum, run_out)

    start_state = (
        jnp.full((groups, local_rows, heads_dev), NEG, jnp.float32),
        jnp.zeros((groups, local_rows, heads_dev), jnp.float32),
        jnp.zeros(four_shape, jnp.float32),
    )
    kv_home = jnp.stack([k_heads, v_heads])
    first_state = forward_step(start_state, kv_home, 0)

    def forward_turn(step_id, loop_state):
        flash_state, kv_stack = loop_state
        moved = passed_along(kv_stack, "blk", 1)
        return (forward_step(flash_state, moved, step_id), moved)

    final_state, unused_kv = lax.fori_loop(1, blk_size, forward_turn, (first_state, kv_home))
    run_max, run_sum, run_out = final_state
    o_four = (run_out / run_sum[..., None]).astype(jnp.bfloat16)
    log_total = run_max + jnp.log(run_sum)
    o_heads = o_four.reshape(groups * local_rows, heads_dev * HEAD_DIM)
    attended = to_token_layout(o_heads)
    residual = layer_in + jnp.dot(attended, w_o, preferred_element_type=jnp.float32)
    normed_two_f, norm_two_back = jax.vjp(norm_rows, residual, gain_two)
    normed_two = normed_two_f.astype(jnp.bfloat16)
    experts_n = devices // 2
    topk = expert_ids.shape[1]
    per_source = 2 * local_rows * topk // experts_n
    half_slots = per_source // 2
    capacity = 9 * local_rows * devices * topk // (8 * experts_n)
    slots_all = experts_n * per_source
    tokens_local = jnp.arange(local_rows, dtype=jnp.int32)
    chosen = jnp.sum(
        (expert_ids[:, :, None] == jnp.arange(experts_n, dtype=jnp.int32)[None, None, :]).astype(
            jnp.int32
        ),
        axis=1,
    )
    by_fill = jnp.zeros((local_rows,), jnp.int32).at[fill_order].set(tokens_local)
    sorted_rows = chosen[by_fill]
    before = jnp.cumsum(sorted_rows, axis=0) - sorted_rows
    rank_all = before[fill_order]
    pair_rank = jnp.take_along_axis(rank_all, expert_ids, axis=1)
    counts = jnp.sum(chosen, axis=0)
    offsets = prefix(counts, ("ulysses", "blk"), add_counts, jnp.zeros_like(counts))
    kept_pair = offsets[expert_ids] + pair_rank < capacity
    pair_slot = expert_ids * per_source + pair_rank
    pair_index = tokens_local[:, None] * topk + jnp.arange(topk, dtype=jnp.int32)[None, :]
    slot_pair = (
        jnp.zeros((slots_all,), jnp.int32).at[pair_slot.reshape(-1)].set(pair_index.reshape(-1))
    )
    slot_live = (
        jnp.zeros((slots_all,), jnp.bool_).at[pair_slot.reshape(-1)].set(kept_pair.reshape(-1))
    )
    slot_token = slot_pair // topk
    send_rows = jnp.where(slot_live[:, None], normed_two[slot_token], jnp.zeros((), jnp.bfloat16))
    received = expert_move(send_rows.reshape(devices, half_slots, model_width)).reshape(
        devices * half_slots, model_width
    )
    parity = jnp.mod(blk_index, 2)
    partner = partner_2((expert_gate, expert_up, expert_down), "blk", 0)

    def joined(own_half, other_half):
        lower_part = jnp.where(parity == 0, own_half, other_half)
        upper_part = jnp.where(parity == 0, other_half, own_half)
        return jnp.concatenate([lower_part, upper_part], axis=0)

    gate_full = joined(expert_gate, partner[0])
    up_full = joined(expert_up, partner[1])
    down_full = joined(expert_down, partner[2])
    gate_pre = jnp.dot(received, gate_full, preferred_element_type=jnp.float32)
    up_pre = jnp.dot(received, up_full, preferred_element_type=jnp.float32)
    hidden = (jax.nn.silu(gate_pre) * up_pre).astype(jnp.bfloat16)
    produced = jnp.dot(hidden, down_full, preferred_element_type=jnp.float32).astype(jnp.bfloat16)
    returned = expert_move(produced.reshape(devices, half_slots, model_width)).reshape(
        slots_all, model_width
    )
    pair_share = jnp.where(kept_pair, gate_weights, 0.0)
    mixed = jnp.einsum("tk,tkd->td", pair_share, returned[pair_slot].astype(jnp.float32))
    output = residual + mixed
    grad_out = cotangent.astype(jnp.float32)
    slot_share = jnp.where(slot_live, gate_weights.reshape(-1)[slot_pair], 0.0)
    grad_send = (slot_share[:, None] * grad_out[slot_token]).astype(jnp.bfloat16)
    grad_rows = expert_move(grad_send.reshape(devices, half_slots, model_width)).reshape(
        devices * half_slots, model_width
    )
    d_down_full = jnp.einsum("rf,rd->fd", hidden, grad_rows, preferred_element_type=jnp.float32)
    d_hidden = jnp.einsum("rd,fd->rf", grad_rows, down_full, preferred_element_type=jnp.float32)
    sigma = jax.nn.sigmoid(gate_pre)
    d_gate_pre = (d_hidden * up_pre * sigma * (1.0 + gate_pre * (1.0 - sigma))).astype(jnp.bfloat16)
    d_up_pre = (d_hidden * gate_pre * sigma).astype(jnp.bfloat16)
    d_gate_full = jnp.einsum("rd,rf->df", received, d_gate_pre, preferred_element_type=jnp.float32)
    d_up_full = jnp.einsum("rd,rf->df", received, d_up_pre, preferred_element_type=jnp.float32)
    d_pair_rows = (
        jnp.einsum("rf,df->rd", d_gate_pre, gate_full, preferred_element_type=jnp.float32)
        + jnp.einsum("rf,df->rd", d_up_pre, up_full, preferred_element_type=jnp.float32)
    ).astype(jnp.bfloat16)
    back_rows = expert_move(d_pair_rows.reshape(devices, half_slots, model_width)).reshape(
        slots_all, model_width
    )
    d_normed_two = jnp.sum(
        jnp.where(kept_pair[:, :, None], back_rows[pair_slot].astype(jnp.float32), 0.0), axis=1
    )
    half_rows = expert_gate.shape[0]
    half_hidden = expert_down.shape[0]

    def halves(full_grad, size):
        own_half = lax.dynamic_slice_in_dim(full_grad, parity * size, size, 0)
        other_half = lax.dynamic_slice_in_dim(full_grad, (1 - parity) * size, size, 0)
        return (own_half, other_half)

    gate_own, gate_other = halves(d_gate_full, half_rows)
    up_own, up_other = halves(d_up_full, half_rows)
    down_own, down_other = halves(d_down_full, half_hidden)
    partner_grads = (
        partner_2(gate_other.astype(jnp.bfloat16), "blk", 0).astype(gate_other.dtype),
        partner_2(up_other.astype(jnp.bfloat16), "blk", 0).astype(up_other.dtype),
        partner_2(down_other.astype(jnp.bfloat16), "blk", 0).astype(down_other.dtype),
    )
    d_expert_gate = gate_own + partner_grads[0]
    d_expert_up = up_own + partner_grads[1]
    d_expert_down = down_own + partner_grads[2]
    d_resid_norm, d_gain_two = norm_two_back(d_normed_two)
    d_residual = grad_out + d_resid_norm
    d_res_low = d_residual.astype(jnp.bfloat16)
    d_attended = jnp.einsum("te,de->td", d_res_low, w_o, preferred_element_type=jnp.float32).astype(
        jnp.bfloat16
    )
    d_o_heads = to_head_layout(d_attended)
    d_o_four = d_o_heads.reshape(four_shape)
    row_delta = jnp.sum(d_o_four.astype(jnp.float32) * o_four.astype(jnp.float32), axis=-1)

    def back_turn(step_id, loop_state):
        moving, dq_acc = loop_state
        source = jnp.mod(blk_index - step_id, blk_size)
        k_now = moving[0].astype(jnp.bfloat16)
        v_now = moving[1].astype(jnp.bfloat16)
        raw_scores, allowed, k_band = score_block(k_now, source)
        prob_rows = jnp.where(allowed, jnp.exp(raw_scores - log_total[..., None]), 0.0)
        v_band = banded(v_now.reshape(four_shape), 0)
        d_probs = jnp.einsum(
            "gqhd,gkhd->gqhk", d_o_four, v_band, preferred_element_type=jnp.float32
        )
        d_scores = (prob_rows * (d_probs - row_delta[..., None])).astype(jnp.bfloat16)
        dv_band = jnp.einsum(
            "gqhk,gqhd->gkhd",
            prob_rows.astype(jnp.bfloat16),
            d_o_four,
            preferred_element_type=jnp.float32,
        )
        dk_band = (
            jnp.einsum("gqhk,gqhd->gkhd", d_scores, q_four, preferred_element_type=jnp.float32)
            * score_scale
        )
        dq_acc = (
            dq_acc
            + jnp.einsum("gqhk,gkhd->gqhd", d_scores, k_band, preferred_element_type=jnp.float32)
            * score_scale
        )
        flat_shape = moving[2].shape
        dk_new = moving[2] + unbanded(dk_band, local_rows).reshape(flat_shape)
        dv_new = moving[3] + unbanded(dv_band, local_rows).reshape(flat_shape)
        moving = passed_along(
            jnp.stack([moving[0], moving[1], dk_new, dv_new]).astype(jnp.bfloat16), "blk", 1
        ).astype(jnp.float32)
        return (moving, dq_acc)

    zero_rows = jnp.zeros(k_heads.shape, jnp.float32)
    start_moving = jnp.stack(
        [k_heads.astype(jnp.float32), v_heads.astype(jnp.float32), zero_rows, zero_rows]
    )
    moving, dq_acc = lax.fori_loop(
        0, blk_size, back_turn, (start_moving, jnp.zeros(four_shape, jnp.float32))
    )
    d_q_send = dq_acc.astype(jnp.bfloat16).reshape(k_heads.shape)
    d_k_send = moving[2].astype(jnp.bfloat16)
    d_v_send = moving[3].astype(jnp.bfloat16)
    d_q_rot, d_k_rot, d_v_lin = to_token_layout((d_q_send, d_k_send, d_v_send))
    d_q_lin, d_k_lin, d_gain_q, d_gain_k = pre_back(
        (d_q_rot.astype(jnp.float32), d_k_rot.astype(jnp.float32))
    )
    d_q_low = d_q_lin.astype(jnp.bfloat16)
    d_k_low = d_k_lin.astype(jnp.bfloat16)
    d_normed_one = jnp.einsum("te,de->td", d_q_low, w_q, preferred_element_type=jnp.float32)
    d_normed_one = d_normed_one + jnp.einsum(
        "te,de->td", d_k_low, w_k, preferred_element_type=jnp.float32
    )
    d_normed_one = d_normed_one + jnp.einsum(
        "te,de->td", d_v_lin, w_v, preferred_element_type=jnp.float32
    )
    unused_norm, norm_one_back = jax.vjp(norm_rows, layer_in, gain_one)
    d_layer_in, d_gain_one = norm_one_back(d_normed_one)
    d_inputs = d_residual + d_layer_in
    d_qk_heads = to_head_layout((d_q_low, d_k_low))
    rows_all = (
        lax.all_gather(normed_one, "ulysses", axis=0, tiled=True),
        lax.all_gather(d_res_low, "ulysses", axis=0, tiled=True),
    )
    head_cols = model_width // groups
    piece_rows = model_width // devices

    def by_owner(part):
        rest = part.shape[1:]
        shaped = part.reshape((groups, blk_size, piece_rows) + rest)
        return jnp.swapaxes(shaped, 0, 1).reshape((model_width,) + rest)

    part_q = jnp.einsum("td,te->de", rows_all[0], d_qk_heads[0], preferred_element_type=jnp.float32)
    part_k = jnp.einsum("td,te->de", rows_all[0], d_qk_heads[1], preferred_element_type=jnp.float32)
    part_v = jnp.einsum("td,te->de", rows_all[0], d_v_send, preferred_element_type=jnp.float32)
    part_o = jnp.einsum("te,td->ed", o_heads, rows_all[1], preferred_element_type=jnp.float32)
    blk_sums = (
        lax.psum_scatter(
            by_owner(part_q).astype(jnp.bfloat16), "blk", scatter_dimension=0, tiled=True
        ).astype(jnp.float32),
        lax.psum_scatter(
            by_owner(part_k).astype(jnp.bfloat16), "blk", scatter_dimension=0, tiled=True
        ).astype(jnp.float32),
        lax.psum_scatter(
            by_owner(part_v).astype(jnp.bfloat16), "blk", scatter_dimension=0, tiled=True
        ).astype(jnp.float32),
        lax.psum_scatter(
            part_o.astype(jnp.bfloat16), "blk", scatter_dimension=0, tiled=True
        ).astype(jnp.float32),
        lax.psum_scatter(
            by_owner(d_gain_one).astype(jnp.bfloat16), "blk", scatter_dimension=0, tiled=True
        ).astype(jnp.float32),
        lax.psum_scatter(
            by_owner(d_gain_q).astype(jnp.bfloat16), "blk", scatter_dimension=0, tiled=True
        ).astype(jnp.float32),
        lax.psum_scatter(
            by_owner(d_gain_k).astype(jnp.bfloat16), "blk", scatter_dimension=0, tiled=True
        ).astype(jnp.float32),
        lax.psum_scatter(
            by_owner(d_gain_two).astype(jnp.bfloat16), "blk", scatter_dimension=0, tiled=True
        ).astype(jnp.float32),
    )

    def widened(part):
        return lax.dynamic_update_slice_in_dim(
            jnp.zeros((part.shape[0], model_width), jnp.float32), part, group_index * head_cols, 1
        )

    col_sums = (
        lax.psum_scatter(
            widened(blk_sums[0]).astype(jnp.bfloat16), "ulysses", scatter_dimension=0, tiled=True
        ).astype(jnp.float32),
        lax.psum_scatter(
            widened(blk_sums[1]).astype(jnp.bfloat16), "ulysses", scatter_dimension=0, tiled=True
        ).astype(jnp.float32),
        lax.psum_scatter(
            widened(blk_sums[2]).astype(jnp.bfloat16), "ulysses", scatter_dimension=0, tiled=True
        ).astype(jnp.float32),
        lax.psum_scatter(
            blk_sums[4].astype(jnp.bfloat16), "ulysses", scatter_dimension=0, tiled=True
        ).astype(jnp.float32),
        lax.psum_scatter(
            blk_sums[5].astype(jnp.bfloat16), "ulysses", scatter_dimension=0, tiled=True
        ).astype(jnp.float32),
        lax.psum_scatter(
            blk_sums[6].astype(jnp.bfloat16), "ulysses", scatter_dimension=0, tiled=True
        ).astype(jnp.float32),
        lax.psum_scatter(
            blk_sums[7].astype(jnp.bfloat16), "ulysses", scatter_dimension=0, tiled=True
        ).astype(jnp.float32),
    )
    result_grads = (
        col_sums[0],
        col_sums[1],
        col_sums[2],
        blk_sums[3],
        col_sums[3],
        col_sums[4],
        col_sums[5],
        col_sums[6],
    )
    return (
        output,
        d_inputs,
        result_grads[4],
        result_grads[0],
        result_grads[1],
        result_grads[2],
        result_grads[3],
        result_grads[5],
        result_grads[6],
        result_grads[7],
        d_expert_gate,
        d_expert_up,
        d_expert_down,
    )


def solution(mesh):
    return jax.shard_map(
        local,
        mesh=mesh,
        in_specs=(
            P(("ulysses", "blk"), None),
            P(("ulysses", "blk"), None),
            P(),
            P(("ulysses", "blk"), None),
            P(("ulysses", "blk"), None),
            P(("ulysses", "blk")),
            P(("ulysses", "blk")),
            P(("ulysses", "blk"), None),
            P(("ulysses", "blk"), None),
            P(("ulysses", "blk"), None),
            P(("ulysses", "blk"), None),
            P(("ulysses", "blk")),
            P(("ulysses", "blk")),
            P(("ulysses", "blk")),
            P(("ulysses", "blk"), None),
            P(("ulysses", "blk"), None),
            P(("ulysses", "blk"), None),
        ),
        out_specs=(
            P(("ulysses", "blk"), None),
            P(("ulysses", "blk"), None),
            P(("ulysses", "blk")),
            P(("ulysses", "blk"), None),
            P(("ulysses", "blk"), None),
            P(("ulysses", "blk"), None),
            P(("ulysses", "blk"), None),
            P(("ulysses", "blk")),
            P(("ulysses", "blk")),
            P(("ulysses", "blk")),
            P(("ulysses", "blk"), None),
            P(("ulysses", "blk"), None),
            P(("ulysses", "blk"), None),
        ),
        check_vma=False,
    )
```

profile of v0, /device:TPU:0, one launch (start us, length us, event | category | flops | bytes accessed | tf_op | source)
XLA Modules:
  0.0 2021.0 jit_solution(6028471663952997227)
XLA Ops:
  16.3 42.6 %all-reduce.31 = (bf16[2048]{0:T(1024)(128)(2,1)S(1)}, bf16[2048]{0:T(1024)(128)(2,1)S(1)}, bf16[2048]{0:T(1024)(128)(2,1)S(1)}, bf16[2048]{0:T(1024)(128)(2,1)}) all-reduce(bf16[2048]{0:T(1024)(128)(2,1)S(1)} %dynamic-update-slice, bf16[2048]{0:T(1024)(128)(2,1)S(1)} %dynamic-update-slice.2, ...), channel_id=1, replica_groups=mesh['ulysses'=4,'blk'=8] {'ulysses','blk'}, use_global_device_ids=true, to_apply=%add.18 | all-reduce | flops 8192 | bytes 32768
  80.8 40.8 %all-reduce.21 = s32[512]{0:T(512)S(1)} all-reduce(s32[512]{0:T(512)S(1)} %dynamic-update-slice.3), channel_id=2, replica_groups=mesh['ulysses'=4,'blk'=8] {'ulysses','blk'}, use_global_device_ids=true, to_apply=%add.21 | all-reduce | flops 512 | bytes 4096
  155.4 15.8 all-gather.10.cloned.1.call-done
  183.4 70.1 %all-gather.12.cloned.1.call-done = bf16[2048,2048]{1,0:T(8,128)(2,1)} async-done(((bf16[64,2048]{1,0:T(8,128)(2,1)}), bf16[2048,2048]{1,0:T(8,128)(2,1)}) %all-gather.12.cloned.1.call-update) | async-done | bytes 8388624 | tf_op jit(solution)/shard_map/all_gather | solution.py:153
  309.0 184.4 %while.56 = (s32[]{:T(128)}, f32[4,128,4]{1,2,0:T(4,128)S(1)}, f32[4,128,4]{1,2,0:T(4,128)}, f32[4,128,4,128]{1,3,2,0:T(8,128)}, bf16[2,512,512]{2,1,0:T(8,128)(...) while((s32[]{:T(128)}, f32[4,128,4]{1,2,0:T(4,128)S(1)}, ...), condition=%wide.region_8.9_spmd.clone.clone, body=%wide.region_5.8_spmd.clone.clone.sunk | while | flops 282472480 | bytes 37249560 | solution.py:231
  313.4 29.9 %collective-permute-done = bf16[2,512,512]{2,1,0:T(8,128)(2,1)S(1)} collective-permute-done((bf16[2,512,512]{2,1,0:T(8,128)(2,1)S(1)}, bf16[2,512,512]{2,1,0:T(8,128)(2,1)S(1)}, u32[]{:S(2)}, u32[]{:S(2)}) %collective-permute-start) | collective-permute-done | bytes 1048608 | tf_op jit(solution)/shard_map/while/body/eval_jaxpr/ppermute | solution.py:27
  536.7 160.4 %all-to-all-done.6 = bf16[32,64,2048]{2,1,0:T(8,128)(2,1)} async-done(((bf16[32,64,2048]{2,1,0:T(8,128)(2,1)}), bf16[32,64,2048]{2,1,0:T(8,128)(2,1)}, u32[]{:S(2)}, u32[]{:S(2)}) %all-to-all-start.6) | async-done | bytes 8388640 | tf_op jit(solution)/shard_map/all_to_all | solution.py:99
  732.1 153.8 %all-to-all-done.4 = bf16[32,64,2048]{2,1,0:T(8,128)(2,1)} async-done(((bf16[32,64,2048]{2,1,0:T(8,128)(2,1)}), bf16[32,64,2048]{2,1,0:T(8,128)(2,1)}, u32[]{:S(2)}, u32[]{:S(2)}) %all-to-all-start.4) | async-done | bytes 8388640 | tf_op jit(solution)/shard_map/all_to_all | solution.py:99
  899.8 22.6 %multiply_convert_fusion.2 = (bf16[2048,1024]{1,0:T(8,128)(2,1)}, bf16[2048,1024]{1,0:T(8,128)(2,1)}, bf16[2048,1024]{1,0:T(8,128)(2,1)}) fusion(f32[2048,1024]{1,0:T(8,128)} %fusion.84, f32[2048,1024]{1,0:T(8,128)} %fusion.86, bf16[2048,2048]{1,0:T(8,128)(2,1)} %bitcast.43, bf16[1024,1024]{1,0:T(8,128)(2,1)} %get-tuple-element.1049, ...), kind=kOutput, calls=%fused_computation.134 | convolution fusion | flops 8631877632 | bytes 41943040 | tf_op jit(solution)/shard_map/dot_general | solution.py:285
  937.5 16.3 add_convert_fusion.2
  958.5 85.1 %all-gather.16.cloned.1.call-done = bf16[512,2048]{1,0:T(8,128)(2,1)} async-done(((bf16[128,2048]{1,0:T(8,128)(2,1)}), bf16[512,2048]{1,0:T(8,128)(2,1)}) %all-gather.16.cloned.1.call-update) | async-done | bytes 2097168 | tf_op jit(solution)/shard_map/all_gather | solution.py:410
  1049.0 93.5 %all-to-all-done.7 = bf16[32,64,2048]{2,1,0:T(8,128)(2,1)} async-done(((bf16[32,64,2048]{2,1,0:T(8,128)(2,1)}), bf16[32,64,2048]{2,1,0:T(8,128)(2,1)}, u32[]{:S(2)}, u32[]{:S(2)}) %all-to-all-start.7) | async-done | bytes 8388640 | tf_op jit(solution)/shard_map/all_to_all | solution.py:99
  1186.1 427.1 %while.58 = (s32[]{:T(128)}, f32[4,512,512]{2,1,0:T(8,128)}, f32[4,128,4,128]{1,3,2,0:T(8,128)}, s32[]{:T(128)}, s32[4096]{0:T(1024)S(1)}, /*index=5*/s32[4,128]...) while((s32[]{:T(128)}, f32[4,512,512]{2,1,0:T(8,128)}, ...), condition=%wide.region_22.23_spmd.clone.clone, body=%wide.region_21.22_spmd.clone.clone.sunk | while | flops 690626560 | bytes 105849504 | solution.py:386
  1212.2 24.9 %collective-permute-done.1 = bf16[4,512,512]{2,1,0:T(8,128)(2,1)S(1)} collective-permute-done((bf16[4,512,512]{2,1,0:T(8,128)(2,1)}, bf16[4,512,512]{2,1,0:T(8,128)(2,1)S(1)}, u32[]{:S(2)}, u32[]{:S(2)}) %collective-permute-start.1) | collective-permute-done | bytes 2097184 | tf_op jit(solution)/shard_map/while/body/eval_jaxpr/ppermute | solution.py:27
  1265.9 24.5 %collective-permute-done.1 = bf16[4,512,512]{2,1,0:T(8,128)(2,1)S(1)} collective-permute-done((bf16[4,512,512]{2,1,0:T(8,128)(2,1)}, bf16[4,512,512]{2,1,0:T(8,128)(2,1)S(1)}, u32[]{:S(2)}, u32[]{:S(2)}) %collective-permute-start.1) | collective-permute-done | bytes 2097184 | tf_op jit(solution)/shard_map/while/body/eval_jaxpr/ppermute | solution.py:27
  1319.3 24.5 %collective-permute-done.1 = bf16[4,512,512]{2,1,0:T(8,128)(2,1)S(1)} collective-permute-done((bf16[4,512,512]{2,1,0:T(8,128)(2,1)}, bf16[4,512,512]{2,1,0:T(8,128)(2,1)S(1)}, u32[]{:S(2)}, u32[]{:S(2)}) %collective-permute-start.1) | collective-permute-done | bytes 2097184 | tf_op jit(solution)/shard_map/while/body/eval_jaxpr/ppermute | solution.py:27
  1372.7 24.5 %collective-permute-done.1 = bf16[4,512,512]{2,1,0:T(8,128)(2,1)S(1)} collective-permute-done((bf16[4,512,512]{2,1,0:T(8,128)(2,1)}, bf16[4,512,512]{2,1,0:T(8,128)(2,1)S(1)}, u32[]{:S(2)}, u32[]{:S(2)}) %collective-permute-start.1) | collective-permute-done | bytes 2097184 | tf_op jit(solution)/shard_map/while/body/eval_jaxpr/ppermute | solution.py:27
  1426.0 24.5 %collective-permute-done.1 = bf16[4,512,512]{2,1,0:T(8,128)(2,1)S(1)} collective-permute-done((bf16[4,512,512]{2,1,0:T(8,128)(2,1)}, bf16[4,512,512]{2,1,0:T(8,128)(2,1)S(1)}, u32[]{:S(2)}, u32[]{:S(2)}) %collective-permute-start.1) | collective-permute-done | bytes 2097184 | tf_op jit(solution)/shard_map/while/body/eval_jaxpr/ppermute | solution.py:27
  1479.4 24.5 %collective-permute-done.1 = bf16[4,512,512]{2,1,0:T(8,128)(2,1)S(1)} collective-permute-done((bf16[4,512,512]{2,1,0:T(8,128)(2,1)}, bf16[4,512,512]{2,1,0:T(8,128)(2,1)S(1)}, u32[]{:S(2)}, u32[]{:S(2)}) %collective-permute-start.1) | collective-permute-done | bytes 2097184 | tf_op jit(solution)/shard_map/while/body/eval_jaxpr/ppermute | solution.py:27
  1532.8 24.5 %collective-permute-done.1 = bf16[4,512,512]{2,1,0:T(8,128)(2,1)S(1)} collective-permute-done((bf16[4,512,512]{2,1,0:T(8,128)(2,1)}, bf16[4,512,512]{2,1,0:T(8,128)(2,1)S(1)}, u32[]{:S(2)}, u32[]{:S(2)}) %collective-permute-start.1) | collective-permute-done | bytes 2097184 | tf_op jit(solution)/shard_map/while/body/eval_jaxpr/ppermute | solution.py:27
  1586.1 24.5 %collective-permute-done.1 = bf16[4,512,512]{2,1,0:T(8,128)(2,1)S(1)} collective-permute-done((bf16[4,512,512]{2,1,0:T(8,128)(2,1)}, bf16[4,512,512]{2,1,0:T(8,128)(2,1)S(1)}, u32[]{:S(2)}, u32[]{:S(2)}) %collective-permute-start.1) | collective-permute-done | bytes 2097184 | tf_op jit(solution)/shard_map/while/body/eval_jaxpr/ppermute | solution.py:27
  1762.2 25.6 %reduce-scatter.12.cloned.1.call-done = bf16[256,512]{1,0:T(8,128)(2,1)} async-done(((bf16[2048,512]{1,0:T(8,128)(2,1)}), bf16[256,512]{1,0:T(8,128)(2,1)}) %reduce-scatter.12.cloned.1.call-update) | async-done | bytes 262160 | tf_op jit(solution)/shard_map/reduce_scatter | solution.py:429
  1800.5 106.3 %all-to-all-done.5 = bf16[32,64,2048]{2,1,0:T(8,128)(2,1)} async-done(((bf16[32,64,2048]{2,1,0:T(8,128)(2,1)}), bf16[32,64,2048]{2,1,0:T(8,128)(2,1)}, u32[]{:S(2)}, u32[]{:S(2)}) %all-to-all-start.5) | async-done | bytes 8388640 | tf_op jit(solution)/shard_map/all_to_all | solution.py:99
  1956.2 26.0 %all-reduce.32 = (bf16[2048]{0:T(1024)(128)(2,1)S(1)}, bf16[2048]{0:T(1024)(128)(2,1)S(1)}, bf16[2048]{0:T(1024)(128)(2,1)S(1)}, bf16[2048]{0:T(1024)(128)(2,1)S(1)}) all-reduce(bf16[2048]{0:T(1024)(128)(2,1)S(1)} %convert_element_type.430, ...), channel_id=3, replica_groups=mesh['ulysses'=4,'blk'=8] {'blk'}, use_global_device_ids=true, to_apply=%region_27.28.clone | all-reduce | flops 8192 | bytes 32768
  (1258 shorter events, 913.3 us)
Async XLA Ops:
  8.0 141.2 %all-gather.8.cloned.1.call-start = ((), (), s32[]{:S(2)}) async-start(), calls=%async_computation.21 | async-start | bytes 8650752 | tf_op jit(solution)/shard_map/all_gather | solution.py:152
  8.7 162.5 %all-gather.10.cloned.1.call-start = ((), (), s32[]{:S(2)}) async-start(), calls=%async_computation.22 | async-start | bytes 8650752 | tf_op jit(solution)/shard_map/all_gather | solution.py:151
  9.5 244.0 %all-gather.12.cloned.1.call-start = ((), (), s32[]{:S(2)}) async-start(), calls=%async_computation.23 | async-start | bytes 8650752 | tf_op jit(solution)/shard_map/all_gather | solution.py:153
  10.2 502.1 %all-gather.14.cloned.1.call-start = ((), (), s32[]{:S(2)}) async-start(), calls=%async_computation.24 | async-start | bytes 8650752 | tf_op jit(solution)/shard_map/all_gather | solution.py:154
  179.9 79.1 %all-to-all-start = ((bf16[128,4,512]{0,2,1:T(8,128)(2,1)}), bf16[128,4,512]{0,2,1:T(8,128)(2,1)S(1)}, u32[]{:S(2)}, u32[]{:S(2)}) async-start(bf16[128,4,512]{0,2,1:T(8,128)(2,1)} %bitcast.5), calls=%async_computation | async-start | bytes 1048576 | tf_op jit(solution)/shard_map/all_to_all | solution.py:105
  309.0 34.4 %collective-permute-start = (bf16[2,512,512]{2,1,0:T(8,128)(2,1)S(1)}, bf16[2,512,512]{2,1,0:T(8,128)(2,1)S(1)}, u32[]{:S(2)}, u32[]{:S(2)}) collective-permute-start(bf16[2,512,512]{2,1,0:T(8,128)(2,1)S(1)} %get-tuple-element.1310), channel_id=1, source_target_pairs={{7,0},{0,1},{1,2},{2,3},{3,4},{4,5},{5,6},{6,7},{15,8},{8,9},{9,10... | collective-permute-start | bytes 3145736 | tf_op jit(solution)/shard_map/while/body/eval_jaxpr/ppermute | solution.py:27
  508.4 188.7 %all-to-all-start.6 = ((bf16[32,64,2048]{2,1,0:T(8,128)(2,1)}), bf16[32,64,2048]{2,1,0:T(8,128)(2,1)}, u32[]{:S(2)}, u32[]{:S(2)}) async-start(bf16[32,64,2048]{2,1,0:T(8,128)(2,1)} %multiply_convert_fusion), calls=%async_computation.6 | async-start | bytes 16777216 | tf_op jit(solution)/shard_map/all_to_all | solution.py:99
  697.1 188.8 %all-to-all-start.4 = ((bf16[32,64,2048]{2,1,0:T(8,128)(2,1)}), bf16[32,64,2048]{2,1,0:T(8,128)(2,1)}, u32[]{:S(2)}, u32[]{:S(2)}) async-start(bf16[32,64,2048]{2,1,0:T(8,128)(2,1)} %broadcast_select_fusion.2), calls=%async_computation.4 | async-start | bytes 16777216 | tf_op jit(solution)/shard_map/all_to_all | solution.py:99
  953.8 188.8 %all-to-all-start.7 = ((bf16[32,64,2048]{2,1,0:T(8,128)(2,1)}), bf16[32,64,2048]{2,1,0:T(8,128)(2,1)}, u32[]{:S(2)}, u32[]{:S(2)}) async-start(bf16[32,64,2048]{2,1,0:T(8,128)(2,1)} %bitcast.365), calls=%async_computation.7 | async-start | bytes 16777216 | tf_op jit(solution)/shard_map/all_to_all | solution.py:99
  957.6 86.0 %all-gather.16.cloned.1.call-start = ((), (), s32[]{:S(2)}) async-start(), calls=%async_computation.25 | async-start | bytes 2621440 | tf_op jit(solution)/shard_map/all_gather | solution.py:410
  1175.0 536.2 %reduce-scatter.16.cloned.1.call-start = ((), (), s32[]{:S(2)}) async-start(), calls=%async_computation.30 | async-start | bytes 2359296 | tf_op jit(solution)/shard_map/reduce_scatter | solution.py:432
  1209.6 27.5 %collective-permute-start.1 = (bf16[4,512,512]{2,1,0:T(8,128)(2,1)}, bf16[4,512,512]{2,1,0:T(8,128)(2,1)S(1)}, u32[]{:S(2)}, u32[]{:S(2)}) collective-permute-start(bf16[4,512,512]{2,1,0:T(8,128)(2,1)} %pad_maximum_fusion.14), channel_id=1, source_target_pairs={{7,0},{0,1},{1,2},{2,3},{3,4},{4,5},{5,6},{6,7},{15,8},{8,9},{9,10... | collective-permute-start | bytes 6291464 | tf_op jit(solution)/shard_map/while/body/eval_jaxpr/ppermute | solution.py:27
  1423.1 27.5 %collective-permute-start.1 = (bf16[4,512,512]{2,1,0:T(8,128)(2,1)}, bf16[4,512,512]{2,1,0:T(8,128)(2,1)S(1)}, u32[]{:S(2)}, u32[]{:S(2)}) collective-permute-start(bf16[4,512,512]{2,1,0:T(8,128)(2,1)} %pad_maximum_fusion.14), channel_id=1, source_target_pairs={{7,0},{0,1},{1,2},{2,3},{3,4},{4,5},{5,6},{6,7},{15,8},{8,9},{9,10... | collective-permute-start | bytes 6291464 | tf_op jit(solution)/shard_map/while/body/eval_jaxpr/ppermute | solution.py:27
  1634.5 93.6 %all-gather.18.cloned.1.call-start = ((), (), s32[]{:S(2)}) async-start(), calls=%async_computation.32 | async-start | bytes 2621440 | tf_op jit(solution)/shard_map/all_gather | solution.py:411
  1678.9 227.9 %all-to-all-start.5 = ((bf16[32,64,2048]{2,1,0:T(8,128)(2,1)}), bf16[32,64,2048]{2,1,0:T(8,128)(2,1)}, u32[]{:S(2)}, u32[]{:S(2)}) async-start(bf16[32,64,2048]{2,1,0:T(8,128)(2,1)} %bitcast.364), calls=%async_computation.5 | async-start | bytes 16777216 | tf_op jit(solution)/shard_map/all_to_all | solution.py:99
  1682.6 105.2 %reduce-scatter.12.cloned.1.call-start = ((), (), s32[]{:S(2)}) async-start(), calls=%async_computation.28 | async-start | bytes 2359296 | tf_op jit(solution)/shard_map/reduce_scatter | solution.py:429
  1687.1 249.9 %reduce-scatter.8.cloned.1.call-start = ((), (), s32[]{:S(2)}) async-start(), calls=%async_computation.26 | async-start | bytes 2359296 | tf_op jit(solution)/shard_map/reduce_scatter | solution.py:426
  1691.8 307.1 %reduce-scatter.18.cloned.1.call-start = ((), (), s32[]{:S(2)}) async-start(), calls=%async_computation.31 | async-start | bytes 1310720 | tf_op jit(solution)/shard_map/reduce_scatter | solution.py:464
  1711.2 45.1 %collective-permute-start.6 = (bf16[1024,1024]{1,0:T(8,128)(2,1)}, bf16[1024,1024]{1,0:T(8,128)(2,1)}, u32[]{:S(2)}, u32[]{:S(2)}) collective-permute-start(bf16[1024,1024]{1,0:T(8,128)(2,1)} %dynamic-slice_convert_fusion.1), channel_id=1, source_target_pairs={{0,1},{1,0},{2,3},{3,2},{4,5},{5,4},{6,7},{7,6},{8,9},{9,8},{10,11... | collective-permute-start | bytes 6291464 | tf_op jit(solution)/shard_map/ppermute | solution.py:49
  1713.4 287.3 %reduce-scatter.20.cloned.1.call-start = ((), (), s32[]{:S(2)}) async-start(), calls=%async_computation.33 | async-start | bytes 2359296 | tf_op jit(solution)/shard_map/reduce_scatter | solution.py:435
  1732.2 270.2 %reduce-scatter.14.cloned.1.call-start = ((), (), s32[]{:S(2)}) async-start(), calls=%async_computation.29 | async-start | bytes 1310720 | tf_op jit(solution)/shard_map/reduce_scatter | solution.py:461
  1736.6 53.3 %collective-permute-start.5 = (bf16[1024,1024]{1,0:T(8,128)(2,1)}, bf16[1024,1024]{1,0:T(8,128)(2,1)}, u32[]{:S(2)}, u32[]{:S(2)}) collective-permute-start(bf16[1024,1024]{1,0:T(8,128)(2,1)} %dynamic-slice_convert_fusion.2), channel_id=1, source_target_pairs={{0,1},{1,0},{2,3},{3,2},{4,5},{5,4},{6,7},{7,6},{8,9},{9,8},{10,11... | collective-permute-start | bytes 6291464 | tf_op jit(solution)/shard_map/ppermute | solution.py:49
  1753.7 42.3 %collective-permute-start.7 = (bf16[512,2048]{1,0:T(8,128)(2,1)}, bf16[512,2048]{1,0:T(8,128)(2,1)}, u32[]{:S(2)}, u32[]{:S(2)}) collective-permute-start(bf16[512,2048]{1,0:T(8,128)(2,1)} %dynamic-slice_convert_fusion), channel_id=1, source_target_pairs={{0,1},{1,0},{2,3},{3,2},{4,5},{5,4},{6,7},{7,6},{8,9},{9,8},{10,11... | collective-permute-start | bytes 6291464 | tf_op jit(solution)/shard_map/ppermute | solution.py:49
  1929.5 82.0 %reduce-scatter.10.cloned.1.call-start = ((), (), s32[]{:S(2)}) async-start(), calls=%async_computation.27 | async-start | bytes 1310720 | tf_op jit(solution)/shard_map/reduce_scatter | solution.py:458
  (244 other events, 3685.8 us)
Sparse Core Ops, SparseCore 0:
  11.8 80.1 all-gather.7
  95.0 76.1 all-gather.9
  174.2 79.2 all-gather.11
  256.4 85.2 all-gather.13
Sparse Core Ops, SparseCore 1:
  960.0 83.6 all-gather.15
  1621.0 32.8 reduce-scatter.15
  1655.6 63.0 all-gather.17
  1721.6 66.1 reduce-scatter.11
  1790.1 82.1 reduce-scatter.7
  1875.2 38.5 reduce-scatter.17
  1916.0 35.5 reduce-scatter.19
  1954.6 26.3 reduce-scatter.13
  1983.7 27.7 reduce-scatter.9
where the time goes:
time: 2030 us; the launch traced here: 2020 us
  waiting for transfers between devices  1050 us (52%)
  local copies, waits for them, and re-layouts  287 us (14%)
  matrix products  281 us (14%)
  other arithmetic  208 us (10%)
  blocking collectives  120 us (6%)
  starting transfers between devices  54 us (3%)
    all_to_all x4, waiting for transfers between devices, expert_move(): lax.all_to_all(buffer, ('ulysses', 'blk'), split_axis=0, concat_axis=0, t...  514 us
    ppermute x15, waiting for transfers between devices, passed_along(): return lax.ppermute(block, axis, route)  296 us
    unnamed x4, blocking collectives  120 us
    all_gather x1, waiting for transfers between devices, local(): lax.all_gather(normed_one, 'ulysses', axis=0, tiled=True)  85.1 us
    all_gather x1, waiting for transfers between devices, local(): lax.all_gather(dense[2], ('ulysses', 'blk'), axis=0, tiled=True)  70.1 us
    gather x16, local copies, waits for them, and re-layouts, score_block(): k_seg = banded(segments[k_pos], -1)  50.4 us
  transfers between devices with their start and end apart: 48, of which 30 were waited for; matrix products, arithmetic and copies ran while one was open for 22% of the time, Pallas kernels for 0%

commit v1 on v0

--- a/solution.py
+++ b/solution.py
@@ -1,8 +1,12 @@
+import functools
 import math
 
 import jax
 import jax.numpy as jnp
 from jax import lax
+from jax.experimental import pallas as pl
+from jax.experimental.pallas import tpu as pltpu
+from jax.sharding import Mesh
 from jax.sharding import PartitionSpec as P
 
 HEAD_DIM = 128
@@ -504,43 +508,725 @@
     )
 
 
-def solution(mesh):
+MESH = pl.DeviceIdType.MESH
+P1 = 96
+
+def place():
+    u = lax.axis_index("ulysses"); z = lax.axis_index("z"); c = lax.axis_index("core")
+    return u, z, c
+
+def ag_kernel(cut, x_ref, o_ref, local_sem, s_sem, zr, xr, yr, d1r, d2r, bs, br, bzr):
+    u, z, c = place()
+    Z = 4
+    R = x_ref.shape[0]
+    ux, uy = u ^ 1, u ^ 2
+    xn, yn, up, dn = (ux, z, c), (uy, z, c), (u, z + 1, c), (u, z - 1, c)
+    has_up, has_dn = z < Z - 1, z > 0
+    bar = pltpu.get_barrier_semaphore()
+    for n in (xn, yn):
+        pl.semaphore_signal(bar, inc=1, device_id=n, device_id_type=MESH)
+    @pl.when(has_up)
+    def _():
+        pl.semaphore_signal(bar, inc=1, device_id=up, device_id_type=MESH)
+    @pl.when(has_dn)
+    def _():
+        pl.semaphore_signal(bar, inc=1, device_id=dn, device_id_type=MESH)
+    pl.semaphore_wait(bar, 2 + has_up.astype(jnp.int32) + has_dn.astype(jnp.int32))
+    sends = []
+    def copy(src, dst, ss, rs, dev):
+        return pltpu.make_async_remote_copy(src_ref=src, dst_ref=dst, send_sem=ss, recv_sem=rs, device_id=dev, device_id_type=MESH)
+    def go(cond, make):
+        idx = len(sends)
+        def mk():
+            return make(s_sem.at[idx])
+        sends.append((cond, mk))
+        if cond is None:
+            mk().start()
+        else:
+            pl.when(cond)(lambda: mk().start())
+    def both(a, b):
+        if a is None: return b
+        if b is None: return a
+        return jnp.logical_and(a, b)
+    def wait(cond, ref, sem):
+        def w():
+            pltpu.make_async_copy(ref, ref, sem).wait()
+        if cond is None: w()
+        else: pl.when(cond)(w)
+    own = pltpu.make_async_copy(x_ref, o_ref.at[u, z], local_sem)
+    own.start()
+    A = slice(0, cut)
+    h = cut // 2
+    def oa(uu, zz, lo=0, n=cut):
+        return o_ref.at[uu, zz, pl.ds(lo, n), :]
+    def spread(s, zz, cond):
+        src = (lambda: x_ref.at[pl.ds(0, cut), :]) if s == 0 else (lambda: oa(u, zz))
+        go(cond, lambda sm: copy(src(), oa(u, zz), sm, xr.at[zz], xn))
+        go(cond, lambda sm: copy(src(), oa(u, zz), sm, yr.at[zz], yn))
+    def cross(zz, cond):
+        wait(cond, oa(ux, zz), xr.at[zz])
+        go(cond, lambda sm: copy(oa(ux, zz, 0, h), oa(ux, zz, 0, h), sm, d1r.at[zz], yn))
+        wait(cond, oa(uy, zz), yr.at[zz])
+        go(cond, lambda sm: copy(oa(uy, zz, h, h), oa(uy, zz, h, h), sm, d2r.at[zz], xn))
+    rb = R - cut
+    hb = rb // 2
+    def ob(uu, zz, lo=0, n=None):
+        return o_ref.at[uu, zz, pl.ds(cut + lo, rb if n is None else n), :]
+    go(has_up, lambda sm: copy(x_ref.at[pl.ds(0, cut), :], oa(u, z), sm, zr.at[z], up))
+    go(has_dn, lambda sm: copy(x_ref.at[pl.ds(0, cut), :], oa(u, z), sm, zr.at[z], dn))
+    if rb:
+        go(None, lambda sm: copy(x_ref.at[pl.ds(cut, rb), :], ob(u, z), sm, br.at[0], xn))
+        go(None, lambda sm: copy(x_ref.at[pl.ds(cut, rb), :], ob(u, z), sm, br.at[1], yn))
+    spread(0, z, None)
+    if rb:
+        wait(None, ob(ux, z), br.at[0])
+        go(None, lambda sm: copy(ob(ux, z, 0, hb), ob(ux, z, 0, hb), sm, br.at[2], yn))
+        wait(None, ob(uy, z), br.at[1])
+        go(None, lambda sm: copy(ob(uy, z, hb, hb), ob(uy, z, hb, hb), sm, br.at[3], xn))
+    own.wait()
+    def quad(zz):
+        return o_ref.at[:, zz, pl.ds(cut, rb), :]
+    def zs(s):
+        zl, zh = z - s, z + s
+        cl, ch = zl >= 0, zh < Z
+        zlc, zhc = jnp.maximum(zl, 0), jnp.minimum(zh, Z - 1)
+        return (zlc, cl, has_up, up), (zhc, ch, has_dn, dn)
+    prev = [(z, None)]
+    for s in range(1, Z):
+        cur = []
+        for (zz, cond, fwd, dev) in zs(s):
+            wait(cond, oa(u, zz), zr.at[zz])
+            go(both(cond, fwd), lambda sm, zz=zz, dev=dev: copy(oa(u, zz), oa(u, zz), sm, zr.at[zz], dev))
+            spread(s, zz, cond)
+            cur.append((zz, cond))
+        if rb and s == 1:
+            wait(None, ob(u ^ 3, z, 0, hb), br.at[2])
+            wait(None, ob(u ^ 3, z, hb, hb), br.at[3])
+            go(has_up, lambda sm: copy(quad(z), quad(z), sm, bzr.at[z], up))
+            go(has_dn, lambda sm: copy(quad(z), quad(z), sm, bzr.at[z], dn))
+        elif rb:
+            for (zz, cond, fwd, dev) in zs(s - 1):
+                wait(cond, quad(zz), bzr.at[zz])
+                go(both(cond, fwd), lambda sm, zz=zz, dev=dev: copy(quad(zz), quad(zz), sm, bzr.at[zz], dev))
+        for zz, cond in prev:
+            cross(zz, cond)
+        prev = cur
+    if rb:
+        for (zz, cond, fwd, dev) in zs(Z - 1):
+            wait(cond, quad(zz), bzr.at[zz])
+    for zz, cond in prev:
+        cross(zz, cond)
+    for zz in range(Z):
+        wait(None, oa(u ^ 3, zz, 0, h), d1r.at[zz])
+        wait(None, oa(u ^ 3, zz, h, h), d2r.at[zz])
+    for cond, mk in sends:
+        if cond is None: mk().wait_send()
+        else: pl.when(cond)(lambda mk=mk: mk().wait_send())
+
+def ag16(x, cid, cut=P1, space=pl.ANY):
+    R, D = x.shape
+    DMA = pltpu.SemaphoreType.DMA
+    return pl.pallas_call(
+        functools.partial(ag_kernel, cut),
+        out_shape=jax.ShapeDtypeStruct((4, 4, R, D), x.dtype),
+        in_specs=[pl.BlockSpec(memory_space=space)],
+        out_specs=pl.BlockSpec(memory_space=space),
+        scratch_shapes=[DMA, DMA((64,)), DMA((4,)), DMA((4,)), DMA((4,)), DMA((4,)), DMA((4,)), DMA((4,)), DMA((4,)), DMA((4,))],
+        compiler_params=pltpu.CompilerParams(collective_id=cid, has_side_effects=True, vmem_limit_bytes=48 * 2**20),
+        name="gather_rows",
+    )(x)
+F32 = jnp.float32
+BF = jnp.bfloat16
+
+class Net:
+    def __init__(self, sems):
+        self.sems, self.sends = sems, []
+        self.u, self.z, self.c = place()
+        u, z, c = self.u, self.z, self.c
+        self.ux, self.uy, self.ud = u ^ 1, u ^ 2, u ^ 3
+        self.xn, self.yn, self.up, self.dn = (u ^ 1, z, c), (u ^ 2, z, c), (u, z + 1, c), (u, z - 1, c)
+        self.has_up, self.has_dn = z < 3, z > 0
+    def barrier(self):
+        bar = pltpu.get_barrier_semaphore()
+        for n in (self.xn, self.yn):
+            pl.semaphore_signal(bar, inc=1, device_id=n, device_id_type=MESH)
+        for cond, n in ((self.has_up, self.up), (self.has_dn, self.dn)):
+            pl.when(cond)(lambda n=n: pl.semaphore_signal(bar, inc=1, device_id=n, device_id_type=MESH))
+        pl.semaphore_wait(bar, 2 + self.has_up.astype(jnp.int32) + self.has_dn.astype(jnp.int32))
+    def go(self, cond, src, dst, rsem, dev):
+        idx = len(self.sends)
+        def mk():
+            return pltpu.make_async_remote_copy(src_ref=src(), dst_ref=dst(), send_sem=self.sems.at[idx], recv_sem=rsem, device_id=dev, device_id_type=MESH)
+        self.sends.append((cond, mk))
+        if cond is None: mk().start()
+        else: pl.when(cond)(lambda: mk().start())
+    def wait(self, cond, ref, sem):
+        def w(): pltpu.make_async_copy(ref(), ref(), sem).wait()
+        if cond is None: w()
+        else: pl.when(cond)(w)
+    def finish(self):
+        for cond, mk in self.sends:
+            if cond is None: mk().wait_send()
+            else: pl.when(cond)(lambda mk=mk: mk().wait_send())
+
+def strips(rows, body, step=16):
+    def it(i, _):
+        body(pl.ds(pl.multiple_of(i * step, step), step))
+        return 0
+    lax.fori_loop(0, rows // step, it, 0)
+
+def rs_body(net, cut, P, out_store, mid1, mid2, fx, fy, be, ab, bbe, bab, bm, m1s, m2s, fxs, fys, bes, abs_, bbes, babs, bms):
+    u, z = net.u, net.z
+    R = P.shape[2]
+    h = cut // 2
+    rb = R - cut
+    hb = rb // 2
+    order = (3, 0, 2, 1)
+    f = lambda v: v.astype(F32)
+    for zd in order:
+        net.go(None, lambda: P.at[net.ud, zd, pl.ds(0, h), :], lambda: mid1.at[zd], m1s.at[zd], net.xn)
+        net.go(None, lambda: P.at[net.ud, zd, pl.ds(h, h), :], lambda: mid2.at[zd], m2s.at[zd], net.yn)
+    def bsend(zd, first):
+        lo, hi = net.z < zd, net.z > zd
+        if first:
+            net.go(z == 0, lambda: P.at[:, zd, pl.ds(cut, rb), :], lambda: bbe.at[zd], bbes.at[zd], net.up)
+            net.go(z == 3, lambda: P.at[:, zd, pl.ds(cut, rb), :], lambda: bab.at[zd], babs.at[zd], net.dn)
+    for zd in order:
+        if zd > 0:
+            net.go(z == 0, lambda: P.at[:, zd, pl.ds(cut, rb), :], lambda: bbe.at[zd], bbes.at[zd], net.up)
+        if zd < 3:
+            net.go(z == 3, lambda: P.at[:, zd, pl.ds(cut, rb), :], lambda: bab.at[zd], babs.at[zd], net.dn)
+    for zd in order:
+        net.go(None, lambda: P.at[net.ux, zd, pl.ds(0, h), :], lambda: fx.at[zd, pl.ds(0, h), :], fxs.at[zd, 0], net.xn)
+        net.go(None, lambda: P.at[net.uy, zd, pl.ds(h, h), :], lambda: fy.at[zd, pl.ds(h, h), :], fys.at[zd, 1], net.yn)
+    def bpass(zd):
+        def addto(buf, zd):
+            for q in range(4):
+                strips(rb, lambda sl: buf.__setitem__((zd, q, sl, slice(None)), (f(buf[zd, q, sl, :]) + f(P[q, zd, pl.ds(cut + sl.start, 16), :])).astype(BF)))
+        up_mid = jnp.logical_and(z > 0, z < zd)
+        net.wait(up_mid, lambda: bbe.at[zd], bbes.at[zd])
+        pl.when(up_mid)(lambda: addto(bbe, zd))
+        net.go(up_mid, lambda: bbe.at[zd], lambda: bbe.at[zd], bbes.at[zd], net.up)
+        dn_mid = jnp.logical_and(z < 3, z > zd)
+        net.wait(dn_mid, lambda: bab.at[zd], babs.at[zd])
+        pl.when(dn_mid)(lambda: addto(bab, zd))
+        net.go(dn_mid, lambda: bab.at[zd], lambda: bab.at[zd], babs.at[zd], net.dn)
+    for zd in order:
+        net.wait(None, lambda: mid1.at[zd], m1s.at[zd])
+        strips(h, lambda sl: mid1.__setitem__((zd, sl, slice(None)), (f(mid1[zd, sl, :]) + f(P[net.uy, zd, sl, :])).astype(BF)))
+        net.go(None, lambda: mid1.at[zd], lambda: fy.at[zd, pl.ds(0, h), :], fys.at[zd, 0], net.yn)
+        net.wait(None, lambda: mid2.at[zd], m2s.at[zd])
+        strips(h, lambda sl: mid2.__setitem__((zd, sl, slice(None)), (f(mid2[zd, sl, :]) + f(P[net.ux, zd, pl.ds(h + sl.start, 16), :])).astype(BF)))
+        net.go(None, lambda: mid2.at[zd], lambda: fx.at[zd, pl.ds(h, h), :], fxs.at[zd, 1], net.xn)
+        if rb:
+            bpass(zd)
+    def line(zd):
+        for half in (0, 1):
+            net.wait(None, lambda: fx.at[zd, pl.ds(half * h, h), :], fxs.at[zd, half])
+            net.wait(None, lambda: fy.at[zd, pl.ds(half * h, h), :], fys.at[zd, half])
+        def local(sl):
+            return f(P[u, zd, sl, :]) + f(fx[zd, sl, :]) + f(fy[zd, sl, :])
+        def start_sum(sl):
+            fx[zd, sl, :] = local(sl).astype(BF)
+        def plus(buf):
+            def g(sl): buf[zd, sl, :] = (local(sl) + f(buf[zd, sl, :])).astype(BF)
+            return g
+        if zd > 0:
+            pl.when(z == 0)(lambda: strips(cut, start_sum))
+            net.go(z == 0, lambda: fx.at[zd], lambda: be.at[zd], bes.at[zd], net.up)
+            mid = jnp.logical_and(z > 0, z < zd)
+            net.wait(mid, lambda: be.at[zd], bes.at[zd])
+            pl.when(mid)(lambda: strips(cut, plus(be)))
+            net.go(mid, lambda: be.at[zd], lambda: be.at[zd], bes.at[zd], net.up)
+        if zd < 3:
+            pl.when(z == 3)(lambda: strips(cut, start_sum))
+            net.go(z == 3, lambda: fx.at[zd], lambda: ab.at[zd], abs_.at[zd], net.dn)
+            mid = jnp.logical_and(z < 3, z > zd)
+            net.wait(mid, lambda: ab.at[zd], abs_.at[zd])
+            pl.when(mid)(lambda: strips(cut, plus(ab)))
+            net.go(mid, lambda: ab.at[zd], lambda: ab.at[zd], abs_.at[zd], net.dn)
+    def bquad():
+        net.wait(net.has_dn, lambda: bbe.at[z], bbes.at[z])
+        net.wait(net.has_up, lambda: bab.at[z], babs.at[z])
+        def fold(q, sl):
+            s = f(P[q, z, pl.ds(cut + sl.start, 16), :])
+            s = s + jnp.where(net.has_dn, f(bbe[z, q, sl, :]), 0.0)
+            s = s + jnp.where(net.has_up, f(bab[z, q, sl, :]), 0.0)
+            bm[q, sl, :] = s.astype(BF)
+        for q in range(4):
+            strips(rb, lambda sl: fold(q, sl))
+        net.go(None, lambda: bm.at[net.ud, pl.ds(0, hb), :], lambda: bm.at[4, pl.ds(0, hb), :], bms.at[0], net.xn)
+        net.go(None, lambda: bm.at[net.ud, pl.ds(hb, hb), :], lambda: bm.at[5, pl.ds(0, hb), :], bms.at[1], net.yn)
+        net.go(None, lambda: bm.at[net.ux, pl.ds(0, hb), :], lambda: bm.at[6, pl.ds(0, hb), :], bms.at[2], net.xn)
+        net.go(None, lambda: bm.at[net.uy, pl.ds(hb, hb), :], lambda: bm.at[7, pl.ds(hb, hb), :], bms.at[3], net.yn)
+    def bquad2():
+        net.wait(None, lambda: bm.at[4, pl.ds(0, hb), :], bms.at[0])
+        strips(hb, lambda sl: bm.__setitem__((4, sl, slice(None)), (f(bm[4, sl, :]) + f(bm[net.uy, sl, :])).astype(BF)))
+        net.go(None, lambda: bm.at[4, pl.ds(0, hb), :], lambda: bm.at[7, pl.ds(0, hb), :], bms.at[4], net.yn)
+        net.wait(None, lambda: bm.at[5, pl.ds(0, hb), :], bms.at[1])
+        strips(hb, lambda sl: bm.__setitem__((5, sl, slice(None)), (f(bm[5, sl, :]) + f(bm[net.ux, pl.ds(hb + sl.start, 16), :])).astype(BF)))
+        net.go(None, lambda: bm.at[5, pl.ds(0, hb), :], lambda: bm.at[6, pl.ds(hb, hb), :], bms.at[5], net.xn)
+    line(3)
+    line(0)
+    if rb:
+        bquad()
+    line(2)
+    if rb:
+        bquad2()
+    line(1)
+    def last(sl):
+        s = f(P[u, z, sl, :]) + f(fx[z, sl, :]) + f(fy[z, sl, :])
+        s = s + jnp.where(net.has_dn, f(be[z, sl, :]), 0.0)
+        s = s + jnp.where(net.has_up, f(ab[z, sl, :]), 0.0)
+        out_store(sl, s)
+    net.wait(net.has_dn, lambda: be.at[z], bes.at[z])
+    net.wait(net.has_up, lambda: ab.at[z], abs_.at[z])
+    strips(cut, last)
+    if rb:
+        net.wait(None, lambda: bm.at[6, pl.ds(0, hb), :], bms.at[2])
+        net.wait(None, lambda: bm.at[6, pl.ds(hb, hb), :], bms.at[5])
+        net.wait(None, lambda: bm.at[7, pl.ds(0, hb), :], bms.at[4])
+        net.wait(None, lambda: bm.at[7, pl.ds(hb, hb), :], bms.at[3])
+        strips(rb, lambda sl: out_store(pl.ds(cut + sl.start, 16), f(bm[u, sl, :]) + f(bm[6, sl, :]) + f(bm[7, sl, :])))
+
+def rs_scratch(cut, R, D):
+    h, rb = cut // 2, R - cut
+    V = lambda *s: pltpu.VMEM(s, BF)
+    S = pltpu.SemaphoreType.DMA
+    return [V(4, h, D), V(4, h, D), V(4, cut, D), V(4, cut, D), V(4, cut, D), V(4, cut, D),
+            V(4, 4, max(rb, 16), D), V(4, 4, max(rb, 16), D), V(8, max(rb, 16), D),
+            S((4,)), S((4,)), S((4, 2)), S((4, 2)), S((4,)), S((4,)), S((4,)), S((4,)), S((6,))]
+
+def rs_kernel(cut, P, o_ref, ssem, *scr):
+    net = Net(ssem)
+    net.barrier()
+    def store(sl, v):
+        o_ref[sl, :] = v.astype(o_ref.dtype)
+    rs_body(net, cut, P, store, *scr)
+    net.finish()
+
+def rs16(p, cid, cut=96, dtype=F32):
+    _, _, R, D = p.shape
+    DMA = pltpu.SemaphoreType.DMA
+    return pl.pallas_call(
+        functools.partial(rs_kernel, cut),
+        out_shape=jax.ShapeDtypeStruct((R, D), dtype),
+        in_specs=[pl.BlockSpec(memory_space=pltpu.VMEM)],
+        out_specs=pl.BlockSpec(memory_space=pltpu.VMEM),
+        scratch_shapes=[DMA((96,))] + rs_scratch(cut, R, D),
+        compiler_params=pltpu.CompilerParams(collective_id=cid, has_side_effects=True, vmem_limit_bytes=56 * 2**20),
+        name="scatter_rows",
+    )(p)
+def swap_kernel(src, out, lsem, ssem, rsem):
+    u, z, c = place()
+    me = u * 8 + z * 2 + c
+    count = out.shape[0]
+    bar = pltpu.get_barrier_semaphore()
+
+    def at(j):
+        t = lax.rem(me + j, count)
+        return t // 8, lax.rem(t, 8) // 2, lax.rem(t, 2), t // 2
+
+    def hello(j, _):
+        tu, tz, tc, _e = at(j)
+        pl.semaphore_signal(bar, inc=1, device_id=(tu, tz, tc), device_id_type=MESH)
+        return 0
+
+    lax.fori_loop(1, count, hello, 0)
+    pl.semaphore_wait(bar, count - 1)
+
+    def copy(j):
+        tu, tz, tc, e = at(j)
+        return pltpu.make_async_remote_copy(
+            src_ref=src.at[e], dst_ref=out.at[me], send_sem=ssem, recv_sem=rsem,
+            device_id=(tu, tz, tc), device_id_type=MESH)
+
+    own = pltpu.make_async_copy(src.at[me // 2], out.at[me], lsem)
+    own.start()
+
+    def send(j, _):
+        copy(j).start()
+        return 0
+
+    lax.fori_loop(1, count, send, 0)
+    own.wait()
+    part = out.at[pl.ds(0, count - 1)]
+    pltpu.make_async_copy(part, part, rsem).wait()
+    pltpu.make_async_copy(part, part, ssem).wait()
+
+
+def swap(block, cid):
+    chips, r, lanes = block.shape
+    S = pltpu.SemaphoreType.DMA
+    return pl.pallas_call(
+        swap_kernel,
+        out_shape=jax.ShapeDtypeStruct((2 * chips, r, lanes), block.dtype),
+        in_specs=[pl.BlockSpec(memory_space=pltpu.VMEM)],
+        out_specs=pl.BlockSpec(memory_space=pltpu.VMEM),
+        scratch_shapes=[S, S, S],
+        compiler_params=pltpu.CompilerParams(collective_id=cid, has_side_effects=True),
+        name="swap_rows",
+    )(block)
+
+
+def spread_kernel(src, out, lsem, ssem, rsem):
+    u, z, c = place()
+    me = u * 4 + z
+    count = out.shape[0]
+    bar = pltpu.get_barrier_semaphore()
+
+    def at(j):
+        t = lax.rem(me + j, count)
+        return t // 4, lax.rem(t, 4), c
+
+    def hello(j, _):
+        pl.semaphore_signal(bar, inc=1, device_id=at(j), device_id_type=MESH)
+        return 0
+
+    lax.fori_loop(1, count, hello, 0)
+    pl.semaphore_wait(bar, count - 1)
+    own = pltpu.make_async_copy(src, out.at[me], lsem)
+    own.start()
+
+    def send(j, _):
+        pltpu.make_async_remote_copy(
+            src_ref=src, dst_ref=out.at[me], send_sem=ssem, recv_sem=rsem,
+            device_id=at(j), device_id_type=MESH).start()
+        return 0
+
+    lax.fori_loop(1, count, send, 0)
+    own.wait()
+    part = out.at[pl.ds(0, count - 1)]
+    pltpu.make_async_copy(part, part, rsem).wait()
+    pltpu.make_async_copy(part, part, ssem).wait()
+
+
+def spread(block, cid):
+    S = pltpu.SemaphoreType.DMA
+    return pl.pallas_call(
+        spread_kernel,
+        out_shape=jax.ShapeDtypeStruct((16,) + block.shape, block.dtype),
+        in_specs=[pl.BlockSpec(memory_space=pltpu.VMEM)],
+        out_specs=pl.BlockSpec(memory_space=pltpu.VMEM),
+        scratch_shapes=[S, S, S],
+        compiler_params=pltpu.CompilerParams(collective_id=cid, has_side_effects=True),
+        name="spread_rows",
+    )(block)
+
+
+def band_scores(q, k, q_seg, k_seg, scale, reach):
+    scores = dot(q, k, ((1,), (1,))) * scale
+    q_at = lax.broadcasted_iota(jnp.int32, scores.shape, 0)
+    k_at = lax.broadcasted_iota(jnp.int32, scores.shape, 1)
+    return scores, (k_seg == q_seg) & (k_at <= q_at + reach)
+
+
+def attend_kernel(scale, reach, q_ref, k_ref, v_ref, qs_ref, ks_ref, o_ref, l_ref):
+    rows = q_ref.shape[0]
+    first = pl.multiple_of((pl.program_id(0) * 2 + lax.axis_index("core")) * rows, rows)
+    band = pl.ds(first, rows + reach)
+    scores, allowed = band_scores(q_ref[...], k_ref[band, :], qs_ref[...], ks_ref[:, band], scale, reach)
+    scores = jnp.where(allowed, scores, NEG)
+    top = jnp.max(scores, axis=1, keepdims=True)
+    weights = jnp.where(allowed, jnp.exp(scores - top), 0.0)
+    total = jnp.sum(weights, axis=1, keepdims=True)
+    probs = (weights / total).astype(BF)
+    o_ref[...] = dot(probs, v_ref[band, :], ((1,), (0,))).astype(BF)
+    l_ref[...] = top + jnp.log(total)
+
+
+def attend_back_kernel(scale, reach, q_ref, k_ref, v_ref, qs_ref, ks_ref, l_ref, o_ref, do_ref, dq_ref, dk_ref, dv_ref):
+    rows = q_ref.shape[0]
+
+    @pl.when(pl.program_id(0) == 0)
+    def _():
+        dk_ref[...] = jnp.zeros_like(dk_ref)
+        dv_ref[...] = jnp.zeros_like(dv_ref)
+
+    first = pl.multiple_of((pl.program_id(0) * 2 + lax.axis_index("core")) * rows, rows)
+    band = pl.ds(first, rows + reach)
+    q, k, d_out = q_ref[...], k_ref[band, :], do_ref[...]
+    scores, allowed = band_scores(q, k, qs_ref[...], ks_ref[:, band], scale, reach)
+    probs = jnp.where(allowed, jnp.exp(scores - l_ref[...]), 0.0)
+    d_probs = dot(d_out, v_ref[band, :], ((1,), (1,)))
+    delta = jnp.sum(d_out.astype(F32) * o_ref[...].astype(F32), axis=1, keepdims=True)
+    d_scores = (probs * (d_probs - delta)).astype(BF)
+    dq_ref[...] = (dot(d_scores, k, ((1,), (0,))) * scale).astype(BF)
+    dk_ref[band, :] += dot(d_scores, q, ((0,), (0,))) * scale
+    dv_ref[band, :] += dot(probs.astype(BF), d_out, ((0,), (0,)))
+
+
+def core_pair(value):
+    return lax.ppermute(value, "core", [(0, 1), (1, 0)])
+
+
+def dot(a, b, dims):
+    return lax.dot_general(a, b, (dims, ((), ())), preferred_element_type=jnp.float32)
+
+
+def local_chip(
+    inputs, cotangent, segments, expert_ids, gate_weights, fill_order, norm1_gain, w_query, w_key,
+    w_value, w_output, query_gain, key_gain, norm2_gain, expert_gate, expert_up, expert_down,
+):
+    chips = 16
+    devices = 2 * chips
+    rows, width = inputs.shape
+    u, z, core = place()
+    chip = u * 4 + z
+    device = chip * 2 + core
+    topk = expert_ids.shape[1]
+    experts_n = chips
+    capacity = 9 * rows * devices * topk // (8 * experts_n)
+    one_hot = expert_ids[:, :, None] == jnp.arange(experts_n, dtype=jnp.int32)[None, None, :]
+    chosen = jnp.any(one_hot, axis=1)
+    weight = jnp.sum(jnp.where(one_hot, gate_weights[:, :, None], 0.0), axis=1)
+    earlier = (fill_order[None, :] < fill_order[:, None]).astype(jnp.bfloat16)
+    rank = dot(earlier, chosen.astype(jnp.bfloat16), ((1,), (0,)))
+    rank = jnp.where(chosen, rank, -1.0)
+    gains = jnp.concatenate([norm1_gain, query_gain, key_gain, norm2_gain]).astype(F32)
+    gains = jnp.broadcast_to(gains.reshape(1, 2, 128), (chips, 2, 128))
+    block = jnp.concatenate(
+        [weight.T[:, None, :], rank.T[:, None, :], gains, jnp.zeros((chips, 4, 128), F32)], axis=1)
+    swapped = swap(block, 1)
+    gains = swapped[:, 2:4, :].reshape(devices, 4, 64).transpose(1, 0, 2).reshape(4, width)
+    gain_one, gain_q, gain_k, gain_two = gains[0], gains[1], gains[2], gains[3]
+    rank_all = swapped[:, 1, :]
+    taken = rank_all >= 0.0
+    counts = jnp.sum(taken.astype(F32), axis=1)
+    before = jnp.cumsum(counts) - counts
+    kept = taken & (before[:, None] + rank_all < float(capacity))
+    share = jnp.where(kept, swapped[:, 0, :], 0.0).reshape(chips, 2, rows)
+    share = lax.dynamic_index_in_dim(share, core, 1, keepdims=False).reshape(chips * rows, 1)
+
+
+    layer_in = inputs.astype(F32)
+    mine = ("ulysses", "z")
+
+    def in_order(own, other):
+        return jnp.where(core == 0, own, other), jnp.where(core == 0, other, own)
+
+    cols = jnp.stack([w_query, w_key, w_value]).reshape(3, 64, chips, HEAD_DIM).transpose(2, 0, 1, 3)
+    cols = lax.all_to_all(cols, mine, split_axis=0, concat_axis=0, tiled=True)
+    cols = jnp.stack(in_order(cols, core_pair(cols)), axis=1)
+    w_qkv = cols.transpose(0, 1, 3, 2, 4).reshape(width, 3 * HEAD_DIM)
+    w_o = jnp.concatenate(in_order(w_output, core_pair(w_output)), axis=0)
+
+    def my_head(gain):
+        return lax.dynamic_slice_in_dim(gain, chip * HEAD_DIM, HEAD_DIM, 0)
+
+    x_rows = ag16(inputs, 2).reshape(chips * rows, width).astype(F32)
+    n1_rows = norm_rows(x_rows, gain_one).astype(BF)
+    lin = dot(n1_rows, w_qkv, ((1,), (0,)))
+    q_lin, k_lin, v_lin = lin[:, :HEAD_DIM], lin[:, HEAD_DIM : 2 * HEAD_DIM], lin[:, 2 * HEAD_DIM :]
+
+    def over_chips(a, b, cid):
+        both = jnp.stack([a, b]).reshape(2 * chips, rows)
+        both = jnp.sum(spread(both, cid), axis=0).reshape(2, chips * rows, 1)
+        return both[0], both[1]
+
+    square_q, square_k = over_chips(jnp.sum(q_lin * q_lin, axis=1), jnp.sum(k_lin * k_lin, axis=1), 3)
+    rq = lax.rsqrt(square_q / width + EPS)
+    rk = lax.rsqrt(square_k / width + EPS)
+    positions = (jnp.arange(chips, dtype=jnp.int32)[:, None] * 2 + core) * rows + jnp.arange(rows, dtype=jnp.int32)
+    half_dim = HEAD_DIM // 2
+    inv_freq = jnp.exp(jnp.arange(half_dim, dtype=F32) * (-2.0 * math.log(ROPE_BASE) / HEAD_DIM))
+    angles = positions.reshape(-1).astype(F32)[:, None] * inv_freq[None, :]
+    cosine, sine = jnp.cos(angles), jnp.sin(angles)
+    cosine = jnp.concatenate([cosine, cosine], axis=1)
+    sine = jnp.concatenate([-sine, sine], axis=1)
+
+    def halves_swapped(v):
+        return jnp.concatenate([v[:, half_dim:], v[:, :half_dim]], axis=1)
+
+    def turn(v):
+        return v * cosine + halves_swapped(v) * sine
+
+    def turn_back(v):
+        return v * cosine - halves_swapped(v) * sine
+
+    gq, gk = my_head(gain_q), my_head(gain_k)
+    q_rot = turn(q_lin * rq * gq).astype(BF)
+    k_rot = turn(k_lin * rk * gk).astype(BF)
+    kv = jnp.stack([k_rot, v_lin.astype(BF)]).reshape(2, chips, 1, rows, HEAD_DIM)
+    kv = jnp.concatenate(in_order(kv, core_pair(kv)), axis=2).reshape(2, devices * rows, HEAD_DIM)
+    reach = devices * rows // 4
+    kv = jnp.concatenate([jnp.zeros((2, reach, HEAD_DIM), BF), kv], axis=1)
+    k_seg = jnp.concatenate([jnp.full((reach,), -1, jnp.int32), segments]).reshape(1, -1)
+    q_seg = lax.dynamic_index_in_dim(segments.reshape(chips, 2, rows), core, 1, keepdims=False).reshape(-1, 1)
+    scale = 1.0 / math.sqrt(HEAD_DIM)
+    row_block = pl.BlockSpec((rows, HEAD_DIM), lambda i: (i, 0))
+    one_block = pl.BlockSpec((rows, 1), lambda i: (i, 0))
+
+    def whole_block(value):
+        return pl.BlockSpec(value.shape, lambda i: (0,) * value.ndim)
+
+    tokens = chips * rows
+    attended, log_total = pl.pallas_call(
+        functools.partial(attend_kernel, scale, reach),
+        grid=(chips,),
+        out_shape=(jax.ShapeDtypeStruct((tokens, HEAD_DIM), BF), jax.ShapeDtypeStruct((tokens, 1), F32)),
+        in_specs=[row_block, whole_block(kv[0]), whole_block(kv[1]), one_block, whole_block(k_seg)],
+        out_specs=(row_block, one_block),
+        compiler_params=pltpu.CompilerParams(vmem_limit_bytes=32 * 2**20),
+        name="attend",
+    )(q_rot, kv[0], kv[1], q_seg, k_seg)
+
+    def to_blocks(part):
+        return part.astype(BF).reshape(4, 4, rows, width)
+
+    residual = layer_in + rs16(to_blocks(dot(attended, w_o, ((1,), (0,)))), 4)
+    r2 = lax.rsqrt(jnp.mean(residual * residual, axis=1, keepdims=True) + EPS)
+    normed_two = (residual * r2 * gain_two).astype(BF)
+    n2_rows = ag16(normed_two, 5).reshape(tokens, width)
+    cot_rows = lax.all_gather(cotangent, mine, axis=0, tiled=True)
+
+    joined = [
+        jnp.concatenate(in_order(part, core_pair(part)), axis=0)
+        for part in (expert_gate, expert_up, expert_down)
+    ]
+    gate_full, up_full, down_full = joined
+    gate_pre = dot(n2_rows, gate_full, ((1,), (0,)))
+    up_pre = dot(n2_rows, up_full, ((1,), (0,)))
+    sigma = jax.nn.sigmoid(gate_pre)
+    hidden = (gate_pre * sigma * up_pre).astype(BF)
+    produced = dot(hidden, down_full, ((1,), (0,))).astype(BF)
+    mixed = lax.psum_scatter(
+        (share * produced.astype(F32)).astype(BF), mine, scatter_dimension=0, tiled=True)
+    output = residual + mixed.astype(F32)
+    d_produced = (share * cot_rows.astype(F32)).astype(BF)
+    d_hidden = dot(d_produced, down_full, ((1,), (1,)))
+    d_gate_pre = (d_hidden * up_pre * sigma * (1.0 + gate_pre * (1.0 - sigma))).astype(BF)
+    d_up_pre = (d_hidden * gate_pre * sigma).astype(BF)
+    d_pair = dot(d_gate_pre, gate_full, ((1,), (1,))) + dot(d_up_pre, up_full, ((1,), (1,)))
+    d_normed_two = rs16(to_blocks(d_pair), 6)
+
+    def shared_grad(full):
+        size = full.shape[0] // 2
+        own = lax.dynamic_slice_in_dim(full, core * size, size, 0)
+        other = lax.dynamic_slice_in_dim(full, (1 - core) * size, size, 0)
+        return own + core_pair(other.astype(BF)).astype(F32)
+
+    d_expert_gate = shared_grad(dot(n2_rows, d_gate_pre, ((0,), (0,))))
+    d_expert_up = shared_grad(dot(n2_rows, d_up_pre, ((0,), (0,))))
+    d_expert_down = shared_grad(dot(hidden, d_produced, ((0,), (0,))))
+
+    def norm_back(d_out, values, r, gain):
+        d_scaled = d_out * gain
+        inner = jnp.mean(d_scaled * values, axis=1, keepdims=True)
+        d_gain = jnp.sum(d_out * values * r, axis=0)
+        return r * d_scaled - values * (r * r * r * inner), d_gain
+
+    d_resid_norm, d_gain_two = norm_back(d_normed_two, residual, r2, gain_two)
+    d_residual = cotangent.astype(F32) + d_resid_norm
+    d_res_rows = ag16(d_residual.astype(BF), 7).reshape(tokens, width)
+    d_attended = dot(d_res_rows, w_o, ((1,), (1,))).astype(BF)
+    d_w_output = shared_grad(dot(attended, d_res_rows, ((0,), (0,))))
+    padded = jax.ShapeDtypeStruct((reach + devices * rows, HEAD_DIM), F32)
+    d_q, d_k, d_v = pl.pallas_call(
+        functools.partial(attend_back_kernel, scale, reach),
+        grid=(chips,),
+        out_shape=(jax.ShapeDtypeStruct((tokens, HEAD_DIM), BF), padded, padded),
+        in_specs=[row_block, whole_block(kv[0]), whole_block(kv[1]), one_block, whole_block(k_seg), one_block, row_block, row_block],
+        out_specs=(row_block, whole_block(padded), whole_block(padded)),
+        compiler_params=pltpu.CompilerParams(vmem_limit_bytes=48 * 2**20),
+        name="attend_back",
+    )(q_rot, kv[0], kv[1], q_seg, k_seg, log_total, attended, d_attended)
+    d_kv = jnp.stack([d_k[reach:], d_v[reach:]]).reshape(2, chips, 2, rows, HEAD_DIM)
+    d_kv_own = lax.dynamic_index_in_dim(d_kv, core, 2, keepdims=False)
+    d_kv_other = lax.dynamic_index_in_dim(d_kv, 1 - core, 2, keepdims=False)
+    d_kv = (d_kv_own + core_pair(d_kv_other.astype(BF)).astype(F32)).astype(BF).reshape(2, tokens, HEAD_DIM)
+    d_q_un = turn_back(d_q.astype(F32))
+    d_k_un = turn_back(d_kv[0].astype(F32))
+    inner_q, inner_k = over_chips(
+        jnp.sum(d_q_un * gq * q_lin, axis=1), jnp.sum(d_k_un * gk * k_lin, axis=1), 8)
+    d_q_lin = rq * (d_q_un * gq) - q_lin * (rq * rq * rq * (inner_q / width))
+    d_k_lin = rk * (d_k_un * gk) - k_lin * (rk * rk * rk * (inner_k / width))
+    d_gain_q = jnp.sum(d_q_un * q_lin * rq, axis=0)
+    d_gain_k = jnp.sum(d_k_un * k_lin * rk, axis=0)
+    d_lin = jnp.concatenate([d_q_lin.astype(BF), d_k_lin.astype(BF), d_kv[1]], axis=1)
+    d_normed_one = rs16(to_blocks(dot(d_lin, w_qkv, ((1,), (1,)))), 9)
+    d_cols = dot(n1_rows, d_lin, ((0,), (0,))).reshape(chips, 2, 64, 3 * HEAD_DIM)
+    d_cols_own = lax.dynamic_index_in_dim(d_cols, core, 1, keepdims=False)
+    d_cols_other = lax.dynamic_index_in_dim(d_cols, 1 - core, 1, keepdims=False)
+    d_cols = (d_cols_own + core_pair(d_cols_other.astype(BF)).astype(F32)).astype(BF)
+    d_cols = lax.all_to_all(d_cols, mine, split_axis=0, concat_axis=0, tiled=True)
+    d_cols = d_cols.reshape(chips, 64, 3, HEAD_DIM).transpose(2, 1, 0, 3).reshape(3, 64, width).astype(F32)
+    r1 = lax.rsqrt(jnp.mean(layer_in * layer_in, axis=1, keepdims=True) + EPS)
+    d_layer_in, d_gain_one = norm_back(d_normed_one, layer_in, r1, gain_one)
+    d_inputs = d_residual + d_layer_in
+    block = jnp.concatenate(
+        [d_gain_one.reshape(chips, 1, 128), d_gain_two.reshape(chips, 1, 128), jnp.zeros((chips, 6, 128), F32)], axis=1)
+    d_gains = jnp.sum(swap(block, 10)[:, :2, :], axis=0)
+
+    def my_half(row):
+        return lax.dynamic_slice_in_dim(row, core * 64, 64, 0)
+
+    d_qk_gains = jnp.stack([d_gain_q, d_gain_k])
+    d_qk_gains = d_qk_gains + core_pair(d_qk_gains)
+    return (
+        output,
+        d_inputs,
+        my_half(d_gains[0]),
+        d_cols[0],
+        d_cols[1],
+        d_cols[2],
+        d_w_output,
+        my_half(d_qk_gains[0]),
+        my_half(d_qk_gains[1]),
+        my_half(d_gains[1]),
+        d_expert_gate,
+        d_expert_up,
+        d_expert_down,
+    )
+def whole(mesh, step, rows):
     return jax.shard_map(
-        local,
+        step,
         mesh=mesh,
         in_specs=(
-            P(("ulysses", "blk"), None),
-            P(("ulysses", "blk"), None),
+            P(rows, None),
+            P(rows, None),
             P(),
-            P(("ulysses", "blk"), None),
-            P(("ulysses", "blk"), None),
-            P(("ulysses", "blk")),
-            P(("ulysses", "blk")),
-            P(("ulysses", "blk"), None),
-            P(("ulysses", "blk"), None),
-            P(("ulysses", "blk"), None),
-            P(("ulysses", "blk"), None),
-            P(("ulysses", "blk")),
-            P(("ulysses", "blk")),
-            P(("ulysses", "blk")),
-            P(("ulysses", "blk"), None),
-            P(("ulysses", "blk"), None),
-            P(("ulysses", "blk"), None),
+            P(rows, None),
+            P(rows, None),
+            P(rows),
+            P(rows),
+            P(rows, None),
+            P(rows, None),
+            P(rows, None),
+            P(rows, None),
+            P(rows),
+            P(rows),
+            P(rows),
+            P(rows, None),
+            P(rows, None),
+            P(rows, None),
         ),
         out_specs=(
-            P(("ulysses", "blk"), None),
-            P(("ulysses", "blk"), None),
-            P(("ulysses", "blk")),
-            P(("ulysses", "blk"), None),
-            P(("ulysses", "blk"), None),
-            P(("ulysses", "blk"), None),
-            P(("ulysses", "blk"), None),
-            P(("ulysses", "blk")),
-            P(("ulysses", "blk")),
-            P(("ulysses", "blk")),
-            P(("ulysses", "blk"), None),
-            P(("ulysses", "blk"), None),
-            P(("ulysses", "blk"), None),
+            P(rows, None),
+            P(rows, None),
+            P(rows),
+            P(rows, None),
+            P(rows, None),
+            P(rows, None),
+            P(rows, None),
+            P(rows),
+            P(rows),
+            P(rows),
+            P(rows, None),
+            P(rows, None),
+            P(rows, None),
         ),
         check_vma=False,
     )
+
+
+def solution(mesh):
+    groups, blk_size = mesh.shape["ulysses"], mesh.shape["blk"]
+
+    def step(*args):
+        if groups != 4 or blk_size != 8 or args[7].shape[1] // HEAD_DIM != groups * blk_size // 2:
+            return whole(mesh, local, ("ulysses", "blk"))(*args)
+        chips = Mesh(mesh.devices.reshape(groups, blk_size // 2, 2), ("ulysses", "z", "core"))
+        return whole(chips, local_chip, ("ulysses", "z", "core"))(*args)
+
+    return step

time: 2030 us -> 1070 us (0.53)
  waiting for transfers between devices: 1050 us -> 8.06 us
  Pallas kernels: 0 us -> 704 us
  local copies, waits for them, and re-layouts: 287 us -> 67.4 us
  matrix products: 281 us -> 158 us
  blocking collectives: 120 us -> 0 us
  other arithmetic: 208 us -> 91.4 us
  starting transfers between devices: 54 us -> 15.5 us
    pallas_call x0 -> x12, Pallas kernels: none -> 704 us  [the longest x3 330 us: rs16(): pl.pallas_call(functools.partial(rs_kernel, cut), out_shape=jax.ShapeDtyp...]
    all_to_all x14 -> x2, waiting for transfers between devices: 541 us -> 5.11 us  [the longest x1 5.11 us: local_chip(): lax.all_to_all(d_cols, mine, split_axis=0, concat_axis=0, tiled=True)]
    ppermute x21 -> x13, waiting for transfers between devices: 301 us -> 2.25 us  [core_pair(): return lax.ppermute(value, 'core', [(0, 1), (1, 0)])]
    all_gather x6 -> x1, waiting for transfers between devices: 171 us -> 0.01 us  [local_chip(): cot_rows = lax.all_gather(cotangent, mine, axis=0, tiled=True)]
    dot_general x78 -> x16, matrix products: 281 us -> 158 us  [dot(): lax.dot_general(a, b, (dims, ((), ())), preferred_element_type=jnp.float32)]
    gather x30 -> x0, local copies, waits for them, and re-layouts: 122 us -> none  [the longest x16 50.4 us: score_block(): k_seg = banded(segments[k_pos], -1)]
    unnamed x4 -> x0, blocking collectives: 120 us -> none
    all_to_all x14 -> x2, starting transfers between devices: 51 us -> 13.4 us  [the longest x1 8.31 us: local_chip(): cols = lax.all_to_all(cols, mine, split_axis=0, concat_axis=0, tiled=True)]
  transfers between devices with their start and end apart: 48 -> 17, of which waited for: 30 -> 3; matrix products, arithmetic and copies ran while one was open for 22% -> 23% of each run, Pallas kernels for 0% -> 66%
where the time goes in v1:
time: 1070 us; the launch traced here: 1060 us
  Pallas kernels  704 us (66%)
  matrix products  158 us (15%)
  other arithmetic  91.4 us (9%)
  local copies, waits for them, and re-layouts  67.4 us (6%)
  between operations  16 us (1%)
  starting transfers between devices  15.5 us (1%)
    pallas_call x3, Pallas kernels, rs16(): pl.pallas_call(functools.partial(rs_kernel, cut), out_shape=jax.ShapeDtyp...  330 us
    pallas_call x3, Pallas kernels, ag16(): pl.pallas_call(functools.partial(ag_kernel, cut), out_shape=jax.ShapeDtyp...  275 us
    dot_general x16, matrix products, dot(): lax.dot_general(a, b, (dims, ((), ())), preferred_element_type=jnp.float32)  158 us
    pallas_call x2, Pallas kernels, swap(): pl.pallas_call(swap_kernel, out_shape=jax.ShapeDtypeStruct((2 * chips, r,...  47.8 us
    unnamed x178, local copies, waits for them, and re-layouts  26.4 us
    pallas_call x2, Pallas kernels, spread(): pl.pallas_call(spread_kernel, out_shape=jax.ShapeDtypeStruct((16,) + bloc...  24.6 us
  transfers between devices with their start and end apart: 17, of which 3 were waited for; matrix products, arithmetic and copies ran while one was open for 23% of the time, Pallas kernels for 66%

profile of v1, /device:TPU:0, one launch (start us, length us, event | category | flops | bytes accessed | tf_op | source)
XLA Modules:
  0.0 1060.2 jit_solution(325539756860106919)
XLA Ops:
  22.8 33.5 %swap_rows.2 = f32[32,8,128]{2,1,0:T(8,128)} custom-call(f32[16,8,128]{2,1,0:T(8,128)} %maximum_maximum_fusion.src), custom_call_target="tpu_custom_call" | custom-call | tf_op jit(solution)/shard_map/swap_rows/pallas_call | solution.py:861
  57.6 135.6 %gather_rows.3 = bf16[4,4,128,2048]{3,2,1,0:T(8,128)(2,1)} custom-call(bf16[128,2048]{1,0:T(8,128)(2,1)S(1)} %copy-done.5), custom_call_target="tpu_custom_call" | custom-call | tf_op jit(solution)/shard_map/gather_rows/pallas_call | solution.py:629
  198.3 8.6 multiply_convert_fusion.2
  207.0 8.6 fusion.1
  224.8 12.4 %copy.122 = bf16[2048,2048]{1,0:T(8,128)(2,1)} copy(bf16[2048,2048]{0,1:T(8,128)(2,1)} %bitcast.178) | data formatting | bytes 16777216 | tf_op jit(solution)/shard_map/dot_general | solution.py:964
  266.3 12.1 %spread_rows.2 = f32[16,32,128]{2,1,0:T(8,128)} custom-call(f32[32,128]{1,0:T(8,128)} %reshape.344.src), custom_call_target="tpu_custom_call" | custom-call | tf_op jit(solution)/shard_map/spread_rows/pallas_call | solution.py:906
  285.9 11.5 %attend.1 = (bf16[2048,128]{1,0:T(8,128)(2,1)S(1)}, f32[2048,1]{1,0:T(8,128)S(1)}) custom-call(bf16[2048,128]{1,0:T(8,128)(2,1)S(1)} %fusion.32.q_ref, bf16[5120,128]{1,0:T(8,128)(2,1)S(1)} %get-tuple-element.59.k_ref, bf16[5120,128]{1,0:T(8,128)(2,1)S(1)} %get-tuple-element.58.v_ref, s32[2048,1]{1,0:T(8,128)S(1)} %copy.117.qs_ref, s32[1,5120]{1,0:T(1,128)S(1)} %bitcast.171), custom_call_target="tpu_custom_call" | custom-call | tf_op jit(solution)/shard_map/attend/pallas_call | solution.py:1064
  304.1 80.4 %scatter_rows.3 = f32[128,2048]{1,0:T(8,128)} custom-call(bf16[4,4,128,2048]{3,2,1,0:T(8,128)(2,1)} %bitcast.177), custom_call_target="tpu_custom_call" | custom-call | tf_op jit(solution)/shard_map/scatter_rows/pallas_call | solution.py:811
  386.3 71.8 %gather_rows.4 = bf16[4,4,128,2048]{3,2,1,0:T(8,128)(2,1)} custom-call(bf16[128,2048]{1,0:T(8,128)(2,1)S(1)} %multiply_convert_fusion.8.x_ref), custom_call_target="tpu_custom_call" | custom-call | tf_op jit(solution)/shard_map/gather_rows/pallas_call | solution.py:629
  458.6 13.6 %fusion.5 = f32[2048,1024]{1,0:T(8,128)} fusion(bf16[2048,2048]{1,0:T(8,128)(2,1)} %bitcast.191, bf16[1024,1024]{1,0:T(8,128)(2,1)S(1)} %copy-done.33, bf16[1024,1024]{1,0:T(8,128)(2,1)S(1)} %copy-done.31), kind=kOutput, calls=%fused_computation.30 | convolution fusion | flops 8598323200 | bytes 20971520 | tf_op jit(solution)/shard_map/dot_general | solution.py:964
  472.2 14.5 %fusion.3 = f32[2048,1024]{1,0:T(8,128)} fusion(bf16[2048,2048]{1,0:T(8,128)(2,1)} %all-gather.2.cloned.1.call-done, f32[2048]{0:T(1024)S(1)} %bitcast.234, bf16[512,2048]{1,0:T(8,128)(2,1)} %get-tuple-element.45, bf16[512,2048]{1,0:T(8,128)(2,1)} %get-tuple-element.44), kind=kOutput, calls=%fused_computation.28 | convolution fusion | flops 8610906112 | bytes 20979712 | tf_op jit(solution)/shard_map/dot_general | solution.py:964
  486.7 22.5 %multiply_convert_fusion.4 = (bf16[2048,1024]{1,0:T(8,128)(2,1)}, bf16[2048,1024]{1,0:T(8,128)(2,1)}, bf16[2048,1024]{1,0:T(8,128)(2,1)}) fusion(f32[2048,1024]{1,0:T(8,128)} %fusion.3, f32[2048,1024]{1,0:T(8,128)} %fusion.5, bf16[2048,2048]{1,0:T(8,128)(2,1)} %bitcast.192, bf16[1024,1024]{1,0:T(8,128)(2,1)} %get-tuple-element.47, ...), kind=kOutput, calls=%fused_computation.9 | convolution fusion | flops 8631877632 | bytes 41943040 | tf_op jit(solution)/shard_map/dot_general | solution.py:964
  509.2 14.0 %multiply_convert_fusion.1 = bf16[2048,2048]{1,0:T(8,128)(2,1)} fusion(f32[2048]{0:T(1024)S(1)} %bitcast.235, bf16[2048,1024]{1,0:T(8,128)(2,1)} %get-tuple-element.42, bf16[512,2048]{1,0:T(8,128)(2,1)} %get-tuple-element.45, bf16[512,2048]{1,0:T(8,128)(2,1)} %get-tuple-element.44), kind=kOutput, calls=%fused_computation.5 | convolution fusion | flops 8615100416 | bytes 16785408 | tf_op jit(solution)/shard_map/dot_general | solution.py:964
  523.1 13.7 %fusion.2 = f32[1024,2048]{1,0:T(8,128)S(1)} fusion(bf16[2048,1024]{1,0:T(8,128)(2,1)} %get-tuple-element.42, bf16[2048,2048]{1,0:T(8,128)(2,1)} %all-gather.2.cloned.1.call-done, f32[2048]{0:T(1024)S(1)} %bitcast.236), kind=kOutput, calls=%fused_computation.27 | convolution fusion | flops 8602517504 | bytes 20979712 | tf_op jit(solution)/shard_map/dot_general | solution.py:964
  541.8 12.5 %fusion.85 = f32[2048,1024]{1,0:T(8,128)S(1)} fusion(bf16[2048,2048]{1,0:T(8,128)(2,1)} %bitcast.193, bf16[2048,1024]{1,0:T(8,128)(2,1)S(1)} %copy-done.73), kind=kOutput, calls=%fused_computation.203 | convolution fusion | flops 8589934592 | bytes 20971520 | tf_op jit(solution)/shard_map/dot_general | solution.py:964
  559.5 9.1 fusion.86
  574.9 11.7 %fusion.4 = f32[2048,2048]{1,0:T(8,128)} fusion(bf16[2048,1024]{1,0:T(8,128)(2,1)S(1)} %copy-done.74, bf16[1024,1024]{1,0:T(8,128)(2,1)S(1)} %copy-done.34, bf16[1024,1024]{1,0:T(8,128)(2,1)S(1)} %copy-done.32), kind=kOutput, calls=%fused_computation.29 | convolution fusion | flops 8598323200 | bytes 25165824 | tf_op jit(solution)/shard_map/dot_general | solution.py:964
  586.7 16.5 %add_convert_fusion = bf16[2048,2048]{1,0:T(8,128)(2,1)} fusion(f32[2048,2048]{1,0:T(8,128)} %fusion.4, bf16[2048,1024]{1,0:T(8,128)(2,1)} %get-tuple-element.41, bf16[1024,1024]{1,0:T(8,128)(2,1)} %get-tuple-element.47, bf16[1024,1024]{1,0:T(8,128)(2,1)} %get-tuple-element.46), kind=kOutput, calls=%fused_computation.3 | convolution fusion | flops 8606711808 | bytes 33554432 | tf_op jit(solution)/shard_map/dot_general | solution.py:964
  603.2 171.5 %scatter_rows.4 = f32[128,2048]{1,0:T(8,128)} custom-call(bf16[4,4,128,2048]{3,2,1,0:T(8,128)(2,1)} %bitcast.187), custom_call_target="tpu_custom_call" | custom-call | tf_op jit(solution)/shard_map/scatter_rows/pallas_call | solution.py:811
  777.8 67.7 %gather_rows.5 = bf16[4,4,128,2048]{3,2,1,0:T(8,128)(2,1)} custom-call(bf16[128,2048]{1,0:T(8,128)(2,1)S(1)} %fusion.72.x_ref), custom_call_target="tpu_custom_call" | custom-call | tf_op jit(solution)/shard_map/gather_rows/pallas_call | solution.py:629
  851.5 15.5 %attend_back.1 = (bf16[2048,128]{1,0:T(8,128)(2,1)S(1)}, f32[5120,128]{1,0:T(8,128)}, f32[5120,128]{1,0:T(8,128)}) custom-call(bf16[2048,128]{1,0:T(8,128)(2,1)S(1)} %copy-done.8, bf16[5120,128]{1,0:T(8,128)(2,1)S(1)} %copy-done.2, bf16[5120,128]{1,0:T(8,128)(2,1)} %copy-done, s32[2048,1]{1,0:T(8,128)S(1)} %copy.117.qs_ref, s32[1,5120]{1,0:T(1,128)S(1)} %bitcast.172, ...), custom_call_target="tpu_custom_call" | custom-call | tf_op jit(solution)/shard_map/attend_back/pallas_call | solution.py:1125
  881.0 12.6 %spread_rows.3 = f32[16,32,128]{2,1,0:T(8,128)} custom-call(f32[32,128]{1,0:T(8,128)} %reshape.355.src), custom_call_target="tpu_custom_call" | custom-call | tf_op jit(solution)/shard_map/spread_rows/pallas_call | solution.py:906
  913.1 78.0 %scatter_rows.5 = f32[128,2048]{1,0:T(8,128)} custom-call(bf16[4,4,128,2048]{3,2,1,0:T(8,128)(2,1)} %bitcast.186), custom_call_target="tpu_custom_call" | custom-call | tf_op jit(solution)/shard_map/scatter_rows/pallas_call | solution.py:811
  993.4 14.3 %swap_rows.3 = f32[32,8,128]{2,1,0:T(8,128)} custom-call(f32[16,8,128]{2,1,0:T(8,128)} %maximum_maximum_fusion.1.src), custom_call_target="tpu_custom_call" | custom-call | tf_op jit(solution)/shard_map/swap_rows/pallas_call | solution.py:861
  (338 shorter events, 182.3 us)
Async XLA Ops:
  7.3 464.9 %all-gather.2.cloned.1.call-start = ((), (), s32[]{:S(2)}) async-start(), calls=%async_computation.4 | async-start | bytes 8912896 | tf_op jit(solution)/shard_map/all_gather | solution.py:1081
  12.2 225.8 %all-to-all-start = ((bf16[16,3,64,128]{3,2,1,0:T(8,128)(2,1)}), bf16[16,3,64,128]{3,2,1,0:T(8,128)(2,1)S(1)}, u32[]{:S(2)}, u32[]{:S(2)}) async-start(bf16[16,3,64,128]{3,2,1,0:T(8,128)(2,1)} %copy.111), calls=%async_computation | async-start | bytes 1572864 | tf_op jit(solution)/shard_map/all_to_all | solution.py:1009
  20.5 1029.2 %reduce-scatter.2.cloned.1.call-start = ((), (), s32[]{:S(2)}) async-start(), calls=%async_computation.3 | async-start | bytes 8912896 | tf_op jit(solution)/shard_map/reduce_scatter | solution.py:1093
  20.6 216.7 %collective-permute-start.2 = (bf16[64,2048]{1,0:T(8,128)(2,1)S(1)}, bf16[64,2048]{1,0:T(8,128)(2,1)S(1)}, u32[]{:S(2)}, u32[]{:S(2)}) collective-permute-start(bf16[64,2048]{1,0:T(8,128)(2,1)S(1)} %copy-done.42), channel_id=1, source_target_pairs={{0,1},{1,0},{2,3},{3,2},{4,5},{5,4},{6,7},{7,6},{8,9},{9,8},{10,11... | collective-permute-start | bytes 786440 | tf_op jit(solution)/shard_map/ppermute | solution.py:960
  20.6 217.4 %collective-permute-start.3 = (bf16[1024,1024]{1,0:T(8,128)(2,1)}, bf16[1024,1024]{1,0:T(8,128)(2,1)}, u32[]{:S(2)}, u32[]{:S(2)}) collective-permute-start(bf16[1024,1024]{1,0:T(8,128)(2,1)} %param.31), channel_id=1, source_target_pairs={{0,1},{1,0},{2,3},{3,2},{4,5},{5,4},{6,7},{7,6},{8,9},{9,8},{10,11... | collective-permute-start | bytes 6291464 | tf_op jit(solution)/shard_map/ppermute | solution.py:960
  21.1 221.5 %collective-permute-start.4 = (bf16[1024,1024]{1,0:T(8,128)(2,1)}, bf16[1024,1024]{1,0:T(8,128)(2,1)}, u32[]{:S(2)}, u32[]{:S(2)}) collective-permute-start(bf16[1024,1024]{1,0:T(8,128)(2,1)} %param.32), channel_id=1, source_target_pairs={{0,1},{1,0},{2,3},{3,2},{4,5},{5,4},{6,7},{7,6},{8,9},{9,8},{10,11... | collective-permute-start | bytes 6291464 | tf_op jit(solution)/shard_map/ppermute | solution.py:960
  21.2 225.8 %collective-permute-start.5 = (bf16[512,2048]{1,0:T(8,128)(2,1)}, bf16[512,2048]{1,0:T(8,128)(2,1)}, u32[]{:S(2)}, u32[]{:S(2)}) collective-permute-start(bf16[512,2048]{1,0:T(8,128)(2,1)} %param.33), channel_id=1, source_target_pairs={{0,1},{1,0},{2,3},{3,2},{4,5},{5,4},{6,7},{7,6},{8,9},{9,8},{10,11... | collective-permute-start | bytes 6291464 | tf_op jit(solution)/shard_map/ppermute | solution.py:960
  57.6 149.3 %copy-start.43 = (f32[2048]{0:T(1024)}, f32[2048]{0:T(1024)S(1)}, u32[]{:S(2)}) copy-start(f32[2048]{0:T(1024)S(1)} %mul.467) | copy-start | bytes 24580
  224.1 162.0 %copy-start.45 = (f32[2048]{0:T(1024)}, f32[2048]{0:T(1024)S(1)}, u32[]{:S(2)}) copy-start(f32[2048]{0:T(1024)S(1)} %mul.498) | copy-start | bytes 24580
  238.0 13.3 %collective-permute-start = (bf16[16,3,64,128]{3,2,1,0:T(8,128)(2,1)S(1)}, bf16[16,3,64,128]{3,2,1,0:T(8,128)(2,1)S(1)}, u32[]{:S(2)}, u32[]{:S(2)}) collective-permute-start(bf16[16,3,64,128]{3,2,1,0:T(8,128)(2,1)S(1)} %all-to-all-done), channel_id=1, source_target_pairs={{0,1},{1,0},{2,3},{3,2},{4,5},{5,4},{6,7},{7,6},{8,9},{9,8},{10,11... | collective-permute-start | bytes 2359304 | tf_op jit(solution)/shard_map/ppermute | solution.py:960
  282.6 2.7 collective-permute-start.1
  541.7 488.4 %collective-permute-start.12 = (bf16[512,2048]{1,0:T(8,128)(2,1)}, bf16[512,2048]{1,0:T(8,128)(2,1)}, u32[]{:S(2)}, u32[]{:S(2)}) collective-permute-start(bf16[512,2048]{1,0:T(8,128)(2,1)} %dynamic-slice_convert_fusion), channel_id=1, source_target_pairs={{0,1},{1,0},{2,3},{3,2},{4,5},{5,4},{6,7},{7,6},{8,9},{9,8},{10,11... | collective-permute-start | bytes 6291464 | tf_op jit(solution)/shard_map/ppermute | solution.py:960
  555.9 462.2 %collective-permute-start.10 = (bf16[1024,1024]{1,0:T(8,128)(2,1)}, bf16[1024,1024]{1,0:T(8,128)(2,1)}, u32[]{:S(2)}, u32[]{:S(2)}) collective-permute-start(bf16[1024,1024]{1,0:T(8,128)(2,1)} %dynamic-slice_convert_fusion.2), channel_id=1, source_target_pairs={{0,1},{1,0},{2,3},{3,2},{4,5},{5,4},{6,7},{7,6},{8,9},{9,8},{10,11... | collective-permute-start | bytes 6291464 | tf_op jit(solution)/shard_map/ppermute | solution.py:960
  573.6 450.5 %collective-permute-start.11 = (bf16[1024,1024]{1,0:T(8,128)(2,1)}, bf16[1024,1024]{1,0:T(8,128)(2,1)}, u32[]{:S(2)}, u32[]{:S(2)}) collective-permute-start(bf16[1024,1024]{1,0:T(8,128)(2,1)} %dynamic-slice_convert_fusion.1), channel_id=1, source_target_pairs={{0,1},{1,0},{2,3},{3,2},{4,5},{5,4},{6,7},{7,6},{8,9},{9,8},{10,11... | collective-permute-start | bytes 6291464 | tf_op jit(solution)/shard_map/ppermute | solution.py:960
  603.2 171.5 %copy-start.14 = (f32[128,2048]{1,0:T(8,128)S(1)}, f32[128,2048]{1,0:T(8,128)}, u32[]{:S(2)}) copy-start(f32[128,2048]{1,0:T(8,128)} %copy-done.13) | copy-start | bytes 3145732
  603.2 171.5 %copy-start.46 = (f32[2048]{0:T(1024)S(1)}, f32[2048]{0:T(1024)}, u32[]{:S(2)}) copy-start(f32[2048]{0:T(1024)} %copy-done.45) | copy-start | bytes 24580
  603.2 171.5 %copy-start.60 = (f32[128]{0:T(128)S(1)}, f32[128]{0:T(128)}, u32[]{:S(2)}) copy-start(f32[128]{0:T(128)} %copy-done.59) | copy-start | bytes 1540
  603.2 173.0 %copy-start.67 = (f32[128]{0:T(128)S(1)}, f32[128]{0:T(128)}, u32[]{:S(2)}) copy-start(f32[128]{0:T(128)} %copy-done.66) | copy-start | bytes 1540
  603.2 173.0 %copy-start.24 = (bf16[128,2048]{1,0:T(8,128)(2,1)S(1)}, bf16[128,2048]{1,0:T(8,128)(2,1)}, u32[]{:S(2)}) copy-start(bf16[128,2048]{1,0:T(8,128)(2,1)} %param.18) | copy-start | bytes 1572868
  869.7 4.7 collective-permute-start.6
  871.9 1.6 collective-permute-start.8
  880.9 129.0 %collective-permute-start.9 = (f32[2,128]{1,0:T(2,128)S(1)}, f32[2,128]{1,0:T(2,128)S(1)}, u32[]{:S(2)}, u32[]{:S(2)}) collective-permute-start(f32[2,128]{1,0:T(2,128)S(1)} %pad_maximum_fusion.21), channel_id=1, source_target_pairs={{0,1},{1,0},{2,3},{3,2},{4,5},{5,4},{6,7},{7,6},{8,9},{9,8},{10,11... | collective-permute-start | bytes 3080 | tf_op jit(solution)/shard_map/ppermute | solution.py:960
  911.6 98.3 %collective-permute-start.7 = (bf16[16,64,384]{2,1,0:T(8,128)(2,1)S(1)}, bf16[16,64,384]{2,1,0:T(8,128)(2,1)S(1)}, u32[]{:S(2)}, u32[]{:S(2)}) collective-permute-start(bf16[16,64,384]{2,1,0:T(8,128)(2,1)S(1)} %fusion.37), channel_id=1, source_target_pairs={{0,1},{1,0},{2,3},{3,2},{4,5},{5,4},{6,7},{7,6},{8,9},{9,8},{10,11... | collective-permute-start | bytes 2359304 | tf_op jit(solution)/shard_map/ppermute | solution.py:960
  1012.4 27.2 %all-to-all-start.1 = ((bf16[16,64,384]{2,1,0:T(8,128)(2,1)}), bf16[16,64,384]{2,1,0:T(8,128)(2,1)S(1)}, u32[]{:S(2)}, u32[]{:S(2)}) async-start(bf16[16,64,384]{2,1,0:T(8,128)(2,1)} %fusion.19), calls=%async_computation.2 | async-start | bytes 1572864 | tf_op jit(solution)/shard_map/all_to_all | solution.py:1152
  (78 other events, 1641.0 us)
Sparse Core Ops, SparseCore 0:
  10.9 172.7 all-gather.1
  523.3 238.3 reduce-scatter.1

commit v2 on v1

--- a/solution.py
+++ b/solution.py
@@ -638,6 +638,7 @@
 F32 = jnp.float32
 BF = jnp.bfloat16
 
+
 class Net:
     def __init__(self, sems):
         self.sems, self.sends = sems, []
@@ -646,148 +647,207 @@
         self.ux, self.uy, self.ud = u ^ 1, u ^ 2, u ^ 3
         self.xn, self.yn, self.up, self.dn = (u ^ 1, z, c), (u ^ 2, z, c), (u, z + 1, c), (u, z - 1, c)
         self.has_up, self.has_dn = z < 3, z > 0
-    def barrier(self):
+        self.at = [z == i for i in range(4)]
+
+    def barrier(self, more=()):
         bar = pltpu.get_barrier_semaphore()
-        for n in (self.xn, self.yn):
+        for n in (self.xn, self.yn) + tuple(more):
             pl.semaphore_signal(bar, inc=1, device_id=n, device_id_type=MESH)
         for cond, n in ((self.has_up, self.up), (self.has_dn, self.dn)):
             pl.when(cond)(lambda n=n: pl.semaphore_signal(bar, inc=1, device_id=n, device_id_type=MESH))
-        pl.semaphore_wait(bar, 2 + self.has_up.astype(jnp.int32) + self.has_dn.astype(jnp.int32))
+        pl.semaphore_wait(bar, 2 + len(more) + self.has_up.astype(jnp.int32) + self.has_dn.astype(jnp.int32))
+
     def go(self, cond, src, dst, rsem, dev):
         idx = len(self.sends)
+
         def mk():
-            return pltpu.make_async_remote_copy(src_ref=src(), dst_ref=dst(), send_sem=self.sems.at[idx], recv_sem=rsem, device_id=dev, device_id_type=MESH)
+            return pltpu.make_async_remote_copy(
+                src_ref=src(), dst_ref=dst(), send_sem=self.sems.at[idx], recv_sem=rsem(),
+                device_id=dev, device_id_type=MESH)
+
         self.sends.append((cond, mk))
-        if cond is None: mk().start()
-        else: pl.when(cond)(lambda: mk().start())
+        if cond is None:
+            mk().start()
+        else:
+            pl.when(cond)(lambda: mk().start())
+
     def wait(self, cond, ref, sem):
-        def w(): pltpu.make_async_copy(ref(), ref(), sem).wait()
-        if cond is None: w()
-        else: pl.when(cond)(w)
+        def w():
+            pltpu.make_async_copy(ref(), ref(), sem).wait()
+
+        if cond is None:
+            w()
+        else:
+            pl.when(cond)(w)
+
     def finish(self):
         for cond, mk in self.sends:
-            if cond is None: mk().wait_send()
-            else: pl.when(cond)(lambda mk=mk: mk().wait_send())
+            if cond is None:
+                mk().wait_send()
+            else:
+                pl.when(cond)(lambda mk=mk: mk().wait_send())
+
 
 def strips(rows, body, step=16):
     def it(i, _):
         body(pl.ds(pl.multiple_of(i * step, step), step))
         return 0
+
     lax.fori_loop(0, rows // step, it, 0)
 
-def rs_body(net, cut, P, out_store, mid1, mid2, fx, fy, be, ab, bbe, bab, bm, m1s, m2s, fxs, fys, bes, abs_, bbes, babs, bms):
-    u, z = net.u, net.z
-    R = P.shape[2]
-    h = cut // 2
-    rb = R - cut
-    hb = rb // 2
-    order = (3, 0, 2, 1)
-    f = lambda v: v.astype(F32)
-    for zd in order:
-        net.go(None, lambda: P.at[net.ud, zd, pl.ds(0, h), :], lambda: mid1.at[zd], m1s.at[zd], net.xn)
-        net.go(None, lambda: P.at[net.ud, zd, pl.ds(h, h), :], lambda: mid2.at[zd], m2s.at[zd], net.yn)
-    def bsend(zd, first):
-        lo, hi = net.z < zd, net.z > zd
-        if first:
-            net.go(z == 0, lambda: P.at[:, zd, pl.ds(cut, rb), :], lambda: bbe.at[zd], bbes.at[zd], net.up)
-            net.go(z == 3, lambda: P.at[:, zd, pl.ds(cut, rb), :], lambda: bab.at[zd], babs.at[zd], net.dn)
-    for zd in order:
-        if zd > 0:
-            net.go(z == 0, lambda: P.at[:, zd, pl.ds(cut, rb), :], lambda: bbe.at[zd], bbes.at[zd], net.up)
-        if zd < 3:
-            net.go(z == 3, lambda: P.at[:, zd, pl.ds(cut, rb), :], lambda: bab.at[zd], babs.at[zd], net.dn)
-    for zd in order:
-        net.go(None, lambda: P.at[net.ux, zd, pl.ds(0, h), :], lambda: fx.at[zd, pl.ds(0, h), :], fxs.at[zd, 0], net.xn)
-        net.go(None, lambda: P.at[net.uy, zd, pl.ds(h, h), :], lambda: fy.at[zd, pl.ds(h, h), :], fys.at[zd, 1], net.yn)
-    def bpass(zd):
-        def addto(buf, zd):
+
+def wide(v):
+    return v.astype(F32)
+
+
+class Scatter:
+    def __init__(self, net, cut, P, bufs):
+        self.net, self.cut, self.P = net, cut, P
+        (self.mid1, self.mid2, self.fx, self.fy, self.be, self.ab, self.bbe, self.bab, self.bm,
+         self.m1s, self.m2s, self.fxs, self.fys, self.bes, self.abs_, self.bbes, self.babs, self.bms) = bufs
+        self.R = P.shape[2]
+        self.h = cut // 2
+        self.rb = self.R - cut
+        self.hb = self.rb // 2
+
+    def first(self, zd):
+        net, P, h, cut, rb = self.net, self.P, self.h, self.cut, self.rb
+        net.go(None, lambda: P.at[net.ud, zd, pl.ds(0, h), :], lambda: self.mid1.at[zd], lambda: self.m1s.at[zd], net.xn)
+        net.go(None, lambda: P.at[net.ud, zd, pl.ds(h, h), :], lambda: self.mid2.at[zd], lambda: self.m2s.at[zd], net.yn)
+        if rb and zd > 0:
+            net.go(net.at[0], lambda: P.at[:, zd, pl.ds(cut, rb), :], lambda: self.bbe.at[zd], lambda: self.bbes.at[zd], net.up)
+        if rb and zd < 3:
+            net.go(net.at[3], lambda: P.at[:, zd, pl.ds(cut, rb), :], lambda: self.bab.at[zd], lambda: self.babs.at[zd], net.dn)
+        net.go(None, lambda: P.at[net.ux, zd, pl.ds(0, h), :], lambda: self.fx.at[zd, pl.ds(0, h), :], lambda: self.fxs.at[zd, 0], net.xn)
+        net.go(None, lambda: P.at[net.uy, zd, pl.ds(h, h), :], lambda: self.fy.at[zd, pl.ds(h, h), :], lambda: self.fys.at[zd, 1], net.yn)
+
+    def mids(self, zd):
+        net, P, h, mid1, mid2 = self.net, self.P, self.h, self.mid1, self.mid2
+
+        def add1(sl):
+            mid1[zd, sl, :] = (wide(mid1[zd, sl, :]) + wide(P[net.uy, zd, sl, :])).astype(BF)
+
+        def add2(sl):
+            mid2[zd, sl, :] = (wide(mid2[zd, sl, :]) + wide(P[net.ux, zd, pl.ds(h + sl.start, 16), :])).astype(BF)
+
+        net.wait(None, lambda: mid1.at[zd], self.m1s.at[zd])
+        strips(h, add1)
+        net.go(None, lambda: mid1.at[zd], lambda: self.fy.at[zd, pl.ds(0, h), :], lambda: self.fys.at[zd, 0], net.yn)
+        net.wait(None, lambda: mid2.at[zd], self.m2s.at[zd])
+        strips(h, add2)
+        net.go(None, lambda: mid2.at[zd], lambda: self.fx.at[zd, pl.ds(h, h), :], lambda: self.fxs.at[zd, 1], net.xn)
+
+    def route(self, zd, zz):
+        if zz < zd:
+            return True, self.net.up
+        return False, self.net.dn
+
+    def bhop(self, zd, zz):
+        net, P, cut, rb = self.net, self.P, self.cut, self.rb
+        if not rb:
+            return
+        upward, dev = self.route(zd, zz)
+        buf, sems = (self.bbe, self.bbes) if upward else (self.bab, self.babs)
+        here = net.at[zz]
+        net.wait(here, lambda: buf.at[zd], sems.at[zd])
+
+        def add():
             for q in range(4):
-                strips(rb, lambda sl: buf.__setitem__((zd, q, sl, slice(None)), (f(buf[zd, q, sl, :]) + f(P[q, zd, pl.ds(cut + sl.start, 16), :])).astype(BF)))
-        up_mid = jnp.logical_and(z > 0, z < zd)
-        net.wait(up_mid, lambda: bbe.at[zd], bbes.at[zd])
-        pl.when(up_mid)(lambda: addto(bbe, zd))
-        net.go(up_mid, lambda: bbe.at[zd], lambda: bbe.at[zd], bbes.at[zd], net.up)
-        dn_mid = jnp.logical_and(z < 3, z > zd)
-        net.wait(dn_mid, lambda: bab.at[zd], babs.at[zd])
-        pl.when(dn_mid)(lambda: addto(bab, zd))
-        net.go(dn_mid, lambda: bab.at[zd], lambda: bab.at[zd], babs.at[zd], net.dn)
-    for zd in order:
-        net.wait(None, lambda: mid1.at[zd], m1s.at[zd])
-        strips(h, lambda sl: mid1.__setitem__((zd, sl, slice(None)), (f(mid1[zd, sl, :]) + f(P[net.uy, zd, sl, :])).astype(BF)))
-        net.go(None, lambda: mid1.at[zd], lambda: fy.at[zd, pl.ds(0, h), :], fys.at[zd, 0], net.yn)
-        net.wait(None, lambda: mid2.at[zd], m2s.at[zd])
-        strips(h, lambda sl: mid2.__setitem__((zd, sl, slice(None)), (f(mid2[zd, sl, :]) + f(P[net.ux, zd, pl.ds(h + sl.start, 16), :])).astype(BF)))
-        net.go(None, lambda: mid2.at[zd], lambda: fx.at[zd, pl.ds(h, h), :], fxs.at[zd, 1], net.xn)
+                def one(sl, q=q):
+                    buf[zd, q, sl, :] = (wide(buf[zd, q, sl, :]) + wide(P[q, zd, pl.ds(cut + sl.start, 16), :])).astype(BF)
+                strips(rb, one)
+
+        pl.when(here)(add)
+        net.go(here, lambda: buf.at[zd], lambda: buf.at[zd], lambda: sems.at[zd], dev)
+
+    def square(self, zd, cond):
+        net, h = self.net, self.h
+        for half in (0, 1):
+            net.wait(cond, lambda: self.fx.at[zd, pl.ds(half * h, h), :], self.fxs.at[zd, half])
+            net.wait(cond, lambda: self.fy.at[zd, pl.ds(half * h, h), :], self.fys.at[zd, half])
+
+    def local(self, zd, sl):
+        return wide(self.P[self.net.u, zd, sl, :]) + wide(self.fx[zd, sl, :]) + wide(self.fy[zd, sl, :])
+
+    def hop(self, zd, zz):
+        net = self.net
+        upward, dev = self.route(zd, zz)
+        buf, sems = (self.be, self.bes) if upward else (self.ab, self.abs_)
+        here = net.at[zz]
+        self.square(zd, here)
+        if zz in (0, 3):
+            def begin(sl):
+                self.fx[zd, sl, :] = self.local(zd, sl).astype(BF)
+
+            pl.when(here)(lambda: strips(self.cut, begin))
+            net.go(here, lambda: self.fx.at[zd], lambda: buf.at[zd], lambda: sems.at[zd], dev)
+        else:
+            def plus(sl):
+                buf[zd, sl, :] = (self.local(zd, sl) + wide(buf[zd, sl, :])).astype(BF)
+
+            net.wait(here, lambda: buf.at[zd], sems.at[zd])
+            pl.when(here)(lambda: strips(self.cut, plus))
+            net.go(here, lambda: buf.at[zd], lambda: buf.at[zd], lambda: sems.at[zd], dev)
+
+    def bquad(self):
+        net, P, cut, rb, hb, bm, bms = self.net, self.P, self.cut, self.rb, self.hb, self.bm, self.bms
+        if not rb:
+            return
+        z = net.z
+        net.wait(net.has_dn, lambda: self.bbe.at[z], self.bbes.at[z])
+        net.wait(net.has_up, lambda: self.bab.at[z], self.babs.at[z])
+        for q in range(4):
+            def fold(sl, q=q):
+                s = wide(P[q, z, pl.ds(cut + sl.start, 16), :])
+                s = s + jnp.where(net.has_dn, wide(self.bbe[z, q, sl, :]), 0.0)
+                s = s + jnp.where(net.has_up, wide(self.bab[z, q, sl, :]), 0.0)
+                bm[q, sl, :] = s.astype(BF)
+            strips(rb, fold)
+        net.go(None, lambda: bm.at[net.ud, pl.ds(0, hb), :], lambda: bm.at[4, pl.ds(0, hb), :], lambda: bms.at[0], net.xn)
+        net.go(None, lambda: bm.at[net.ud, pl.ds(hb, hb), :], lambda: bm.at[5, pl.ds(0, hb), :], lambda: bms.at[1], net.yn)
+        net.go(None, lambda: bm.at[net.ux, pl.ds(0, hb), :], lambda: bm.at[6, pl.ds(0, hb), :], lambda: bms.at[2], net.xn)
+        net.go(None, lambda: bm.at[net.uy, pl.ds(hb, hb), :], lambda: bm.at[7, pl.ds(hb, hb), :], lambda: bms.at[3], net.yn)
+
+    def bquad2(self):
+        net, rb, hb, bm, bms = self.net, self.rb, self.hb, self.bm, self.bms
+        if not rb:
+            return
+
+        def add4(sl):
+            bm[4, sl, :] = (wide(bm[4, sl, :]) + wide(bm[net.uy, sl, :])).astype(BF)
+
+        def add5(sl):
+            bm[5, sl, :] = (wide(bm[5, sl, :]) + wide(bm[net.ux, pl.ds(hb + sl.start, 16), :])).astype(BF)
+
+        net.wait(None, lambda: bm.at[4, pl.ds(0, hb), :], bms.at[0])
+        strips(hb, add4)
+        net.go(None, lambda: bm.at[4, pl.ds(0, hb), :], lambda: bm.at[7, pl.ds(0, hb), :], lambda: bms.at[4], net.yn)
+        net.wait(None, lambda: bm.at[5, pl.ds(0, hb), :], bms.at[1])
+        strips(hb, add5)
+        net.go(None, lambda: bm.at[5, pl.ds(0, hb), :], lambda: bm.at[6, pl.ds(hb, hb), :], lambda: bms.at[5], net.xn)
+
+    def last(self, store):
+        net, cut, rb, hb, bm, bms = self.net, self.cut, self.rb, self.hb, self.bm, self.bms
+        z = net.z
+        self.square(z, None)
+
+        def own(sl):
+            s = self.local(z, sl)
+            s = s + jnp.where(net.has_dn, wide(self.be[z, sl, :]), 0.0)
+            s = s + jnp.where(net.has_up, wide(self.ab[z, sl, :]), 0.0)
+            store(sl, s)
+
+        net.wait(net.has_dn, lambda: self.be.at[z], self.bes.at[z])
+        net.wait(net.has_up, lambda: self.ab.at[z], self.abs_.at[z])
+        strips(cut, own)
         if rb:
-            bpass(zd)
-    def line(zd):
-        for half in (0, 1):
-            net.wait(None, lambda: fx.at[zd, pl.ds(half * h, h), :], fxs.at[zd, half])
-            net.wait(None, lambda: fy.at[zd, pl.ds(half * h, h), :], fys.at[zd, half])
-        def local(sl):
-            return f(P[u, zd, sl, :]) + f(fx[zd, sl, :]) + f(fy[zd, sl, :])
-        def start_sum(sl):
-            fx[zd, sl, :] = local(sl).astype(BF)
-        def plus(buf):
-            def g(sl): buf[zd, sl, :] = (local(sl) + f(buf[zd, sl, :])).astype(BF)
-            return g
-        if zd > 0:
-            pl.when(z == 0)(lambda: strips(cut, start_sum))
-            net.go(z == 0, lambda: fx.at[zd], lambda: be.at[zd], bes.at[zd], net.up)
-            mid = jnp.logical_and(z > 0, z < zd)
-            net.wait(mid, lambda: be.at[zd], bes.at[zd])
-            pl.when(mid)(lambda: strips(cut, plus(be)))
-            net.go(mid, lambda: be.at[zd], lambda: be.at[zd], bes.at[zd], net.up)
-        if zd < 3:
-            pl.when(z == 3)(lambda: strips(cut, start_sum))
-            net.go(z == 3, lambda: fx.at[zd], lambda: ab.at[zd], abs_.at[zd], net.dn)
-            mid = jnp.logical_and(z < 3, z > zd)
-            net.wait(mid, lambda: ab.at[zd], abs_.at[zd])
-            pl.when(mid)(lambda: strips(cut, plus(ab)))
-            net.go(mid, lambda: ab.at[zd], lambda: ab.at[zd], abs_.at[zd], net.dn)
-    def bquad():
-        net.wait(net.has_dn, lambda: bbe.at[z], bbes.at[z])
-        net.wait(net.has_up, lambda: bab.at[z], babs.at[z])
-        def fold(q, sl):
-            s = f(P[q, z, pl.ds(cut + sl.start, 16), :])
-            s = s + jnp.where(net.has_dn, f(bbe[z, q, sl, :]), 0.0)
-            s = s + jnp.where(net.has_up, f(bab[z, q, sl, :]), 0.0)
-            bm[q, sl, :] = s.astype(BF)
-        for q in range(4):
-            strips(rb, lambda sl: fold(q, sl))
-        net.go(None, lambda: bm.at[net.ud, pl.ds(0, hb), :], lambda: bm.at[4, pl.ds(0, hb), :], bms.at[0], net.xn)
-        net.go(None, lambda: bm.at[net.ud, pl.ds(hb, hb), :], lambda: bm.at[5, pl.ds(0, hb), :], bms.at[1], net.yn)
-        net.go(None, lambda: bm.at[net.ux, pl.ds(0, hb), :], lambda: bm.at[6, pl.ds(0, hb), :], bms.at[2], net.xn)
-        net.go(None, lambda: bm.at[net.uy, pl.ds(hb, hb), :], lambda: bm.at[7, pl.ds(hb, hb), :], bms.at[3], net.yn)
-    def bquad2():
-        net.wait(None, lambda: bm.at[4, pl.ds(0, hb), :], bms.at[0])
-        strips(hb, lambda sl: bm.__setitem__((4, sl, slice(None)), (f(bm[4, sl, :]) + f(bm[net.uy, sl, :])).astype(BF)))
-        net.go(None, lambda: bm.at[4, pl.ds(0, hb), :], lambda: bm.at[7, pl.ds(0, hb), :], bms.at[4], net.yn)
-        net.wait(None, lambda: bm.at[5, pl.ds(0, hb), :], bms.at[1])
-        strips(hb, lambda sl: bm.__setitem__((5, sl, slice(None)), (f(bm[5, sl, :]) + f(bm[net.ux, pl.ds(hb + sl.start, 16), :])).astype(BF)))
-        net.go(None, lambda: bm.at[5, pl.ds(0, hb), :], lambda: bm.at[6, pl.ds(hb, hb), :], bms.at[5], net.xn)
-    line(3)
-    line(0)
-    if rb:
-        bquad()
-    line(2)
-    if rb:
-        bquad2()
-    line(1)
-    def last(sl):
-        s = f(P[u, z, sl, :]) + f(fx[z, sl, :]) + f(fy[z, sl, :])
-        s = s + jnp.where(net.has_dn, f(be[z, sl, :]), 0.0)
-        s = s + jnp.where(net.has_up, f(ab[z, sl, :]), 0.0)
-        out_store(sl, s)
-    net.wait(net.has_dn, lambda: be.at[z], bes.at[z])
-    net.wait(net.has_up, lambda: ab.at[z], abs_.at[z])
-    strips(cut, last)
-    if rb:
-        net.wait(None, lambda: bm.at[6, pl.ds(0, hb), :], bms.at[2])
-        net.wait(None, lambda: bm.at[6, pl.ds(hb, hb), :], bms.at[5])
-        net.wait(None, lambda: bm.at[7, pl.ds(0, hb), :], bms.at[4])
-        net.wait(None, lambda: bm.at[7, pl.ds(hb, hb), :], bms.at[3])
-        strips(rb, lambda sl: out_store(pl.ds(cut + sl.start, 16), f(bm[u, sl, :]) + f(bm[6, sl, :]) + f(bm[7, sl, :])))
+            net.wait(None, lambda: bm.at[6, pl.ds(0, hb), :], bms.at[2])
+            net.wait(None, lambda: bm.at[6, pl.ds(hb, hb), :], bms.at[5])
+            net.wait(None, lambda: bm.at[7, pl.ds(0, hb), :], bms.at[4])
+            net.wait(None, lambda: bm.at[7, pl.ds(hb, hb), :], bms.at[3])
+            strips(rb, lambda sl: store(
+                pl.ds(cut + sl.start, 16), wide(bm[net.u, sl, :]) + wide(bm[6, sl, :]) + wide(bm[7, sl, :])))
+
 
 def rs_scratch(cut, R, D):
     h, rb = cut // 2, R - cut
@@ -797,13 +857,28 @@
             V(4, 4, max(rb, 16), D), V(4, 4, max(rb, 16), D), V(8, max(rb, 16), D),
             S((4,)), S((4,)), S((4, 2)), S((4, 2)), S((4,)), S((4,)), S((4,)), S((4,)), S((6,))]
 
+
 def rs_kernel(cut, P, o_ref, ssem, *scr):
     net = Net(ssem)
     net.barrier()
+    sc = Scatter(net, cut, P, scr)
+
     def store(sl, v):
         o_ref[sl, :] = v.astype(o_ref.dtype)
-    rs_body(net, cut, P, store, *scr)
+
+    for zd in (3, 0, 2, 1):
+        sc.first(zd)
+    for zd in (3, 0, 2, 1):
+        sc.mids(zd)
+    sc.hop(3, 0); sc.hop(0, 3); sc.bhop(3, 1); sc.bhop(0, 2)
+    sc.hop(2, 0); sc.hop(1, 3); sc.bhop(2, 1); sc.bhop(1, 2)
+    sc.hop(3, 1); sc.hop(0, 2); sc.bhop(3, 2); sc.bhop(0, 1)
+    sc.hop(1, 0); sc.hop(2, 3); sc.bquad()
+    sc.hop(2, 1); sc.hop(1, 2)
+    sc.hop(3, 2); sc.hop(0, 1); sc.bquad2()
+    sc.last(store)
     net.finish()
+
 
 def rs16(p, cid, cut=96, dtype=F32):
     _, _, R, D = p.shape
@@ -817,6 +892,158 @@
         compiler_params=pltpu.CompilerParams(collective_id=cid, has_side_effects=True, vmem_limit_bytes=56 * 2**20),
         name="scatter_rows",
     )(p)
+
+def group_of(t):
+    g = t // 2
+    return jnp.where(g == 0, 3, jnp.where(g == 1, 0, jnp.where(g == 2, 2, 1)))
+
+
+def expert_kernel(cut, n2, cot, share, gate, up, down, d_n2, p_out, hid_o, dg_o, du_o, dp_o,
+                  P, G, U, W, hid, dg, du, xb, cb, pb, wsem, xsem, csem, psem, osem, ssem, *scr):
+    net = Net(ssem)
+    for i, (src, dst) in enumerate(((gate, G), (up, U), (down, W))):
+        pltpu.make_async_copy(src, dst, wsem.at[i]).start()
+
+    def load(t, slot, start):
+        zd, j = group_of(t), lax.rem(t, 2)
+        for src, dst, sem in ((n2, xb, xsem), (cot, cb, csem)):
+            copy = pltpu.make_async_copy(src.at[pl.ds(2 * j, 2), zd], dst.at[slot], sem.at[slot])
+            if start:
+                copy.start()
+            else:
+                copy.wait()
+
+    load(0, 0, True)
+    net.barrier()
+    sc = Scatter(net, cut, P, scr)
+    for i, (src, dst) in enumerate(((gate, G), (up, U), (down, W))):
+        pltpu.make_async_copy(src, dst, wsem.at[i]).wait()
+    rows, width = P.shape[2], P.shape[3]
+    ff = G.shape[1]
+    tile = 256
+
+    def outs(t, slot):
+        zd, j = group_of(t), lax.rem(t, 2)
+        quads = pl.ds(2 * j, 2)
+        return (pltpu.make_async_copy(pb.at[slot], p_out.at[quads, zd], psem.at[slot]),
+                pltpu.make_async_copy(cb.at[slot], dp_o.at[quads, zd], osem.at[slot]))
+
+    def compute(t):
+        slot = lax.rem(t, 2)
+        zd, j = group_of(t), lax.rem(t, 2)
+        quads = pl.ds(2 * j, 2)
+
+        @pl.when(t >= 1)
+        def _():
+            for o in outs(t - 1, 1 - slot):
+                o.wait()
+
+        @pl.when(t < 7)
+        def _():
+            load(t + 1, 1 - slot, True)
+
+        load(t, slot, False)
+        weight = share[quads, zd]
+
+        def scale(i, _):
+            sl = pl.ds(pl.multiple_of(i * 16, 16), 16)
+            cb[slot, :, sl, :] = (share[quads, zd, sl, :] * cb[slot, :, sl, :].astype(F32)).astype(BF)
+            return 0
+
+        lax.fori_loop(0, rows // 16, scale, 0)
+        x = xb.at[slot]
+        d_prod = cb.at[slot]
+
+        def inner(n, _):
+            cols = pl.ds(pl.multiple_of(n * tile, tile), tile)
+            xv = x[...].reshape(2 * rows, width)
+            g = dot(xv, G[:, cols], ((1,), (0,)))
+            uu = dot(xv, U[:, cols], ((1,), (0,)))
+            dh = dot(d_prod[...].reshape(2 * rows, width), W[cols, :], ((1,), (1,)))
+            s = jax.nn.sigmoid(g)
+            gs = g * s
+            hid[quads, zd, :, cols] = (gs * uu).astype(BF).reshape(2, rows, tile)
+            dg[quads, zd, :, cols] = (dh * uu * s * (1.0 + g * (1.0 - s))).astype(BF).reshape(2, rows, tile)
+            du[quads, zd, :, cols] = (dh * gs).astype(BF).reshape(2, rows, tile)
+            return 0
+
+        lax.fori_loop(0, ff // tile, inner, 0)
+
+        def outer(n, _):
+            cols = pl.ds(pl.multiple_of(n * tile, tile), tile)
+            dgv = dg[quads, zd].reshape(2 * rows, ff)
+            duv = du[quads, zd].reshape(2 * rows, ff)
+            back = dot(dgv, G[cols, :], ((1,), (1,))) + dot(duv, U[cols, :], ((1,), (1,)))
+            P[quads, zd, :, cols] = back.astype(BF).reshape(2, rows, tile)
+            made = dot(hid[quads, zd].reshape(2 * rows, ff), W[:, cols], ((1,), (0,)))
+            made = made.astype(BF).astype(F32).reshape(2, rows, tile)
+            pb[slot, :, :, cols] = (weight * made).astype(BF)
+            return 0
+
+        lax.fori_loop(0, width // tile, outer, 0)
+        for o in outs(t, slot):
+            o.start()
+
+    steps = {
+        1: [lambda: sc.first(3)],
+        2: [lambda: sc.mids(3)],
+        3: [lambda: sc.first(0), lambda: sc.bhop(3, 1), lambda: sc.hop(3, 0)],
+        4: [lambda: sc.mids(0), lambda: sc.bhop(3, 2), lambda: sc.hop(3, 1)],
+        5: [lambda: sc.first(2), lambda: sc.bhop(0, 2), lambda: sc.hop(0, 3), lambda: sc.hop(3, 2)],
+        6: [lambda: sc.mids(2), lambda: sc.bhop(0, 1), lambda: sc.hop(0, 2)],
+        7: [lambda: sc.first(1), lambda: sc.bhop(2, 1), lambda: sc.hop(0, 1), lambda: sc.hop(2, 0), lambda: sc.hop(2, 3)],
+    }
+
+    def turn(t, _):
+        compute(t)
+        for at, todo in steps.items():
+            def act(todo=todo):
+                for one in todo:
+                    one()
+            pl.when(t == at)(act)
+        return 0
+
+    lax.fori_loop(0, 8, turn, 0)
+    for o in outs(7, 1):
+        o.wait()
+    keep = [pltpu.make_async_copy(a, b, wsem.at[i]) for i, (a, b) in enumerate(((hid, hid_o), (dg, dg_o), (du, du_o)))]
+    for k in keep:
+        k.start()
+    sc.mids(1)
+    sc.hop(2, 1); sc.bhop(1, 2)
+    sc.hop(1, 0); sc.hop(1, 3)
+    sc.bquad()
+    sc.hop(1, 2)
+    sc.bquad2()
+
+    def store(sl, v):
+        d_n2[sl, :] = v
+
+    sc.last(store)
+    for k in keep:
+        k.wait()
+    net.finish()
+
+
+def run_expert(n2, cot, share, gate, up, down, cid, cut=96):
+    _, _, R, D = n2.shape
+    ff = gate.shape[1]
+    DMA = pltpu.SemaphoreType.DMA
+    S = jax.ShapeDtypeStruct
+    V = lambda *s: pltpu.VMEM(s, BF)
+    A = pl.BlockSpec(memory_space=pl.ANY)
+    M = pl.BlockSpec(memory_space=pltpu.VMEM)
+    return pl.pallas_call(
+        functools.partial(expert_kernel, cut),
+        out_shape=(S((R, D), F32), S((4, 4, R, D), BF), S((4, 4, R, ff), BF), S((4, 4, R, ff), BF), S((4, 4, R, ff), BF), S((4, 4, R, D), BF)),
+        in_specs=[A, A, M, A, A, A],
+        out_specs=(M, A, A, A, A, A),
+        scratch_shapes=[V(4, 4, R, D), V(D, ff), V(D, ff), V(ff, D), V(4, 4, R, ff), V(4, 4, R, ff), V(4, 4, R, ff),
+                        V(2, 2, R, D), V(2, 2, R, D), V(2, 2, R, D),
+                        DMA((3,)), DMA((2,)), DMA((2,)), DMA((2,)), DMA((2,)), DMA((96,))] + rs_scratch(cut, R, D),
+        compiler_params=pltpu.CompilerParams(collective_id=cid, has_side_effects=True, vmem_limit_bytes=62 * 2**20),
+        name="expert",
+    )(n2, cot, share, gate, up, down)
 def swap_kernel(src, out, lsem, ssem, rsem):
     u, z, c = place()
     me = u * 8 + z * 2 + c
@@ -1014,7 +1241,10 @@
     def my_head(gain):
         return lax.dynamic_slice_in_dim(gain, chip * HEAD_DIM, HEAD_DIM, 0)
 
-    x_rows = ag16(inputs, 2).reshape(chips * rows, width).astype(F32)
+    x_rows = ag16(inputs, 2).reshape(chips * rows, width)
+    cotangent_later, x_rows = lax.optimization_barrier((cotangent, x_rows))
+    cot_rows = lax.all_gather(cotangent_later, mine, axis=0, tiled=True)
+    x_rows = x_rows.astype(F32)
     n1_rows = norm_rows(x_rows, gain_one).astype(BF)
     lin = dot(n1_rows, w_qkv, ((1,), (0,)))
     q_lin, k_lin, v_lin = lin[:, :HEAD_DIM], lin[:, HEAD_DIM : 2 * HEAD_DIM], lin[:, 2 * HEAD_DIM :]
@@ -1078,27 +1308,20 @@
     r2 = lax.rsqrt(jnp.mean(residual * residual, axis=1, keepdims=True) + EPS)
     normed_two = (residual * r2 * gain_two).astype(BF)
     n2_rows = ag16(normed_two, 5).reshape(tokens, width)
-    cot_rows = lax.all_gather(cotangent, mine, axis=0, tiled=True)
 
     joined = [
         jnp.concatenate(in_order(part, core_pair(part)), axis=0)
         for part in (expert_gate, expert_up, expert_down)
     ]
     gate_full, up_full, down_full = joined
-    gate_pre = dot(n2_rows, gate_full, ((1,), (0,)))
-    up_pre = dot(n2_rows, up_full, ((1,), (0,)))
-    sigma = jax.nn.sigmoid(gate_pre)
-    hidden = (gate_pre * sigma * up_pre).astype(BF)
-    produced = dot(hidden, down_full, ((1,), (0,))).astype(BF)
-    mixed = lax.psum_scatter(
-        (share * produced.astype(F32)).astype(BF), mine, scatter_dimension=0, tiled=True)
+    blocks = (4, 4, rows, width)
+    d_normed_two, mixed, hidden, d_gate_pre, d_up_pre, d_produced = run_expert(
+        n2_rows.reshape(blocks), cot_rows.reshape(blocks), share.reshape(4, 4, rows, 1),
+        gate_full, up_full, down_full, 6)
+    mixed = lax.psum_scatter(mixed.reshape(tokens, width), mine, scatter_dimension=0, tiled=True)
     output = residual + mixed.astype(F32)
-    d_produced = (share * cot_rows.astype(F32)).astype(BF)
-    d_hidden = dot(d_produced, down_full, ((1,), (1,)))
-    d_gate_pre = (d_hidden * up_pre * sigma * (1.0 + gate_pre * (1.0 - sigma))).astype(BF)
-    d_up_pre = (d_hidden * gate_pre * sigma).astype(BF)
-    d_pair = dot(d_gate_pre, gate_full, ((1,), (1,))) + dot(d_up_pre, up_full, ((1,), (1,)))
-    d_normed_two = rs16(to_blocks(d_pair), 6)
+    hidden, d_gate_pre, d_up_pre, d_produced = (
+        v.reshape(tokens, v.shape[-1]) for v in (hidden, d_gate_pre, d_up_pre, d_produced))
 
     def shared_grad(full):
         size = full.shape[0] // 2

time: 1070 us -> 910 us (0.85)
  matrix products: 158 us -> 70.6 us
  Pallas kernels: 704 us -> 663 us
  other arithmetic: 91.4 us -> 79.3 us
  local copies, waits for them, and re-layouts: 67.4 us -> 55.9 us
    pallas_call x0 -> x1, Pallas kernels: none -> 119 us  [run_expert(): pl.pallas_call(functools.partial(expert_kernel, cut), out_shape=(S((R, D)...]
    pallas_call x3 -> x2, Pallas kernels: 330 us -> 230 us  [rs16(): pl.pallas_call(functools.partial(rs_kernel, cut), out_shape=jax.ShapeDtyp...]
    dot_general x16 -> x10, matrix products: 158 us -> 70.6 us  [dot(): lax.dot_general(a, b, (dims, ((), ())), preferred_element_type=jnp.float32)]
    pallas_call x3, Pallas kernels: 275 us -> 211 us  [ag16(): pl.pallas_call(functools.partial(ag_kernel, cut), out_shape=jax.ShapeDtyp...]
    convert_element_type x2 -> x1, other arithmetic: 17.2 us -> 0.92 us  [local_chip(): d_q_lin.astype(BF)]
    dot_general x1 -> x0, local copies, waits for them, and re-layouts: 12.4 us -> none  [dot(): lax.dot_general(a, b, (dims, ((), ())), preferred_element_type=jnp.float32)]
    unnamed x178 -> x140, local copies, waits for them, and re-layouts: 26.4 us -> 23.1 us
  transfers between devices with their start and end apart: 17 -> 17, of which waited for: 3 -> 3; matrix products, arithmetic and copies ran while one was open for 23% -> 19% of each run, Pallas kernels for 66% -> 42%
where the time goes in v2:
time: 910 us; the launch traced here: 903 us
  Pallas kernels  663 us (73%)
  other arithmetic  79.3 us (9%)
  matrix products  70.6 us (8%)
  local copies, waits for them, and re-layouts  55.9 us (6%)
  between operations  15.5 us (2%)
  starting transfers between devices  12.1 us (1%)
    pallas_call x2, Pallas kernels, rs16(): pl.pallas_call(functools.partial(rs_kernel, cut), out_shape=jax.ShapeDtyp...  230 us
    pallas_call x3, Pallas kernels, ag16(): pl.pallas_call(functools.partial(ag_kernel, cut), out_shape=jax.ShapeDtyp...  211 us
    pallas_call x1, Pallas kernels, run_expert(): pl.pallas_call(functools.partial(expert_kernel, cut), out_shape=(S((R, D)...  119 us
    dot_general x10, matrix products, dot(): lax.dot_general(a, b, (dims, ((), ())), preferred_element_type=jnp.float32)  70.6 us
    pallas_call x2, Pallas kernels, swap(): pl.pallas_call(swap_kernel, out_shape=jax.ShapeDtypeStruct((2 * chips, r,...  41.7 us
    pallas_call x2, Pallas kernels, spread(): pl.pallas_call(spread_kernel, out_shape=jax.ShapeDtypeStruct((16,) + bloc...  34.7 us
    unnamed x140, local copies, waits for them, and re-layouts  23.1 us
  transfers between devices with their start and end apart: 17, of which 3 were waited for; matrix products, arithmetic and copies ran while one was open for 19% of the time, Pallas kernels for 42%

profile of v2, /device:TPU:0, one launch (start us, length us, event | category | flops | bytes accessed | tf_op | source)
XLA Modules:
  0.0 903.2 jit_solution(14059240799248819537)
XLA Ops:
  8.3 72.2 %gather_rows.3 = bf16[4,4,128,2048]{3,2,1,0:T(8,128)(2,1)} custom-call(bf16[128,2048]{1,0:T(8,128)(2,1)S(1)} %copy-done.5), custom_call_target="tpu_custom_call" | custom-call | tf_op jit(solution)/shard_map/gather_rows/pallas_call | solution.py:629
  88.6 31.4 %swap_rows.2 = f32[32,8,128]{2,1,0:T(8,128)} custom-call(f32[16,8,128]{2,1,0:T(8,128)} %maximum_maximum_fusion.src), custom_call_target="tpu_custom_call" | custom-call | tf_op jit(solution)/shard_map/swap_rows/pallas_call | solution.py:1088
  122.1 5.7 fusion.35
  128.8 5.1 fusion
  166.3 17.4 %spread_rows.2 = f32[16,32,128]{2,1,0:T(8,128)} custom-call(f32[32,128]{1,0:T(8,128)} %reshape.329.src), custom_call_target="tpu_custom_call" | custom-call | tf_op jit(solution)/shard_map/spread_rows/pallas_call | solution.py:1133
  193.2 11.5 %attend.1 = (bf16[2048,128]{1,0:T(8,128)(2,1)S(1)}, f32[2048,1]{1,0:T(8,128)S(1)}) custom-call(bf16[2048,128]{1,0:T(8,128)(2,1)S(1)} %fusion.29.q_ref, bf16[5120,128]{1,0:T(8,128)(2,1)S(1)} %get-tuple-element.72.k_ref, bf16[5120,128]{1,0:T(8,128)(2,1)S(1)} %get-tuple-element.71.v_ref, s32[2048,1]{1,0:T(8,128)S(1)} %copy.153.qs_ref, s32[1,5120]{1,0:T(1,128)S(1)} %bitcast.168), custom_call_target="tpu_custom_call" | custom-call | tf_op jit(solution)/shard_map/attend/pallas_call | solution.py:1294
  206.7 5.6 convolution_convert_fusion.1
  212.3 82.1 %scatter_rows.2 = f32[128,2048]{1,0:T(8,128)} custom-call(bf16[4,4,128,2048]{3,2,1,0:T(8,128)(2,1)} %bitcast.172), custom_call_target="tpu_custom_call" | custom-call | tf_op jit(solution)/shard_map/scatter_rows/pallas_call | solution.py:886
  298.3 65.3 %gather_rows.4.n2 = bf16[4,4,128,2048]{3,2,1,0:T(8,128)(2,1)} custom-call(bf16[128,2048]{1,0:T(8,128)(2,1)S(1)} %multiply_convert_fusion.x_ref), custom_call_target="tpu_custom_call" | custom-call | tf_op jit(solution)/shard_map/gather_rows/pallas_call | solution.py:629
  363.6 118.8 %expert.1 = (f32[128,2048]{1,0:T(8,128)}, bf16[4,4,128,2048]{3,2,1,0:T(8,128)(2,1)}, bf16[4,4,128,1024]{3,2,1,0:T(8,128)(2,1)}, bf16[4,4,128,1024]{3,2,1,0:T(8,1...) custom-call(bf16[4,4,128,2048]{3,2,1,0:T(8,128)(2,1)} %gather_rows.4.n2, ...), custom_call_target="tpu_custom_call" | custom-call | tf_op jit(solution)/shard_map/expert/pallas_call | solution.py:1036
  486.3 73.7 %gather_rows.5 = bf16[4,4,128,2048]{3,2,1,0:T(8,128)(2,1)} custom-call(bf16[128,2048]{1,0:T(8,128)(2,1)S(1)} %fusion.64.x_ref), custom_call_target="tpu_custom_call" | custom-call | tf_op jit(solution)/shard_map/gather_rows/pallas_call | solution.py:629
  560.0 5.9 convolution_convert_fusion.2.do_ref
  568.3 15.5 %attend_back.1 = (bf16[2048,128]{1,0:T(8,128)(2,1)S(1)}, f32[5120,128]{1,0:T(8,128)}, f32[5120,128]{1,0:T(8,128)}) custom-call(bf16[2048,128]{1,0:T(8,128)(2,1)S(1)} %copy-done.8, bf16[5120,128]{1,0:T(8,128)(2,1)S(1)} %copy-done.2, bf16[5120,128]{1,0:T(8,128)(2,1)} %copy-done, s32[2048,1]{1,0:T(8,128)S(1)} %copy-done.4, s32[1,5120]{1,0:T(1,128)S(1)} %bitcast.169, ...), custom_call_target="tpu_custom_call" | custom-call | tf_op jit(solution)/shard_map/attend_back/pallas_call | solution.py:1348
  589.5 13.5 %convolution_bitcast_fusion.2 = f32[2048,1024]{1,0:T(8,128)S(1)} fusion(bf16[4,4,128,2048]{3,2,1,0:T(8,128)(2,1)} %gather_rows.4.n2, bf16[4,4,128,1024]{3,2,1,0:T(8,128)(2,1)} %get-tuple-element.35), kind=kOutput, calls=%fused_computation.13 | convolution fusion | flops 8589934592 | bytes 20971520 | tf_op jit(solution)/shard_map/dot_general | solution.py:1191
  607.9 12.0 %convolution_bitcast_fusion.1 = f32[2048,1024]{1,0:T(8,128)S(1)} fusion(bf16[4,4,128,2048]{3,2,1,0:T(8,128)(2,1)} %gather_rows.4.n2, bf16[4,4,128,1024]{3,2,1,0:T(8,128)(2,1)S(1)} %copy-done.58), kind=kOutput, calls=%fused_computation.12 | convolution fusion | flops 8589934592 | bytes 20971520 | tf_op jit(solution)/shard_map/dot_general | solution.py:1191
  625.3 9.1 %convolution_bitcast_fusion = f32[1024,2048]{1,0:T(8,128)S(1)} fusion(bf16[4,4,128,1024]{3,2,1,0:T(8,128)(2,1)S(1)} %copy-done.57, bf16[4,4,128,2048]{3,2,1,0:T(8,128)(2,1)S(1)} %bitcast.230), kind=kOutput, calls=%fused_computation.11 | convolution fusion | flops 8589934592 | bytes 20971520 | tf_op jit(solution)/shard_map/dot_general | solution.py:1191
  648.8 17.2 %spread_rows.3 = f32[16,32,128]{2,1,0:T(8,128)} custom-call(f32[32,128]{1,0:T(8,128)} %reshape.340.src), custom_call_target="tpu_custom_call" | custom-call | tf_op jit(solution)/shard_map/spread_rows/pallas_call | solution.py:1133
  669.9 8.1 convolution_convert_fusion
  678.0 147.5 %scatter_rows.3 = f32[128,2048]{1,0:T(8,128)} custom-call(bf16[4,4,128,2048]{3,2,1,0:T(8,128)(2,1)} %bitcast.182), custom_call_target="tpu_custom_call" | custom-call | tf_op jit(solution)/shard_map/scatter_rows/pallas_call | solution.py:886
  827.1 9.9 %fusion.3 = f32[2048,384]{1,0:T(8,128)} fusion(bf16[2048,2048]{1,0:T(8,128)(2,1)} %bitcast.174, f32[2048]{0:T(1024)S(1)} %mul.416, f32[2048]{0:T(1024)S(1)} %add_rsqrt_fusion, bf16[2048,128]{1,0:T(8,128)(2,1)S(1)} %bitcast.207, bf16[2048,128]{1,0:T(8,128)(2,1)S(1)} %subtract_convert_fusion, bf16[2048,128]{1,0:T(8,128)(2,1)S(1)} %subtract_convert_fusion.1), kind=kOutput, calls=%fused_computation.25 | convolution fusion | flops 3242721280 | bytes 13123584 | tf_op jit(solution)/shard_map/dot_general | solution.py:1191
  837.6 10.3 %swap_rows.3 = f32[32,8,128]{2,1,0:T(8,128)} custom-call(f32[16,8,128]{2,1,0:T(8,128)} %maximum_maximum_fusion.1.src), custom_call_target="tpu_custom_call" | custom-call | tf_op jit(solution)/shard_map/swap_rows/pallas_call | solution.py:1088
  861.2 6.0 convert_add_fusion.2
  867.2 6.0 convert_add_fusion.1
  877.6 5.1 all-to-all-done.1
  (296 shorter events, 132.6 us)
Async XLA Ops:
  7.2 356.4 %all-gather.2.cloned.1.call-start = ((), (), s32[]{:S(2)}) async-start(), calls=%async_computation.3 | async-start | bytes 8912896 | tf_op jit(solution)/shard_map/all_gather | solution.py:1246
  8.3 72.2 %copy-start.46 = (bf16[64,2048]{1,0:T(8,128)(2,1)S(1)}, bf16[64,2048]{1,0:T(8,128)(2,1)}, u32[]{:S(2)}) copy-start(bf16[64,2048]{1,0:T(8,128)(2,1)} %param.26) | copy-start | bytes 786436
  8.3 72.4 %copy-start.47 = (bf16[64,2048]{1,0:T(8,128)(2,1)S(1)}, bf16[64,2048]{1,0:T(8,128)(2,1)}, u32[]{:S(2)}) copy-start(bf16[64,2048]{1,0:T(8,128)(2,1)} %param.25) | copy-start | bytes 786436
  8.3 72.4 %copy-start.48 = (bf16[64,2048]{1,0:T(8,128)(2,1)S(1)}, bf16[64,2048]{1,0:T(8,128)(2,1)}, u32[]{:S(2)}) copy-start(bf16[64,2048]{1,0:T(8,128)(2,1)} %param.24) | copy-start | bytes 786436
  82.0 56.8 %all-to-all-start = ((bf16[16,3,64,128]{3,2,1,0:T(8,128)(2,1)}), bf16[16,3,64,128]{3,2,1,0:T(8,128)(2,1)}, u32[]{:S(2)}, u32[]{:S(2)}) async-start(bf16[16,3,64,128]{3,2,1,0:T(8,128)(2,1)} %copy.147), calls=%async_computation | async-start | bytes 1572864 | tf_op jit(solution)/shard_map/all_to_all | solution.py:1236
  86.2 806.5 %reduce-scatter.2.cloned.1.call-start = ((), (), s32[]{:S(2)}) async-start(), calls=%async_computation.4 | async-start | bytes 8912896 | tf_op jit(solution)/shard_map/reduce_scatter | solution.py:1321
  86.3 50.6 %collective-permute-start.2 = (bf16[64,2048]{1,0:T(8,128)(2,1)}, bf16[64,2048]{1,0:T(8,128)(2,1)}, u32[]{:S(2)}, u32[]{:S(2)}) collective-permute-start(bf16[64,2048]{1,0:T(8,128)(2,1)} %param.27), channel_id=1, source_target_pairs={{0,1},{1,0},{2,3},{3,2},{4,5},{5,4},{6,7},{7,6},{8,9},{9,8},{10,11... | collective-permute-start | bytes 786440 | tf_op jit(solution)/shard_map/ppermute | solution.py:1187
  86.4 55.2 %collective-permute-start.4 = (bf16[1024,1024]{1,0:T(8,128)(2,1)S(1)}, bf16[1024,1024]{1,0:T(8,128)(2,1)}, u32[]{:S(2)}, u32[]{:S(2)}) collective-permute-start(bf16[1024,1024]{1,0:T(8,128)(2,1)S(1)} %copy-done.35), channel_id=1, source_target_pairs={{0,1},{1,0},{2,3},{3,2},{4,5},{5,4},{6,7},{7,6},{8,9},{9,8},{10,11... | collective-permute-start | bytes 6291464 | tf_op jit(solution)/shard_map/ppermute | solution.py:1187
  86.9 54.7 %collective-permute-start.3 = (bf16[1024,1024]{1,0:T(8,128)(2,1)}, bf16[1024,1024]{1,0:T(8,128)(2,1)}, u32[]{:S(2)}, u32[]{:S(2)}) collective-permute-start(bf16[1024,1024]{1,0:T(8,128)(2,1)} %param.31), channel_id=1, source_target_pairs={{0,1},{1,0},{2,3},{3,2},{4,5},{5,4},{6,7},{7,6},{8,9},{9,8},{10,11... | collective-permute-start | bytes 6291464 | tf_op jit(solution)/shard_map/ppermute | solution.py:1187
  87.0 52.0 %collective-permute-start.5 = (bf16[512,2048]{1,0:T(8,128)(2,1)}, bf16[512,2048]{1,0:T(8,128)(2,1)}, u32[]{:S(2)}, u32[]{:S(2)}) collective-permute-start(bf16[512,2048]{1,0:T(8,128)(2,1)} %param.33), channel_id=1, source_target_pairs={{0,1},{1,0},{2,3},{3,2},{4,5},{5,4},{6,7},{7,6},{8,9},{9,8},{10,11... | collective-permute-start | bytes 6291464 | tf_op jit(solution)/shard_map/ppermute | solution.py:1187
  138.8 13.9 %collective-permute-start = (bf16[16,3,64,128]{3,2,1,0:T(8,128)(2,1)}, bf16[16,3,64,128]{3,2,1,0:T(8,128)(2,1)S(1)}, u32[]{:S(2)}, u32[]{:S(2)}) collective-permute-start(bf16[16,3,64,128]{3,2,1,0:T(8,128)(2,1)} %all-to-all-done), channel_id=1, source_target_pairs={{0,1},{1,0},{2,3},{3,2},{4,5},{5,4},{6,7},{7,6},{8,9},{9,8},{10,11... | collective-permute-start | bytes 2359304 | tf_op jit(solution)/shard_map/ppermute | solution.py:1187
  189.9 2.7 collective-permute-start.1
  212.3 82.1 %copy-start.6 = (bf16[128,2048]{1,0:T(8,128)(2,1)S(1)}, bf16[128,2048]{1,0:T(8,128)(2,1)}, u32[]{:S(2)}) copy-start(bf16[128,2048]{1,0:T(8,128)(2,1)} %x_ref.1) | copy-start | bytes 1572868
  486.3 73.7 %copy-start.42 = (bf16[64,2048]{1,0:T(8,128)(2,1)S(1)}, bf16[64,2048]{1,0:T(8,128)(2,1)}, u32[]{:S(2)}) copy-start(bf16[64,2048]{1,0:T(8,128)(2,1)} %get-tuple-element.90) | copy-start | bytes 786436
  486.3 73.7 %copy-start.44 = (bf16[64,2048]{1,0:T(8,128)(2,1)S(1)}, bf16[64,2048]{1,0:T(8,128)(2,1)}, u32[]{:S(2)}) copy-start(bf16[64,2048]{1,0:T(8,128)(2,1)} %get-tuple-element.91) | copy-start | bytes 786436
  587.6 51.9 %collective-permute-start.6 = (bf16[2,16,128,128]{3,2,1,0:T(8,128)(2,1)}, bf16[2,16,128,128]{3,2,1,0:T(8,128)(2,1)}, u32[]{:S(2)}, u32[]{:S(2)}) collective-permute-start(bf16[2,16,128,128]{3,2,1,0:T(8,128)(2,1)} %fusion.27), channel_id=1, source_target_pairs={{0,1},{1,0},{2,3},{3,2},{4,5},{5,4},{6,7},{7,6},{8,9},{9,8},{10,11... | collective-permute-start | bytes 3145736 | tf_op jit(solution)/shard_map/ppermute | solution.py:1187
  589.2 49.5 %collective-permute-start.8 = (bf16[64,2048]{1,0:T(8,128)(2,1)S(1)}, bf16[64,2048]{1,0:T(8,128)(2,1)S(1)}, u32[]{:S(2)}, u32[]{:S(2)}) collective-permute-start(bf16[64,2048]{1,0:T(8,128)(2,1)S(1)} %dynamic-slice_convert_fusion.3), channel_id=1, source_target_pairs={{0,1},{1,0},{2,3},{3,2},{4,5},{5,4},{6,7},{7,6},{8,9},{9,8},{10,11... | collective-permute-start | bytes 786440 | tf_op jit(solution)/shard_map/ppermute | solution.py:1187
  604.6 256.6 %collective-permute-start.10 = (bf16[1024,1024]{1,0:T(8,128)(2,1)}, bf16[1024,1024]{1,0:T(8,128)(2,1)}, u32[]{:S(2)}, u32[]{:S(2)}) collective-permute-start(bf16[1024,1024]{1,0:T(8,128)(2,1)} %dynamic-slice_convert_fusion.2), channel_id=1, source_target_pairs={{0,1},{1,0},{2,3},{3,2},{4,5},{5,4},{6,7},{7,6},{8,9},{9,8},{10,11... | collective-permute-start | bytes 6291464 | tf_op jit(solution)/shard_map/ppermute | solution.py:1187
  621.7 245.6 %collective-permute-start.11 = (bf16[1024,1024]{1,0:T(8,128)(2,1)}, bf16[1024,1024]{1,0:T(8,128)(2,1)}, u32[]{:S(2)}, u32[]{:S(2)}) collective-permute-start(bf16[1024,1024]{1,0:T(8,128)(2,1)} %dynamic-slice_convert_fusion.1), channel_id=1, source_target_pairs={{0,1},{1,0},{2,3},{3,2},{4,5},{5,4},{6,7},{7,6},{8,9},{9,8},{10,11... | collective-permute-start | bytes 6291464 | tf_op jit(solution)/shard_map/ppermute | solution.py:1187
  636.4 236.9 %collective-permute-start.12 = (bf16[512,2048]{1,0:T(8,128)(2,1)}, bf16[512,2048]{1,0:T(8,128)(2,1)}, u32[]{:S(2)}, u32[]{:S(2)}) collective-permute-start(bf16[512,2048]{1,0:T(8,128)(2,1)} %dynamic-slice_convert_fusion), channel_id=1, source_target_pairs={{0,1},{1,0},{2,3},{3,2},{4,5},{5,4},{6,7},{7,6},{8,9},{9,8},{10,11... | collective-permute-start | bytes 6291464 | tf_op jit(solution)/shard_map/ppermute | solution.py:1187
  678.0 149.1 %copy-start.45 = (bf16[1,16,128,128]{3,2,1,0:T(8,128)(2,1)S(1)}, bf16[1,16,128,128]{3,2,1,0:T(8,128)(2,1)}, u32[]{:S(2)}) copy-start(bf16[1,16,128,128]{3,2,1,0:T(8,128)(2,1)} %get-tuple-element.82) | copy-start | bytes 1572868
  850.5 3.0 collective-permute-start.7
  850.7 2.2 collective-permute-start.9
  856.0 26.8 %all-to-all-start.1 = ((bf16[16,64,384]{2,1,0:T(8,128)(2,1)}), bf16[16,64,384]{2,1,0:T(8,128)(2,1)S(1)}, u32[]{:S(2)}, u32[]{:S(2)}) async-start(bf16[16,64,384]{2,1,0:T(8,128)(2,1)} %fusion.16), calls=%async_computation.2 | async-start | bytes 1572864 | tf_op jit(solution)/shard_map/all_to_all | solution.py:1375
  (59 other events, 467.0 us)
Sparse Core Ops, SparseCore 0:
  80.6 126.2 all-gather.1
  588.1 242.4 reduce-scatter.1

commit v3 on v2

--- a/solution.py
+++ b/solution.py
@@ -893,96 +893,424 @@
         name="scatter_rows",
     )(p)
 
+
+class Gather:
+    def __init__(self, net, rows, cut, at, plane, sems):
+        self.net, self.rows, self.cut, self.ref, self.plane = net, rows, cut, at, plane
+        self.zr, self.xr, self.yr, self.d1, self.d2, self.br, self.bz = sems
+        self.h, self.rb = cut // 2, rows - cut
+        self.hb = self.rb // 2
+        z = net.z
+        self.near = []
+        for s in range(4):
+            zl, zh = z - s, z + s
+            self.near.append((
+                (jnp.maximum(zl, 0), zl >= 0, jnp.logical_and(zl >= 0, net.has_up), net.up),
+                (jnp.minimum(zh, 3), zh < 4, jnp.logical_and(zh < 4, net.has_dn), net.dn)))
+
+    def same(self, cond, uu, zz, lo, n, sem, dev):
+        ref = lambda: self.ref(uu, zz, lo, n)
+        self.net.go(cond, ref, ref, sem, dev)
+
+    def outward(self, zz, cond):
+        net, cut = self.net, self.cut
+        self.same(cond, net.u, zz, 0, cut, lambda: self.xr.at[zz], net.xn)
+        self.same(cond, net.u, zz, 0, cut, lambda: self.yr.at[zz], net.yn)
+
+    def begin(self):
+        net, cut, rb, z = self.net, self.cut, self.rb, self.net.z
+        self.same(net.has_up, net.u, z, 0, cut, lambda: self.zr.at[z], net.up)
+        self.same(net.has_dn, net.u, z, 0, cut, lambda: self.zr.at[z], net.dn)
+        if rb:
+            self.same(None, net.u, z, cut, rb, lambda: self.br.at[0], net.xn)
+            self.same(None, net.u, z, cut, rb, lambda: self.br.at[1], net.yn)
+        self.outward(z, None)
+
+    def begin2(self):
+        net, cut, rb, hb, z = self.net, self.cut, self.rb, self.hb, self.net.z
+        if rb:
+            net.wait(None, lambda: self.ref(net.ux, z, cut, rb), self.br.at[0])
+            self.same(None, net.ux, z, cut, hb, lambda: self.br.at[2], net.yn)
+            net.wait(None, lambda: self.ref(net.uy, z, cut, rb), self.br.at[1])
+            self.same(None, net.uy, z, cut + hb, hb, lambda: self.br.at[3], net.xn)
+
+    def along(self, s):
+        net = self.net
+        for zz, cond, fwd, dev in self.near[s]:
+            net.wait(cond, lambda zz=zz: self.ref(net.u, zz, 0, self.cut), self.zr.at[zz])
+            self.same(fwd, net.u, zz, 0, self.cut, lambda zz=zz: self.zr.at[zz], dev)
+            self.outward(zz, cond)
+
+    def quads(self, s):
+        net, cut, rb, hb, z = self.net, self.cut, self.rb, self.hb, self.net.z
+        if not rb:
+            return
+        if s == 0:
+            net.wait(None, lambda: self.ref(net.ud, z, cut, hb), self.br.at[2])
+            net.wait(None, lambda: self.ref(net.ud, z, cut + hb, hb), self.br.at[3])
+            whole = lambda: self.plane(z, cut, rb)
+            net.go(net.has_up, whole, whole, lambda: self.bz.at[z], net.up)
+            net.go(net.has_dn, whole, whole, lambda: self.bz.at[z], net.dn)
+            return
+        for zz, cond, fwd, dev in self.near[s]:
+            whole = lambda zz=zz: self.plane(zz, cut, rb)
+            net.wait(cond, whole, self.bz.at[zz])
+            net.go(fwd, whole, whole, lambda zz=zz: self.bz.at[zz], dev)
+
+    def planes(self, s):
+        if s == 0:
+            return ((self.net.z, None),)
+        return tuple((zz, cond) for zz, cond, _f, _d in self.near[s])
+
+    def cross(self, s):
+        net, h, cut = self.net, self.h, self.cut
+        for zz, cond in self.planes(s):
+            net.wait(cond, lambda zz=zz: self.ref(net.ux, zz, 0, cut), self.xr.at[zz])
+            self.same(cond, net.ux, zz, 0, h, lambda zz=zz: self.d1.at[zz], net.yn)
+            net.wait(cond, lambda zz=zz: self.ref(net.uy, zz, 0, cut), self.yr.at[zz])
+            self.same(cond, net.uy, zz, h, h, lambda zz=zz: self.d2.at[zz], net.xn)
+
+    def settle(self, s):
+        net, h = self.net, self.h
+        for zz, cond in self.planes(s):
+            net.wait(cond, lambda zz=zz: self.ref(net.ud, zz, 0, h), self.d1.at[zz])
+            net.wait(cond, lambda zz=zz: self.ref(net.ud, zz, h, h), self.d2.at[zz])
+
+
+def ag_sems():
+    S = pltpu.SemaphoreType.DMA
+    return [S((4,)) for _ in range(7)]
+
+
+def greet(net, chips=16):
+    bar = pltpu.get_barrier_semaphore()
+
+    def hello(j, _):
+        t = lax.rem(net.u * 4 + net.z + j, chips)
+        pl.semaphore_signal(bar, inc=1, device_id=(t // 4, lax.rem(t, 4), net.c), device_id_type=MESH)
+        return 0
+
+    lax.fori_loop(1, chips, hello, 0)
+    pl.semaphore_signal(bar, inc=1, device_id=(net.u, net.z, 1 - net.c), device_id_type=MESH)
+    pl.semaphore_wait(bar, chips)
+
+
+def each_chip(net, body, chips=16):
+    def one(j, _):
+        t = lax.rem(net.u * 4 + net.z + j, chips)
+        body(t, (t // 4, lax.rem(t, 4), net.c))
+        return 0
+
+    lax.fori_loop(1, chips, one, 0)
+
+
+def remote(src, dst, ssem, rsem, dev):
+    return pltpu.make_async_remote_copy(
+        src_ref=src, dst_ref=dst, send_sem=ssem, recv_sem=rsem, device_id=dev, device_id_type=MESH)
+
+
+def landed(ref, sem):
+    pltpu.make_async_copy(ref, ref, sem).wait()
+
+
+def row_sums(v):
+    return jnp.sum(v.T, axis=0, keepdims=True)
+
+
+def column(row):
+    return jnp.broadcast_to(row, (row.shape[1], row.shape[1])).T
+
+
+def share_sums(net, sums, sums_all, out, lsem, ssem, rsem):
+    me = net.u * 4 + net.z
+    own = pltpu.make_async_copy(sums, sums_all.at[me], lsem)
+    own.start()
+    each_chip(net, lambda t, dev: remote(sums, sums_all.at[me], ssem, rsem, dev).start())
+    own.wait()
+    part = sums_all.at[pl.ds(0, 15)]
+    landed(part, rsem)
+    total = sums_all[0]
+    for i in range(1, 16):
+        total = total + sums_all[i]
+    out[...] = total
+    landed(part, ssem)
+
+
+def qkv_kernel(cut, x_ref, cols, gain, n1_o, lin, wf, tot, X, nb, sums, sums_all, lsem, nsem, msem, ssem, *gs):
+    net = Net(ssem)
+    u, z, c = net.u, net.z, net.c
+    me = u * 4 + z
+    rows, width = X.shape[2], X.shape[3]
+    partner = (u, z, 1 - c)
+    own = pltpu.make_async_copy(x_ref, X.at[u, z], lsem.at[0])
+    own.start()
+    own_w = pltpu.make_async_copy(cols.at[me], wf.at[me, c], lsem.at[1])
+    own_w.start()
+    greet(net)
+    own.wait()
+    ga = Gather(net, rows, cut, lambda uu, zz, lo, n: X.at[uu, zz, pl.ds(lo, n), :],
+                lambda zz, lo, n: X.at[:, zz, pl.ds(lo, n), :], gs)
+    ga.begin()
+    each_chip(net, lambda t, dev: remote(cols.at[t], wf.at[me, c], msem.at[0], msem.at[1], dev).start())
+
+    def plane(zz):
+        def chunk(uu, _):
+            slot = lax.rem(uu, 2)
+            k = uu * 4 + zz
+
+            def norm(i, _):
+                sl = pl.ds(pl.multiple_of(i * 16, 16), 16)
+                v = X[uu, zz, sl, :].astype(F32)
+                r = lax.rsqrt(jnp.mean(v * v, axis=1, keepdims=True) + EPS)
+                nb[slot, sl, :] = (v * r * gain[...]).astype(BF)
+                return 0
+
+            def stored(s):
+                return pltpu.make_async_copy(nb.at[s], n1_o.at[k], nsem.at[s])
+
+            pl.when(uu >= 2)(lambda: stored(slot).wait())
+            lax.fori_loop(0, rows // 16, norm, 0)
+            stored(slot).start()
+            got = dot(nb[slot], wf[...].reshape(width, wf.shape[-1]), ((1,), (0,)))
+            lin[k] = got
+            q, kk = got[:, :128], got[:, 128:256]
+            sums[pl.ds(k, 1), :] = row_sums(q * q)
+            sums[pl.ds(16 + k, 1), :] = row_sums(kk * kk)
+            return 0
+
+        lax.fori_loop(0, 4, chunk, 0)
+        for s in (0, 1):
+            pltpu.make_async_copy(nb.at[s], n1_o.at[0], nsem.at[s]).wait()
+
+    def compute(s):
+        for zz, cond in ga.planes(s):
+            if cond is None:
+                plane(zz)
+            else:
+                pl.when(cond)(lambda zz=zz: plane(zz))
+
+    ga.begin2()
+    ga.along(1)
+    ga.quads(0)
+    ga.cross(0)
+    own_w.wait()
+    landed(wf.at[pl.ds(0, 15), 0], msem.at[1])
+    to_partner = remote(wf.at[:, c], wf.at[:, c], msem.at[2], msem.at[3], partner)
+    to_partner.start()
+    ga.along(2)
+    ga.quads(1)
+    ga.cross(1)
+    ga.settle(0)
+    landed(wf.at[:, 1 - c], msem.at[3])
+    compute(0)
+    ga.along(3)
+    ga.quads(2)
+    ga.cross(2)
+    ga.settle(1)
+    compute(1)
+    ga.quads(3)
+    ga.cross(3)
+    ga.settle(2)
+    compute(2)
+    ga.settle(3)
+    compute(3)
+    landed(wf.at[pl.ds(0, 15), 0], msem.at[0])
+    landed(wf.at[:, c], msem.at[2])
+    share_sums(net, sums, sums_all, tot, lsem.at[2], msem.at[4], msem.at[5])
+    net.finish()
+
+
+def run_qkv(x, cols, gain, cid, cut=96):
+    R, D = x.shape
+    N = cols.shape[2]
+    DMA = pltpu.SemaphoreType.DMA
+    S = jax.ShapeDtypeStruct
+    V = lambda *s: pltpu.VMEM(s, BF)
+    A = pl.BlockSpec(memory_space=pl.ANY)
+    M = pl.BlockSpec(memory_space=pltpu.VMEM)
+    return pl.pallas_call(
+        functools.partial(qkv_kernel, cut),
+        out_shape=(S((16, R, D), BF), S((16, R, N), F32), S((16, 2, R // 2, N), BF), S((32, 128), F32)),
+        in_specs=[A, A, M],
+        out_specs=(A, M, M, M),
+        scratch_shapes=[V(4, 4, R, D), V(2, R, D), pltpu.VMEM((32, 128), F32), pltpu.VMEM((16, 32, 128), F32),
+                        DMA((3,)), DMA((2,)), DMA((6,)), DMA((64,))] + ag_sems(),
+        compiler_params=pltpu.CompilerParams(collective_id=cid, has_side_effects=True, vmem_limit_bytes=40 * 2**20),
+        name="project",
+    )(x, cols, gain)
+
+
 def group_of(t):
     g = t // 2
     return jnp.where(g == 0, 3, jnp.where(g == 1, 0, jnp.where(g == 2, 2, 1)))
 
 
-def expert_kernel(cut, n2, cot, share, gate, up, down, d_n2, p_out, hid_o, dg_o, du_o, dp_o,
-                  P, G, U, W, hid, dg, du, xb, cb, pb, wsem, xsem, csem, psem, osem, ssem, *scr):
-    net = Net(ssem)
-    for i, (src, dst) in enumerate(((gate, G), (up, U), (down, W))):
-        pltpu.make_async_copy(src, dst, wsem.at[i]).start()
-
-    def load(t, slot, start):
-        zd, j = group_of(t), lax.rem(t, 2)
-        for src, dst, sem in ((n2, xb, xsem), (cot, cb, csem)):
-            copy = pltpu.make_async_copy(src.at[pl.ds(2 * j, 2), zd], dst.at[slot], sem.at[slot])
-            if start:
-                copy.start()
-            else:
-                copy.wait()
-
-    load(0, 0, True)
-    net.barrier()
-    sc = Scatter(net, cut, P, scr)
-    for i, (src, dst) in enumerate(((gate, G), (up, U), (down, W))):
-        pltpu.make_async_copy(src, dst, wsem.at[i]).wait()
-    rows, width = P.shape[2], P.shape[3]
-    ff = G.shape[1]
+def expert_kernel(cut, n2, cot, share, gate, up, down, d_n2, p_out, n2_o, other, dg_o, du_o, dd_o,
+                  X, C, GU, W, A, hid, pb, fs, lsem, wsem, wrs, psem, tsem, osem, ors, fsem, sa, sc_, sr, *scr):
+    ga_sems, gc_sems, rs_bufs = scr[:7], scr[7:14], scr[14:]
+    na, nc, nr = Net(sa), Net(sc_), Net(sr)
+    u, z, c = na.u, na.z, na.c
+    partner = (u, z, 1 - c)
+    rows, width = X.shape[2], X.shape[3]
+    ff = W.shape[0]
+    half, half_ff = gate.shape[0], down.shape[0]
+    tokens = 16 * rows
     tile = 256
-
-    def outs(t, slot):
+    first = [pltpu.make_async_copy(n2, X.at[u, z], lsem.at[0]), pltpu.make_async_copy(cot, C.at[u, z], lsem.at[1])]
+
+    def weights():
+        mine = pl.ds(pl.multiple_of(c * half, half), half)
+        mine_ff = pl.ds(pl.multiple_of(c * half_ff, half_ff), half_ff)
+        return ((gate, GU.at[mine, pl.ds(0, ff)]), (up, GU.at[mine, pl.ds(ff, ff)]), (down, W.at[mine_ff, :]))
+
+    own_w = [pltpu.make_async_copy(a, b, lsem.at[2 + i]) for i, (a, b) in enumerate(weights())]
+    for one in first + own_w:
+        one.start()
+    na.barrier((partner,))
+    first[0].wait()
+
+    def gather(net, buf, sems):
+        return Gather(net, rows, cut, lambda uu, zz, lo, n: buf.at[uu, zz, pl.ds(lo, n), :],
+                      lambda zz, lo, n: buf.at[:, zz, pl.ds(lo, n), :], sems)
+
+    ga, gc = gather(na, X, ga_sems), gather(nc, C, gc_sems)
+    ga.begin()
+    sent_w = [remote(a, b, wsem.at[i], wrs.at[i], partner) for i, (a, b) in enumerate(weights())]
+    for one in sent_w:
+        one.start()
+
+    def forward(zz):
+        pltpu.make_async_copy(X.at[:, zz], n2_o.at[:, zz], psem.at[1]).start()
+
+        def part(j, _):
+            quads = pl.ds(2 * j, 2)
+
+            def inner(n, _):
+                gcols = pl.ds(pl.multiple_of(n * tile, tile), tile)
+                ucols = pl.ds(pl.multiple_of(ff + n * tile, tile), tile)
+                xv = X[quads, zz].reshape(2 * rows, width)
+                g = dot(xv, GU[:, gcols], ((1,), (0,)))
+                uu = dot(xv, GU[:, ucols], ((1,), (0,)))
+                hid[quads, zz, :, gcols] = (g * jax.nn.sigmoid(g) * uu).astype(BF).reshape(2, rows, tile)
+                A[quads, zz, :, gcols] = g.astype(BF).reshape(2, rows, tile)
+                A[quads, zz, :, ucols] = uu.astype(BF).reshape(2, rows, tile)
+                return 0
+
+            lax.fori_loop(0, ff // tile, inner, 0)
+            weight = share[quads, zz]
+
+            def outer(n, _):
+                cols = pl.ds(pl.multiple_of(n * tile, tile), tile)
+                made = dot(hid[quads, zz].reshape(2 * rows, ff), W[:, cols], ((1,), (0,)))
+                made = made.astype(BF).astype(F32).reshape(2, rows, tile)
+                pb[:, :, cols] = (weight * made).astype(BF)
+                return 0
+
+            lax.fori_loop(0, width // tile, outer, 0)
+            out = pltpu.make_async_copy(pb, p_out.at[quads, zz], psem.at[0])
+            out.start()
+            out.wait()
+            return 0
+
+        lax.fori_loop(0, 2, part, 0)
+
+    def planes(s):
+        if s == 0:
+            forward(z)
+            return
+
+        def one(d, _):
+            zz = jnp.where(d == 0, z - s, z + s)
+            pl.when(jnp.logical_and(zz >= 0, zz < 4))(lambda: forward(zz))
+            return 0
+
+        lax.fori_loop(0, 2, one, 0)
+
+    ga.begin2()
+    ga.along(1)
+    ga.quads(0)
+    ga.cross(0)
+    ga.along(2)
+    ga.quads(1)
+    ga.cross(1)
+    first[1].wait()
+    gc.begin()
+    ga.settle(0)
+    for one in own_w:
+        one.wait()
+    for one in sent_w:
+        one.wait_recv()
+    planes(0)
+    gc.begin2()
+    ga.along(3)
+    ga.quads(2)
+    ga.cross(2)
+    ga.settle(1)
+    gc.along(1)
+    gc.quads(0)
+    gc.cross(0)
+    planes(1)
+    ga.quads(3)
+    ga.cross(3)
+    ga.settle(2)
+    gc.along(2)
+    gc.quads(1)
+    gc.cross(1)
+    planes(2)
+    ga.settle(3)
+    gc.along(3)
+    gc.quads(2)
+    gc.cross(2)
+    planes(3)
+    gc.quads(3)
+    gc.cross(3)
+    for s in range(4):
+        gc.settle(s)
+    na.finish()
+    nc.finish()
+    for one in sent_w:
+        one.wait_send()
+    landed(X, psem.at[1])
+    sc = Scatter(nr, cut, X, rs_bufs)
+
+    def backward(t):
         zd, j = group_of(t), lax.rem(t, 2)
         quads = pl.ds(2 * j, 2)
-        return (pltpu.make_async_copy(pb.at[slot], p_out.at[quads, zd], psem.at[slot]),
-                pltpu.make_async_copy(cb.at[slot], dp_o.at[quads, zd], osem.at[slot]))
-
-    def compute(t):
-        slot = lax.rem(t, 2)
-        zd, j = group_of(t), lax.rem(t, 2)
-        quads = pl.ds(2 * j, 2)
-
-        @pl.when(t >= 1)
-        def _():
-            for o in outs(t - 1, 1 - slot):
-                o.wait()
-
-        @pl.when(t < 7)
-        def _():
-            load(t + 1, 1 - slot, True)
-
-        load(t, slot, False)
-        weight = share[quads, zd]
 
         def scale(i, _):
             sl = pl.ds(pl.multiple_of(i * 16, 16), 16)
-            cb[slot, :, sl, :] = (share[quads, zd, sl, :] * cb[slot, :, sl, :].astype(F32)).astype(BF)
+            C[quads, zd, sl, :] = (share[quads, zd, sl, :] * C[quads, zd, sl, :].astype(F32)).astype(BF)
             return 0
 
         lax.fori_loop(0, rows // 16, scale, 0)
-        x = xb.at[slot]
-        d_prod = cb.at[slot]
 
         def inner(n, _):
-            cols = pl.ds(pl.multiple_of(n * tile, tile), tile)
-            xv = x[...].reshape(2 * rows, width)
-            g = dot(xv, G[:, cols], ((1,), (0,)))
-            uu = dot(xv, U[:, cols], ((1,), (0,)))
-            dh = dot(d_prod[...].reshape(2 * rows, width), W[cols, :], ((1,), (1,)))
+            gcols = pl.ds(pl.multiple_of(n * tile, tile), tile)
+            ucols = pl.ds(pl.multiple_of(ff + n * tile, tile), tile)
+            dh = dot(C[quads, zd].reshape(2 * rows, width), W[gcols, :], ((1,), (1,)))
+            g = wide(A[quads, zd, :, gcols]).reshape(2 * rows, tile)
+            uu = wide(A[quads, zd, :, ucols]).reshape(2 * rows, tile)
             s = jax.nn.sigmoid(g)
-            gs = g * s
-            hid[quads, zd, :, cols] = (gs * uu).astype(BF).reshape(2, rows, tile)
-            dg[quads, zd, :, cols] = (dh * uu * s * (1.0 + g * (1.0 - s))).astype(BF).reshape(2, rows, tile)
-            du[quads, zd, :, cols] = (dh * gs).astype(BF).reshape(2, rows, tile)
+            A[quads, zd, :, gcols] = (dh * uu * s * (1.0 + g * (1.0 - s))).astype(BF).reshape(2, rows, tile)
+            A[quads, zd, :, ucols] = (dh * g * s).astype(BF).reshape(2, rows, tile)
             return 0
 
         lax.fori_loop(0, ff // tile, inner, 0)
 
         def outer(n, _):
             cols = pl.ds(pl.multiple_of(n * tile, tile), tile)
-            dgv = dg[quads, zd].reshape(2 * rows, ff)
-            duv = du[quads, zd].reshape(2 * rows, ff)
-            back = dot(dgv, G[cols, :], ((1,), (1,))) + dot(duv, U[cols, :], ((1,), (1,)))
-            P[quads, zd, :, cols] = back.astype(BF).reshape(2, rows, tile)
-            made = dot(hid[quads, zd].reshape(2 * rows, ff), W[:, cols], ((1,), (0,)))
-            made = made.astype(BF).astype(F32).reshape(2, rows, tile)
-            pb[slot, :, :, cols] = (weight * made).astype(BF)
+            back = dot(A[quads, zd].reshape(2 * rows, 2 * ff), GU[cols, :], ((1,), (1,)))
+            X[quads, zd, :, cols] = back.astype(BF).reshape(2, rows, tile)
             return 0
 
         lax.fori_loop(0, width // tile, outer, 0)
-        for o in outs(t, slot):
-            o.start()
+
+    def acts(steps, t):
+        for at, todo in steps.items():
+            def act(todo=todo):
+                for one in todo:
+                    one()
+            pl.when(t == at)(act)
 
     steps = {
         1: [lambda: sc.first(3)],
@@ -995,39 +1323,147 @@
     }
 
     def turn(t, _):
-        compute(t)
-        for at, todo in steps.items():
-            def act(todo=todo):
-                for one in todo:
-                    one()
-            pl.when(t == at)(act)
+        backward(t)
+        acts(steps, t)
         return 0
 
     lax.fori_loop(0, 8, turn, 0)
-    for o in outs(7, 1):
-        o.wait()
-    keep = [pltpu.make_async_copy(a, b, wsem.at[i]) for i, (a, b) in enumerate(((hid, hid_o), (dg, dg_o), (du, du_o)))]
-    for k in keep:
-        k.start()
-    sc.mids(1)
-    sc.hop(2, 1); sc.bhop(1, 2)
-    sc.hop(1, 0); sc.hop(1, 3)
-    sc.bquad()
-    sc.hop(1, 2)
-    sc.bquad2()
-
-    def store(sl, v):
+
+    GU4 = GU.reshape(4, 4, rows, width)
+    left = W.at[pl.ds(0, tile), :]
+
+    def tile_load(k, which):
+        slot = lax.rem(k, 2)
+        cols = pl.ds(pl.multiple_of((which * 4 + k) * tile, tile), tile)
+        return pltpu.make_async_copy(
+            n2_o.at[:, :, :, cols], GU4.at[:, :, :, pl.ds(pl.multiple_of(slot * tile, tile), tile)], tsem.at[slot])
+
+    def left_tokens(k):
+        cols = pl.ds(pl.multiple_of(lax.rem(k, 2) * tile, tile), tile)
+
+        def one(b, _):
+            sl = pl.ds(pl.multiple_of(b * tile, tile), tile)
+            left[:, sl] = GU[sl, cols].T
+            return 0
+
+        lax.fori_loop(0, tokens // tile, one, 0)
+
+    def left_hidden(k, which):
+        cols = pl.ds(pl.multiple_of((which * 2 + k) * tile, tile), tile)
+        flat = hid.reshape(tokens, ff)
+
+        def one(b, _):
+            sl = pl.ds(pl.multiple_of(b * tile, tile), tile)
+            left[:, sl] = flat[sl, cols].T
+            return 0
+
+        lax.fori_loop(0, tokens // tile, one, 0)
+
+    def products(right, store):
+        flat = right.reshape(tokens, width)
+
+        def one(n, _):
+            cols = pl.ds(pl.multiple_of(n * 512, 512), 512)
+            store(cols, n, dot(left[...], flat[:, cols], ((1,), (0,))))
+            return 0
+
+        lax.fori_loop(0, width // 512, one, 0)
+
+    def sent(k):
+        slot = W.at[pl.ds(pl.multiple_of(tile + lax.rem(k, 2) * tile, tile), tile), :]
+        return slot, remote(slot, other.at[k], osem.at[k], ors.at[k], partner)
+
+    tile_load(0, 1 - c).start()
+
+    def other_tile(k, _):
+        slot, copy = sent(k)
+
+        @pl.when(k >= 2)
+        def _():
+            sent(k - 2)[1].wait_send()
+
+        def store(cols, n, v):
+            slot[:, cols] = v.astype(BF)
+
+        @pl.when(k < 4)
+        def _():
+            pl.when(k < 3)(lambda: tile_load(k + 1, 1 - c).start())
+            tile_load(k, 1 - c).wait()
+            left_tokens(k)
+            products(A, store)
+
+        @pl.when(k >= 4)
+        def _():
+            left_hidden(k - 4, 1 - c)
+            products(C, store)
+
+        copy.start()
+        acts({0: [lambda: sc.mids(1)],
+              1: [lambda: sc.hop(2, 1), lambda: sc.bhop(1, 2)],
+              2: [lambda: sc.hop(1, 0), lambda: sc.hop(1, 3)],
+              3: [sc.bquad],
+              4: [lambda: sc.hop(1, 2)],
+              5: [sc.bquad2]}, k)
+        return 0
+
+    lax.fori_loop(0, 6, other_tile, 0)
+
+    def store_out(sl, v):
         d_n2[sl, :] = v
 
-    sc.last(store)
-    for k in keep:
-        k.wait()
-    net.finish()
+    tile_load(0, c).start()
+    got = W.at[pl.ds(3 * tile, tile), :]
+
+    def flush(k, h):
+        i = pl.ds(pl.multiple_of(lax.rem(k, 4) * tile, tile), tile)
+
+        def go(dst):
+            pltpu.make_async_copy(fs.at[h], dst, fsem.at[h]).start()
+
+        pl.when(k < 4)(lambda: go((dg_o, du_o)[h].at[i, :]))
+        pl.when(k >= 4)(lambda: go(dd_o.at[i, pl.ds(h * 1024, 1024)]))
+
+    def own_tile(k, _):
+        fetch = pltpu.make_async_copy(other.at[k], got, lsem.at[0])
+        landed(other.at[k], ors.at[k])
+        fetch.start()
+
+        def finish(right):
+            flat = right.reshape(tokens, width)
+            fetch.wait()
+            for h in (0, 1):
+                pl.when(k > 0)(lambda: landed(fs.at[h], fsem.at[h]))
+                for n in (0, 1):
+                    cols = pl.ds(h * 1024 + n * 512, 512)
+                    fs[h, :, n * 512 : (n + 1) * 512] = dot(left[...], flat[:, cols], ((1,), (0,))) + wide(got[:, cols])
+                flush(k, h)
+
+        @pl.when(k < 4)
+        def _():
+            pl.when(k < 3)(lambda: tile_load(k + 1, c).start())
+            tile_load(k, c).wait()
+            left_tokens(k)
+            finish(A)
+
+        @pl.when(k >= 4)
+        def _():
+            left_hidden(k - 4, c)
+            finish(C)
+
+        acts({0: [lambda: sc.last(store_out)]}, k)
+        return 0
+
+    lax.fori_loop(0, 6, own_tile, 0)
+    for h in (0, 1):
+        landed(fs.at[h], fsem.at[h])
+    for k in (4, 5):
+        sent(k)[1].wait_send()
+    nr.finish()
 
 
 def run_expert(n2, cot, share, gate, up, down, cid, cut=96):
-    _, _, R, D = n2.shape
-    ff = gate.shape[1]
+    R, D = n2.shape
+    half, ff = gate.shape
     DMA = pltpu.SemaphoreType.DMA
     S = jax.ShapeDtypeStruct
     V = lambda *s: pltpu.VMEM(s, BF)
@@ -1035,15 +1471,273 @@
     M = pl.BlockSpec(memory_space=pltpu.VMEM)
     return pl.pallas_call(
         functools.partial(expert_kernel, cut),
-        out_shape=(S((R, D), F32), S((4, 4, R, D), BF), S((4, 4, R, ff), BF), S((4, 4, R, ff), BF), S((4, 4, R, ff), BF), S((4, 4, R, D), BF)),
+        out_shape=(S((R, D), F32), S((4, 4, R, D), BF), S((4, 4, R, D), BF), S((6, 256, D), BF),
+                   S((half, ff), F32), S((half, ff), F32), S(down.shape, F32)),
         in_specs=[A, A, M, A, A, A],
-        out_specs=(M, A, A, A, A, A),
-        scratch_shapes=[V(4, 4, R, D), V(D, ff), V(D, ff), V(ff, D), V(4, 4, R, ff), V(4, 4, R, ff), V(4, 4, R, ff),
-                        V(2, 2, R, D), V(2, 2, R, D), V(2, 2, R, D),
-                        DMA((3,)), DMA((2,)), DMA((2,)), DMA((2,)), DMA((2,)), DMA((96,))] + rs_scratch(cut, R, D),
-        compiler_params=pltpu.CompilerParams(collective_id=cid, has_side_effects=True, vmem_limit_bytes=62 * 2**20),
+        out_specs=(M,) + (A,) * 6,
+        scratch_shapes=[V(4, 4, R, D), V(4, 4, R, D), V(D, 2 * ff), V(ff, D), V(4, 4, R, 2 * ff), V(4, 4, R, ff),
+                        V(2, R, D), pltpu.VMEM((2, 256, 1024), F32),
+                        DMA((5,)), DMA((3,)), DMA((3,)), DMA((2,)), DMA((2,)), DMA((6,)), DMA((6,)), DMA((2,)),
+                        DMA((64,)), DMA((64,)), DMA((96,))] + ag_sems() + ag_sems() + rs_scratch(cut, R, D),
+        compiler_params=pltpu.CompilerParams(collective_id=cid, has_side_effects=True, vmem_limit_bytes=63 * 2**20),
         name="expert",
     )(n2, cot, share, gate, up, down)
+
+def band_scores(q, k, q_seg, k_seg, scale, reach):
+    scores = dot(q, k, ((1,), (1,))) * scale
+    q_at = lax.broadcasted_iota(jnp.int32, scores.shape, 0)
+    k_at = lax.broadcasted_iota(jnp.int32, scores.shape, 1)
+    return scores, (k_seg == q_seg) & (k_at <= q_at + reach)
+
+
+def turned(v, cosine, sine):
+    return v * cosine + pltpu.roll(v, 64, axis=1) * sine
+
+
+def turned_back(v, cosine, sine):
+    return v * cosine - pltpu.roll(v, 64, axis=1) * sine
+
+
+def attend_kernel(scale, pads, lin, tot, cosine, sine, gq, gk, q_seg, k_seg, w_own, x_in, gain, wo_o, q_rot, kv, o_ref, lse,
+                  att, residual, n2, wo, lsem, msem, ssem, *gs):
+    net = Net(ssem)
+    u, z, c = net.u, net.z, net.c
+    me = u * 4 + z
+    rows = x_in.shape[0]
+    width = x_in.shape[1]
+    reach = pads * 2 * rows
+    partner = (u, z, 1 - c)
+    own = pltpu.make_async_copy(w_own, wo.at[u, z, c], lsem.at[0])
+    own.start()
+    greet(net)
+    own.wait()
+    ga = Gather(net, rows // 2, rows // 2, lambda uu, zz, lo, n: wo.at[uu, zz, c, pl.ds(lo, n), :], None, gs)
+    ga.begin()
+    for i in range(pads):
+        kv[:, i] = jnp.zeros(kv.shape[:1] + kv.shape[2:], BF)
+
+    def ready(i, _):
+        both = lin[i]
+        rq = lax.rsqrt(column(tot[pl.ds(i, 1), :]) / width + EPS)
+        rk = lax.rsqrt(column(tot[pl.ds(16 + i, 1), :]) / width + EPS)
+        cs, sn = cosine[i], sine[i]
+        q_rot[i] = turned(both[:, :128] * rq * gq[...], cs, sn).astype(BF)
+        kv[0, pads + i, c] = turned(both[:, 128:256] * rk * gk[...], cs, sn).astype(BF)
+        kv[1, pads + i, c] = both[:, 256:].astype(BF)
+        return 0
+
+    lax.fori_loop(0, 16, ready, 0)
+    mine = kv.at[:, pl.ds(pads, 16), c]
+    to_partner = remote(mine, mine, msem.at[0], msem.at[1], partner)
+    to_partner.start()
+    ga.along(1)
+    ga.cross(0)
+    landed(kv.at[:, pl.ds(pads, 16), 1 - c], msem.at[1])
+
+    def block(j, _):
+        i = lax.rem(me + 1 + j, 16)
+        first = 2 * i + c
+        band = pl.ds(pl.multiple_of(first * rows, rows), rows + reach)
+        kf, vf = kv.at[0].reshape((pads + 16) * 2 * rows, 128), kv.at[1].reshape((pads + 16) * 2 * rows, 128)
+        scores, allowed = band_scores(q_rot[i], kf[band, :], q_seg[i], k_seg[:, band], scale, reach)
+        scores = jnp.where(allowed, scores, NEG)
+        top = jnp.max(scores, axis=1, keepdims=True)
+        weights = jnp.where(allowed, jnp.exp(scores - top), 0.0)
+        total = jnp.sum(weights, axis=1, keepdims=True)
+        probs = (weights / total).astype(BF)
+        o_ref[i] = dot(probs, vf[band, :], ((1,), (0,))).astype(BF)
+        lse[i] = top + jnp.log(total)
+
+        @pl.when(j < 15)
+        def _():
+            remote(o_ref.at[i], att.at[me], msem.at[2], msem.at[3], (i // 4, lax.rem(i, 4), c)).start()
+
+        return 0
+
+    lax.fori_loop(0, 5, block, 0)
+    ga.along(2)
+    ga.cross(1)
+    lax.fori_loop(5, 10, block, 0)
+    ga.along(3)
+    ga.cross(2)
+    lax.fori_loop(10, 16, block, 0)
+    ga.cross(3)
+    for s in range(4):
+        ga.settle(s)
+    rest = remote(wo.at[:, :, c], wo.at[:, :, c], msem.at[4], msem.at[5], partner)
+    rest.start()
+    att[me] = o_ref[me]
+    part = att.at[pl.ds(0, 15)]
+    landed(part, msem.at[3])
+    landed(wo.at[:, :, 1 - c], msem.at[5])
+    keep = pltpu.make_async_copy(wo, wo_o, lsem.at[1])
+    keep.start()
+    tile = 256
+
+    def out(n, _):
+        cols = pl.ds(pl.multiple_of(n * tile, tile), tile)
+        acc = x_in[:, cols].astype(F32)
+        for e in range(0, 16, 2):
+            pair = jnp.concatenate([att[e], att[e + 1]], axis=1)
+            acc = acc + dot(pair, wo[e // 4, pl.ds(e % 4, 2), :, :, cols].reshape(256, tile), ((1,), (0,)))
+        residual[:, cols] = acc
+        return 0
+
+    lax.fori_loop(0, width // tile, out, 0)
+
+    def norm(i, _):
+        sl = pl.ds(pl.multiple_of(i * 16, 16), 16)
+        v = residual[sl, :]
+        r = lax.rsqrt(jnp.mean(v * v, axis=1, keepdims=True) + EPS)
+        n2[sl, :] = (v * r * gain[...]).astype(BF)
+        return 0
+
+    lax.fori_loop(0, rows // 16, norm, 0)
+    landed(mine, msem.at[0])
+    landed(part, msem.at[2])
+    landed(wo.at[:, :, c], msem.at[4])
+    keep.wait()
+    net.finish()
+
+
+def run_attend(scale, pads, lin, tot, cosine, sine, gq, gk, q_seg, k_seg, w_own, x_in, gain, cid):
+    R, D = x_in.shape
+    DMA = pltpu.SemaphoreType.DMA
+    S = jax.ShapeDtypeStruct
+    A = pl.BlockSpec(memory_space=pl.ANY)
+    M = pl.BlockSpec(memory_space=pltpu.VMEM)
+    wo = (4, 4, 2, R // 2, D)
+    return pl.pallas_call(
+        functools.partial(attend_kernel, scale, pads),
+        out_shape=(S(wo, BF), S((16, R, 128), BF), S((2, pads + 16, 2, R, 128), BF), S((16, R, 128), BF),
+                   S((16, R, 1), F32), S((16, R, 128), BF), S((R, D), F32), S((R, D), BF)),
+        in_specs=[M] * 8 + [A, M, M],
+        out_specs=(A,) + (M,) * 7,
+        scratch_shapes=[pltpu.VMEM(wo, BF), DMA((2,)), DMA((6,)), DMA((64,))] + ag_sems(),
+        compiler_params=pltpu.CompilerParams(collective_id=cid, has_side_effects=True, vmem_limit_bytes=48 * 2**20),
+        name="attend",
+    )(lin, tot, cosine, sine, gq, gk, q_seg, k_seg, w_own, x_in, gain)
+
+
+def attend_back_kernel(scale, pads, d_res, wo_h, q_rot, kv, q_seg, k_seg, lse, o_ref, lin, tot, cosine, sine, gq, gk,
+                       d_lin, d_gains, wo, d_mine, d_out, d_q, d_k, d_v, other, got, d_un, sums, sums_all, inner,
+                       lsem, msem, ssem):
+    net = Net(ssem)
+    u, z, c = net.u, net.z, net.c
+    me = u * 4 + z
+    rows, width = d_res.shape
+    reach = pads * 2 * rows
+    partner = (u, z, 1 - c)
+    load = pltpu.make_async_copy(wo_h, wo, lsem.at[0])
+    load.start()
+    greet(net)
+    load.wait()
+
+    def send(j, _):
+        e = lax.rem(me + 1 + j, 16)
+        piece = dot(d_res[...], wo[e // 4, lax.rem(e, 4)].reshape(128, width), ((1,), (1,))).astype(BF)
+
+        @pl.when(j < 15)
+        def _():
+            d_mine[e] = piece
+            remote(d_mine.at[e], d_out.at[me], msem.at[0], msem.at[1], (e // 4, lax.rem(e, 4), c)).start()
+
+        @pl.when(j == 15)
+        def _():
+            d_out[me] = piece
+
+        return 0
+
+    lax.fori_loop(0, 16, send, 0)
+    d_k[...] = jnp.zeros_like(d_k)
+    d_v[...] = jnp.zeros_like(d_v)
+    landed(d_out.at[pl.ds(0, 15)], msem.at[1])
+    count = (pads + 16) * 2 * rows
+
+    def block(i, _):
+        band = pl.ds(pl.multiple_of((2 * i + c) * rows, rows), rows + reach)
+        kf, vf = kv.at[0].reshape(count, 128), kv.at[1].reshape(count, 128)
+        q, k, dd = q_rot[i], kf[band, :], d_out[i]
+        scores, allowed = band_scores(q, k, q_seg[i], k_seg[:, band], scale, reach)
+        probs = jnp.where(allowed, jnp.exp(scores - lse[i]), 0.0)
+        d_probs = dot(dd, vf[band, :], ((1,), (1,)))
+        delta = jnp.sum(dd.astype(F32) * o_ref[i].astype(F32), axis=1, keepdims=True)
+        d_scores = (probs * (d_probs - delta)).astype(BF)
+        d_q[i] = (dot(d_scores, k, ((1,), (0,))) * scale).astype(BF)
+        d_k[band, :] += dot(d_scores, q, ((0,), (0,))) * scale
+        d_v[band, :] += dot(probs.astype(BF), dd, ((0,), (0,)))
+        return 0
+
+    lax.fori_loop(0, 16, block, 0)
+
+    def pack(i, _):
+        at = pl.ds(pl.multiple_of(((pads + i) * 2 + 1 - c) * rows, rows), rows)
+        other[0, i] = d_k[at, :].astype(BF)
+        other[1, i] = d_v[at, :].astype(BF)
+        return 0
+
+    lax.fori_loop(0, 16, pack, 0)
+    remote(other, got, msem.at[2], msem.at[3], partner).start()
+    landed(got, msem.at[3])
+    d_gains[...] = jnp.zeros_like(d_gains)
+
+    def undo(i, _):
+        at = pl.ds(pl.multiple_of(((pads + i) * 2 + c) * rows, rows), rows)
+        cs, sn = cosine[i], sine[i]
+        both = lin[i]
+        rq = lax.rsqrt(column(tot[pl.ds(i, 1), :]) / width + EPS)
+        rk = lax.rsqrt(column(tot[pl.ds(16 + i, 1), :]) / width + EPS)
+        dk = (d_k[at, :] + wide(got[0, i])).astype(BF).astype(F32)
+        d_lin[i, :, 256:] = (d_v[at, :] + wide(got[1, i])).astype(BF)
+        uq = turned_back(wide(d_q[i]), cs, sn)
+        uk = turned_back(dk, cs, sn)
+        q, k = both[:, :128], both[:, 128:256]
+        d_gains[0:1, :] += jnp.sum(uq * q * rq, axis=0, keepdims=True)
+        d_gains[1:2, :] += jnp.sum(uk * k * rk, axis=0, keepdims=True)
+        uq, uk = uq * gq[...], uk * gk[...]
+        d_un[0, i] = uq
+        d_un[1, i] = uk
+        sums[pl.ds(i, 1), :] = row_sums(uq * q)
+        sums[pl.ds(16 + i, 1), :] = row_sums(uk * k)
+        return 0
+
+    lax.fori_loop(0, 16, undo, 0)
+    share_sums(net, sums, sums_all, inner, lsem.at[1], msem.at[4], msem.at[5])
+
+    def finish(i, _):
+        both = lin[i]
+        for s in (0, 1):
+            r = lax.rsqrt(column(tot[pl.ds(16 * s + i, 1), :]) / width + EPS)
+            mean = column(inner[pl.ds(16 * s + i, 1), :]) / width
+            own = both[:, 128 * s : 128 * (s + 1)]
+            d_lin[i, :, 128 * s : 128 * (s + 1)] = (r * d_un[s, i] - own * (r * r * r * mean)).astype(BF)
+        return 0
+
+    lax.fori_loop(0, 16, finish, 0)
+    landed(d_out.at[pl.ds(0, 15)], msem.at[0])
+    landed(other, msem.at[2])
+
+
+def run_attend_back(scale, pads, d_res, wo, q_rot, kv, q_seg, k_seg, lse, o, lin, tot, cosine, sine, gq, gk, cid):
+    R, D = d_res.shape
+    DMA = pltpu.SemaphoreType.DMA
+    S = jax.ShapeDtypeStruct
+    A = pl.BlockSpec(memory_space=pl.ANY)
+    M = pl.BlockSpec(memory_space=pltpu.VMEM)
+    V = pltpu.VMEM
+    span = (pads + 16) * 2 * R
+    return pl.pallas_call(
+        functools.partial(attend_back_kernel, scale, pads),
+        out_shape=(S((16, R, 384), BF), S((8, 128), F32)),
+        in_specs=[M, A] + [M] * 12,
+        out_specs=(M, M),
+        scratch_shapes=[V(wo.shape, BF), V((16, R, 128), BF), V((16, R, 128), BF), V((16, R, 128), BF),
+                        V((span, 128), F32), V((span, 128), F32), V((2, 16, R, 128), BF), V((2, 16, R, 128), BF),
+                        V((2, 16, R, 128), F32), V((32, 128), F32), V((16, 32, 128), F32), V((32, 128), F32),
+                        DMA((2,)), DMA((6,)), DMA((4,))],
+        compiler_params=pltpu.CompilerParams(collective_id=cid, has_side_effects=True, vmem_limit_bytes=48 * 2**20),
+        name="attend_back",
+    )(d_res, wo, q_rot, kv, q_seg, k_seg, lse, o, lin, tot, cosine, sine, gq, gk)
 def swap_kernel(src, out, lsem, ssem, rsem):
     u, z, c = place()
     me = u * 8 + z * 2 + c
@@ -1139,48 +1833,6 @@
         compiler_params=pltpu.CompilerParams(collective_id=cid, has_side_effects=True),
         name="spread_rows",
     )(block)
-
-
-def band_scores(q, k, q_seg, k_seg, scale, reach):
-    scores = dot(q, k, ((1,), (1,))) * scale
-    q_at = lax.broadcasted_iota(jnp.int32, scores.shape, 0)
-    k_at = lax.broadcasted_iota(jnp.int32, scores.shape, 1)
-    return scores, (k_seg == q_seg) & (k_at <= q_at + reach)
-
-
-def attend_kernel(scale, reach, q_ref, k_ref, v_ref, qs_ref, ks_ref, o_ref, l_ref):
-    rows = q_ref.shape[0]
-    first = pl.multiple_of((pl.program_id(0) * 2 + lax.axis_index("core")) * rows, rows)
-    band = pl.ds(first, rows + reach)
-    scores, allowed = band_scores(q_ref[...], k_ref[band, :], qs_ref[...], ks_ref[:, band], scale, reach)
-    scores = jnp.where(allowed, scores, NEG)
-    top = jnp.max(scores, axis=1, keepdims=True)
-    weights = jnp.where(allowed, jnp.exp(scores - top), 0.0)
-    total = jnp.sum(weights, axis=1, keepdims=True)
-    probs = (weights / total).astype(BF)
-    o_ref[...] = dot(probs, v_ref[band, :], ((1,), (0,))).astype(BF)
-    l_ref[...] = top + jnp.log(total)
-
-
-def attend_back_kernel(scale, reach, q_ref, k_ref, v_ref, qs_ref, ks_ref, l_ref, o_ref, do_ref, dq_ref, dk_ref, dv_ref):
-    rows = q_ref.shape[0]
-
-    @pl.when(pl.program_id(0) == 0)
-    def _():
-        dk_ref[...] = jnp.zeros_like(dk_ref)
-        dv_ref[...] = jnp.zeros_like(dv_ref)
-
-    first = pl.multiple_of((pl.program_id(0) * 2 + lax.axis_index("core")) * rows, rows)
-    band = pl.ds(first, rows + reach)
-    q, k, d_out = q_ref[...], k_ref[band, :], do_ref[...]
-    scores, allowed = band_scores(q, k, qs_ref[...], ks_ref[:, band], scale, reach)
-    probs = jnp.where(allowed, jnp.exp(scores - l_ref[...]), 0.0)
-    d_probs = dot(d_out, v_ref[band, :], ((1,), (1,)))
-    delta = jnp.sum(d_out.astype(F32) * o_ref[...].astype(F32), axis=1, keepdims=True)
-    d_scores = (probs * (d_probs - delta)).astype(BF)
-    dq_ref[...] = (dot(d_scores, k, ((1,), (0,))) * scale).astype(BF)
-    dk_ref[band, :] += dot(d_scores, q, ((0,), (0,))) * scale
-    dv_ref[band, :] += dot(probs.astype(BF), d_out, ((0,), (0,)))
 
 
 def core_pair(value):
@@ -1232,106 +1884,36 @@
     def in_order(own, other):
         return jnp.where(core == 0, own, other), jnp.where(core == 0, other, own)
 
-    cols = jnp.stack([w_query, w_key, w_value]).reshape(3, 64, chips, HEAD_DIM).transpose(2, 0, 1, 3)
-    cols = lax.all_to_all(cols, mine, split_axis=0, concat_axis=0, tiled=True)
-    cols = jnp.stack(in_order(cols, core_pair(cols)), axis=1)
-    w_qkv = cols.transpose(0, 1, 3, 2, 4).reshape(width, 3 * HEAD_DIM)
-    w_o = jnp.concatenate(in_order(w_output, core_pair(w_output)), axis=0)
-
+    cols = jnp.stack([w_query, w_key, w_value]).reshape(3, 64, chips, HEAD_DIM)
+    cols = cols.transpose(2, 1, 0, 3).reshape(chips, 64, 3 * HEAD_DIM)
     def my_head(gain):
         return lax.dynamic_slice_in_dim(gain, chip * HEAD_DIM, HEAD_DIM, 0)
 
-    x_rows = ag16(inputs, 2).reshape(chips * rows, width)
-    cotangent_later, x_rows = lax.optimization_barrier((cotangent, x_rows))
-    cot_rows = lax.all_gather(cotangent_later, mine, axis=0, tiled=True)
-    x_rows = x_rows.astype(F32)
-    n1_rows = norm_rows(x_rows, gain_one).astype(BF)
-    lin = dot(n1_rows, w_qkv, ((1,), (0,)))
-    q_lin, k_lin, v_lin = lin[:, :HEAD_DIM], lin[:, HEAD_DIM : 2 * HEAD_DIM], lin[:, 2 * HEAD_DIM :]
-
-    def over_chips(a, b, cid):
-        both = jnp.stack([a, b]).reshape(2 * chips, rows)
-        both = jnp.sum(spread(both, cid), axis=0).reshape(2, chips * rows, 1)
-        return both[0], both[1]
-
-    square_q, square_k = over_chips(jnp.sum(q_lin * q_lin, axis=1), jnp.sum(k_lin * k_lin, axis=1), 3)
-    rq = lax.rsqrt(square_q / width + EPS)
-    rk = lax.rsqrt(square_k / width + EPS)
+    n1_rows, lin, w_qkv, squares = run_qkv(inputs, cols, gain_one.reshape(1, width), 2)
+    n1_rows, w_qkv = n1_rows.reshape(chips * rows, width), w_qkv.reshape(width, 3 * HEAD_DIM)
     positions = (jnp.arange(chips, dtype=jnp.int32)[:, None] * 2 + core) * rows + jnp.arange(rows, dtype=jnp.int32)
     half_dim = HEAD_DIM // 2
     inv_freq = jnp.exp(jnp.arange(half_dim, dtype=F32) * (-2.0 * math.log(ROPE_BASE) / HEAD_DIM))
     angles = positions.reshape(-1).astype(F32)[:, None] * inv_freq[None, :]
     cosine, sine = jnp.cos(angles), jnp.sin(angles)
-    cosine = jnp.concatenate([cosine, cosine], axis=1)
-    sine = jnp.concatenate([-sine, sine], axis=1)
-
-    def halves_swapped(v):
-        return jnp.concatenate([v[:, half_dim:], v[:, :half_dim]], axis=1)
-
-    def turn(v):
-        return v * cosine + halves_swapped(v) * sine
-
-    def turn_back(v):
-        return v * cosine - halves_swapped(v) * sine
-
-    gq, gk = my_head(gain_q), my_head(gain_k)
-    q_rot = turn(q_lin * rq * gq).astype(BF)
-    k_rot = turn(k_lin * rk * gk).astype(BF)
-    kv = jnp.stack([k_rot, v_lin.astype(BF)]).reshape(2, chips, 1, rows, HEAD_DIM)
-    kv = jnp.concatenate(in_order(kv, core_pair(kv)), axis=2).reshape(2, devices * rows, HEAD_DIM)
-    reach = devices * rows // 4
-    kv = jnp.concatenate([jnp.zeros((2, reach, HEAD_DIM), BF), kv], axis=1)
-    k_seg = jnp.concatenate([jnp.full((reach,), -1, jnp.int32), segments]).reshape(1, -1)
-    q_seg = lax.dynamic_index_in_dim(segments.reshape(chips, 2, rows), core, 1, keepdims=False).reshape(-1, 1)
+    cosine = jnp.concatenate([cosine, cosine], axis=1).reshape(chips, rows, HEAD_DIM)
+    sine = jnp.concatenate([-sine, sine], axis=1).reshape(chips, rows, HEAD_DIM)
+    gq, gk = my_head(gain_q).reshape(1, HEAD_DIM), my_head(gain_k).reshape(1, HEAD_DIM)
+    pads = chips // 4
+    k_seg = jnp.concatenate([jnp.full((pads * 2 * rows,), -1, jnp.int32), segments]).reshape(1, -1)
+    q_seg = lax.dynamic_index_in_dim(segments.reshape(chips, 2, rows, 1), core, 1, keepdims=False)
     scale = 1.0 / math.sqrt(HEAD_DIM)
-    row_block = pl.BlockSpec((rows, HEAD_DIM), lambda i: (i, 0))
-    one_block = pl.BlockSpec((rows, 1), lambda i: (i, 0))
-
-    def whole_block(value):
-        return pl.BlockSpec(value.shape, lambda i: (0,) * value.ndim)
-
     tokens = chips * rows
-    attended, log_total = pl.pallas_call(
-        functools.partial(attend_kernel, scale, reach),
-        grid=(chips,),
-        out_shape=(jax.ShapeDtypeStruct((tokens, HEAD_DIM), BF), jax.ShapeDtypeStruct((tokens, 1), F32)),
-        in_specs=[row_block, whole_block(kv[0]), whole_block(kv[1]), one_block, whole_block(k_seg)],
-        out_specs=(row_block, one_block),
-        compiler_params=pltpu.CompilerParams(vmem_limit_bytes=32 * 2**20),
-        name="attend",
-    )(q_rot, kv[0], kv[1], q_seg, k_seg)
+    w_o, q_rot, kv, head_out, log_total, attended, residual, normed_two = run_attend(
+        scale, pads, lin, squares, cosine, sine, gq, gk, q_seg, k_seg, w_output, inputs, gain_two.reshape(1, width), 4)
+    r2 = lax.rsqrt(jnp.mean(residual * residual, axis=1, keepdims=True) + EPS)
 
     def to_blocks(part):
-        return part.astype(BF).reshape(4, 4, rows, width)
-
-    residual = layer_in + rs16(to_blocks(dot(attended, w_o, ((1,), (0,)))), 4)
-    r2 = lax.rsqrt(jnp.mean(residual * residual, axis=1, keepdims=True) + EPS)
-    normed_two = (residual * r2 * gain_two).astype(BF)
-    n2_rows = ag16(normed_two, 5).reshape(tokens, width)
-
-    joined = [
-        jnp.concatenate(in_order(part, core_pair(part)), axis=0)
-        for part in (expert_gate, expert_up, expert_down)
-    ]
-    gate_full, up_full, down_full = joined
-    blocks = (4, 4, rows, width)
-    d_normed_two, mixed, hidden, d_gate_pre, d_up_pre, d_produced = run_expert(
-        n2_rows.reshape(blocks), cot_rows.reshape(blocks), share.reshape(4, 4, rows, 1),
-        gate_full, up_full, down_full, 6)
-    mixed = lax.psum_scatter(mixed.reshape(tokens, width), mine, scatter_dimension=0, tiled=True)
-    output = residual + mixed.astype(F32)
-    hidden, d_gate_pre, d_up_pre, d_produced = (
-        v.reshape(tokens, v.shape[-1]) for v in (hidden, d_gate_pre, d_up_pre, d_produced))
-
-    def shared_grad(full):
-        size = full.shape[0] // 2
-        own = lax.dynamic_slice_in_dim(full, core * size, size, 0)
-        other = lax.dynamic_slice_in_dim(full, (1 - core) * size, size, 0)
-        return own + core_pair(other.astype(BF)).astype(F32)
-
-    d_expert_gate = shared_grad(dot(n2_rows, d_gate_pre, ((0,), (0,))))
-    d_expert_up = shared_grad(dot(n2_rows, d_up_pre, ((0,), (0,))))
-    d_expert_down = shared_grad(dot(hidden, d_produced, ((0,), (0,))))
+        return part.astype(BF).reshape(4, 4, rows, part.shape[-1])
+
+    d_normed_two, mixed, _n2, _other, d_expert_gate, d_expert_up, d_expert_down = run_expert(
+        normed_two, cotangent, share.reshape(4, 4, rows, 1), expert_gate, expert_up, expert_down, 6)
+    output = residual + rs16(mixed, 5)
 
     def norm_back(d_out, values, r, gain):
         d_scaled = d_out * gain
@@ -1341,32 +1923,20 @@
 
     d_resid_norm, d_gain_two = norm_back(d_normed_two, residual, r2, gain_two)
     d_residual = cotangent.astype(F32) + d_resid_norm
-    d_res_rows = ag16(d_residual.astype(BF), 7).reshape(tokens, width)
-    d_attended = dot(d_res_rows, w_o, ((1,), (1,))).astype(BF)
-    d_w_output = shared_grad(dot(attended, d_res_rows, ((0,), (0,))))
-    padded = jax.ShapeDtypeStruct((reach + devices * rows, HEAD_DIM), F32)
-    d_q, d_k, d_v = pl.pallas_call(
-        functools.partial(attend_back_kernel, scale, reach),
-        grid=(chips,),
-        out_shape=(jax.ShapeDtypeStruct((tokens, HEAD_DIM), BF), padded, padded),
-        in_specs=[row_block, whole_block(kv[0]), whole_block(kv[1]), one_block, whole_block(k_seg), one_block, row_block, row_block],
-        out_specs=(row_block, whole_block(padded), whole_block(padded)),
-        compiler_params=pltpu.CompilerParams(vmem_limit_bytes=48 * 2**20),
-        name="attend_back",
-    )(q_rot, kv[0], kv[1], q_seg, k_seg, log_total, attended, d_attended)
-    d_kv = jnp.stack([d_k[reach:], d_v[reach:]]).reshape(2, chips, 2, rows, HEAD_DIM)
-    d_kv_own = lax.dynamic_index_in_dim(d_kv, core, 2, keepdims=False)
-    d_kv_other = lax.dynamic_index_in_dim(d_kv, 1 - core, 2, keepdims=False)
-    d_kv = (d_kv_own + core_pair(d_kv_other.astype(BF)).astype(F32)).astype(BF).reshape(2, tokens, HEAD_DIM)
-    d_q_un = turn_back(d_q.astype(F32))
-    d_k_un = turn_back(d_kv[0].astype(F32))
-    inner_q, inner_k = over_chips(
-        jnp.sum(d_q_un * gq * q_lin, axis=1), jnp.sum(d_k_un * gk * k_lin, axis=1), 8)
-    d_q_lin = rq * (d_q_un * gq) - q_lin * (rq * rq * rq * (inner_q / width))
-    d_k_lin = rk * (d_k_un * gk) - k_lin * (rk * rk * rk * (inner_k / width))
-    d_gain_q = jnp.sum(d_q_un * q_lin * rq, axis=0)
-    d_gain_k = jnp.sum(d_k_un * k_lin * rk, axis=0)
-    d_lin = jnp.concatenate([d_q_lin.astype(BF), d_k_lin.astype(BF), d_kv[1]], axis=1)
+    d_res_low = d_residual.astype(BF)
+    d_lin, d_qk_gains = run_attend_back(
+        scale, pads, d_res_low, w_o, q_rot, kv, q_seg, k_seg, log_total, head_out, lin, squares, cosine, sine, gq, gk, 7)
+    d_lin = d_lin.reshape(tokens, 3 * HEAD_DIM)
+    d_qk_gains = d_qk_gains[:2] + core_pair(d_qk_gains[:2])
+    d_wo = dot(attended.transpose(0, 2, 1).reshape(width, rows), d_res_low, ((1,), (0,)))
+    d_wo = d_wo.reshape(4, 4, HEAD_DIM, 2, width // 2)
+    d_wo_own = lax.dynamic_index_in_dim(d_wo, core, 3, keepdims=False)
+    d_wo_other = lax.dynamic_index_in_dim(d_wo, 1 - core, 3, keepdims=False)
+    d_wo = rs16((d_wo_own + core_pair(d_wo_other.astype(BF)).astype(F32)).astype(BF), 8, dtype=BF)
+    d_wo = d_wo.reshape(2, 64, width // 2)
+    d_wo_mine = lax.dynamic_index_in_dim(d_wo, core, 0, keepdims=False)
+    d_wo_other = core_pair(lax.dynamic_index_in_dim(d_wo, 1 - core, 0, keepdims=False))
+    d_w_output = jnp.concatenate(in_order(d_wo_mine, d_wo_other), axis=1).astype(F32)
     d_normed_one = rs16(to_blocks(dot(d_lin, w_qkv, ((1,), (1,)))), 9)
     d_cols = dot(n1_rows, d_lin, ((0,), (0,))).reshape(chips, 2, 64, 3 * HEAD_DIM)
     d_cols_own = lax.dynamic_index_in_dim(d_cols, core, 1, keepdims=False)
@@ -1384,8 +1954,6 @@
     def my_half(row):
         return lax.dynamic_slice_in_dim(row, core * 64, 64, 0)
 
-    d_qk_gains = jnp.stack([d_gain_q, d_gain_k])
-    d_qk_gains = d_qk_gains + core_pair(d_qk_gains)
     return (
         output,
         d_inputs,

time: 910 us -> 838 us (0.921)
  matrix products: 70.6 us -> 19 us
  other arithmetic: 79.3 us -> 34.3 us
  Pallas kernels: 663 us -> 707 us
  between operations: 15.5 us -> 1.41 us
  local copies, waits for them, and re-layouts: 55.9 us -> 65.2 us
    pallas_call x1, Pallas kernels: 119 us -> 249 us  [run_expert(): pl.pallas_call(functools.partial(expert_kernel, cut), out_shape=(S((R, D)...]
    dot_general x10 -> x4, matrix products: 70.6 us -> 19 us  [dot(): lax.dot_general(a, b, (dims, ((), ())), preferred_element_type=jnp.float32)]
    pallas_call x7 -> x3, Pallas kernels: 273 us -> 223 us  [the longest x1 107 us: run_qkv(): pl.pallas_call(functools.partial(qkv_kernel, cut), out_shape=(S((16, R, D...]
    pallas_call x2, Pallas kernels: 41.7 us -> 22.6 us  [swap(): pl.pallas_call(swap_kernel, out_shape=jax.ShapeDtypeStruct((2 * chips, r,...]
    add x5 -> x1, other arithmetic: 17.2 us -> 0.01 us  [local_chip(): d_qk_gains = d_qk_gains[:2] + core_pair(d_qk_gains[:2])]
    pallas_call x2 -> x3, Pallas kernels: 230 us -> 213 us  [rs16(): pl.pallas_call(functools.partial(rs_kernel, cut), out_shape=jax.ShapeDtyp...]
    dot_general x0 -> x2, local copies, waits for them, and re-layouts: none -> 12.6 us  [dot(): lax.dot_general(a, b, (dims, ((), ())), preferred_element_type=jnp.float32)]
    reduce_sum x6 -> x1, other arithmetic: 10.8 us -> 0.19 us  [local_chip(): r1 = lax.rsqrt(jnp.mean(layer_in * layer_in, axis=1, keepdims=True) + EPS)]
  transfers between devices with their start and end apart: 17 -> 5, of which waited for: 3 -> 0; matrix products, arithmetic and copies ran while one was open for 19% -> 6% of each run, Pallas kernels for 42% -> 21%
where the time goes in v3:
time: 838 us; the launch traced here: 833 us
  Pallas kernels  707 us (84%)
  local copies, waits for them, and re-layouts  65.2 us (8%)
  other arithmetic  34.3 us (4%)
  matrix products  19 us (2%)
    pallas_call x1, Pallas kernels, run_expert(): pl.pallas_call(functools.partial(expert_kernel, cut), out_shape=(S((R, D)...  249 us
    pallas_call x3, Pallas kernels, rs16(): pl.pallas_call(functools.partial(rs_kernel, cut), out_shape=jax.ShapeDtyp...  213 us
    pallas_call x1, Pallas kernels, run_qkv(): pl.pallas_call(functools.partial(qkv_kernel, cut), out_shape=(S((16, R, D...  107 us
    pallas_call x1, Pallas kernels, run_attend_back(): pl.pallas_call(functools.partial(attend_back_kernel, scale, pads), out_sh...  59.3 us
    pallas_call x1, Pallas kernels, run_attend(): pl.pallas_call(functools.partial(attend_kernel, scale, pads), out_shape=(...  56.6 us
    unnamed x69, local copies, waits for them, and re-layouts  33.2 us
    pallas_call x2, Pallas kernels, swap(): pl.pallas_call(swap_kernel, out_shape=jax.ShapeDtypeStruct((2 * chips, r,...  22.6 us
    dot_general x4, matrix products, dot(): lax.dot_general(a, b, (dims, ((), ())), preferred_element_type=jnp.float32)  19 us
  transfers between devices with their start and end apart: 5, of which 0 were waited for; matrix products, arithmetic and copies ran while one was open for 6% of the time, Pallas kernels for 21%

profile of v3, /device:TPU:0, one launch (start us, length us, event | category | flops | bytes accessed | tf_op | source)
XLA Modules:
  0.0 833.3 jit_solution(9451388565468185838)
XLA Ops:
  4.6 12.7 %swap_rows.2 = f32[32,8,128]{2,1,0:T(8,128)} custom-call(f32[16,8,128]{2,1,0:T(8,128)} %maximum_maximum_fusion.src), custom_call_target="tpu_custom_call" | custom-call | tf_op jit(solution)/shard_map/swap_rows/pallas_call | solution.py:1782
  32.0 3.7 fusion.10
  37.4 106.9 %project.1 = (bf16[16,128,2048]{2,1,0:T(8,128)(2,1)S(1)}, f32[16,128,384]{2,1,0:T(8,128)S(1)}, bf16[16,2,64,384]{3,2,1,0:T(8,128)(2,1)S(1)}, f32[32,128]{1,0:T(8,128)S(1)}) custom-call(bf16[128,2048]{1,0:T(8,128)(2,1)S(1)} %copy-done.2, bf16[16,64,384]{2,1,0:T(8,128)(2,1)S(1)} %reshape.252.cols, f32[1,2048]{1,0:T(1,128)S(1)} %slice.62.gain), custom_call_target="tpu_custom_call" | custom-call | tf_op jit(solution)/shard_map/project/pallas_call | solution.py:1131
  145.9 3.2 copy-done.8
  150.3 56.6 %attend.1 = (bf16[4,4,2,64,2048]{4,3,2,1,0:T(8,128)(2,1)}, bf16[16,128,128]{2,1,0:T(8,128)(2,1)S(1)}, bf16[2,20,2,128,128]{4,3,2,1,0:T(8,128)(2,1)}, bf16[16,128...) custom-call(f32[16,128,384]{2,1,0:T(8,128)} %copy-done.3, ...), custom_call_target="tpu_custom_call" | custom-call | tf_op jit(solution)/shard_map/attend/pallas_call | solution.py:1610
  211.5 248.6 %expert.1 = (f32[128,2048]{1,0:T(8,128)}, bf16[4,4,128,2048]{3,2,1,0:T(8,128)(2,1)}, bf16[4,4,128,2048]{3,2,1,0:T(8,128)(2,1)}, bf16[6,256,2048]{2,1,0:T(8,128)(...) custom-call(bf16[128,2048]{1,0:T(8,128)(2,1)} %copy-done.17, bf16[128,2048]{1,0:T(8,128)(2,1)} %cot.1, ...), custom_call_target="tpu_custom_call" | custom-call | tf_op jit(solution)/shard_map/expert/pallas_call | solution.py:1472
  464.4 59.3 %attend_back.1 = (bf16[16,128,384]{2,1,0:T(8,128)(2,1)}, f32[8,128]{1,0:T(8,128)S(1)}) custom-call(bf16[128,2048]{1,0:T(8,128)(2,1)S(1)} %fusion.24.d_res, bf16[4,4,2,64,2048]{4,3,2,1,0:T(8,128)(2,1)} %get-tuple-element.38.wo_h, bf16[16,128,128]{2,1,0:T(8,128)(2,1)S(1)} %copy-done.14, bf16[2,20,2,128,128]{4,3,2,1,0:T(8,128)(2,1)} %get-tuple-element.40.kv, ...), custom_call_target="tpu_custom_call" | custom-call | tf_op jit(solution)/shard_map/attend_back/pallas_call | solution.py:1729
  524.1 2.4 fusion.30
  526.5 5.7 copy-done.21
  532.2 2.7 fusion.1
  535.4 12.4 %copy.99 = bf16[2048,2048]{1,0:T(8,128)(2,1)} copy(bf16[2048,2048]{0,1:T(8,128)(2,1)} %bitcast.115) | data formatting | bytes 16777216 | tf_op jit(solution)/shard_map/dot_general | solution.py:1843
  547.8 7.5 fusion.29
  557.3 8.2 convolution_convert_fusion
  565.5 81.8 %scatter_rows.4 = f32[128,2048]{1,0:T(8,128)} custom-call(bf16[4,4,128,2048]{3,2,1,0:T(8,128)(2,1)} %bitcast.121), custom_call_target="tpu_custom_call" | custom-call | tf_op jit(solution)/shard_map/scatter_rows/pallas_call | solution.py:886
  649.7 9.9 %swap_rows.3 = f32[32,8,128]{2,1,0:T(8,128)} custom-call(f32[16,8,128]{2,1,0:T(8,128)} %maximum_maximum_fusion.1.src), custom_call_target="tpu_custom_call" | custom-call | tf_op jit(solution)/shard_map/swap_rows/pallas_call | solution.py:1782
  660.6 2.7 fusion.2
  663.4 5.4 all-to-all-start
  669.4 85.3 %scatter_rows.3 = f32[128,2048]{1,0:T(8,128)} custom-call(bf16[4,4,128,2048]{3,2,1,0:T(8,128)(2,1)} %get-tuple-element.36.P), custom_call_target="tpu_custom_call" | custom-call | tf_op jit(solution)/shard_map/scatter_rows/pallas_call | solution.py:886
  754.8 3.1 fusion.6
  759.6 2.4 reshape.268
  762.0 8.4 %fusion.P = bf16[4,4,128,1024]{3,2,1,0:T(8,128)(2,1)} fusion(bf16[4,4,128,1024]{3,2,1,0:T(8,128)(2,1)} %collective-permute-done.1, f32[4,4,128,2,1024]{4,2,3,1,0:T(8,128)} %copy-done.21, s32[]{:T(128)S(6)} %select_n.56), kind=kLoop, calls=%fused_computation.2 | loop fusion | flops 6291456 | bytes 16777220 | tf_op jit(solution)/shard_map/convert_element_type | solution.py:1935
  770.4 46.1 %scatter_rows.5 = bf16[128,1024]{1,0:T(8,128)(2,1)} custom-call(bf16[4,4,128,1024]{3,2,1,0:T(8,128)(2,1)} %fusion.P), custom_call_target="tpu_custom_call" | custom-call | tf_op jit(solution)/shard_map/scatter_rows/pallas_call | solution.py:886
  823.7 2.1 copy.134
  827.4 2.1 copy.135
  (147 shorter events, 52.7 us)
Async XLA Ops:
  32.0 5.4 copy-start.2
  32.0 118.3 %copy-start.18 = (bf16[64,2048]{1,0:T(8,128)(2,1)S(1)}, bf16[64,2048]{1,0:T(8,128)(2,1)}, u32[]{:S(2)}) copy-start(bf16[64,2048]{1,0:T(8,128)(2,1)} %w_own.1) | copy-start | bytes 786436
  37.4 169.6 %copy-start.4 = (f32[16,128,128]{2,1,0:T(8,128)}, f32[16,128,128]{2,1,0:T(8,128)S(1)}, u32[]{:S(2)}) copy-start(f32[16,128,128]{2,1,0:T(8,128)S(1)} %get-tuple-element.76.cosine) | copy-start | bytes 3145732
  460.1 4.2 copy-start.5
  460.1 4.2 copy-start.6
  460.1 4.2 copy-start.7
  460.2 4.2 copy-start.10
  460.2 4.2 copy-start.14
  460.2 4.2 copy-start.16
  464.4 59.7 %copy-start.12 = (bf16[16,128,128]{2,1,0:T(8,128)(2,1)S(1)}, bf16[16,128,128]{2,1,0:T(8,128)(2,1)}, u32[]{:S(2)}) copy-start(bf16[16,128,128]{2,1,0:T(8,128)(2,1)} %copy-done.11) | copy-start | bytes 1572868
  523.7 234.7 %collective-permute-start.3 = (f32[2,128]{1,0:T(2,128)S(1)}, f32[2,128]{1,0:T(2,128)S(1)}, u32[]{:S(2)}, u32[]{:S(2)}) collective-permute-start(f32[2,128]{1,0:T(2,128)S(1)} %slice.74), channel_id=1, source_target_pairs={{0,1},{1,0},{2,3},{3,2},{4,5},{5,4},{6,7},{7,6},{8,9},{9,8},{10,11... | collective-permute-start | bytes 3080 | tf_op jit(solution)/shard_map/ppermute | solution.py:1839
  526.5 5.8 copy-start.21
  534.9 227.1 %collective-permute-start.1 = (bf16[4,4,128,1024]{3,2,1,0:T(8,128)(2,1)}, bf16[4,4,128,1024]{3,2,1,0:T(8,128)(2,1)}, u32[]{:S(2)}, u32[]{:S(2)}) collective-permute-start(bf16[4,4,128,1024]{3,2,1,0:T(8,128)(2,1)} %fusion.1), channel_id=1, source_target_pairs={{0,1},{1,0},{2,3},{3,2},{4,5},{5,4},{6,7},{7,6},{8,9},{9,8},{10,11... | collective-permute-start | bytes 12582920 | tf_op jit(solution)/shard_map/ppermute | solution.py:1839
  547.8 9.5 %copy-start.20 = (bf16[16,2,64,384]{3,2,1,0:T(8,128)(2,1)S(1)}, bf16[16,2,64,384]{3,2,1,0:T(8,128)(2,1)}, u32[]{:S(2)}) copy-start(bf16[16,2,64,384]{3,2,1,0:T(8,128)(2,1)} %copy-done.19) | copy-start | bytes 4718596
  557.0 103.6 %collective-permute-start = (bf16[16,64,384]{2,1,0:T(8,128)(2,1)S(1)}, bf16[16,64,384]{2,1,0:T(8,128)(2,1)}, u32[]{:S(2)}, u32[]{:S(2)}) collective-permute-start(bf16[16,64,384]{2,1,0:T(8,128)(2,1)S(1)} %fusion.9), channel_id=1, source_target_pairs={{0,1},{1,0},{2,3},{3,2},{4,5},{5,4},{6,7},{7,6},{8,9},{9,8},{10,11... | collective-permute-start | bytes 2359304 | tf_op jit(solution)/shard_map/ppermute | solution.py:1839
  663.4 96.3 %all-to-all-start = ((bf16[16,64,384]{2,1,0:T(8,128)(2,1)}), bf16[16,64,384]{2,1,0:T(8,128)(2,1)}, u32[]{:S(2)}, u32[]{:S(2)}) async-start(bf16[16,64,384]{2,1,0:T(8,128)(2,1)} %fusion.2), calls=%async_computation | async-start | bytes 1572864 | tf_op jit(solution)/shard_map/all_to_all | solution.py:1945
  669.4 85.4 %copy-start.1 = (f32[128,2048]{1,0:T(8,128)S(1)}, f32[128,2048]{1,0:T(8,128)}, u32[]{:S(2)}) copy-start(f32[128,2048]{1,0:T(8,128)} %copy-done) | copy-start | bytes 3145732
  669.4 85.4 %copy-start.22 = (f32[128,2048]{1,0:T(8,128)S(1)}, f32[128,2048]{1,0:T(8,128)}, u32[]{:S(2)}) copy-start(f32[128,2048]{1,0:T(8,128)} %scatter_rows.4) | copy-start | bytes 3145732
  669.4 85.4 %copy-start.23 = (f32[128,2048]{1,0:T(8,128)S(1)}, f32[128,2048]{1,0:T(8,128)}, u32[]{:S(2)}) copy-start(f32[128,2048]{1,0:T(8,128)} %get-tuple-element.37) | copy-start | bytes 3145732
  669.4 85.4 %copy-start.24 = (bf16[128,2048]{1,0:T(8,128)(2,1)S(1)}, bf16[128,2048]{1,0:T(8,128)(2,1)}, u32[]{:S(2)}) copy-start(bf16[128,2048]{1,0:T(8,128)(2,1)} %cot.1) | copy-start | bytes 1572868
  817.4 5.5 collective-permute-start.2
  817.5 5.4 copy-start.29
  819.1 4.7 copy-start.27
  823.7 3.7 copy-start.26
  (11 other events, 17.0 us)

commit v4 on v3

--- a/solution.py
+++ b/solution.py
@@ -1483,6 +1483,208 @@
         name="expert",
     )(n2, cot, share, gate, up, down)
 
+
+def stages(sc, store):
+    def each(f, *pairs):
+        return [functools.partial(f, *p) for p in pairs]
+
+    return [
+        each(sc.first, (3,), (0,), (2,), (1,)),
+        each(sc.mids, (3,), (0,), (2,), (1,)),
+        each(sc.hop, (3, 0), (0, 3)) + each(sc.bhop, (3, 1), (0, 2)),
+        each(sc.hop, (2, 0), (1, 3)) + each(sc.bhop, (2, 1), (1, 2)),
+        each(sc.hop, (3, 1), (0, 2)) + each(sc.bhop, (3, 2), (0, 1)),
+        each(sc.hop, (1, 0), (2, 3)) + [sc.bquad],
+        each(sc.hop, (2, 1), (1, 2)),
+        each(sc.hop, (3, 2), (0, 1)) + [sc.bquad2],
+        [functools.partial(sc.last, store)],
+    ]
+
+
+def run_steps(steps):
+    for one in steps:
+        one()
+
+
+def greet_all(net, count=32):
+    bar = pltpu.get_barrier_semaphore()
+    me = net.u * 8 + net.z * 2 + net.c
+
+    def hello(j, _):
+        t = lax.rem(me + j, count)
+        pl.semaphore_signal(bar, inc=1, device_id=(t // 8, lax.rem(t, 8) // 2, lax.rem(t, 2)), device_id_type=MESH)
+        return 0
+
+    lax.fori_loop(1, count, hello, 0)
+    pl.semaphore_wait(bar, count - 1)
+
+
+def finish_kernel(cut, d_lin, wf, n1, p_out, x_in, residual, d_res, gain, d_gain_two,
+                  output, d_inputs, d_wq, d_wk, d_wv, gains_o,
+                  P, PO, nt, left, keep, give, got, send, recv, d_n1, d_gain, gb, gr,
+                  lsem, tsem, msem, s1, s2, *bufs):
+    net, net2 = Net(s1), Net(s2)
+    u, z, c = net.u, net.z, net.c
+    me = u * 4 + z
+    rows, width = P.shape[2], P.shape[3]
+    lanes = d_lin.shape[2]
+    tokens = 16 * rows
+    tile = 256
+    partner = (u, z, 1 - c)
+    half = len(bufs) // 2
+    sc1, sc2 = Scatter(net, cut, P, bufs[:half]), Scatter(net2, cut, PO, bufs[half:])
+    load = pltpu.make_async_copy(p_out, PO, lsem.at[0])
+    load.start()
+
+    def tile_load(k):
+        slot = lax.rem(k, 2)
+        return pltpu.make_async_copy(n1.at[:, :, pl.ds(pl.multiple_of(k * tile, tile), tile)], nt.at[slot], tsem.at[slot])
+
+    tile_load(0).start()
+    greet_all(net)
+
+    def group(zd):
+        def one(n, _):
+            cols = pl.ds(pl.multiple_of(n * 512, 512), 512)
+            w = wf.reshape(width, lanes)
+            for q in range(4):
+                P[q, zd, :, cols] = dot(d_lin[q * 4 + zd], w[cols, :], ((1,), (1,))).astype(BF)
+            return 0
+
+        lax.fori_loop(0, width // 512, one, 0)
+
+    for zd in (3, 0, 2, 1):
+        group(zd)
+        sc1.first(zd)
+    load.wait()
+
+    def store1(sl, v):
+        d_n1[sl, :] = v
+
+    def store2(sl, v):
+        output[sl, :] = residual[sl, :] + v
+
+    one, two = stages(sc1, store1), stages(sc2, store2)
+
+    def grads(k):
+        if k < 7:
+            tile_load(k + 1).start()
+        tile_load(k).wait()
+        slot = k % 2
+        flat = nt.at[slot].reshape(tokens, tile)
+
+        def turn(b, _):
+            sl = pl.ds(pl.multiple_of(b * tile, tile), tile)
+            left[:, sl] = flat[sl, :].T
+            return 0
+
+        lax.fori_loop(0, tokens // tile, turn, 0)
+        made = dot(left[...], d_lin[...].reshape(tokens, lanes), ((1,), (0,)))
+        for i in range(2):
+            first, second = made[i * 128 : i * 128 + 64], made[i * 128 + 64 : (i + 1) * 128]
+            keep[2 * k + i] = jnp.where(c == 0, first, second)
+            give[2 * k + i] = jnp.where(c == 0, second, first).astype(BF)
+
+    run_steps(two[0])
+    grads(0)
+    run_steps(one[1])
+    grads(1)
+    run_steps(one[2])
+    grads(2)
+    run_steps(two[1])
+    run_steps(one[3])
+    grads(3)
+    run_steps(two[2])
+    run_steps(one[4])
+    grads(4)
+    run_steps(two[3])
+    run_steps(one[5])
+    grads(5)
+    run_steps(one[6])
+    grads(6)
+    run_steps(two[4])
+    run_steps(one[7])
+    grads(7)
+    across = remote(give, got, msem.at[0], msem.at[1], partner)
+    across.start()
+    run_steps(two[5])
+    landed(got, msem.at[1])
+
+    def total(e, _):
+        send[e] = (keep[e] + wide(got[e])).astype(BF)
+        return 0
+
+    lax.fori_loop(0, 16, total, 0)
+    each_chip(net, lambda t, dev: remote(send.at[t], recv.at[me], msem.at[2], msem.at[3], dev).start())
+    recv[me] = send[me]
+    run_steps(one[8])
+    d_gain[...] = jnp.zeros_like(d_gain)
+
+    def norm_back(i, _):
+        sl = pl.ds(pl.multiple_of(i * 16, 16), 16)
+        v, d = wide(x_in[sl, :]), d_n1[sl, :]
+        r = lax.rsqrt(jnp.mean(v * v, axis=1, keepdims=True) + EPS)
+        scaled = d * gain[...]
+        inner = jnp.mean(scaled * v, axis=1, keepdims=True)
+        d_inputs[sl, :] = d_res[sl, :] + r * scaled - v * (r * r * r * inner)
+        d_gain[...] += jnp.sum(d * v * r, axis=0, keepdims=True)
+        return 0
+
+    lax.fori_loop(0, rows // 16, norm_back, 0)
+    for e in range(16):
+        gb[e, 0:1, :] = d_gain[:, e * 128 : (e + 1) * 128]
+        gb[e, 1:2, :] = d_gain_two[:, e * 128 : (e + 1) * 128]
+    dev_me = me * 2 + c
+
+    def tell(j, _):
+        t = lax.rem(dev_me + j, 32)
+        remote(gb.at[t // 2], gr.at[dev_me], msem.at[4], msem.at[5], (t // 8, lax.rem(t, 8) // 2, lax.rem(t, 2))).start()
+        return 0
+
+    lax.fori_loop(1, 32, tell, 0)
+    gr[dev_me] = gb[me]
+    run_steps(two[6])
+    run_steps(two[7])
+    landed(recv.at[pl.ds(0, 15)], msem.at[3])
+    for e in range(16):
+        piece = wide(recv[e])
+        for i, out in enumerate((d_wq, d_wk, d_wv)):
+            out[:, e * 128 : (e + 1) * 128] = piece[:, i * 128 : (i + 1) * 128]
+    landed(gr.at[pl.ds(0, 31)], msem.at[5])
+    sums = gr[0]
+    for i in range(1, 32):
+        sums = sums + gr[i]
+    gains_o[...] = sums
+    run_steps(two[8])
+    landed(give, msem.at[0])
+    landed(recv.at[pl.ds(0, 15)], msem.at[2])
+    landed(gr.at[pl.ds(0, 31)], msem.at[4])
+    net.finish()
+    net2.finish()
+
+
+def run_finish(d_lin, wf, n1, p_out, x_in, residual, d_res, gain, d_gain_two, cid, cut=96):
+    R, D = x_in.shape
+    N = d_lin.shape[2]
+    DMA = pltpu.SemaphoreType.DMA
+    S = jax.ShapeDtypeStruct
+    V = lambda *s: pltpu.VMEM(s, BF)
+    VF = lambda *s: pltpu.VMEM(s, F32)
+    A = pl.BlockSpec(memory_space=pl.ANY)
+    M = pl.BlockSpec(memory_space=pltpu.VMEM)
+    own = S((R // 2, D), F32)
+    return pl.pallas_call(
+        functools.partial(finish_kernel, cut),
+        out_shape=(S((R, D), F32), S((R, D), F32), own, own, own, S((8, 128), F32)),
+        in_specs=[M, M, A, A] + [M] * 5,
+        out_specs=(M,) * 6,
+        scratch_shapes=[V(4, 4, R, D), V(4, 4, R, D), V(2, 16, R, 256), V(256, 16 * R), VF(16, 64, N), V(16, 64, N),
+                        V(16, 64, N), V(16, 64, N), V(16, 64, N), VF(R, D), VF(1, D), VF(16, 8, 128), VF(32, 8, 128),
+                        DMA((1,)), DMA((2,)), DMA((6,)), DMA((64,)), DMA((64,))] + rs_scratch(cut, R, D) + rs_scratch(cut, R, D),
+        compiler_params=pltpu.CompilerParams(collective_id=cid, has_side_effects=True, vmem_limit_bytes=63 * 2**20),
+        name="finish",
+    )(d_lin, wf, n1, p_out, x_in, residual, d_res, gain, d_gain_two)
+
 def band_scores(q, k, q_seg, k_seg, scale, reach):
     scores = dot(q, k, ((1,), (1,))) * scale
     q_at = lax.broadcasted_iota(jnp.int32, scores.shape, 0)
@@ -1619,10 +1821,11 @@
     )(lin, tot, cosine, sine, gq, gk, q_seg, k_seg, w_own, x_in, gain)
 
 
-def attend_back_kernel(scale, pads, d_res, wo_h, q_rot, kv, q_seg, k_seg, lse, o_ref, lin, tot, cosine, sine, gq, gk,
-                       d_lin, d_gains, wo, d_mine, d_out, d_q, d_k, d_v, other, got, d_un, sums, sums_all, inner,
-                       lsem, msem, ssem):
+def attend_back_kernel(scale, pads, cut, d_res, wo_h, att, q_rot, kv, q_seg, k_seg, lse, o_ref, lin, tot, cosine, sine, gq, gk,
+                       d_lin, d_gains, d_wo, P, PG, PT, wsum, wo, d_mine, d_out, d_q, d_k, d_v, other, got, d_un, sums, sums_all, inner,
+                       lsem, msem, ssem, *bufs):
     net = Net(ssem)
+    sc = Scatter(net, cut, P, bufs)
     u, z, c = net.u, net.z, net.c
     me = u * 4 + z
     rows, width = d_res.shape
@@ -1649,6 +1852,19 @@
         return 0
 
     lax.fori_loop(0, 16, send, 0)
+    side = width // 2
+    own_cols = pl.ds(pl.multiple_of(c * side, side), side)
+    give_cols = pl.ds(pl.multiple_of((1 - c) * side, side), side)
+
+    def outer(e, _):
+        left = att[e].T
+        P[e // 4, lax.rem(e, 4)] = dot(left, d_res[:, own_cols], ((1,), (0,))).astype(BF)
+        PG[e // 4, lax.rem(e, 4)] = dot(left, d_res[:, give_cols], ((1,), (0,))).astype(BF)
+        return 0
+
+    lax.fori_loop(0, 16, outer, 0)
+    across = remote(PG, PT, msem.at[6], msem.at[7], partner)
+    across.start()
     d_k[...] = jnp.zeros_like(d_k)
     d_v[...] = jnp.zeros_like(d_v)
     landed(d_out.at[pl.ds(0, 15)], msem.at[1])
@@ -1668,7 +1884,32 @@
         d_v[band, :] += dot(probs.astype(BF), dd, ((0,), (0,)))
         return 0
 
-    lax.fori_loop(0, 16, block, 0)
+    def store(sl, v):
+        wsum[sl, :] = v
+
+    steps = stages(sc, store)
+    lax.fori_loop(0, 3, block, 0)
+    landed(PT, msem.at[7])
+
+    def join(e, _):
+        def strip(sl):
+            at = (e // 4, lax.rem(e, 4), sl, slice(None))
+            P[at] = (wide(P[at]) + wide(PT[at])).astype(BF)
+
+        strips(rows, strip)
+        return 0
+
+    lax.fori_loop(0, 16, join, 0)
+    run_steps(steps[0])
+    lax.fori_loop(3, 6, block, 0)
+    run_steps(steps[1])
+    lax.fori_loop(6, 8, block, 0)
+    run_steps(steps[2])
+    lax.fori_loop(8, 10, block, 0)
+    run_steps(steps[3])
+    lax.fori_loop(10, 13, block, 0)
+    run_steps(steps[4])
+    lax.fori_loop(13, 16, block, 0)
 
     def pack(i, _):
         at = pl.ds(pl.multiple_of(((pads + i) * 2 + 1 - c) * rows, rows), rows)
@@ -1678,6 +1919,7 @@
 
     lax.fori_loop(0, 16, pack, 0)
     remote(other, got, msem.at[2], msem.at[3], partner).start()
+    run_steps(steps[5])
     landed(got, msem.at[3])
     d_gains[...] = jnp.zeros_like(d_gains)
 
@@ -1702,6 +1944,7 @@
         return 0
 
     lax.fori_loop(0, 16, undo, 0)
+    run_steps(steps[6])
     share_sums(net, sums, sums_all, inner, lsem.at[1], msem.at[4], msem.at[5])
 
     def finish(i, _):
@@ -1714,11 +1957,20 @@
         return 0
 
     lax.fori_loop(0, 16, finish, 0)
+    run_steps(steps[7])
+    run_steps(steps[8])
+    d_wo[:, own_cols] = wsum[pl.ds(pl.multiple_of(c * 64, 64), 64), :]
+    theirs = remote(wsum.at[pl.ds(pl.multiple_of((1 - c) * 64, 64), 64), :], d_wo.at[:, own_cols], msem.at[8], msem.at[9], partner)
+    theirs.start()
     landed(d_out.at[pl.ds(0, 15)], msem.at[0])
     landed(other, msem.at[2])
-
-
-def run_attend_back(scale, pads, d_res, wo, q_rot, kv, q_seg, k_seg, lse, o, lin, tot, cosine, sine, gq, gk, cid):
+    landed(PG, msem.at[6])
+    theirs.wait_send()
+    landed(d_wo.at[:, give_cols], msem.at[9])
+    net.finish()
+
+
+def run_attend_back(scale, pads, d_res, wo, att, q_rot, kv, q_seg, k_seg, lse, o, lin, tot, cosine, sine, gq, gk, cid, cut=96):
     R, D = d_res.shape
     DMA = pltpu.SemaphoreType.DMA
     S = jax.ShapeDtypeStruct
@@ -1727,17 +1979,17 @@
     V = pltpu.VMEM
     span = (pads + 16) * 2 * R
     return pl.pallas_call(
-        functools.partial(attend_back_kernel, scale, pads),
-        out_shape=(S((16, R, 384), BF), S((8, 128), F32)),
-        in_specs=[M, A] + [M] * 12,
-        out_specs=(M, M),
-        scratch_shapes=[V(wo.shape, BF), V((16, R, 128), BF), V((16, R, 128), BF), V((16, R, 128), BF),
+        functools.partial(attend_back_kernel, scale, pads, cut),
+        out_shape=(S((16, R, 384), BF), S((8, 128), F32), S((R // 2, D), F32)),
+        in_specs=[M, A] + [M] * 13,
+        out_specs=(M, M, M),
+        scratch_shapes=[V((4, 4, R, D // 2), BF), V((4, 4, R, D // 2), BF), V((4, 4, R, D // 2), BF), V((R, D // 2), F32), V(wo.shape, BF), V((16, R, 128), BF), V((16, R, 128), BF), V((16, R, 128), BF),
                         V((span, 128), F32), V((span, 128), F32), V((2, 16, R, 128), BF), V((2, 16, R, 128), BF),
                         V((2, 16, R, 128), F32), V((32, 128), F32), V((16, 32, 128), F32), V((32, 128), F32),
-                        DMA((2,)), DMA((6,)), DMA((4,))],
-        compiler_params=pltpu.CompilerParams(collective_id=cid, has_side_effects=True, vmem_limit_bytes=48 * 2**20),
+                        DMA((2,)), DMA((10,)), DMA((64,))] + rs_scratch(cut, R, D // 2),
+        compiler_params=pltpu.CompilerParams(collective_id=cid, has_side_effects=True, vmem_limit_bytes=62 * 2**20),
         name="attend_back",
-    )(d_res, wo, q_rot, kv, q_seg, k_seg, lse, o, lin, tot, cosine, sine, gq, gk)
+    )(d_res, wo, att, q_rot, kv, q_seg, k_seg, lse, o, lin, tot, cosine, sine, gq, gk)
 def swap_kernel(src, out, lsem, ssem, rsem):
     u, z, c = place()
     me = u * 8 + z * 2 + c
@@ -1890,7 +2142,6 @@
         return lax.dynamic_slice_in_dim(gain, chip * HEAD_DIM, HEAD_DIM, 0)
 
     n1_rows, lin, w_qkv, squares = run_qkv(inputs, cols, gain_one.reshape(1, width), 2)
-    n1_rows, w_qkv = n1_rows.reshape(chips * rows, width), w_qkv.reshape(width, 3 * HEAD_DIM)
     positions = (jnp.arange(chips, dtype=jnp.int32)[:, None] * 2 + core) * rows + jnp.arange(rows, dtype=jnp.int32)
     half_dim = HEAD_DIM // 2
     inv_freq = jnp.exp(jnp.arange(half_dim, dtype=F32) * (-2.0 * math.log(ROPE_BASE) / HEAD_DIM))
@@ -1913,8 +2164,6 @@
 
     d_normed_two, mixed, _n2, _other, d_expert_gate, d_expert_up, d_expert_down = run_expert(
         normed_two, cotangent, share.reshape(4, 4, rows, 1), expert_gate, expert_up, expert_down, 6)
-    output = residual + rs16(mixed, 5)
-
     def norm_back(d_out, values, r, gain):
         d_scaled = d_out * gain
         inner = jnp.mean(d_scaled * values, axis=1, keepdims=True)
@@ -1924,32 +2173,11 @@
     d_resid_norm, d_gain_two = norm_back(d_normed_two, residual, r2, gain_two)
     d_residual = cotangent.astype(F32) + d_resid_norm
     d_res_low = d_residual.astype(BF)
-    d_lin, d_qk_gains = run_attend_back(
-        scale, pads, d_res_low, w_o, q_rot, kv, q_seg, k_seg, log_total, head_out, lin, squares, cosine, sine, gq, gk, 7)
-    d_lin = d_lin.reshape(tokens, 3 * HEAD_DIM)
+    d_lin, d_qk_gains, d_w_output = run_attend_back(
+        scale, pads, d_res_low, w_o, attended, q_rot, kv, q_seg, k_seg, log_total, head_out, lin, squares, cosine, sine, gq, gk, 7)
     d_qk_gains = d_qk_gains[:2] + core_pair(d_qk_gains[:2])
-    d_wo = dot(attended.transpose(0, 2, 1).reshape(width, rows), d_res_low, ((1,), (0,)))
-    d_wo = d_wo.reshape(4, 4, HEAD_DIM, 2, width // 2)
-    d_wo_own = lax.dynamic_index_in_dim(d_wo, core, 3, keepdims=False)
-    d_wo_other = lax.dynamic_index_in_dim(d_wo, 1 - core, 3, keepdims=False)
-    d_wo = rs16((d_wo_own + core_pair(d_wo_other.astype(BF)).astype(F32)).astype(BF), 8, dtype=BF)
-    d_wo = d_wo.reshape(2, 64, width // 2)
-    d_wo_mine = lax.dynamic_index_in_dim(d_wo, core, 0, keepdims=False)
-    d_wo_other = core_pair(lax.dynamic_index_in_dim(d_wo, 1 - core, 0, keepdims=False))
-    d_w_output = jnp.concatenate(in_order(d_wo_mine, d_wo_other), axis=1).astype(F32)
-    d_normed_one = rs16(to_blocks(dot(d_lin, w_qkv, ((1,), (1,)))), 9)
-    d_cols = dot(n1_rows, d_lin, ((0,), (0,))).reshape(chips, 2, 64, 3 * HEAD_DIM)
-    d_cols_own = lax.dynamic_index_in_dim(d_cols, core, 1, keepdims=False)
-    d_cols_other = lax.dynamic_index_in_dim(d_cols, 1 - core, 1, keepdims=False)
-    d_cols = (d_cols_own + core_pair(d_cols_other.astype(BF)).astype(F32)).astype(BF)
-    d_cols = lax.all_to_all(d_cols, mine, split_axis=0, concat_axis=0, tiled=True)
-    d_cols = d_cols.reshape(chips, 64, 3, HEAD_DIM).transpose(2, 1, 0, 3).reshape(3, 64, width).astype(F32)
-    r1 = lax.rsqrt(jnp.mean(layer_in * layer_in, axis=1, keepdims=True) + EPS)
-    d_layer_in, d_gain_one = norm_back(d_normed_one, layer_in, r1, gain_one)
-    d_inputs = d_residual + d_layer_in
-    block = jnp.concatenate(
-        [d_gain_one.reshape(chips, 1, 128), d_gain_two.reshape(chips, 1, 128), jnp.zeros((chips, 6, 128), F32)], axis=1)
-    d_gains = jnp.sum(swap(block, 10)[:, :2, :], axis=0)
+    output, d_inputs, d_w_query, d_w_key, d_w_value, d_gains = run_finish(
+        d_lin, w_qkv, n1_rows, mixed, inputs, residual, d_residual, gain_one.reshape(1, width), d_gain_two.reshape(1, width), 8)
 
     def my_half(row):
         return lax.dynamic_slice_in_dim(row, core * 64, 64, 0)
@@ -1958,9 +2186,9 @@
         output,
         d_inputs,
         my_half(d_gains[0]),
-        d_cols[0],
-        d_cols[1],
-        d_cols[2],
+        d_w_query,
+        d_w_key,
+        d_w_value,
         d_w_output,
         my_half(d_qk_gains[0]),
         my_half(d_qk_gains[1]),

time: 838 us -> 749 us (0.89)
  Pallas kernels: 707 us -> 675 us
  local copies, waits for them, and re-layouts: 65.2 us -> 40.8 us
  matrix products: 19 us -> 0.93 us
  other arithmetic: 34.3 us -> 18 us
    dot_general x4 -> x1, matrix products: 19 us -> 0.93 us  [dot(): lax.dot_general(a, b, (dims, ((), ())), preferred_element_type=jnp.float32)]
    dot_general x2 -> x0, local copies, waits for them, and re-layouts: 12.6 us -> none  [dot(): lax.dot_general(a, b, (dims, ((), ())), preferred_element_type=jnp.float32)]
    pallas_call x4 -> x2, Pallas kernels: 273 us -> 260 us  [the longest x1 160 us: run_finish(): pl.pallas_call(functools.partial(finish_kernel, cut), out_shape=(S((R, D)...]
    convert_element_type x3 -> x0, other arithmetic: 11.9 us -> none  [the longest x1 8.36 us: local_chip(): (d_wo_own + core_pair(d_wo_other.astype(BF)).astype(F32)).astype(BF)]
    pallas_call x1, Pallas kernels: 107 us -> 96.2 us  [run_qkv(): pl.pallas_call(functools.partial(qkv_kernel, cut), out_shape=(S((16, R, D...]
    pallas_call x2 -> x1, Pallas kernels: 22.6 us -> 12.7 us  [swap(): pl.pallas_call(swap_kernel, out_shape=jax.ShapeDtypeStruct((2 * chips, r,...]
    unnamed x69 -> x64, local copies, waits for them, and re-layouts: 33.2 us -> 28.7 us
  transfers between devices with their start and end apart: 5 -> 1, of which waited for: 0 -> 0; matrix products, arithmetic and copies ran while one was open for 6% -> 0% of each run, Pallas kernels for 21% -> 22%
where the time goes in v4:
time: 749 us; the launch traced here: 737 us
  Pallas kernels  675 us (90%)
  local copies, waits for them, and re-layouts  40.8 us (5%)
  other arithmetic  18 us (2%)
    pallas_call x1, Pallas kernels, run_expert(): pl.pallas_call(functools.partial(expert_kernel, cut), out_shape=(S((R, D)...  249 us
    pallas_call x1, Pallas kernels, run_finish(): pl.pallas_call(functools.partial(finish_kernel, cut), out_shape=(S((R, D)...  160 us
    pallas_call x1, Pallas kernels, run_attend_back(): pl.pallas_call(functools.partial(attend_back_kernel, scale, pads, cut), o...  100 us
    pallas_call x1, Pallas kernels, run_qkv(): pl.pallas_call(functools.partial(qkv_kernel, cut), out_shape=(S((16, R, D...  96.2 us
    pallas_call x1, Pallas kernels, run_attend(): pl.pallas_call(functools.partial(attend_kernel, scale, pads), out_shape=(...  57.2 us
    unnamed x64, local copies, waits for them, and re-layouts  28.7 us
  transfers between devices with their start and end apart: 1, of which 0 were waited for; matrix products, arithmetic and copies ran while one was open for 0% of the time, Pallas kernels for 22%

profile of v4, /device:TPU:0, one launch (start us, length us, event | category | flops | bytes accessed | tf_op | source)
XLA Modules:
  0.0 736.5 jit_solution(9412884200163153568)
XLA Ops:
  4.7 12.7 %swap_rows.1 = f32[32,8,128]{2,1,0:T(8,128)} custom-call(f32[16,8,128]{2,1,0:T(8,128)} %maximum_maximum_fusion.src), custom_call_target="tpu_custom_call" | custom-call | tf_op jit(solution)/shard_map/swap_rows/pallas_call | solution.py:2034
  18.3 1.3 fusion.5
  23.7 1.0 copy.70
  25.8 1.8 maximum_bitcast_fusion
  28.3 1.3 copy.59.q_seg
  29.8 1.3 copy.65.share
  31.1 3.7 fusion
  34.9 1.6 pad_maximum_fusion
  36.5 96.2 %project.1 = (bf16[16,128,2048]{2,1,0:T(8,128)(2,1)S(1)}, f32[16,128,384]{2,1,0:T(8,128)S(1)}, bf16[16,2,64,384]{3,2,1,0:T(8,128)(2,1)S(1)}, f32[32,128]{1,0:T(8,128)S(1)}) custom-call(bf16[128,2048]{1,0:T(8,128)(2,1)S(1)} %copy-done.4, bf16[16,64,384]{2,1,0:T(8,128)(2,1)S(1)} %reshape.193.cols, f32[1,2048]{1,0:T(1,128)S(1)} %slice.47.gain), custom_call_target="tpu_custom_call" | custom-call | tf_op jit(solution)/shard_map/project/pallas_call | solution.py:1131
  132.8 1.7 copy-done.1
  134.4 3.2 copy-done.3
  137.7 57.2 %attend.1 = (bf16[4,4,2,64,2048]{4,3,2,1,0:T(8,128)(2,1)}, bf16[16,128,128]{2,1,0:T(8,128)(2,1)S(1)}, bf16[2,20,2,128,128]{4,3,2,1,0:T(8,128)(2,1)}, bf16[16,128...) custom-call(f32[16,128,384]{2,1,0:T(8,128)} %copy-done.1, ...), custom_call_target="tpu_custom_call" | custom-call | tf_op jit(solution)/shard_map/attend/pallas_call | solution.py:1812
  199.5 248.7 %expert.1 = (f32[128,2048]{1,0:T(8,128)}, bf16[4,4,128,2048]{3,2,1,0:T(8,128)(2,1)}, bf16[4,4,128,2048]{3,2,1,0:T(8,128)(2,1)}, bf16[6,256,2048]{2,1,0:T(8,128)(...) custom-call(bf16[128,2048]{1,0:T(8,128)(2,1)} %copy-done.10, bf16[128,2048]{1,0:T(8,128)(2,1)} %cot.1, ...), custom_call_target="tpu_custom_call" | custom-call | tf_op jit(solution)/shard_map/expert/pallas_call | solution.py:1472
  448.2 2.4 multiply_reduce_fusion
  450.6 3.0 fusion.13
  453.6 100.1 %attend_back.1 = (bf16[16,128,384]{2,1,0:T(8,128)(2,1)}, f32[8,128]{1,0:T(8,128)}, f32[64,2048]{1,0:T(8,128)}) custom-call(bf16[128,2048]{1,0:T(8,128)(2,1)} %get-tuple-element.67.d_res, bf16[4,4,2,64,2048]{4,3,2,1,0:T(8,128)(2,1)} %get-tuple-element.44.wo_h, bf16[16,128,128]{2,1,0:T(8,128)(2,1)} %copy-done.9, bf16[16,128,128]{2,1,0:T(8,128)(2,1)} %copy-done.7, ...), custom_call_target="tpu_custom_call" | custom-call | tf_op jit(solution)/shard_map/attend_back/pallas_call | solution.py:1981
  554.8 160.2 %finish.1 = (f32[128,2048]{1,0:T(8,128)}, f32[128,2048]{1,0:T(8,128)}, f32[64,2048]{1,0:T(8,128)}, f32[64,2048]{1,0:T(8,128)}, f32[64,2048]{1,0:T(8,128)}, /*index=5*/f32[8,128]{1,0:T(8,128)}) custom-call(bf16[16,128,384]{2,1,0:T(8,128)(2,1)} %get-tuple-element.50.d_lin, bf16[16,2,64,384]{3,2,1,0:T(8,128)(2,1)} %copy-done.5, ...), custom_call_target="tpu_custom_call" | custom-call | tf_op jit(solution)/shard_map/finish/pallas_call | solution.py:1676
  718.9 2.4 copy.85
  721.2 2.4 copy.86
  726.9 2.1 copy.91
  729.0 1.6 copy-done.18
  730.6 2.1 copy.92
  732.7 1.6 copy-done.17
  734.3 2.0 copy.93
  (104 shorter events, 23.5 us)
Async XLA Ops:
  0.6 24.6 %copy-start.25 = (bf16[64,2048]{1,0:T(8,128)(2,1)S(1)}, bf16[64,2048]{1,0:T(8,128)(2,1)}, u32[]{:S(2)}) copy-start(bf16[64,2048]{1,0:T(8,128)(2,1)} %param.26) | copy-start | bytes 786436
  21.3 116.4 %copy-start.12 = (s32[5120]{0:T(1024)}, s32[5120]{0:T(1024)S(1)}, u32[]{:S(2)}) copy-start(s32[5120]{0:T(1024)S(1)} %concatenate.22) | copy-start | bytes 61444
  22.2 14.4 %copy-start.13 = (f32[1,2048]{1,0:T(1,128)}, f32[1,2048]{1,0:T(1,128)S(1)}, u32[]{:S(2)}) copy-start(f32[1,2048]{1,0:T(1,128)S(1)} %slice.47.gain) | copy-start | bytes 24580
  34.8 1.7 copy-start.4
  34.9 102.7 %copy-start.15 = (f32[1,128]{1,0:T(1,128)}, f32[1,128]{1,0:T(1,128)S(1)}, u32[]{:S(2)}) copy-start(f32[1,128]{1,0:T(1,128)S(1)} %get-tuple-element.85.gk) | copy-start | bytes 1540
  34.9 102.8 %copy-start.16 = (f32[1,128]{1,0:T(1,128)}, f32[1,128]{1,0:T(1,128)S(1)}, u32[]{:S(2)}) copy-start(f32[1,128]{1,0:T(1,128)S(1)} %get-tuple-element.86.gq) | copy-start | bytes 1540
  34.9 102.8 %copy-start.11 = (bf16[64,2048]{1,0:T(8,128)(2,1)S(1)}, bf16[64,2048]{1,0:T(8,128)(2,1)}, u32[]{:S(2)}) copy-start(bf16[64,2048]{1,0:T(8,128)(2,1)} %w_own.1) | copy-start | bytes 786436
  36.5 158.4 %copy-start.2 = (f32[16,128,128]{2,1,0:T(8,128)}, f32[16,128,128]{2,1,0:T(8,128)S(1)}, u32[]{:S(2)}) copy-start(f32[16,128,128]{2,1,0:T(8,128)S(1)} %get-tuple-element.83.cosine) | copy-start | bytes 3145732
  132.8 1.7 copy-start.1
  134.4 3.2 copy-start.3
  137.7 57.2 %copy-start.5 = (bf16[16,2,64,384]{3,2,1,0:T(8,128)(2,1)}, bf16[16,2,64,384]{3,2,1,0:T(8,128)(2,1)S(1)}, u32[]{:S(2)}) copy-start(bf16[16,2,64,384]{3,2,1,0:T(8,128)(2,1)S(1)} %get-tuple-element.51.wf) | copy-start | bytes 4718596
  137.7 57.2 %copy-start.14 = (f32[32,128]{1,0:T(8,128)}, f32[32,128]{1,0:T(8,128)S(1)}, u32[]{:S(2)}) copy-start(f32[32,128]{1,0:T(8,128)S(1)} %get-tuple-element.40.tot) | copy-start | bytes 49156
  194.9 0.8 copy-start.7
  198.1 1.0 copy-start
  198.1 1.4 copy-start.6
  199.5 251.2 %copy-start.20 = (bf16[128,2048]{1,0:T(8,128)(2,1)S(1)}, bf16[128,2048]{1,0:T(8,128)(2,1)}, u32[]{:S(2)}) copy-start(bf16[128,2048]{1,0:T(8,128)(2,1)} %cot.1) | copy-start | bytes 1572868
  554.4 162.6 %collective-permute-start = (f32[2,128]{1,0:T(2,128)S(1)}, f32[2,128]{1,0:T(2,128)S(1)}, u32[]{:S(2)}, u32[]{:S(2)}) collective-permute-start(f32[2,128]{1,0:T(2,128)S(1)} %slice.55), channel_id=1, source_target_pairs={{0,1},{1,0},{2,3},{3,2},{4,5},{5,4},{6,7},{7,6},{8,9},{9,8},{10,11... | collective-permute-start | bytes 3080 | tf_op jit(solution)/shard_map/ppermute | solution.py:2091
  715.1 8.6 %copy-start.24 = (f32[64,2048]{1,0:T(8,128)S(1)}, f32[64,2048]{1,0:T(8,128)}, u32[]{:S(2)}) copy-start(f32[64,2048]{1,0:T(8,128)} %get-tuple-element.105) | copy-start | bytes 1572868
  715.1 9.4 %copy-start.23 = (f32[64,2048]{1,0:T(8,128)S(1)}, f32[64,2048]{1,0:T(8,128)}, u32[]{:S(2)}) copy-start(f32[64,2048]{1,0:T(8,128)} %get-tuple-element.106) | copy-start | bytes 1572868
  718.9 6.4 copy-start.22
  721.2 4.8 copy-start.21
  721.2 5.6 copy-start.19
  726.9 3.7 copy-start.18
  730.6 3.7 copy-start.17
  (3 other events, 2.4 us)

commit v5 on v4

--- a/solution.py
+++ b/solution.py
@@ -710,16 +710,27 @@
         self.rb = self.R - cut
         self.hb = self.rb // 2
 
-    def first(self, zd):
-        net, P, h, cut, rb = self.net, self.P, self.h, self.cut, self.rb
+    def mid_send(self, zd):
+        net, P, h = self.net, self.P, self.h
         net.go(None, lambda: P.at[net.ud, zd, pl.ds(0, h), :], lambda: self.mid1.at[zd], lambda: self.m1s.at[zd], net.xn)
         net.go(None, lambda: P.at[net.ud, zd, pl.ds(h, h), :], lambda: self.mid2.at[zd], lambda: self.m2s.at[zd], net.yn)
+
+    def bfirst(self, zd):
+        net, P, cut, rb = self.net, self.P, self.cut, self.rb
         if rb and zd > 0:
             net.go(net.at[0], lambda: P.at[:, zd, pl.ds(cut, rb), :], lambda: self.bbe.at[zd], lambda: self.bbes.at[zd], net.up)
         if rb and zd < 3:
             net.go(net.at[3], lambda: P.at[:, zd, pl.ds(cut, rb), :], lambda: self.bab.at[zd], lambda: self.babs.at[zd], net.dn)
+
+    def direct(self, zd):
+        net, P, h = self.net, self.P, self.h
         net.go(None, lambda: P.at[net.ux, zd, pl.ds(0, h), :], lambda: self.fx.at[zd, pl.ds(0, h), :], lambda: self.fxs.at[zd, 0], net.xn)
         net.go(None, lambda: P.at[net.uy, zd, pl.ds(h, h), :], lambda: self.fy.at[zd, pl.ds(h, h), :], lambda: self.fys.at[zd, 1], net.yn)
+
+    def first(self, zd):
+        self.mid_send(zd)
+        self.bfirst(zd)
+        self.direct(zd)
 
     def mids(self, zd):
         net, P, h, mid1, mid2 = self.net, self.P, self.h, self.mid1, self.mid2
@@ -849,6 +860,16 @@
                 pl.ds(cut + sl.start, 16), wide(bm[net.u, sl, :]) + wide(bm[6, sl, :]) + wide(bm[7, sl, :])))
 
 
+def steps_of(sc, text):
+    names = {"m": sc.mid_send, "f": sc.bfirst, "d": sc.direct, "M": sc.mids, "h": sc.hop, "b": sc.bhop, "Q": sc.bquad, "q": sc.bquad2}
+    return [functools.partial(names[word[0]], *[int(digit) for digit in word[1:]]) for word in text.split()]
+
+
+def run_steps(steps):
+    for one in steps:
+        one()
+
+
 def rs_scratch(cut, R, D):
     h, rb = cut // 2, R - cut
     V = lambda *s: pltpu.VMEM(s, BF)
@@ -1036,7 +1057,20 @@
     landed(part, ssem)
 
 
-def qkv_kernel(cut, x_ref, cols, gain, n1_o, lin, wf, tot, X, nb, sums, sums_all, lsem, nsem, msem, ssem, *gs):
+def greet_all(net, count=32):
+    bar = pltpu.get_barrier_semaphore()
+    me = net.u * 8 + net.z * 2 + net.c
+
+    def hello(j, _):
+        t = lax.rem(me + j, count)
+        pl.semaphore_signal(bar, inc=1, device_id=(t // 8, lax.rem(t, 8) // 2, lax.rem(t, 2)), device_id_type=MESH)
+        return 0
+
+    lax.fori_loop(1, count, hello, 0)
+    pl.semaphore_wait(bar, count - 1)
+
+
+def qkv_kernel(cut, x_ref, wq, wk, wv, block, cot, n1_o, lin, wf, tot, sw, C, X, nb, gain, sums, sums_all, lsem, nsem, msem, ssem, csem, *gs):
     net = Net(ssem)
     u, z, c = net.u, net.z, net.c
     me = u * 4 + z
@@ -1044,14 +1078,38 @@
     partner = (u, z, 1 - c)
     own = pltpu.make_async_copy(x_ref, X.at[u, z], lsem.at[0])
     own.start()
-    own_w = pltpu.make_async_copy(cols.at[me], wf.at[me, c], lsem.at[1])
-    own_w.start()
-    greet(net)
+
+    def piece(t, i):
+        return ((wq, wk, wv)[i].at[:, pl.ds(pl.multiple_of(t * 128, 128), 128)], wf.at[me, c, :, pl.ds(i * 128, 128)])
+
+    own_w = [pltpu.make_async_copy(*piece(me, i), lsem.at[1]) for i in range(3)]
+    for one in own_w:
+        one.start()
+    own_c = pltpu.make_async_copy(cot, C.at[u, z], lsem.at[3])
+    own_c.start()
+    dev_me = me * 2 + c
+    greet_all(net)
     own.wait()
     ga = Gather(net, rows, cut, lambda uu, zz, lo, n: X.at[uu, zz, pl.ds(lo, n), :],
-                lambda zz, lo, n: X.at[:, zz, pl.ds(lo, n), :], gs)
+                lambda zz, lo, n: X.at[:, zz, pl.ds(lo, n), :], gs[:7])
+    netc = Net(csem)
+    gc = Gather(netc, rows, cut, lambda uu, zz, lo, n: C.at[uu, zz, pl.ds(lo, n), :],
+                lambda zz, lo, n: C.at[:, zz, pl.ds(lo, n), :], gs[7:])
     ga.begin()
-    each_chip(net, lambda t, dev: remote(cols.at[t], wf.at[me, c], msem.at[0], msem.at[1], dev).start())
+
+    def tell(j, _):
+        t = lax.rem(dev_me + j, 32)
+        remote(block.at[t // 2], sw.at[dev_me], msem.at[6], msem.at[7], (t // 8, lax.rem(t, 8) // 2, lax.rem(t, 2))).start()
+        return 0
+
+    lax.fori_loop(1, 32, tell, 0)
+    sw[dev_me] = block[me]
+
+    def columns(t, dev):
+        for i in range(3):
+            remote(*piece(t, i), msem.at[0], msem.at[1], dev).start()
+
+    each_chip(net, columns)
 
     def plane(zz):
         def chunk(uu, _):
@@ -1093,154 +1151,21 @@
     ga.along(1)
     ga.quads(0)
     ga.cross(0)
-    own_w.wait()
+    landed(wf.at[0, 0], lsem.at[1])
     landed(wf.at[pl.ds(0, 15), 0], msem.at[1])
     to_partner = remote(wf.at[:, c], wf.at[:, c], msem.at[2], msem.at[3], partner)
     to_partner.start()
+    own_c.wait()
     ga.along(2)
     ga.quads(1)
     ga.cross(1)
+    gc.begin()
+    landed(sw.at[pl.ds(0, 31)], msem.at[7])
+    for e in range(16):
+        gain[:, e * 128 : (e + 1) * 128] = sw[2 * e, 2:3, :] + sw[2 * e + 1, 2:3, :]
     ga.settle(0)
     landed(wf.at[:, 1 - c], msem.at[3])
     compute(0)
-    ga.along(3)
-    ga.quads(2)
-    ga.cross(2)
-    ga.settle(1)
-    compute(1)
-    ga.quads(3)
-    ga.cross(3)
-    ga.settle(2)
-    compute(2)
-    ga.settle(3)
-    compute(3)
-    landed(wf.at[pl.ds(0, 15), 0], msem.at[0])
-    landed(wf.at[:, c], msem.at[2])
-    share_sums(net, sums, sums_all, tot, lsem.at[2], msem.at[4], msem.at[5])
-    net.finish()
-
-
-def run_qkv(x, cols, gain, cid, cut=96):
-    R, D = x.shape
-    N = cols.shape[2]
-    DMA = pltpu.SemaphoreType.DMA
-    S = jax.ShapeDtypeStruct
-    V = lambda *s: pltpu.VMEM(s, BF)
-    A = pl.BlockSpec(memory_space=pl.ANY)
-    M = pl.BlockSpec(memory_space=pltpu.VMEM)
-    return pl.pallas_call(
-        functools.partial(qkv_kernel, cut),
-        out_shape=(S((16, R, D), BF), S((16, R, N), F32), S((16, 2, R // 2, N), BF), S((32, 128), F32)),
-        in_specs=[A, A, M],
-        out_specs=(A, M, M, M),
-        scratch_shapes=[V(4, 4, R, D), V(2, R, D), pltpu.VMEM((32, 128), F32), pltpu.VMEM((16, 32, 128), F32),
-                        DMA((3,)), DMA((2,)), DMA((6,)), DMA((64,))] + ag_sems(),
-        compiler_params=pltpu.CompilerParams(collective_id=cid, has_side_effects=True, vmem_limit_bytes=40 * 2**20),
-        name="project",
-    )(x, cols, gain)
-
-
-def group_of(t):
-    g = t // 2
-    return jnp.where(g == 0, 3, jnp.where(g == 1, 0, jnp.where(g == 2, 2, 1)))
-
-
-def expert_kernel(cut, n2, cot, share, gate, up, down, d_n2, p_out, n2_o, other, dg_o, du_o, dd_o,
-                  X, C, GU, W, A, hid, pb, fs, lsem, wsem, wrs, psem, tsem, osem, ors, fsem, sa, sc_, sr, *scr):
-    ga_sems, gc_sems, rs_bufs = scr[:7], scr[7:14], scr[14:]
-    na, nc, nr = Net(sa), Net(sc_), Net(sr)
-    u, z, c = na.u, na.z, na.c
-    partner = (u, z, 1 - c)
-    rows, width = X.shape[2], X.shape[3]
-    ff = W.shape[0]
-    half, half_ff = gate.shape[0], down.shape[0]
-    tokens = 16 * rows
-    tile = 256
-    first = [pltpu.make_async_copy(n2, X.at[u, z], lsem.at[0]), pltpu.make_async_copy(cot, C.at[u, z], lsem.at[1])]
-
-    def weights():
-        mine = pl.ds(pl.multiple_of(c * half, half), half)
-        mine_ff = pl.ds(pl.multiple_of(c * half_ff, half_ff), half_ff)
-        return ((gate, GU.at[mine, pl.ds(0, ff)]), (up, GU.at[mine, pl.ds(ff, ff)]), (down, W.at[mine_ff, :]))
-
-    own_w = [pltpu.make_async_copy(a, b, lsem.at[2 + i]) for i, (a, b) in enumerate(weights())]
-    for one in first + own_w:
-        one.start()
-    na.barrier((partner,))
-    first[0].wait()
-
-    def gather(net, buf, sems):
-        return Gather(net, rows, cut, lambda uu, zz, lo, n: buf.at[uu, zz, pl.ds(lo, n), :],
-                      lambda zz, lo, n: buf.at[:, zz, pl.ds(lo, n), :], sems)
-
-    ga, gc = gather(na, X, ga_sems), gather(nc, C, gc_sems)
-    ga.begin()
-    sent_w = [remote(a, b, wsem.at[i], wrs.at[i], partner) for i, (a, b) in enumerate(weights())]
-    for one in sent_w:
-        one.start()
-
-    def forward(zz):
-        pltpu.make_async_copy(X.at[:, zz], n2_o.at[:, zz], psem.at[1]).start()
-
-        def part(j, _):
-            quads = pl.ds(2 * j, 2)
-
-            def inner(n, _):
-                gcols = pl.ds(pl.multiple_of(n * tile, tile), tile)
-                ucols = pl.ds(pl.multiple_of(ff + n * tile, tile), tile)
-                xv = X[quads, zz].reshape(2 * rows, width)
-                g = dot(xv, GU[:, gcols], ((1,), (0,)))
-                uu = dot(xv, GU[:, ucols], ((1,), (0,)))
-                hid[quads, zz, :, gcols] = (g * jax.nn.sigmoid(g) * uu).astype(BF).reshape(2, rows, tile)
-                A[quads, zz, :, gcols] = g.astype(BF).reshape(2, rows, tile)
-                A[quads, zz, :, ucols] = uu.astype(BF).reshape(2, rows, tile)
-                return 0
-
-            lax.fori_loop(0, ff // tile, inner, 0)
-            weight = share[quads, zz]
-
-            def outer(n, _):
-                cols = pl.ds(pl.multiple_of(n * tile, tile), tile)
-                made = dot(hid[quads, zz].reshape(2 * rows, ff), W[:, cols], ((1,), (0,)))
-                made = made.astype(BF).astype(F32).reshape(2, rows, tile)
-                pb[:, :, cols] = (weight * made).astype(BF)
-                return 0
-
-            lax.fori_loop(0, width // tile, outer, 0)
-            out = pltpu.make_async_copy(pb, p_out.at[quads, zz], psem.at[0])
-            out.start()
-            out.wait()
-            return 0
-
-        lax.fori_loop(0, 2, part, 0)
-
-    def planes(s):
-        if s == 0:
-            forward(z)
-            return
-
-        def one(d, _):
-            zz = jnp.where(d == 0, z - s, z + s)
-            pl.when(jnp.logical_and(zz >= 0, zz < 4))(lambda: forward(zz))
-            return 0
-
-        lax.fori_loop(0, 2, one, 0)
-
-    ga.begin2()
-    ga.along(1)
-    ga.quads(0)
-    ga.cross(0)
-    ga.along(2)
-    ga.quads(1)
-    ga.cross(1)
-    first[1].wait()
-    gc.begin()
-    ga.settle(0)
-    for one in own_w:
-        one.wait()
-    for one in sent_w:
-        one.wait_recv()
-    planes(0)
     gc.begin2()
     ga.along(3)
     ga.quads(2)
@@ -1249,61 +1174,209 @@
     gc.along(1)
     gc.quads(0)
     gc.cross(0)
-    planes(1)
+    compute(1)
     ga.quads(3)
     ga.cross(3)
     ga.settle(2)
     gc.along(2)
     gc.quads(1)
     gc.cross(1)
-    planes(2)
+    compute(2)
     ga.settle(3)
     gc.along(3)
     gc.quads(2)
     gc.cross(2)
-    planes(3)
+    compute(3)
+    landed(wf.at[pl.ds(0, 15), 0], msem.at[0])
+    landed(wf.at[:, c], msem.at[2])
+    share_sums(net, sums, sums_all, tot, lsem.at[2], msem.at[4], msem.at[5])
     gc.quads(3)
     gc.cross(3)
     for s in range(4):
         gc.settle(s)
+    landed(sw.at[pl.ds(0, 31)], msem.at[6])
+    net.finish()
+    netc.finish()
+
+
+def run_qkv(x, wq, wk, wv, block, cot, cid, cut=96):
+    R, D = x.shape
+    N = 384
+    DMA = pltpu.SemaphoreType.DMA
+    S = jax.ShapeDtypeStruct
+    V = lambda *s: pltpu.VMEM(s, BF)
+    VF = lambda *s: pltpu.VMEM(s, F32)
+    A = pl.BlockSpec(memory_space=pl.ANY)
+    M = pl.BlockSpec(memory_space=pltpu.VMEM)
+    return pl.pallas_call(
+        functools.partial(qkv_kernel, cut),
+        out_shape=(S((16, R, D), BF), S((16, R, N), F32), S((16, 2, R // 2, N), BF), S((32, 128), F32),
+                   S((32, 8, 128), F32), S((4, 4) + cot.shape, BF)),
+        in_specs=[A, A, A, A, M, A],
+        out_specs=(A, M, M, M, M, A),
+        scratch_shapes=[V(4, 4, R, D), V(2, R, D), VF(1, D), VF(32, 128), VF(16, 32, 128),
+                        DMA((4,)), DMA((2,)), DMA((8,)), DMA((64,)), DMA((64,))] + ag_sems() + ag_sems(),
+        compiler_params=pltpu.CompilerParams(collective_id=cid, has_side_effects=True, vmem_limit_bytes=40 * 2**20),
+        name="project",
+    )(x, wq, wk, wv, block, cot)
+
+
+def group_of(t):
+    g = t // 2
+    return jnp.where(g == 0, 3, jnp.where(g == 1, 0, jnp.where(g == 2, 2, 1)))
+
+
+def expert_kernel(cut, n2, cot_a, cot_b, share, gate, up, down, d_n2, p_out, n2_o, other, dg_o, du_o, dd_o,
+                  X, C, GU, W, A, hid, pb, fs, lsem, wsem, wrs, psem, tsem, osem, ors, fsem, sa, sr, *scr):
+    ga_sems, rs_bufs = scr[:7], scr[7:]
+    na, nr = Net(sa), Net(sr)
+    u, z, c = na.u, na.z, na.c
+    partner = (u, z, 1 - c)
+    rows, width = X.shape[2], X.shape[3]
+    ff = W.shape[0]
+    half, half_ff = gate.shape[0], down.shape[0]
+    tokens = 16 * rows
+    tile = 256
+    span = 512
+    side = width // 2
+    first = [pltpu.make_async_copy(n2, X.at[u, z], lsem.at[0]),
+             pltpu.make_async_copy(cot_a, C.at[:, :, :, pl.ds(0, side)], lsem.at[1]),
+             pltpu.make_async_copy(cot_b, C.at[:, :, :, pl.ds(side, side)], lsem.at[5])]
+
+    def weights():
+        mine = pl.ds(pl.multiple_of(c * half, half), half)
+        mine_ff = pl.ds(pl.multiple_of(c * half_ff, half_ff), half_ff)
+        return ((gate, GU.at[mine, pl.ds(0, ff)]), (up, GU.at[mine, pl.ds(ff, ff)]), (down, W.at[mine_ff, :]))
+
+    own_w = [pltpu.make_async_copy(a, b, lsem.at[2 + i]) for i, (a, b) in enumerate(weights())]
+    for one in first + own_w:
+        one.start()
+    na.barrier((partner,))
+    first[0].wait()
+
+    def gather(net, buf, sems):
+        return Gather(net, rows, cut, lambda uu, zz, lo, n: buf.at[uu, zz, pl.ds(lo, n), :],
+                      lambda zz, lo, n: buf.at[:, zz, pl.ds(lo, n), :], sems)
+
+    ga = gather(na, X, ga_sems)
+    ga.begin()
+    sent_w = [remote(a, b, wsem.at[i], wrs.at[i], partner) for i, (a, b) in enumerate(weights())]
+    for one in sent_w:
+        one.start()
+
+    def forward(zz):
+        pltpu.make_async_copy(X.at[:, zz], n2_o.at[:, zz], psem.at[1]).start()
+
+        def inner(n, _):
+            gcols = pl.ds(pl.multiple_of(n * span, span), span)
+            ucols = pl.ds(pl.multiple_of(ff + n * span, span), span)
+            xv = X[:, zz].reshape(4 * rows, width)
+            g = dot(xv, GU[:, gcols], ((1,), (0,)))
+            uu = dot(xv, GU[:, ucols], ((1,), (0,)))
+            hid[:, zz, :, gcols] = (g * jax.nn.sigmoid(g) * uu).astype(BF).reshape(4, rows, span)
+            A[:, zz, :, gcols] = g.astype(BF).reshape(4, rows, span)
+            A[:, zz, :, ucols] = uu.astype(BF).reshape(4, rows, span)
+            return 0
+
+        lax.fori_loop(0, ff // span, inner, 0)
+        weight = share[:, zz]
+
+        def flushed(n):
+            cols = pl.ds(pl.multiple_of(n * span, span), span)
+            slot = lax.rem(n, 2)
+            return pltpu.make_async_copy(pb.at[slot], p_out.at[:, zz, :, cols], osem.at[slot])
+
+        def outer(n, _):
+            cols = pl.ds(pl.multiple_of(n * span, span), span)
+            made = dot(hid[:, zz].reshape(4 * rows, ff), W[:, cols], ((1,), (0,)))
+            made = made.astype(BF).astype(F32).reshape(4, rows, span)
+            pl.when(n >= 2)(lambda: flushed(n - 2).wait())
+            pb[lax.rem(n, 2)] = (weight * made).astype(BF)
+            flushed(n).start()
+            return 0
+
+        count = width // span
+        lax.fori_loop(0, count, outer, 0)
+        flushed(count - 2).wait()
+        flushed(count - 1).wait()
+
+    def planes(s):
+        if s == 0:
+            forward(z)
+            return
+
+        def one(d, _):
+            zz = jnp.where(d == 0, z - s, z + s)
+            pl.when(jnp.logical_and(zz >= 0, zz < 4))(lambda: forward(zz))
+            return 0
+
+        lax.fori_loop(0, 2, one, 0)
+
+    ga.begin2()
+    ga.along(1)
+    ga.quads(0)
+    ga.cross(0)
+    ga.along(2)
+    ga.quads(1)
+    ga.cross(1)
+    ga.settle(0)
+    for one in own_w:
+        one.wait()
+    for one in sent_w:
+        one.wait_recv()
+    planes(0)
+    ga.along(3)
+    ga.quads(2)
+    ga.cross(2)
+    ga.settle(1)
+    planes(1)
+    ga.quads(3)
+    ga.cross(3)
+    ga.settle(2)
+    planes(2)
+    ga.settle(3)
+    planes(3)
     na.finish()
-    nc.finish()
+    first[1].wait()
+    first[2].wait()
     for one in sent_w:
         one.wait_send()
     landed(X, psem.at[1])
     sc = Scatter(nr, cut, X, rs_bufs)
 
     def backward(t):
-        zd, j = group_of(t), lax.rem(t, 2)
-        quads = pl.ds(2 * j, 2)
+        zd = group_of(t)
+
+        def inner(n, _):
+            gcols = pl.ds(pl.multiple_of(n * span, span), span)
+            ucols = pl.ds(pl.multiple_of(ff + n * span, span), span)
+            dh = dot(C[:, zd].reshape(4 * rows, width), W[gcols, :], ((1,), (1,)))
+            g = wide(A[:, zd, :, gcols]).reshape(4 * rows, span)
+            uu = wide(A[:, zd, :, ucols]).reshape(4 * rows, span)
+            s = jax.nn.sigmoid(g)
+            A[:, zd, :, gcols] = (dh * uu * s * (1.0 + g * (1.0 - s))).astype(BF).reshape(4, rows, span)
+            A[:, zd, :, ucols] = (dh * g * s).astype(BF).reshape(4, rows, span)
+            return 0
+
+        def outer(n, _):
+            cols = pl.ds(pl.multiple_of(n * span, span), span)
+            back = dot(A[:, zd].reshape(4 * rows, 2 * ff), GU[cols, :], ((1,), (1,)))
+            X[:, zd, :, cols] = back.astype(BF).reshape(4, rows, span)
+            return 0
 
         def scale(i, _):
             sl = pl.ds(pl.multiple_of(i * 16, 16), 16)
-            C[quads, zd, sl, :] = (share[quads, zd, sl, :] * C[quads, zd, sl, :].astype(F32)).astype(BF)
+            C[:, zd, sl, :] = (share[:, zd, sl, :] * C[:, zd, sl, :].astype(F32)).astype(BF)
             return 0
 
-        lax.fori_loop(0, rows // 16, scale, 0)
-
-        def inner(n, _):
-            gcols = pl.ds(pl.multiple_of(n * tile, tile), tile)
-            ucols = pl.ds(pl.multiple_of(ff + n * tile, tile), tile)
-            dh = dot(C[quads, zd].reshape(2 * rows, width), W[gcols, :], ((1,), (1,)))
-            g = wide(A[quads, zd, :, gcols]).reshape(2 * rows, tile)
-            uu = wide(A[quads, zd, :, ucols]).reshape(2 * rows, tile)
-            s = jax.nn.sigmoid(g)
-            A[quads, zd, :, gcols] = (dh * uu * s * (1.0 + g * (1.0 - s))).astype(BF).reshape(2, rows, tile)
-            A[quads, zd, :, ucols] = (dh * g * s).astype(BF).reshape(2, rows, tile)
-            return 0
-
-        lax.fori_loop(0, ff // tile, inner, 0)
-
-        def outer(n, _):
-            cols = pl.ds(pl.multiple_of(n * tile, tile), tile)
-            back = dot(A[quads, zd].reshape(2 * rows, 2 * ff), GU[cols, :], ((1,), (1,)))
-            X[quads, zd, :, cols] = back.astype(BF).reshape(2, rows, tile)
-            return 0
-
-        lax.fori_loop(0, width // tile, outer, 0)
+        @pl.when(lax.rem(t, 2) == 0)
+        def _():
+            lax.fori_loop(0, rows // 16, scale, 0)
+            lax.fori_loop(0, ff // span, inner, 0)
+
+        @pl.when(lax.rem(t, 2) == 1)
+        def _():
+            lax.fori_loop(0, width // span, outer, 0)
 
     def acts(steps, t):
         for at, todo in steps.items():
@@ -1312,15 +1385,10 @@
                     one()
             pl.when(t == at)(act)
 
-    steps = {
-        1: [lambda: sc.first(3)],
-        2: [lambda: sc.mids(3)],
-        3: [lambda: sc.first(0), lambda: sc.bhop(3, 1), lambda: sc.hop(3, 0)],
-        4: [lambda: sc.mids(0), lambda: sc.bhop(3, 2), lambda: sc.hop(3, 1)],
-        5: [lambda: sc.first(2), lambda: sc.bhop(0, 2), lambda: sc.hop(0, 3), lambda: sc.hop(3, 2)],
-        6: [lambda: sc.mids(2), lambda: sc.bhop(0, 1), lambda: sc.hop(0, 2)],
-        7: [lambda: sc.first(1), lambda: sc.bhop(2, 1), lambda: sc.hop(0, 1), lambda: sc.hop(2, 0), lambda: sc.hop(2, 3)],
-    }
+    def at_turns(table):
+        return {t: steps_of(sc, words) for t, words in table.items()}
+
+    steps = at_turns({1: "m3 f3 d3", 3: "m0 f0 d0 M3", 4: "b31", 5: "m2 f2 d2 M0", 6: "h30 b02 b32", 7: "m1 f1 d1 M2 h03"})
 
     def turn(t, _):
         backward(t)
@@ -1398,12 +1466,7 @@
             products(C, store)
 
         copy.start()
-        acts({0: [lambda: sc.mids(1)],
-              1: [lambda: sc.hop(2, 1), lambda: sc.bhop(1, 2)],
-              2: [lambda: sc.hop(1, 0), lambda: sc.hop(1, 3)],
-              3: [sc.bquad],
-              4: [lambda: sc.hop(1, 2)],
-              5: [sc.bquad2]}, k)
+        acts(at_turns({0: "h31 b01 b21", 1: "M1 h02", 2: "h20", 3: "h23 b12 h32", 4: "h01", 5: "h10"}), k)
         return 0
 
     lax.fori_loop(0, 6, other_tile, 0)
@@ -1450,10 +1513,11 @@
             left_hidden(k - 4, c)
             finish(C)
 
-        acts({0: [lambda: sc.last(store_out)]}, k)
+        acts(at_turns({0: "h21", 1: "h13 Q", 3: "h12", 4: "q"}), k)
         return 0
 
     lax.fori_loop(0, 6, own_tile, 0)
+    sc.last(store_out)
     for h in (0, 1):
         landed(fs.at[h], fsem.at[h])
     for k in (4, 5):
@@ -1461,7 +1525,7 @@
     nr.finish()
 
 
-def run_expert(n2, cot, share, gate, up, down, cid, cut=96):
+def run_expert(n2, cot_a, cot_b, share, gate, up, down, cid, cut=96):
     R, D = n2.shape
     half, ff = gate.shape
     DMA = pltpu.SemaphoreType.DMA
@@ -1473,55 +1537,20 @@
         functools.partial(expert_kernel, cut),
         out_shape=(S((R, D), F32), S((4, 4, R, D), BF), S((4, 4, R, D), BF), S((6, 256, D), BF),
                    S((half, ff), F32), S((half, ff), F32), S(down.shape, F32)),
-        in_specs=[A, A, M, A, A, A],
+        in_specs=[A, A, A, M, A, A, A],
         out_specs=(M,) + (A,) * 6,
         scratch_shapes=[V(4, 4, R, D), V(4, 4, R, D), V(D, 2 * ff), V(ff, D), V(4, 4, R, 2 * ff), V(4, 4, R, ff),
-                        V(2, R, D), pltpu.VMEM((2, 256, 1024), F32),
-                        DMA((5,)), DMA((3,)), DMA((3,)), DMA((2,)), DMA((2,)), DMA((6,)), DMA((6,)), DMA((2,)),
-                        DMA((64,)), DMA((64,)), DMA((96,))] + ag_sems() + ag_sems() + rs_scratch(cut, R, D),
+                        V(2, 4, R, 512), pltpu.VMEM((2, 256, 1024), F32),
+                        DMA((6,)), DMA((3,)), DMA((3,)), DMA((2,)), DMA((2,)), DMA((6,)), DMA((6,)), DMA((2,)),
+                        DMA((64,)), DMA((96,))] + ag_sems() + rs_scratch(cut, R, D),
         compiler_params=pltpu.CompilerParams(collective_id=cid, has_side_effects=True, vmem_limit_bytes=63 * 2**20),
         name="expert",
-    )(n2, cot, share, gate, up, down)
-
-
-def stages(sc, store):
-    def each(f, *pairs):
-        return [functools.partial(f, *p) for p in pairs]
-
-    return [
-        each(sc.first, (3,), (0,), (2,), (1,)),
-        each(sc.mids, (3,), (0,), (2,), (1,)),
-        each(sc.hop, (3, 0), (0, 3)) + each(sc.bhop, (3, 1), (0, 2)),
-        each(sc.hop, (2, 0), (1, 3)) + each(sc.bhop, (2, 1), (1, 2)),
-        each(sc.hop, (3, 1), (0, 2)) + each(sc.bhop, (3, 2), (0, 1)),
-        each(sc.hop, (1, 0), (2, 3)) + [sc.bquad],
-        each(sc.hop, (2, 1), (1, 2)),
-        each(sc.hop, (3, 2), (0, 1)) + [sc.bquad2],
-        [functools.partial(sc.last, store)],
-    ]
-
-
-def run_steps(steps):
-    for one in steps:
-        one()
-
-
-def greet_all(net, count=32):
-    bar = pltpu.get_barrier_semaphore()
-    me = net.u * 8 + net.z * 2 + net.c
-
-    def hello(j, _):
-        t = lax.rem(me + j, count)
-        pl.semaphore_signal(bar, inc=1, device_id=(t // 8, lax.rem(t, 8) // 2, lax.rem(t, 2)), device_id_type=MESH)
-        return 0
-
-    lax.fori_loop(1, count, hello, 0)
-    pl.semaphore_wait(bar, count - 1)
-
-
-def finish_kernel(cut, d_lin, wf, n1, p_out, x_in, residual, d_res, gain, d_gain_two,
-                  output, d_inputs, d_wq, d_wk, d_wv, gains_o,
-                  P, PO, nt, left, keep, give, got, send, recv, d_n1, d_gain, gb, gr,
+    )(n2, cot_a, cot_b, share, gate, up, down)
+
+
+def finish_kernel(cut, d_lin, wf, n1, att, x_in, d_res, gain, d_gain_two,
+                  d_wo, d_inputs, d_wq, d_wk, d_wv, gains_o,
+                  P, PO, PG, PT, wsum, nt, left, keep, give, got, send, recv, d_n1, d_gain, gb, gr,
                   lsem, tsem, msem, s1, s2, *bufs):
     net, net2 = Net(s1), Net(s2)
     u, z, c = net.u, net.z, net.c
@@ -1533,8 +1562,6 @@
     partner = (u, z, 1 - c)
     half = len(bufs) // 2
     sc1, sc2 = Scatter(net, cut, P, bufs[:half]), Scatter(net2, cut, PO, bufs[half:])
-    load = pltpu.make_async_copy(p_out, PO, lsem.at[0])
-    load.start()
 
     def tile_load(k):
         slot = lax.rem(k, 2)
@@ -1556,15 +1583,45 @@
     for zd in (3, 0, 2, 1):
         group(zd)
         sc1.first(zd)
-    load.wait()
+
+    side = width // 2
+    own_cols = pl.ds(pl.multiple_of(c * side, side), side)
+    give_cols = pl.ds(pl.multiple_of((1 - c) * side, side), side)
+
+    def outer(e, _):
+        turned_att = att[e].T
+        PG[e // 4, lax.rem(e, 4)] = dot(turned_att, d_res[:, give_cols].astype(BF), ((1,), (0,))).astype(BF)
+        PO[e // 4, lax.rem(e, 4)] = dot(turned_att, d_res[:, own_cols].astype(BF), ((1,), (0,))).astype(BF)
+        return 0
+
+    lax.fori_loop(0, 16, outer, 0)
+    halves = remote(PG, PT, msem.at[6], msem.at[7], partner)
+    halves.start()
+
+    def join():
+        landed(PT, msem.at[7])
+
+        def add(e, _):
+            def strip(sl):
+                at = (e // 4, lax.rem(e, 4), sl, slice(None))
+                PO[at] = (wide(PO[at]) + wide(PT[at])).astype(BF)
+
+            strips(rows, strip)
+            return 0
+
+        lax.fori_loop(0, 16, add, 0)
 
     def store1(sl, v):
         d_n1[sl, :] = v
 
     def store2(sl, v):
-        output[sl, :] = residual[sl, :] + v
-
-    one, two = stages(sc1, store1), stages(sc2, store2)
+        wsum[sl, :] = v
+
+    def one(words):
+        run_steps(steps_of(sc1, words))
+
+    def two(words):
+        run_steps(steps_of(sc2, words))
 
     def grads(k):
         if k < 7:
@@ -1585,29 +1642,25 @@
             keep[2 * k + i] = jnp.where(c == 0, first, second)
             give[2 * k + i] = jnp.where(c == 0, second, first).astype(BF)
 
-    run_steps(two[0])
     grads(0)
-    run_steps(one[1])
     grads(1)
-    run_steps(one[2])
+    one("M3")
     grads(2)
-    run_steps(two[1])
-    run_steps(one[3])
+    one("M0")
+    join()
+    two("m3 f3 m0 f0 m2 f2 m1 f1 d3 d0 d2 d1")
     grads(3)
-    run_steps(two[2])
-    run_steps(one[4])
+    one("M2 b31 b02")
     grads(4)
-    run_steps(two[3])
-    run_steps(one[5])
+    one("M1")
     grads(5)
-    run_steps(one[6])
+    one("h30 h03")
     grads(6)
-    run_steps(two[4])
-    run_steps(one[7])
     grads(7)
     across = remote(give, got, msem.at[0], msem.at[1], partner)
     across.start()
-    run_steps(two[5])
+    one("b21 b12 b32 b01")
+    two("M3 M0 M2 M1")
     landed(got, msem.at[1])
 
     def total(e, _):
@@ -1617,7 +1670,14 @@
     lax.fori_loop(0, 16, total, 0)
     each_chip(net, lambda t, dev: remote(send.at[t], recv.at[me], msem.at[2], msem.at[3], dev).start())
     recv[me] = send[me]
-    run_steps(one[8])
+    one("h20 h13 h31 h02")
+    two("b31 b02 b21 b12")
+    one("Q h10 h23")
+    two("h30 h03 b32 b01")
+    one("h32 h01")
+    two("h20 h13 h31 h02")
+    one("h21 h12 q")
+    sc1.last(store1)
     d_gain[...] = jnp.zeros_like(d_gain)
 
     def norm_back(i, _):
@@ -1643,8 +1703,7 @@
 
     lax.fori_loop(1, 32, tell, 0)
     gr[dev_me] = gb[me]
-    run_steps(two[6])
-    run_steps(two[7])
+    two("Q h10 h23 h32 h01 h21 h12 q")
     landed(recv.at[pl.ds(0, 15)], msem.at[3])
     for e in range(16):
         piece = wide(recv[e])
@@ -1655,15 +1714,21 @@
     for i in range(1, 32):
         sums = sums + gr[i]
     gains_o[...] = sums
-    run_steps(two[8])
+    sc2.last(store2)
+    d_wo[:, own_cols] = wsum[pl.ds(pl.multiple_of(c * 64, 64), 64), :]
+    theirs = remote(wsum.at[pl.ds(pl.multiple_of((1 - c) * 64, 64), 64), :], d_wo.at[:, own_cols], msem.at[8], msem.at[9], partner)
+    theirs.start()
+    landed(PG, msem.at[6])
     landed(give, msem.at[0])
     landed(recv.at[pl.ds(0, 15)], msem.at[2])
     landed(gr.at[pl.ds(0, 31)], msem.at[4])
+    theirs.wait_send()
+    landed(d_wo.at[:, give_cols], msem.at[9])
     net.finish()
     net2.finish()
 
 
-def run_finish(d_lin, wf, n1, p_out, x_in, residual, d_res, gain, d_gain_two, cid, cut=96):
+def run_finish(d_lin, wf, n1, att, x_in, d_res, gain, d_gain_two, cid, cut=96):
     R, D = x_in.shape
     N = d_lin.shape[2]
     DMA = pltpu.SemaphoreType.DMA
@@ -1675,15 +1740,15 @@
     own = S((R // 2, D), F32)
     return pl.pallas_call(
         functools.partial(finish_kernel, cut),
-        out_shape=(S((R, D), F32), S((R, D), F32), own, own, own, S((8, 128), F32)),
-        in_specs=[M, M, A, A] + [M] * 5,
+        out_shape=(own, S((R, D), F32), own, own, own, S((8, 128), F32)),
+        in_specs=[M, M, A] + [M] * 5,
         out_specs=(M,) * 6,
-        scratch_shapes=[V(4, 4, R, D), V(4, 4, R, D), V(2, 16, R, 256), V(256, 16 * R), VF(16, 64, N), V(16, 64, N),
+        scratch_shapes=[V(4, 4, R, D), V(4, 4, R, D // 2), V(4, 4, R, D // 2), V(4, 4, R, D // 2), VF(R, D // 2), V(2, 16, R, 256), V(256, 16 * R), VF(16, 64, N), V(16, 64, N),
                         V(16, 64, N), V(16, 64, N), V(16, 64, N), VF(R, D), VF(1, D), VF(16, 8, 128), VF(32, 8, 128),
-                        DMA((1,)), DMA((2,)), DMA((6,)), DMA((64,)), DMA((64,))] + rs_scratch(cut, R, D) + rs_scratch(cut, R, D),
+                        DMA((1,)), DMA((2,)), DMA((10,)), DMA((64,)), DMA((64,))] + rs_scratch(cut, R, D) + rs_scratch(cut, R, D // 2),
         compiler_params=pltpu.CompilerParams(collective_id=cid, has_side_effects=True, vmem_limit_bytes=63 * 2**20),
         name="finish",
-    )(d_lin, wf, n1, p_out, x_in, residual, d_res, gain, d_gain_two)
+    )(d_lin, wf, n1, att, x_in, d_res, gain, d_gain_two)
 
 def band_scores(q, k, q_seg, k_seg, scale, reach):
     scores = dot(q, k, ((1,), (1,))) * scale
@@ -1700,8 +1765,8 @@
     return v * cosine - pltpu.roll(v, 64, axis=1) * sine
 
 
-def attend_kernel(scale, pads, lin, tot, cosine, sine, gq, gk, q_seg, k_seg, w_own, x_in, gain, wo_o, q_rot, kv, o_ref, lse,
-                  att, residual, n2, wo, lsem, msem, ssem, *gs):
+def attend_kernel(scale, pads, cut, lin, tot, cosine, sine, gq, gk, q_seg, k_seg, w_own, x_in, gain, cot, wo_o, q_rot, kv, o_ref, lse,
+                  att, residual, n2, C, wo, lsem, msem, psem, ssem, csem, *gs):
     net = Net(ssem)
     u, z, c = net.u, net.z, net.c
     me = u * 4 + z
@@ -1711,9 +1776,21 @@
     partner = (u, z, 1 - c)
     own = pltpu.make_async_copy(w_own, wo.at[u, z, c], lsem.at[0])
     own.start()
+    own_c = pltpu.make_async_copy(cot, C.at[u, z], lsem.at[2])
+    own_c.start()
     greet(net)
     own.wait()
-    ga = Gather(net, rows // 2, rows // 2, lambda uu, zz, lo, n: wo.at[uu, zz, c, pl.ds(lo, n), :], None, gs)
+    ga = Gather(net, rows // 2, rows // 2, lambda uu, zz, lo, n: wo.at[uu, zz, c, pl.ds(lo, n), :], None, gs[:7])
+    netc = Net(csem)
+    gc = Gather(netc, rows, cut, lambda uu, zz, lo, n: C.at[uu, zz, pl.ds(lo, n), :],
+                lambda zz, lo, n: C.at[:, zz, pl.ds(lo, n), :], gs[7:])
+
+    def halves(s):
+        ga.settle(s)
+        for zz, cond in ga.planes(s):
+            ref = lambda zz=zz: wo.at[:, zz, c]
+            net.go(cond, ref, ref, lambda zz=zz: psem.at[zz], partner)
+
     ga.begin()
     for i in range(pads):
         kv[:, i] = jnp.zeros(kv.shape[:1] + kv.shape[2:], BF)
@@ -1734,6 +1811,8 @@
     to_partner.start()
     ga.along(1)
     ga.cross(0)
+    own_c.wait()
+    gc.begin()
     landed(kv.at[:, pl.ds(pads, 16), 1 - c], msem.at[1])
 
     def block(j, _):
@@ -1759,19 +1838,27 @@
     lax.fori_loop(0, 5, block, 0)
     ga.along(2)
     ga.cross(1)
+    halves(0)
+    gc.begin2()
     lax.fori_loop(5, 10, block, 0)
     ga.along(3)
     ga.cross(2)
+    halves(1)
+    gc.along(1)
+    gc.quads(0)
+    gc.cross(0)
     lax.fori_loop(10, 16, block, 0)
     ga.cross(3)
-    for s in range(4):
-        ga.settle(s)
-    rest = remote(wo.at[:, :, c], wo.at[:, :, c], msem.at[4], msem.at[5], partner)
-    rest.start()
+    halves(2)
+    gc.along(2)
+    gc.quads(1)
+    gc.cross(1)
+    halves(3)
     att[me] = o_ref[me]
     part = att.at[pl.ds(0, 15)]
     landed(part, msem.at[3])
-    landed(wo.at[:, :, 1 - c], msem.at[5])
+    for zz in range(4):
+        landed(wo.at[:, zz, 1 - c], psem.at[zz])
     keep = pltpu.make_async_copy(wo, wo_o, lsem.at[1])
     keep.start()
     tile = 256
@@ -1786,6 +1873,9 @@
         return 0
 
     lax.fori_loop(0, width // tile, out, 0)
+    gc.along(3)
+    gc.quads(2)
+    gc.cross(2)
 
     def norm(i, _):
         sl = pl.ds(pl.multiple_of(i * 16, 16), 16)
@@ -1797,12 +1887,16 @@
     lax.fori_loop(0, rows // 16, norm, 0)
     landed(mine, msem.at[0])
     landed(part, msem.at[2])
-    landed(wo.at[:, :, c], msem.at[4])
+    gc.quads(3)
+    gc.cross(3)
+    for s in range(4):
+        gc.settle(s)
     keep.wait()
     net.finish()
-
-
-def run_attend(scale, pads, lin, tot, cosine, sine, gq, gk, q_seg, k_seg, w_own, x_in, gain, cid):
+    netc.finish()
+
+
+def run_attend(scale, pads, lin, tot, cosine, sine, gq, gk, q_seg, k_seg, w_own, x_in, gain, cot, cid, cut=96):
     R, D = x_in.shape
     DMA = pltpu.SemaphoreType.DMA
     S = jax.ShapeDtypeStruct
@@ -1810,19 +1904,19 @@
     M = pl.BlockSpec(memory_space=pltpu.VMEM)
     wo = (4, 4, 2, R // 2, D)
     return pl.pallas_call(
-        functools.partial(attend_kernel, scale, pads),
+        functools.partial(attend_kernel, scale, pads, cut),
         out_shape=(S(wo, BF), S((16, R, 128), BF), S((2, pads + 16, 2, R, 128), BF), S((16, R, 128), BF),
-                   S((16, R, 1), F32), S((16, R, 128), BF), S((R, D), F32), S((R, D), BF)),
-        in_specs=[M] * 8 + [A, M, M],
-        out_specs=(A,) + (M,) * 7,
-        scratch_shapes=[pltpu.VMEM(wo, BF), DMA((2,)), DMA((6,)), DMA((64,))] + ag_sems(),
+                   S((16, R, 1), F32), S((16, R, 128), BF), S((R, D), F32), S((R, D), BF), S((4, 4) + cot.shape, BF)),
+        in_specs=[M] * 8 + [A, M, M, A],
+        out_specs=(A,) + (M,) * 7 + (A,),
+        scratch_shapes=[pltpu.VMEM(wo, BF), DMA((3,)), DMA((4,)), DMA((4,)), DMA((64,)), DMA((64,))] + ag_sems() + ag_sems(),
         compiler_params=pltpu.CompilerParams(collective_id=cid, has_side_effects=True, vmem_limit_bytes=48 * 2**20),
         name="attend",
-    )(lin, tot, cosine, sine, gq, gk, q_seg, k_seg, w_own, x_in, gain)
-
-
-def attend_back_kernel(scale, pads, cut, d_res, wo_h, att, q_rot, kv, q_seg, k_seg, lse, o_ref, lin, tot, cosine, sine, gq, gk,
-                       d_lin, d_gains, d_wo, P, PG, PT, wsum, wo, d_mine, d_out, d_q, d_k, d_v, other, got, d_un, sums, sums_all, inner,
+    )(lin, tot, cosine, sine, gq, gk, q_seg, k_seg, w_own, x_in, gain, cot)
+
+
+def attend_back_kernel(scale, pads, cut, d_res, wo_h, p_out, residual, q_rot, kv, q_seg, k_seg, lse, o_ref, lin, tot, cosine, sine, gq, gk,
+                       d_lin, d_gains, output, P, wo, d_mine, d_out, d_q, d_k, d_v, other, got, d_un, sums, sums_all, inner,
                        lsem, msem, ssem, *bufs):
     net = Net(ssem)
     sc = Scatter(net, cut, P, bufs)
@@ -1833,7 +1927,13 @@
     partner = (u, z, 1 - c)
     load = pltpu.make_async_copy(wo_h, wo, lsem.at[0])
     load.start()
+    load_p = pltpu.make_async_copy(p_out, P, lsem.at[1])
+    load_p.start()
     greet(net)
+
+    def go(words):
+        run_steps(steps_of(sc, words))
+
     load.wait()
 
     def send(j, _):
@@ -1852,19 +1952,8 @@
         return 0
 
     lax.fori_loop(0, 16, send, 0)
-    side = width // 2
-    own_cols = pl.ds(pl.multiple_of(c * side, side), side)
-    give_cols = pl.ds(pl.multiple_of((1 - c) * side, side), side)
-
-    def outer(e, _):
-        left = att[e].T
-        P[e // 4, lax.rem(e, 4)] = dot(left, d_res[:, own_cols], ((1,), (0,))).astype(BF)
-        PG[e // 4, lax.rem(e, 4)] = dot(left, d_res[:, give_cols], ((1,), (0,))).astype(BF)
-        return 0
-
-    lax.fori_loop(0, 16, outer, 0)
-    across = remote(PG, PT, msem.at[6], msem.at[7], partner)
-    across.start()
+    load_p.wait()
+    go("m3 f3 m0 f0 m2 f2 m1 f1")
     d_k[...] = jnp.zeros_like(d_k)
     d_v[...] = jnp.zeros_like(d_v)
     landed(d_out.at[pl.ds(0, 15)], msem.at[1])
@@ -1885,31 +1974,14 @@
         return 0
 
     def store(sl, v):
-        wsum[sl, :] = v
-
-    steps = stages(sc, store)
-    lax.fori_loop(0, 3, block, 0)
-    landed(PT, msem.at[7])
-
-    def join(e, _):
-        def strip(sl):
-            at = (e // 4, lax.rem(e, 4), sl, slice(None))
-            P[at] = (wide(P[at]) + wide(PT[at])).astype(BF)
-
-        strips(rows, strip)
-        return 0
-
-    lax.fori_loop(0, 16, join, 0)
-    run_steps(steps[0])
-    lax.fori_loop(3, 6, block, 0)
-    run_steps(steps[1])
-    lax.fori_loop(6, 8, block, 0)
-    run_steps(steps[2])
-    lax.fori_loop(8, 10, block, 0)
-    run_steps(steps[3])
-    lax.fori_loop(10, 13, block, 0)
-    run_steps(steps[4])
-    lax.fori_loop(13, 16, block, 0)
+        output[sl, :] = residual[sl, :] + v
+
+    go("d3 d0 d2 d1")
+    done = 0
+    for upto, words in ((3, "M3 M0"), (6, "b31 b02 M2 M1"), (9, "b21 b12 h30 h03"), (12, "b32 b01"), (14, "h31 h02"), (16, "h20 h13")):
+        lax.fori_loop(done, upto, block, 0)
+        go(words)
+        done = upto
 
     def pack(i, _):
         at = pl.ds(pl.multiple_of(((pads + i) * 2 + 1 - c) * rows, rows), rows)
@@ -1919,7 +1991,7 @@
 
     lax.fori_loop(0, 16, pack, 0)
     remote(other, got, msem.at[2], msem.at[3], partner).start()
-    run_steps(steps[5])
+    go("h32 h01")
     landed(got, msem.at[3])
     d_gains[...] = jnp.zeros_like(d_gains)
 
@@ -1944,7 +2016,7 @@
         return 0
 
     lax.fori_loop(0, 16, undo, 0)
-    run_steps(steps[6])
+    go("h10 h23 Q")
     share_sums(net, sums, sums_all, inner, lsem.at[1], msem.at[4], msem.at[5])
 
     def finish(i, _):
@@ -1957,20 +2029,14 @@
         return 0
 
     lax.fori_loop(0, 16, finish, 0)
-    run_steps(steps[7])
-    run_steps(steps[8])
-    d_wo[:, own_cols] = wsum[pl.ds(pl.multiple_of(c * 64, 64), 64), :]
-    theirs = remote(wsum.at[pl.ds(pl.multiple_of((1 - c) * 64, 64), 64), :], d_wo.at[:, own_cols], msem.at[8], msem.at[9], partner)
-    theirs.start()
+    go("h21 h12 q")
+    sc.last(store)
     landed(d_out.at[pl.ds(0, 15)], msem.at[0])
     landed(other, msem.at[2])
-    landed(PG, msem.at[6])
-    theirs.wait_send()
-    landed(d_wo.at[:, give_cols], msem.at[9])
     net.finish()
 
 
-def run_attend_back(scale, pads, d_res, wo, att, q_rot, kv, q_seg, k_seg, lse, o, lin, tot, cosine, sine, gq, gk, cid, cut=96):
+def run_attend_back(scale, pads, d_res, wo, p_out, residual, q_rot, kv, q_seg, k_seg, lse, o, lin, tot, cosine, sine, gq, gk, cid, cut=96):
     R, D = d_res.shape
     DMA = pltpu.SemaphoreType.DMA
     S = jax.ShapeDtypeStruct
@@ -1980,113 +2046,16 @@
     span = (pads + 16) * 2 * R
     return pl.pallas_call(
         functools.partial(attend_back_kernel, scale, pads, cut),
-        out_shape=(S((16, R, 384), BF), S((8, 128), F32), S((R // 2, D), F32)),
-        in_specs=[M, A] + [M] * 13,
+        out_shape=(S((16, R, 384), BF), S((8, 128), F32), S((R, D), F32)),
+        in_specs=[M, A, A] + [M] * 13,
         out_specs=(M, M, M),
-        scratch_shapes=[V((4, 4, R, D // 2), BF), V((4, 4, R, D // 2), BF), V((4, 4, R, D // 2), BF), V((R, D // 2), F32), V(wo.shape, BF), V((16, R, 128), BF), V((16, R, 128), BF), V((16, R, 128), BF),
+        scratch_shapes=[V((4, 4, R, D), BF), V(wo.shape, BF), V((16, R, 128), BF), V((16, R, 128), BF), V((16, R, 128), BF),
                         V((span, 128), F32), V((span, 128), F32), V((2, 16, R, 128), BF), V((2, 16, R, 128), BF),
                         V((2, 16, R, 128), F32), V((32, 128), F32), V((16, 32, 128), F32), V((32, 128), F32),
-                        DMA((2,)), DMA((10,)), DMA((64,))] + rs_scratch(cut, R, D // 2),
+                        DMA((2,)), DMA((10,)), DMA((64,))] + rs_scratch(cut, R, D),
         compiler_params=pltpu.CompilerParams(collective_id=cid, has_side_effects=True, vmem_limit_bytes=62 * 2**20),
         name="attend_back",
-    )(d_res, wo, att, q_rot, kv, q_seg, k_seg, lse, o, lin, tot, cosine, sine, gq, gk)
-def swap_kernel(src, out, lsem, ssem, rsem):
-    u, z, c = place()
-    me = u * 8 + z * 2 + c
-    count = out.shape[0]
-    bar = pltpu.get_barrier_semaphore()
-
-    def at(j):
-        t = lax.rem(me + j, count)
-        return t // 8, lax.rem(t, 8) // 2, lax.rem(t, 2), t // 2
-
-    def hello(j, _):
-        tu, tz, tc, _e = at(j)
-        pl.semaphore_signal(bar, inc=1, device_id=(tu, tz, tc), device_id_type=MESH)
-        return 0
-
-    lax.fori_loop(1, count, hello, 0)
-    pl.semaphore_wait(bar, count - 1)
-
-    def copy(j):
-        tu, tz, tc, e = at(j)
-        return pltpu.make_async_remote_copy(
-            src_ref=src.at[e], dst_ref=out.at[me], send_sem=ssem, recv_sem=rsem,
-            device_id=(tu, tz, tc), device_id_type=MESH)
-
-    own = pltpu.make_async_copy(src.at[me // 2], out.at[me], lsem)
-    own.start()
-
-    def send(j, _):
-        copy(j).start()
-        return 0
-
-    lax.fori_loop(1, count, send, 0)
-    own.wait()
-    part = out.at[pl.ds(0, count - 1)]
-    pltpu.make_async_copy(part, part, rsem).wait()
-    pltpu.make_async_copy(part, part, ssem).wait()
-
-
-def swap(block, cid):
-    chips, r, lanes = block.shape
-    S = pltpu.SemaphoreType.DMA
-    return pl.pallas_call(
-        swap_kernel,
-        out_shape=jax.ShapeDtypeStruct((2 * chips, r, lanes), block.dtype),
-        in_specs=[pl.BlockSpec(memory_space=pltpu.VMEM)],
-        out_specs=pl.BlockSpec(memory_space=pltpu.VMEM),
-        scratch_shapes=[S, S, S],
-        compiler_params=pltpu.CompilerParams(collective_id=cid, has_side_effects=True),
-        name="swap_rows",
-    )(block)
-
-
-def spread_kernel(src, out, lsem, ssem, rsem):
-    u, z, c = place()
-    me = u * 4 + z
-    count = out.shape[0]
-    bar = pltpu.get_barrier_semaphore()
-
-    def at(j):
-        t = lax.rem(me + j, count)
-        return t // 4, lax.rem(t, 4), c
-
-    def hello(j, _):
-        pl.semaphore_signal(bar, inc=1, device_id=at(j), device_id_type=MESH)
-        return 0
-
-    lax.fori_loop(1, count, hello, 0)
-    pl.semaphore_wait(bar, count - 1)
-    own = pltpu.make_async_copy(src, out.at[me], lsem)
-    own.start()
-
-    def send(j, _):
-        pltpu.make_async_remote_copy(
-            src_ref=src, dst_ref=out.at[me], send_sem=ssem, recv_sem=rsem,
-            device_id=at(j), device_id_type=MESH).start()
-        return 0
-
-    lax.fori_loop(1, count, send, 0)
-    own.wait()
-    part = out.at[pl.ds(0, count - 1)]
-    pltpu.make_async_copy(part, part, rsem).wait()
-    pltpu.make_async_copy(part, part, ssem).wait()
-
-
-def spread(block, cid):
-    S = pltpu.SemaphoreType.DMA
-    return pl.pallas_call(
-        spread_kernel,
-        out_shape=jax.ShapeDtypeStruct((16,) + block.shape, block.dtype),
-        in_specs=[pl.BlockSpec(memory_space=pltpu.VMEM)],
-        out_specs=pl.BlockSpec(memory_space=pltpu.VMEM),
-        scratch_shapes=[S, S, S],
-        compiler_params=pltpu.CompilerParams(collective_id=cid, has_side_effects=True),
-        name="spread_rows",
-    )(block)
-
-
+    )(d_res, wo, p_out, residual, q_rot, kv, q_seg, k_seg, lse, o, lin, tot, cosine, sine, gq, gk)
 def core_pair(value):
     return lax.ppermute(value, "core", [(0, 1), (1, 0)])
 
@@ -2114,13 +2083,18 @@
     earlier = (fill_order[None, :] < fill_order[:, None]).astype(jnp.bfloat16)
     rank = dot(earlier, chosen.astype(jnp.bfloat16), ((1,), (0,)))
     rank = jnp.where(chosen, rank, -1.0)
-    gains = jnp.concatenate([norm1_gain, query_gain, key_gain, norm2_gain]).astype(F32)
-    gains = jnp.broadcast_to(gains.reshape(1, 2, 128), (chips, 2, 128))
+    gains = jnp.stack([norm1_gain, query_gain, key_gain, norm2_gain]).astype(F32)
+    blank = jnp.zeros_like(gains)
+    gains = jnp.where(core == 0, jnp.concatenate([gains, blank], axis=1), jnp.concatenate([blank, gains], axis=1))
+    gains = jnp.broadcast_to(gains[None], (chips, 4, 128))
     block = jnp.concatenate(
-        [weight.T[:, None, :], rank.T[:, None, :], gains, jnp.zeros((chips, 4, 128), F32)], axis=1)
-    swapped = swap(block, 1)
-    gains = swapped[:, 2:4, :].reshape(devices, 4, 64).transpose(1, 0, 2).reshape(4, width)
-    gain_one, gain_q, gain_k, gain_two = gains[0], gains[1], gains[2], gains[3]
+        [weight.T[:, None, :], rank.T[:, None, :], gains, jnp.zeros((chips, 2, 128), F32)], axis=1)
+    side = width // 2
+    n1_rows, lin, w_qkv, squares, swapped, cot_a = run_qkv(
+        inputs, w_query, w_key, w_value, block, cotangent[:, :side], 2)
+    gains = jnp.sum(swapped.reshape(chips, 2, 8, 128), axis=1)
+    gain_one, gain_two = gains[:, 2].reshape(1, width), gains[:, 5].reshape(1, width)
+    gq, gk = (lax.dynamic_slice_in_dim(gains[:, i], chip, 1, 0) for i in (3, 4))
     rank_all = swapped[:, 1, :]
     taken = rank_all >= 0.0
     counts = jnp.sum(taken.astype(F32), axis=1)
@@ -2130,18 +2104,6 @@
     share = lax.dynamic_index_in_dim(share, core, 1, keepdims=False).reshape(chips * rows, 1)
 
 
-    layer_in = inputs.astype(F32)
-    mine = ("ulysses", "z")
-
-    def in_order(own, other):
-        return jnp.where(core == 0, own, other), jnp.where(core == 0, other, own)
-
-    cols = jnp.stack([w_query, w_key, w_value]).reshape(3, 64, chips, HEAD_DIM)
-    cols = cols.transpose(2, 1, 0, 3).reshape(chips, 64, 3 * HEAD_DIM)
-    def my_head(gain):
-        return lax.dynamic_slice_in_dim(gain, chip * HEAD_DIM, HEAD_DIM, 0)
-
-    n1_rows, lin, w_qkv, squares = run_qkv(inputs, cols, gain_one.reshape(1, width), 2)
     positions = (jnp.arange(chips, dtype=jnp.int32)[:, None] * 2 + core) * rows + jnp.arange(rows, dtype=jnp.int32)
     half_dim = HEAD_DIM // 2
     inv_freq = jnp.exp(jnp.arange(half_dim, dtype=F32) * (-2.0 * math.log(ROPE_BASE) / HEAD_DIM))
@@ -2149,21 +2111,17 @@
     cosine, sine = jnp.cos(angles), jnp.sin(angles)
     cosine = jnp.concatenate([cosine, cosine], axis=1).reshape(chips, rows, HEAD_DIM)
     sine = jnp.concatenate([-sine, sine], axis=1).reshape(chips, rows, HEAD_DIM)
-    gq, gk = my_head(gain_q).reshape(1, HEAD_DIM), my_head(gain_k).reshape(1, HEAD_DIM)
     pads = chips // 4
     k_seg = jnp.concatenate([jnp.full((pads * 2 * rows,), -1, jnp.int32), segments]).reshape(1, -1)
     q_seg = lax.dynamic_index_in_dim(segments.reshape(chips, 2, rows, 1), core, 1, keepdims=False)
     scale = 1.0 / math.sqrt(HEAD_DIM)
     tokens = chips * rows
-    w_o, q_rot, kv, head_out, log_total, attended, residual, normed_two = run_attend(
-        scale, pads, lin, squares, cosine, sine, gq, gk, q_seg, k_seg, w_output, inputs, gain_two.reshape(1, width), 4)
+    w_o, q_rot, kv, head_out, log_total, attended, residual, normed_two, cot_b = run_attend(
+        scale, pads, lin, squares, cosine, sine, gq, gk, q_seg, k_seg, w_output, inputs, gain_two, cotangent[:, side:], 4)
     r2 = lax.rsqrt(jnp.mean(residual * residual, axis=1, keepdims=True) + EPS)
 
-    def to_blocks(part):
-        return part.astype(BF).reshape(4, 4, rows, part.shape[-1])
-
     d_normed_two, mixed, _n2, _other, d_expert_gate, d_expert_up, d_expert_down = run_expert(
-        normed_two, cotangent, share.reshape(4, 4, rows, 1), expert_gate, expert_up, expert_down, 6)
+        normed_two, cot_a, cot_b, share.reshape(4, 4, rows, 1), expert_gate, expert_up, expert_down, 6)
     def norm_back(d_out, values, r, gain):
         d_scaled = d_out * gain
         inner = jnp.mean(d_scaled * values, axis=1, keepdims=True)
@@ -2173,11 +2131,11 @@
     d_resid_norm, d_gain_two = norm_back(d_normed_two, residual, r2, gain_two)
     d_residual = cotangent.astype(F32) + d_resid_norm
     d_res_low = d_residual.astype(BF)
-    d_lin, d_qk_gains, d_w_output = run_attend_back(
-        scale, pads, d_res_low, w_o, attended, q_rot, kv, q_seg, k_seg, log_total, head_out, lin, squares, cosine, sine, gq, gk, 7)
+    d_lin, d_qk_gains, output = run_attend_back(
+        scale, pads, d_res_low, w_o, mixed, residual, q_rot, kv, q_seg, k_seg, log_total, head_out, lin, squares, cosine, sine, gq, gk, 7)
     d_qk_gains = d_qk_gains[:2] + core_pair(d_qk_gains[:2])
-    output, d_inputs, d_w_query, d_w_key, d_w_value, d_gains = run_finish(
-        d_lin, w_qkv, n1_rows, mixed, inputs, residual, d_residual, gain_one.reshape(1, width), d_gain_two.reshape(1, width), 8)
+    d_w_output, d_inputs, d_w_query, d_w_key, d_w_value, d_gains = run_finish(
+        d_lin, w_qkv, n1_rows, attended, inputs, d_residual, gain_one, d_gain_two.reshape(1, width), 8)
 
     def my_half(row):
         return lax.dynamic_slice_in_dim(row, core * 64, 64, 0)

time: 749 us -> 691 us (0.923); the launches traced: 737 us -> 687 us
  Pallas kernels: 675 us -> 631 us
    pallas_call x1, Pallas kernels: 249 us -> 181 us  [run_expert(): pl.pallas_call(functools.partial(expert_kernel, cut), out_shape=(S((R, D)...]
    pallas_call x1, Pallas kernels: 96.2 us -> 126 us  [run_qkv(): pl.pallas_call(functools.partial(qkv_kernel, cut), out_shape=(S((16, R, D...]
    pallas_call x3 -> x2, Pallas kernels: 230 us -> 225 us  [the longest x1 142 us: run_finish(): pl.pallas_call(functools.partial(finish_kernel, cut), out_shape=(own, S((...]
    unnamed x64 -> x65, local copies, waits for them, and re-layouts: 28.7 us -> 30.4 us
  transfers between devices with their start and end apart: 1 -> 1, of which waited for: 0 -> 0; matrix products, arithmetic and copies ran while one was open for 0% -> 0% of each run, Pallas kernels for 22% -> 21%
where the time goes in v5:
time: 691 us; the launch traced here: 687 us
  Pallas kernels  631 us (91%)
  local copies, waits for them, and re-layouts  39.8 us (6%)
  other arithmetic  14.8 us (2%)
    pallas_call x1, Pallas kernels, run_expert(): pl.pallas_call(functools.partial(expert_kernel, cut), out_shape=(S((R, D)...  181 us
    pallas_call x1, Pallas kernels, run_finish(): pl.pallas_call(functools.partial(finish_kernel, cut), out_shape=(own, S((...  142 us
    pallas_call x1, Pallas kernels, run_qkv(): pl.pallas_call(functools.partial(qkv_kernel, cut), out_shape=(S((16, R, D...  126 us
    pallas_call x1, Pallas kernels, run_attend_back(): pl.pallas_call(functools.partial(attend_back_kernel, scale, pads, cut), o...  98.2 us
    pallas_call x1, Pallas kernels, run_attend(): pl.pallas_call(functools.partial(attend_kernel, scale, pads, cut), out_sh...  83 us
    unnamed x65, local copies, waits for them, and re-layouts  30.4 us
  transfers between devices with their start and end apart: 1, of which 0 were waited for; matrix products, arithmetic and copies ran while one was open for 0% of the time, Pallas kernels for 21%

profile of v5, /device:TPU:0, one launch (start us, length us, event | category | flops | bytes accessed | tf_op | source)
XLA Modules:
  0.0 687.4 jit_solution(18353049796441797816)
XLA Ops:
  2.1 1.1 fusion.14
  5.0 1.0 copy-done.2
  8.9 126.2 %project.1 = (bf16[16,128,2048]{2,1,0:T(8,128)(2,1)}, f32[16,128,384]{2,1,0:T(8,128)S(1)}, bf16[16,2,64,384]{3,2,1,0:T(8,128)(2,1)S(1)}, f32[32,128]{1,0:T(8,128...) custom-call(bf16[128,2048]{1,0:T(8,128)(2,1)S(1)} %copy-done.2, bf16[64,2048]{1,0:T(8,128)(2,1)S(1)} %copy-done.11, ...), custom_call_target="tpu_custom_call" | custom-call | tf_op jit(solution)/shard_map/project/pallas_call | solution.py:1211
  135.1 1.7 copy-done.1
  136.7 2.0 copy-done.4
  138.7 1.1 copy-done.5
  141.6 1.4 copy.39.q_seg
  143.7 1.4 copy.41.share
  145.0 3.7 fusion
  148.8 1.9 pad_maximum_fusion
  150.7 83.0 %attend.1 = (bf16[4,4,2,64,2048]{4,3,2,1,0:T(8,128)(2,1)}, bf16[16,128,128]{2,1,0:T(8,128)(2,1)S(1)}, bf16[2,20,2,128,128]{4,3,2,1,0:T(8,128)(2,1)}, bf16[16,128...) custom-call(f32[16,128,384]{2,1,0:T(8,128)} %copy-done.1, ...), custom_call_target="tpu_custom_call" | custom-call | tf_op jit(solution)/shard_map/attend/pallas_call | solution.py:1906
  236.9 1.0 copy-done
  238.3 181.2 %expert.1 = (f32[128,2048]{1,0:T(8,128)}, bf16[4,4,128,2048]{3,2,1,0:T(8,128)(2,1)}, bf16[4,4,128,2048]{3,2,1,0:T(8,128)(2,1)}, bf16[6,256,2048]{2,1,0:T(8,128)(...) custom-call(bf16[128,2048]{1,0:T(8,128)(2,1)} %copy-done.9, ...), custom_call_target="tpu_custom_call" | custom-call | tf_op jit(solution)/shard_map/expert/pallas_call | solution.py:1536
  419.5 2.4 multiply_reduce_fusion
  421.9 3.0 fusion.13
  424.9 98.2 %attend_back.1 = (bf16[16,128,384]{2,1,0:T(8,128)(2,1)}, f32[8,128]{1,0:T(8,128)}, f32[128,2048]{1,0:T(8,128)}) custom-call(bf16[128,2048]{1,0:T(8,128)(2,1)} %get-tuple-element.73.d_res, bf16[4,4,2,64,2048]{4,3,2,1,0:T(8,128)(2,1)} %get-tuple-element.50.wo_h, bf16[4,4,128,2048]{3,2,1,0:T(8,128)(2,1)} %get-tuple-element.51.p_out, f32[128,2048]{1,0:T(8,128)} %copy-done, ...), custom_call_target="tpu_custom_call" | custom-call | tf_op jit(solution)/shard_map/attend_back/pallas_call | solution.py:2047
  523.8 142.2 %finish.1 = (f32[64,2048]{1,0:T(8,128)}, f32[128,2048]{1,0:T(8,128)}, f32[64,2048]{1,0:T(8,128)}, f32[64,2048]{1,0:T(8,128)}, f32[64,2048]{1,0:T(8,128)}, /*index=5*/f32[8,128]{1,0:T(8,128)}) custom-call(bf16[16,128,384]{2,1,0:T(8,128)(2,1)} %get-tuple-element.57.d_lin, bf16[16,2,64,384]{3,2,1,0:T(8,128)(2,1)} %copy-done.5, ...), custom_call_target="tpu_custom_call" | custom-call | tf_op jit(solution)/shard_map/finish/pallas_call | solution.py:1741
  669.9 2.4 copy.52
  672.3 2.3 copy.53
  677.8 2.1 copy.58
  680.0 1.6 copy-done.20
  681.5 2.1 copy.59
  683.7 1.6 copy-done.19
  685.2 2.0 copy.60
  (91 shorter events, 19.7 us)
Async XLA Ops:
  0.6 142.4 %copy-start.27 = (s32[4096]{0:T(1024)S(1)}, s32[4096]{0:T(1024)}, u32[]{:S(2)}) copy-start(s32[4096]{0:T(1024)} %param.19) | copy-start | bytes 49156
  5.0 1.0 copy-start.2
  6.0 0.9 copy-start.11
  7.0 0.9 copy-start.12
  135.1 1.7 copy-start.1
  136.7 2.0 copy-start.4
  138.7 1.1 copy-start.5
  139.9 10.8 %copy-start.16 = (f32[32,128]{1,0:T(8,128)}, f32[32,128]{1,0:T(8,128)S(1)}, u32[]{:S(2)}) copy-start(f32[32,128]{1,0:T(8,128)S(1)} %get-tuple-element.43.tot) | copy-start | bytes 49156
  143.0 7.7 %copy-start.15 = (s32[5120]{0:T(1024)}, s32[5120]{0:T(1024)S(1)}, u32[]{:S(2)}) copy-start(s32[5120]{0:T(1024)S(1)} %concatenate.25) | copy-start | bytes 61444
  145.0 5.7 copy-start.3
  145.0 5.7 copy-start.14
  148.8 85.0 %copy-start.17 = (f32[1,128]{1,0:T(1,128)}, f32[1,128]{1,0:T(1,128)S(1)}, u32[]{:S(2)}) copy-start(f32[1,128]{1,0:T(1,128)S(1)} %get-tuple-element.94.gq) | copy-start | bytes 1540
  148.8 85.0 %copy-start.18 = (f32[1,128]{1,0:T(1,128)}, f32[1,128]{1,0:T(1,128)S(1)}, u32[]{:S(2)}) copy-start(f32[1,128]{1,0:T(1,128)S(1)} %get-tuple-element.95.gk) | copy-start | bytes 1540
  236.9 1.0 copy-start
  236.9 1.3 copy-start.6
  238.2 183.7 %copy-start.22 = (bf16[128,2048]{1,0:T(8,128)(2,1)S(1)}, bf16[128,2048]{1,0:T(8,128)(2,1)}, u32[]{:S(2)}) copy-start(bf16[128,2048]{1,0:T(8,128)(2,1)} %param.18) | copy-start | bytes 1572868
  523.8 144.2 %collective-permute-start = (f32[2,128]{1,0:T(2,128)S(1)}, f32[2,128]{1,0:T(2,128)S(1)}, u32[]{:S(2)}, u32[]{:S(2)}) collective-permute-start(f32[2,128]{1,0:T(2,128)S(1)} %slice.49), channel_id=1, source_target_pairs={{0,1},{1,0},{2,3},{3,2},{4,5},{5,4},{6,7},{7,6},{8,9},{9,8},{10,11... | collective-permute-start | bytes 3080 | tf_op jit(solution)/shard_map/ppermute | solution.py:2060
  666.0 8.6 %copy-start.26 = (f32[64,2048]{1,0:T(8,128)S(1)}, f32[64,2048]{1,0:T(8,128)}, u32[]{:S(2)}) copy-start(f32[64,2048]{1,0:T(8,128)} %get-tuple-element.112) | copy-start | bytes 1572868
  666.0 9.4 %copy-start.25 = (f32[64,2048]{1,0:T(8,128)S(1)}, f32[64,2048]{1,0:T(8,128)}, u32[]{:S(2)}) copy-start(f32[64,2048]{1,0:T(8,128)} %get-tuple-element.113) | copy-start | bytes 1572868
  666.0 10.2 %copy-start.24 = (f32[64,2048]{1,0:T(8,128)S(1)}, f32[64,2048]{1,0:T(8,128)}, u32[]{:S(2)}) copy-start(f32[64,2048]{1,0:T(8,128)} %get-tuple-element.114) | copy-start | bytes 1572868
  666.0 11.0 %copy-start.23 = (f32[64,2048]{1,0:T(8,128)S(1)}, f32[64,2048]{1,0:T(8,128)}, u32[]{:S(2)}) copy-start(f32[64,2048]{1,0:T(8,128)} %get-tuple-element.115) | copy-start | bytes 1572868
  669.9 7.9 %copy-start.21 = (f32[1024,1024]{1,0:T(8,128)S(1)}, f32[1024,1024]{1,0:T(8,128)}, u32[]{:S(2)}) copy-start(f32[1024,1024]{1,0:T(8,128)} %get-tuple-element.119) | copy-start | bytes 12582916
  677.8 3.7 copy-start.20
  681.5 3.7 copy-start.19
  (5 other events, 4.1 us)

commit v6 on v5

--- a/solution.py
+++ b/solution.py
@@ -1034,6 +1034,17 @@
     pltpu.make_async_copy(ref, ref, sem).wait()
 
 
+def segment_rows(segments, k_seg, reach):
+    k_seg[:, 0:reach] = jnp.full((1, reach), -1.0, F32)
+    k_seg[:, reach:] = segments[...]
+
+
+def rope_at(near, far, i):
+    cf, sf = far[0, pl.ds(i, 1), :], far[1, pl.ds(i, 1), :]
+    cn, sn = near[0], near[1]
+    return cf * cn - sf * sn, sf * cn + cf * sn
+
+
 def row_sums(v):
     return jnp.sum(v.T, axis=0, keepdims=True)
 
@@ -1070,7 +1081,7 @@
     pl.semaphore_wait(bar, count - 1)
 
 
-def qkv_kernel(cut, x_ref, wq, wk, wv, block, cot, n1_o, lin, wf, tot, sw, C, X, nb, gain, sums, sums_all, lsem, nsem, msem, ssem, csem, *gs):
+def qkv_kernel(cut, x_ref, wq, wk, wv, block, cot, n1_o, lin_o, wf_o, tot, sw, C, X, lin, wf, nb, gain, sums, sums_all, lsem, nsem, msem, ssem, csem, *gs):
     net = Net(ssem)
     u, z, c = net.u, net.z, net.c
     me = u * 4 + z
@@ -1165,6 +1176,8 @@
         gain[:, e * 128 : (e + 1) * 128] = sw[2 * e, 2:3, :] + sw[2 * e + 1, 2:3, :]
     ga.settle(0)
     landed(wf.at[:, 1 - c], msem.at[3])
+    keep_w = pltpu.make_async_copy(wf, wf_o, lsem.at[0])
+    keep_w.start()
     compute(0)
     gc.begin2()
     ga.along(3)
@@ -1187,6 +1200,8 @@
     gc.quads(2)
     gc.cross(2)
     compute(3)
+    keep = pltpu.make_async_copy(lin, lin_o, lsem.at[1])
+    keep.start()
     landed(wf.at[pl.ds(0, 15), 0], msem.at[0])
     landed(wf.at[:, c], msem.at[2])
     share_sums(net, sums, sums_all, tot, lsem.at[2], msem.at[4], msem.at[5])
@@ -1195,6 +1210,8 @@
     for s in range(4):
         gc.settle(s)
     landed(sw.at[pl.ds(0, 31)], msem.at[6])
+    keep_w.wait()
+    keep.wait()
     net.finish()
     netc.finish()
 
@@ -1213,10 +1230,10 @@
         out_shape=(S((16, R, D), BF), S((16, R, N), F32), S((16, 2, R // 2, N), BF), S((32, 128), F32),
                    S((32, 8, 128), F32), S((4, 4) + cot.shape, BF)),
         in_specs=[A, A, A, A, M, A],
-        out_specs=(A, M, M, M, M, A),
-        scratch_shapes=[V(4, 4, R, D), V(2, R, D), VF(1, D), VF(32, 128), VF(16, 32, 128),
+        out_specs=(A, A, A, M, M, A),
+        scratch_shapes=[V(4, 4, R, D), VF(16, R, N), V(16, 2, R // 2, N), V(2, R, D), VF(1, D), VF(32, 128), VF(16, 32, 128),
                         DMA((4,)), DMA((2,)), DMA((8,)), DMA((64,)), DMA((64,))] + ag_sems() + ag_sems(),
-        compiler_params=pltpu.CompilerParams(collective_id=cid, has_side_effects=True, vmem_limit_bytes=40 * 2**20),
+        compiler_params=pltpu.CompilerParams(collective_id=cid, has_side_effects=True, vmem_limit_bytes=63 * 2**20),
         name="project",
     )(x, wq, wk, wv, block, cot)
 
@@ -1226,8 +1243,8 @@
     return jnp.where(g == 0, 3, jnp.where(g == 1, 0, jnp.where(g == 2, 2, 1)))
 
 
-def expert_kernel(cut, n2, cot_a, cot_b, share, gate, up, down, d_n2, p_out, n2_o, other, dg_o, du_o, dd_o,
-                  X, C, GU, W, A, hid, pb, fs, lsem, wsem, wrs, psem, tsem, osem, ors, fsem, sa, sr, *scr):
+def expert_kernel(cut, n2, cot_a, cot_b, share_rows, gate, up, down, d_n2, p_out, n2_o, other, dg_o, du_o, dd_o,
+                  X, C, GU, W, A, hid, pb, fs, share, lsem, wsem, wrs, psem, tsem, osem, ors, fsem, sa, sr, *scr):
     ga_sems, rs_bufs = scr[:7], scr[7:]
     na, nr = Net(sa), Net(sr)
     u, z, c = na.u, na.z, na.c
@@ -1251,6 +1268,8 @@
     own_w = [pltpu.make_async_copy(a, b, lsem.at[2 + i]) for i, (a, b) in enumerate(weights())]
     for one in first + own_w:
         one.start()
+    for k in range(16):
+        share[k // 4, k % 4] = column(share_rows[k : k + 1, :])[:, 0:1]
     na.barrier((partner,))
     first[0].wait()
 
@@ -1266,6 +1285,13 @@
 
     def forward(zz):
         pltpu.make_async_copy(X.at[:, zz], n2_o.at[:, zz], psem.at[1]).start()
+
+        def scale(i, _):
+            sl = pl.ds(pl.multiple_of(i * 16, 16), 16)
+            C[:, zz, sl, :] = (share[:, zz, sl, :] * C[:, zz, sl, :].astype(F32)).astype(BF)
+            return 0
+
+        lax.fori_loop(0, rows // 16, scale, 0)
 
         def inner(n, _):
             gcols = pl.ds(pl.multiple_of(n * span, span), span)
@@ -1273,9 +1299,12 @@
             xv = X[:, zz].reshape(4 * rows, width)
             g = dot(xv, GU[:, gcols], ((1,), (0,)))
             uu = dot(xv, GU[:, ucols], ((1,), (0,)))
-            hid[:, zz, :, gcols] = (g * jax.nn.sigmoid(g) * uu).astype(BF).reshape(4, rows, span)
-            A[:, zz, :, gcols] = g.astype(BF).reshape(4, rows, span)
-            A[:, zz, :, ucols] = uu.astype(BF).reshape(4, rows, span)
+            s = jax.nn.sigmoid(g)
+            gs = g * s
+            hid[:, zz, :, gcols] = (gs * uu).astype(BF).reshape(4, rows, span)
+            dh = dot(C[:, zz].reshape(4 * rows, width), W[gcols, :], ((1,), (1,)))
+            A[:, zz, :, gcols] = (dh * uu * s * (1.0 + g * (1.0 - s))).astype(BF).reshape(4, rows, span)
+            A[:, zz, :, ucols] = (dh * gs).astype(BF).reshape(4, rows, span)
             return 0
 
         lax.fori_loop(0, ff // span, inner, 0)
@@ -1324,6 +1353,8 @@
         one.wait()
     for one in sent_w:
         one.wait_recv()
+    first[1].wait()
+    first[2].wait()
     planes(0)
     ga.along(3)
     ga.quads(2)
@@ -1337,8 +1368,6 @@
     ga.settle(3)
     planes(3)
     na.finish()
-    first[1].wait()
-    first[2].wait()
     for one in sent_w:
         one.wait_send()
     landed(X, psem.at[1])
@@ -1346,37 +1375,15 @@
 
     def backward(t):
         zd = group_of(t)
-
-        def inner(n, _):
-            gcols = pl.ds(pl.multiple_of(n * span, span), span)
-            ucols = pl.ds(pl.multiple_of(ff + n * span, span), span)
-            dh = dot(C[:, zd].reshape(4 * rows, width), W[gcols, :], ((1,), (1,)))
-            g = wide(A[:, zd, :, gcols]).reshape(4 * rows, span)
-            uu = wide(A[:, zd, :, ucols]).reshape(4 * rows, span)
-            s = jax.nn.sigmoid(g)
-            A[:, zd, :, gcols] = (dh * uu * s * (1.0 + g * (1.0 - s))).astype(BF).reshape(4, rows, span)
-            A[:, zd, :, ucols] = (dh * g * s).astype(BF).reshape(4, rows, span)
-            return 0
+        base = lax.rem(t, 2) * (width // 2)
 
         def outer(n, _):
-            cols = pl.ds(pl.multiple_of(n * span, span), span)
+            cols = pl.ds(pl.multiple_of(base + n * span, span), span)
             back = dot(A[:, zd].reshape(4 * rows, 2 * ff), GU[cols, :], ((1,), (1,)))
             X[:, zd, :, cols] = back.astype(BF).reshape(4, rows, span)
             return 0
 
-        def scale(i, _):
-            sl = pl.ds(pl.multiple_of(i * 16, 16), 16)
-            C[:, zd, sl, :] = (share[:, zd, sl, :] * C[:, zd, sl, :].astype(F32)).astype(BF)
-            return 0
-
-        @pl.when(lax.rem(t, 2) == 0)
-        def _():
-            lax.fori_loop(0, rows // 16, scale, 0)
-            lax.fori_loop(0, ff // span, inner, 0)
-
-        @pl.when(lax.rem(t, 2) == 1)
-        def _():
-            lax.fori_loop(0, width // span, outer, 0)
+        lax.fori_loop(0, width // 2 // span, outer, 0)
 
     def acts(steps, t):
         for at, todo in steps.items():
@@ -1388,7 +1395,7 @@
     def at_turns(table):
         return {t: steps_of(sc, words) for t, words in table.items()}
 
-    steps = at_turns({1: "m3 f3 d3", 3: "m0 f0 d0 M3", 4: "b31", 5: "m2 f2 d2 M0", 6: "h30 b02 b32", 7: "m1 f1 d1 M2 h03"})
+    steps = at_turns({1: "m3 f3 d3", 3: "m0 f0 d0", 5: "m2 f2 d2 M3", 6: "b31", 7: "m1 f1 d1 M0 b02"})
 
     def turn(t, _):
         backward(t)
@@ -1466,7 +1473,7 @@
             products(C, store)
 
         copy.start()
-        acts(at_turns({0: "h31 b01 b21", 1: "M1 h02", 2: "h20", 3: "h23 b12 h32", 4: "h01", 5: "h10"}), k)
+        acts(at_turns({0: "M2", 1: "h30 b32 b21", 2: "M1 h03 b01", 3: "h31 b12", 4: "h02 h20", 5: "h32 h23"}), k)
         return 0
 
     lax.fori_loop(0, 6, other_tile, 0)
@@ -1513,7 +1520,7 @@
             left_hidden(k - 4, c)
             finish(C)
 
-        acts(at_turns({0: "h21", 1: "h13 Q", 3: "h12", 4: "q"}), k)
+        acts(at_turns({0: "h01 h10", 1: "Q h21", 2: "h13", 4: "h12", 5: "q"}), k)
         return 0
 
     lax.fori_loop(0, 6, own_tile, 0)
@@ -1540,7 +1547,7 @@
         in_specs=[A, A, A, M, A, A, A],
         out_specs=(M,) + (A,) * 6,
         scratch_shapes=[V(4, 4, R, D), V(4, 4, R, D), V(D, 2 * ff), V(ff, D), V(4, 4, R, 2 * ff), V(4, 4, R, ff),
-                        V(2, 4, R, 512), pltpu.VMEM((2, 256, 1024), F32),
+                        V(2, 4, R, 512), pltpu.VMEM((2, 256, 1024), F32), pltpu.VMEM((4, 4, R, 1), F32),
                         DMA((6,)), DMA((3,)), DMA((3,)), DMA((2,)), DMA((2,)), DMA((6,)), DMA((6,)), DMA((2,)),
                         DMA((64,)), DMA((96,))] + ag_sems() + rs_scratch(cut, R, D),
         compiler_params=pltpu.CompilerParams(collective_id=cid, has_side_effects=True, vmem_limit_bytes=63 * 2**20),
@@ -1548,7 +1555,7 @@
     )(n2, cot_a, cot_b, share, gate, up, down)
 
 
-def finish_kernel(cut, d_lin, wf, n1, att, x_in, d_res, gain, d_gain_two,
+def finish_kernel(cut, d_lin, wf, n1, att, x_in, d_res, gain, d_gain_two, d_gains,
                   d_wo, d_inputs, d_wq, d_wk, d_wv, gains_o,
                   P, PO, PG, PT, wsum, nt, left, keep, give, got, send, recv, d_n1, d_gain, gb, gr,
                   lsem, tsem, msem, s1, s2, *bufs):
@@ -1570,6 +1577,12 @@
     tile_load(0).start()
     greet_all(net)
 
+    def one(words):
+        run_steps(steps_of(sc1, words))
+
+    def two(words):
+        run_steps(steps_of(sc2, words))
+
     def group(zd):
         def one(n, _):
             cols = pl.ds(pl.multiple_of(n * 512, 512), 512)
@@ -1582,7 +1595,7 @@
 
     for zd in (3, 0, 2, 1):
         group(zd)
-        sc1.first(zd)
+        one(f"m{zd}" + (f" f{zd}" if zd in (3, 0) else ""))
 
     side = width // 2
     own_cols = pl.ds(pl.multiple_of(c * side, side), side)
@@ -1617,11 +1630,6 @@
     def store2(sl, v):
         wsum[sl, :] = v
 
-    def one(words):
-        run_steps(steps_of(sc1, words))
-
-    def two(words):
-        run_steps(steps_of(sc2, words))
 
     def grads(k):
         if k < 7:
@@ -1642,25 +1650,25 @@
             keep[2 * k + i] = jnp.where(c == 0, first, second)
             give[2 * k + i] = jnp.where(c == 0, second, first).astype(BF)
 
+    one("d3 d0")
     grads(0)
     grads(1)
-    one("M3")
+    one("f2 f1 d2 d1")
+    join()
+    two("m3 m0 m2 m1 f3 f0")
     grads(2)
-    one("M0")
-    join()
-    two("m3 f3 m0 f0 m2 f2 m1 f1 d3 d0 d2 d1")
     grads(3)
-    one("M2 b31 b02")
+    one("M3 M0 M2 M1")
+    two("d3 d0 d2 d1 f2 f1")
     grads(4)
-    one("M1")
     grads(5)
-    one("h30 h03")
+    one("b31 b02")
     grads(6)
     grads(7)
     across = remote(give, got, msem.at[0], msem.at[1], partner)
     across.start()
-    one("b21 b12 b32 b01")
     two("M3 M0 M2 M1")
+    one("b21 b12 b32 b01 h30 h03")
     landed(got, msem.at[1])
 
     def total(e, _):
@@ -1670,12 +1678,11 @@
     lax.fori_loop(0, 16, total, 0)
     each_chip(net, lambda t, dev: remote(send.at[t], recv.at[me], msem.at[2], msem.at[3], dev).start())
     recv[me] = send[me]
-    one("h20 h13 h31 h02")
-    two("b31 b02 b21 b12")
-    one("Q h10 h23")
-    two("h30 h03 b32 b01")
-    one("h32 h01")
-    two("h20 h13 h31 h02")
+    two("b31 b02 b21 b12 b32 b01")
+    one("h31 h02 h20 h13 Q")
+    two("h30 h03 h20 h13 Q")
+    one("h32 h01 h10 h23")
+    two("h31 h02 h10 h23")
     one("h21 h12 q")
     sc1.last(store1)
     d_gain[...] = jnp.zeros_like(d_gain)
@@ -1691,6 +1698,8 @@
         return 0
 
     lax.fori_loop(0, rows // 16, norm_back, 0)
+    gb[...] = jnp.zeros_like(gb)
+    gb[me, 2:4, :] = d_gains[0:2, :]
     for e in range(16):
         gb[e, 0:1, :] = d_gain[:, e * 128 : (e + 1) * 128]
         gb[e, 1:2, :] = d_gain_two[:, e * 128 : (e + 1) * 128]
@@ -1703,7 +1712,7 @@
 
     lax.fori_loop(1, 32, tell, 0)
     gr[dev_me] = gb[me]
-    two("Q h10 h23 h32 h01 h21 h12 q")
+    two("h32 h01 h21 h12 q")
     landed(recv.at[pl.ds(0, 15)], msem.at[3])
     for e in range(16):
         piece = wide(recv[e])
@@ -1713,7 +1722,7 @@
     sums = gr[0]
     for i in range(1, 32):
         sums = sums + gr[i]
-    gains_o[...] = sums
+    gains_o[...] = jnp.where(c == 0, sums[:, :64], sums[:, 64:])
     sc2.last(store2)
     d_wo[:, own_cols] = wsum[pl.ds(pl.multiple_of(c * 64, 64), 64), :]
     theirs = remote(wsum.at[pl.ds(pl.multiple_of((1 - c) * 64, 64), 64), :], d_wo.at[:, own_cols], msem.at[8], msem.at[9], partner)
@@ -1728,7 +1737,7 @@
     net2.finish()
 
 
-def run_finish(d_lin, wf, n1, att, x_in, d_res, gain, d_gain_two, cid, cut=96):
+def run_finish(d_lin, wf, n1, att, x_in, d_res, gain, d_gain_two, d_gains, cid, cut=96):
     R, D = x_in.shape
     N = d_lin.shape[2]
     DMA = pltpu.SemaphoreType.DMA
@@ -1740,15 +1749,15 @@
     own = S((R // 2, D), F32)
     return pl.pallas_call(
         functools.partial(finish_kernel, cut),
-        out_shape=(own, S((R, D), F32), own, own, own, S((8, 128), F32)),
-        in_specs=[M, M, A] + [M] * 5,
+        out_shape=(own, S((R, D), F32), own, own, own, S((8, 64), F32)),
+        in_specs=[M, M, A] + [M] * 6,
         out_specs=(M,) * 6,
         scratch_shapes=[V(4, 4, R, D), V(4, 4, R, D // 2), V(4, 4, R, D // 2), V(4, 4, R, D // 2), VF(R, D // 2), V(2, 16, R, 256), V(256, 16 * R), VF(16, 64, N), V(16, 64, N),
                         V(16, 64, N), V(16, 64, N), V(16, 64, N), VF(R, D), VF(1, D), VF(16, 8, 128), VF(32, 8, 128),
                         DMA((1,)), DMA((2,)), DMA((10,)), DMA((64,)), DMA((64,))] + rs_scratch(cut, R, D) + rs_scratch(cut, R, D // 2),
         compiler_params=pltpu.CompilerParams(collective_id=cid, has_side_effects=True, vmem_limit_bytes=63 * 2**20),
         name="finish",
-    )(d_lin, wf, n1, att, x_in, d_res, gain, d_gain_two)
+    )(d_lin, wf, n1, att, x_in, d_res, gain, d_gain_two, d_gains)
 
 def band_scores(q, k, q_seg, k_seg, scale, reach):
     scores = dot(q, k, ((1,), (1,))) * scale
@@ -1765,8 +1774,9 @@
     return v * cosine - pltpu.roll(v, 64, axis=1) * sine
 
 
-def attend_kernel(scale, pads, cut, lin, tot, cosine, sine, gq, gk, q_seg, k_seg, w_own, x_in, gain, cot, wo_o, q_rot, kv, o_ref, lse,
-                  att, residual, n2, C, wo, lsem, msem, psem, ssem, csem, *gs):
+def attend_kernel(scale, pads, cut, lin_h, tot, near, far, gq, gk, q_seg, segments, w_own, x_in, gain, cot,
+                  wo_o, q_rot_o, kv_o, o_o, lse, att_o, residual_o, n2, C,
+                  lin, k_seg, q_rot, kv, o_ref, att, residual, wo, lsem, msem, psem, ksem, ssem, csem, *gs):
     net = Net(ssem)
     u, z, c = net.u, net.z, net.c
     me = u * 4 + z
@@ -1776,6 +1786,8 @@
     partner = (u, z, 1 - c)
     own = pltpu.make_async_copy(w_own, wo.at[u, z, c], lsem.at[0])
     own.start()
+    load = pltpu.make_async_copy(lin_h, lin, ksem.at[0])
+    load.start()
     own_c = pltpu.make_async_copy(cot, C.at[u, z], lsem.at[2])
     own_c.start()
     greet(net)
@@ -1792,6 +1804,8 @@
             net.go(cond, ref, ref, lambda zz=zz: psem.at[zz], partner)
 
     ga.begin()
+    segment_rows(segments, k_seg, reach)
+    load.wait()
     for i in range(pads):
         kv[:, i] = jnp.zeros(kv.shape[:1] + kv.shape[2:], BF)
 
@@ -1799,7 +1813,7 @@
         both = lin[i]
         rq = lax.rsqrt(column(tot[pl.ds(i, 1), :]) / width + EPS)
         rk = lax.rsqrt(column(tot[pl.ds(16 + i, 1), :]) / width + EPS)
-        cs, sn = cosine[i], sine[i]
+        cs, sn = rope_at(near, far, i)
         q_rot[i] = turned(both[:, :128] * rq * gq[...], cs, sn).astype(BF)
         kv[0, pads + i, c] = turned(both[:, 128:256] * rk * gk[...], cs, sn).astype(BF)
         kv[1, pads + i, c] = both[:, 256:].astype(BF)
@@ -1820,7 +1834,7 @@
         first = 2 * i + c
         band = pl.ds(pl.multiple_of(first * rows, rows), rows + reach)
         kf, vf = kv.at[0].reshape((pads + 16) * 2 * rows, 128), kv.at[1].reshape((pads + 16) * 2 * rows, 128)
-        scores, allowed = band_scores(q_rot[i], kf[band, :], q_seg[i], k_seg[:, band], scale, reach)
+        scores, allowed = band_scores(q_rot[i], kf[band, :], column(q_seg[pl.ds(i, 1), :])[:, 0:1], k_seg[:, band], scale, reach)
         scores = jnp.where(allowed, scores, NEG)
         top = jnp.max(scores, axis=1, keepdims=True)
         weights = jnp.where(allowed, jnp.exp(scores - top), 0.0)
@@ -1859,8 +1873,10 @@
     landed(part, msem.at[3])
     for zz in range(4):
         landed(wo.at[:, zz, 1 - c], psem.at[zz])
-    keep = pltpu.make_async_copy(wo, wo_o, lsem.at[1])
-    keep.start()
+    keep = [pltpu.make_async_copy(a, o, ksem.at[j]) for j, (a, o) in enumerate(
+        ((wo, wo_o), (q_rot, q_rot_o), (kv, kv_o), (o_ref, o_o), (att, att_o)))]
+    for one in keep:
+        one.start()
     tile = 256
 
     def out(n, _):
@@ -1873,6 +1889,8 @@
         return 0
 
     lax.fori_loop(0, width // tile, out, 0)
+    keep.append(pltpu.make_async_copy(residual, residual_o, ksem.at[5]))
+    keep[5].start()
     gc.along(3)
     gc.quads(2)
     gc.cross(2)
@@ -1891,38 +1909,42 @@
     gc.cross(3)
     for s in range(4):
         gc.settle(s)
-    keep.wait()
+    for one in keep:
+        one.wait()
     net.finish()
     netc.finish()
 
 
-def run_attend(scale, pads, lin, tot, cosine, sine, gq, gk, q_seg, k_seg, w_own, x_in, gain, cot, cid, cut=96):
+def run_attend(scale, pads, lin, tot, near, far, gq, gk, q_seg, segments, w_own, x_in, gain, cot, cid, cut=96):
     R, D = x_in.shape
     DMA = pltpu.SemaphoreType.DMA
     S = jax.ShapeDtypeStruct
     A = pl.BlockSpec(memory_space=pl.ANY)
     M = pl.BlockSpec(memory_space=pltpu.VMEM)
+    V = pltpu.VMEM
     wo = (4, 4, 2, R // 2, D)
     return pl.pallas_call(
         functools.partial(attend_kernel, scale, pads, cut),
         out_shape=(S(wo, BF), S((16, R, 128), BF), S((2, pads + 16, 2, R, 128), BF), S((16, R, 128), BF),
                    S((16, R, 1), F32), S((16, R, 128), BF), S((R, D), F32), S((R, D), BF), S((4, 4) + cot.shape, BF)),
-        in_specs=[M] * 8 + [A, M, M, A],
-        out_specs=(A,) + (M,) * 7 + (A,),
-        scratch_shapes=[pltpu.VMEM(wo, BF), DMA((3,)), DMA((4,)), DMA((4,)), DMA((64,)), DMA((64,))] + ag_sems() + ag_sems(),
-        compiler_params=pltpu.CompilerParams(collective_id=cid, has_side_effects=True, vmem_limit_bytes=48 * 2**20),
+        in_specs=[A] + [M] * 7 + [A, M, M, A],
+        out_specs=(A, A, A, A, M, A, A, M, A),
+        scratch_shapes=[V((16, R, 384), F32), V((1, (pads + 16) * 2 * R), F32), V((16, R, 128), BF),
+                        V((2, pads + 16, 2, R, 128), BF), V((16, R, 128), BF), V((16, R, 128), BF), V((R, D), F32),
+                        V(wo, BF), DMA((3,)), DMA((4,)), DMA((4,)), DMA((6,)), DMA((64,)), DMA((64,))] + ag_sems() + ag_sems(),
+        compiler_params=pltpu.CompilerParams(collective_id=cid, has_side_effects=True, vmem_limit_bytes=63 * 2**20),
         name="attend",
-    )(lin, tot, cosine, sine, gq, gk, q_seg, k_seg, w_own, x_in, gain, cot)
-
-
-def attend_back_kernel(scale, pads, cut, d_res, wo_h, p_out, residual, q_rot, kv, q_seg, k_seg, lse, o_ref, lin, tot, cosine, sine, gq, gk,
-                       d_lin, d_gains, output, P, wo, d_mine, d_out, d_q, d_k, d_v, other, got, d_un, sums, sums_all, inner,
+    )(lin, tot, near, far, gq, gk, q_seg, segments, w_own, x_in, gain, cot)
+
+
+def attend_back_kernel(scale, pads, cut, d_n2, cot, gain, wo_h, p_out, residual, q_rot, kv, q_seg, segments, lse, o_ref, lin, tot, near, far, gq, gk,
+                       d_lin, d_gains, output, d_residual, d_gain, d_res, k_seg, P, wo, d_mine, d_out, d_q, d_k, d_v, other, got, d_un, sums, sums_all, inner,
                        lsem, msem, ssem, *bufs):
     net = Net(ssem)
     sc = Scatter(net, cut, P, bufs)
     u, z, c = net.u, net.z, net.c
     me = u * 4 + z
-    rows, width = d_res.shape
+    rows, width = d_n2.shape
     reach = pads * 2 * rows
     partner = (u, z, 1 - c)
     load = pltpu.make_async_copy(wo_h, wo, lsem.at[0])
@@ -1934,26 +1956,41 @@
     def go(words):
         run_steps(steps_of(sc, words))
 
+    load_p.wait()
+    go("m3 m0 m2 m1")
+    d_gain[...] = jnp.zeros_like(d_gain)
+
+    def norm_back(i, _):
+        sl = pl.ds(pl.multiple_of(i * 16, 16), 16)
+        v, d = residual[sl, :], d_n2[sl, :]
+        r = lax.rsqrt(jnp.mean(v * v, axis=1, keepdims=True) + EPS)
+        scaled = d * gain[...]
+        mean = jnp.mean(scaled * v, axis=1, keepdims=True)
+        total = wide(cot[sl, :]) + r * scaled - v * (r * r * r * mean)
+        d_residual[sl, :] = total
+        d_res[sl, :] = total.astype(BF)
+        d_gain[...] += jnp.sum(d * v * r, axis=0, keepdims=True)
+        return 0
+
+    lax.fori_loop(0, rows // 16, norm_back, 0)
+    segment_rows(segments, k_seg, reach)
     load.wait()
 
     def send(j, _):
-        e = lax.rem(me + 1 + j, 16)
-        piece = dot(d_res[...], wo[e // 4, lax.rem(e, 4)].reshape(128, width), ((1,), (1,))).astype(BF)
-
-        @pl.when(j < 15)
-        def _():
-            d_mine[e] = piece
-            remote(d_mine.at[e], d_out.at[me], msem.at[0], msem.at[1], (e // 4, lax.rem(e, 4), c)).start()
-
-        @pl.when(j == 15)
-        def _():
-            d_out[me] = piece
+        pair = lax.rem(me // 2 + 1 + j, 8)
+        both = dot(d_res[...], wo[pair // 2, pl.ds(lax.rem(pair, 2) * 2, 2)].reshape(256, width), ((1,), (1,))).astype(BF)
+        for i in (0, 1):
+            e = pair * 2 + i
+            d_mine[e] = both[:, i * 128 : (i + 1) * 128]
+
+            @pl.when(e != me)
+            def _():
+                remote(d_mine.at[e], d_out.at[me], msem.at[0], msem.at[1], (e // 4, lax.rem(e, 4), c)).start()
 
         return 0
 
-    lax.fori_loop(0, 16, send, 0)
-    load_p.wait()
-    go("m3 f3 m0 f0 m2 f2 m1 f1")
+    lax.fori_loop(0, 8, send, 0)
+    d_out[me] = d_mine[me]
     d_k[...] = jnp.zeros_like(d_k)
     d_v[...] = jnp.zeros_like(d_v)
     landed(d_out.at[pl.ds(0, 15)], msem.at[1])
@@ -1963,7 +2000,7 @@
         band = pl.ds(pl.multiple_of((2 * i + c) * rows, rows), rows + reach)
         kf, vf = kv.at[0].reshape(count, 128), kv.at[1].reshape(count, 128)
         q, k, dd = q_rot[i], kf[band, :], d_out[i]
-        scores, allowed = band_scores(q, k, q_seg[i], k_seg[:, band], scale, reach)
+        scores, allowed = band_scores(q, k, column(q_seg[pl.ds(i, 1), :])[:, 0:1], k_seg[:, band], scale, reach)
         probs = jnp.where(allowed, jnp.exp(scores - lse[i]), 0.0)
         d_probs = dot(dd, vf[band, :], ((1,), (1,)))
         delta = jnp.sum(dd.astype(F32) * o_ref[i].astype(F32), axis=1, keepdims=True)
@@ -1976,9 +2013,9 @@
     def store(sl, v):
         output[sl, :] = residual[sl, :] + v
 
-    go("d3 d0 d2 d1")
+    go("f3 f0 d3 d0")
     done = 0
-    for upto, words in ((3, "M3 M0"), (6, "b31 b02 M2 M1"), (9, "b21 b12 h30 h03"), (12, "b32 b01"), (14, "h31 h02"), (16, "h20 h13")):
+    for upto, words in ((3, "M3 M0 M2 M1 d2 d1"), (6, "f2 f1"), (11, "b31 b02"), (16, "")):
         lax.fori_loop(done, upto, block, 0)
         go(words)
         done = upto
@@ -1991,13 +2028,13 @@
 
     lax.fori_loop(0, 16, pack, 0)
     remote(other, got, msem.at[2], msem.at[3], partner).start()
-    go("h32 h01")
+    go("h30 h03")
     landed(got, msem.at[3])
     d_gains[...] = jnp.zeros_like(d_gains)
 
     def undo(i, _):
         at = pl.ds(pl.multiple_of(((pads + i) * 2 + c) * rows, rows), rows)
-        cs, sn = cosine[i], sine[i]
+        cs, sn = rope_at(near, far, i)
         both = lin[i]
         rq = lax.rsqrt(column(tot[pl.ds(i, 1), :]) / width + EPS)
         rk = lax.rsqrt(column(tot[pl.ds(16 + i, 1), :]) / width + EPS)
@@ -2016,7 +2053,7 @@
         return 0
 
     lax.fori_loop(0, 16, undo, 0)
-    go("h10 h23 Q")
+    go("b21 b12 b32 b01")
     share_sums(net, sums, sums_all, inner, lsem.at[1], msem.at[4], msem.at[5])
 
     def finish(i, _):
@@ -2029,15 +2066,15 @@
         return 0
 
     lax.fori_loop(0, 16, finish, 0)
-    go("h21 h12 q")
+    go("h31 h02 h20 h13 Q h32 h01 h10 h23 h21 h12 q")
     sc.last(store)
     landed(d_out.at[pl.ds(0, 15)], msem.at[0])
     landed(other, msem.at[2])
     net.finish()
 
 
-def run_attend_back(scale, pads, d_res, wo, p_out, residual, q_rot, kv, q_seg, k_seg, lse, o, lin, tot, cosine, sine, gq, gk, cid, cut=96):
-    R, D = d_res.shape
+def run_attend_back(scale, pads, d_n2, cot, gain, wo, p_out, residual, q_rot, kv, q_seg, segments, lse, o, lin, tot, near, far, gq, gk, cid, cut=96):
+    R, D = d_n2.shape
     DMA = pltpu.SemaphoreType.DMA
     S = jax.ShapeDtypeStruct
     A = pl.BlockSpec(memory_space=pl.ANY)
@@ -2046,20 +2083,16 @@
     span = (pads + 16) * 2 * R
     return pl.pallas_call(
         functools.partial(attend_back_kernel, scale, pads, cut),
-        out_shape=(S((16, R, 384), BF), S((8, 128), F32), S((R, D), F32)),
-        in_specs=[M, A, A] + [M] * 13,
-        out_specs=(M, M, M),
-        scratch_shapes=[V((4, 4, R, D), BF), V(wo.shape, BF), V((16, R, 128), BF), V((16, R, 128), BF), V((16, R, 128), BF),
+        out_shape=(S((16, R, 384), BF), S((8, 128), F32), S((R, D), F32), S((R, D), F32), S((1, D), F32)),
+        in_specs=[M, M, M, A, A] + [M] * 13,
+        out_specs=(M,) * 5,
+        scratch_shapes=[V((R, D), BF), V((1, span), F32), V((4, 4, R, D), BF), V(wo.shape, BF), V((16, R, 128), BF), V((16, R, 128), BF), V((16, R, 128), BF),
                         V((span, 128), F32), V((span, 128), F32), V((2, 16, R, 128), BF), V((2, 16, R, 128), BF),
                         V((2, 16, R, 128), F32), V((32, 128), F32), V((16, 32, 128), F32), V((32, 128), F32),
                         DMA((2,)), DMA((10,)), DMA((64,))] + rs_scratch(cut, R, D),
-        compiler_params=pltpu.CompilerParams(collective_id=cid, has_side_effects=True, vmem_limit_bytes=62 * 2**20),
+        compiler_params=pltpu.CompilerParams(collective_id=cid, has_side_effects=True, vmem_limit_bytes=63 * 2**20),
         name="attend_back",
-    )(d_res, wo, p_out, residual, q_rot, kv, q_seg, k_seg, lse, o, lin, tot, cosine, sine, gq, gk)
-def core_pair(value):
-    return lax.ppermute(value, "core", [(0, 1), (1, 0)])
-
-
+    )(d_n2, cot, gain, wo, p_out, residual, q_rot, kv, q_seg, segments, lse, o, lin, tot, near, far, gq, gk)
 def dot(a, b, dims):
     return lax.dot_general(a, b, (dims, ((), ())), preferred_element_type=jnp.float32)
 
@@ -2101,56 +2134,44 @@
     before = jnp.cumsum(counts) - counts
     kept = taken & (before[:, None] + rank_all < float(capacity))
     share = jnp.where(kept, swapped[:, 0, :], 0.0).reshape(chips, 2, rows)
-    share = lax.dynamic_index_in_dim(share, core, 1, keepdims=False).reshape(chips * rows, 1)
-
-
-    positions = (jnp.arange(chips, dtype=jnp.int32)[:, None] * 2 + core) * rows + jnp.arange(rows, dtype=jnp.int32)
+    share = lax.dynamic_index_in_dim(share, core, 1, keepdims=False)
+
+
     half_dim = HEAD_DIM // 2
     inv_freq = jnp.exp(jnp.arange(half_dim, dtype=F32) * (-2.0 * math.log(ROPE_BASE) / HEAD_DIM))
-    angles = positions.reshape(-1).astype(F32)[:, None] * inv_freq[None, :]
-    cosine, sine = jnp.cos(angles), jnp.sin(angles)
-    cosine = jnp.concatenate([cosine, cosine], axis=1).reshape(chips, rows, HEAD_DIM)
-    sine = jnp.concatenate([-sine, sine], axis=1).reshape(chips, rows, HEAD_DIM)
+    inv_freq = jnp.concatenate([inv_freq, inv_freq])[None, :]
+    sign = jnp.where(jnp.arange(HEAD_DIM) < half_dim, -1.0, 1.0)[None, :]
+    within = jnp.arange(rows, dtype=F32)[:, None] * inv_freq
+    starts = ((jnp.arange(chips, dtype=jnp.int32) * 2 + core) * rows).astype(F32)[:, None] * inv_freq
+    near = jnp.stack([jnp.cos(within), sign * jnp.sin(within)])
+    far = jnp.stack([jnp.cos(starts), sign * jnp.sin(starts)])
     pads = chips // 4
-    k_seg = jnp.concatenate([jnp.full((pads * 2 * rows,), -1, jnp.int32), segments]).reshape(1, -1)
-    q_seg = lax.dynamic_index_in_dim(segments.reshape(chips, 2, rows, 1), core, 1, keepdims=False)
+    marks = segments.astype(F32)
+    q_seg = lax.dynamic_index_in_dim(marks.reshape(chips, 2, rows), core, 1, keepdims=False)
+    marks = marks.reshape(1, -1)
     scale = 1.0 / math.sqrt(HEAD_DIM)
     tokens = chips * rows
     w_o, q_rot, kv, head_out, log_total, attended, residual, normed_two, cot_b = run_attend(
-        scale, pads, lin, squares, cosine, sine, gq, gk, q_seg, k_seg, w_output, inputs, gain_two, cotangent[:, side:], 4)
-    r2 = lax.rsqrt(jnp.mean(residual * residual, axis=1, keepdims=True) + EPS)
+        scale, pads, lin, squares, near, far, gq, gk, q_seg, marks, w_output, inputs, gain_two, cotangent[:, side:], 4)
 
     d_normed_two, mixed, _n2, _other, d_expert_gate, d_expert_up, d_expert_down = run_expert(
-        normed_two, cot_a, cot_b, share.reshape(4, 4, rows, 1), expert_gate, expert_up, expert_down, 6)
-    def norm_back(d_out, values, r, gain):
-        d_scaled = d_out * gain
-        inner = jnp.mean(d_scaled * values, axis=1, keepdims=True)
-        d_gain = jnp.sum(d_out * values * r, axis=0)
-        return r * d_scaled - values * (r * r * r * inner), d_gain
-
-    d_resid_norm, d_gain_two = norm_back(d_normed_two, residual, r2, gain_two)
-    d_residual = cotangent.astype(F32) + d_resid_norm
-    d_res_low = d_residual.astype(BF)
-    d_lin, d_qk_gains, output = run_attend_back(
-        scale, pads, d_res_low, w_o, mixed, residual, q_rot, kv, q_seg, k_seg, log_total, head_out, lin, squares, cosine, sine, gq, gk, 7)
-    d_qk_gains = d_qk_gains[:2] + core_pair(d_qk_gains[:2])
+        normed_two, cot_a, cot_b, share, expert_gate, expert_up, expert_down, 6)
+    d_lin, d_qk_gains, output, d_residual, d_gain_two = run_attend_back(
+        scale, pads, d_normed_two, cotangent, gain_two, w_o, mixed, residual, q_rot, kv, q_seg, marks, log_total, head_out,
+        lin, squares, near, far, gq, gk, 7)
     d_w_output, d_inputs, d_w_query, d_w_key, d_w_value, d_gains = run_finish(
-        d_lin, w_qkv, n1_rows, attended, inputs, d_residual, gain_one, d_gain_two.reshape(1, width), 8)
-
-    def my_half(row):
-        return lax.dynamic_slice_in_dim(row, core * 64, 64, 0)
-
+        d_lin, w_qkv, n1_rows, attended, inputs, d_residual, gain_one, d_gain_two, d_qk_gains, 8)
     return (
         output,
         d_inputs,
-        my_half(d_gains[0]),
+        d_gains[0],
         d_w_query,
         d_w_key,
         d_w_value,
         d_w_output,
-        my_half(d_qk_gains[0]),
-        my_half(d_qk_gains[1]),
-        my_half(d_gains[1]),
+        d_gains[2],
+        d_gains[3],
+        d_gains[1],
         d_expert_gate,
         d_expert_up,
         d_expert_down,

time: 691 us -> 660 us (0.955)
  local copies, waits for them, and re-layouts: 39.8 us -> 22 us
  Pallas kernels: 631 us -> 619 us
    unnamed x65 -> x25, local copies, waits for them, and re-layouts: 30.4 us -> 17.4 us
    pallas_call x1, Pallas kernels: 142 us -> 132 us  [run_finish(): pl.pallas_call(functools.partial(finish_kernel, cut), out_shape=(own, S((...]
  transfers between devices with their start and end apart: 1 -> 0, of which waited for: 0 -> 0; matrix products, arithmetic and copies ran while one was open for 0% -> 0% of each run, Pallas kernels for 21% -> 0%
where the time goes in v6:
time: 660 us; the launch traced here: 652 us
  Pallas kernels  619 us (94%)
  local copies, waits for them, and re-layouts  22 us (3%)
  other arithmetic  8.47 us (1%)
    pallas_call x1, Pallas kernels, run_expert(): pl.pallas_call(functools.partial(expert_kernel, cut), out_shape=(S((R, D)...  180 us
    pallas_call x1, Pallas kernels, run_finish(): pl.pallas_call(functools.partial(finish_kernel, cut), out_shape=(own, S((...  132 us
    pallas_call x1, Pallas kernels, run_qkv(): pl.pallas_call(functools.partial(qkv_kernel, cut), out_shape=(S((16, R, D...  127 us
    pallas_call x1, Pallas kernels, run_attend_back(): pl.pallas_call(functools.partial(attend_back_kernel, scale, pads, cut), o...  99 us
    pallas_call x1, Pallas kernels, run_attend(): pl.pallas_call(functools.partial(attend_kernel, scale, pads, cut), out_sh...  81.2 us
    unnamed x25, local copies, waits for them, and re-layouts  17.4 us

profile of v6, /device:TPU:0, one launch (start us, length us, event | category | flops | bytes accessed | tf_op | source)
XLA Modules:
  0.0 651.9 jit_solution(16949931282924006890)
XLA Ops:
  0.8 0.7 maximum_convert_fusion
  2.3 0.9 convolution_select_fusion
  3.2 0.7 select_reduce_fusion
  4.7 0.7 convert_element_type.21
  7.0 1.9 fusion.9
  8.8 127.1 %project.1 = (bf16[16,128,2048]{2,1,0:T(8,128)(2,1)}, f32[16,128,384]{2,1,0:T(8,128)}, bf16[16,2,64,384]{3,2,1,0:T(8,128)(2,1)}, f32[32,128]{1,0:T(8,128)}, f32[...) custom-call(bf16[128,2048]{1,0:T(8,128)(2,1)} %x_in.3, bf16[64,2048]{1,0:T(8,128)(2,1)} %wq.1, bf16[64,2048]{1,0:T(8,128)(2,1)} %wk.1, ...), custom_call_target="tpu_custom_call" | custom-call | tf_op jit(solution)/shard_map/project/pallas_call | solution.py:1228
  135.9 1.3 fusion.5
  137.2 0.9 bitcast_reduce_fusion
  140.5 81.2 %attend.1 = (bf16[4,4,2,64,2048]{4,3,2,1,0:T(8,128)(2,1)}, bf16[16,128,128]{2,1,0:T(8,128)(2,1)}, bf16[2,20,2,128,128]{4,3,2,1,0:T(8,128)(2,1)}, bf16[16,128,128...) custom-call(f32[16,128,384]{2,1,0:T(8,128)} %get-tuple-element.44.li, ...), custom_call_target="tpu_custom_call" | custom-call | tf_op jit(solution)/shard_map/attend/pallas_call | solution.py:1926
  221.8 179.7 %expert.1 = (f32[128,2048]{1,0:T(8,128)}, bf16[4,4,128,2048]{3,2,1,0:T(8,128)(2,1)}, bf16[4,4,128,2048]{3,2,1,0:T(8,128)(2,1)}, bf16[6,256,2048]{2,1,0:T(8,128)(...) custom-call(bf16[128,2048]{1,0:T(8,128)(2,1)} %get-tuple-element.47.n2, ...), custom_call_target="tpu_custom_call" | custom-call | tf_op jit(solution)/shard_map/expert/pallas_call | solution.py:1543
  401.5 99.0 %attend_back.1 = (bf16[16,128,384]{2,1,0:T(8,128)(2,1)}, f32[8,128]{1,0:T(8,128)}, f32[128,2048]{1,0:T(8,128)}, f32[128,2048]{1,0:T(8,128)}, f32[1,2048]{1,0:T(1,128)}) custom-call(f32[128,2048]{1,0:T(8,128)} %get-tuple-element.50.d_n2, bf16[128,2048]{1,0:T(8,128)(2,1)} %cot.1, f32[1,2048]{1,0:T(1,128)} %get-tuple-element.81.gain, ...), custom_call_target="tpu_custom_call" | custom-call | tf_op jit(solution)/shard_map/attend_back/pallas_call | solution.py:2084
  500.5 132.4 %finish.1 = (f32[64,2048]{1,0:T(8,128)}, f32[128,2048]{1,0:T(8,128)}, f32[64,2048]{1,0:T(8,128)}, f32[64,2048]{1,0:T(8,128)}, f32[64,2048]{1,0:T(8,128)}, /*index=5*/f32[8,64]{1,0:T(8,128)}) custom-call(bf16[16,128,384]{2,1,0:T(8,128)(2,1)} %get-tuple-element.59.d_lin, bf16[16,2,64,384]{3,2,1,0:T(8,128)(2,1)} %get-tuple-element.60.wf, ...), custom_call_target="tpu_custom_call" | custom-call | tf_op jit(solution)/shard_map/finish/pallas_call | solution.py:1750
  633.0 1.3 slice_bitcast_fusion.2
  634.3 2.4 copy.46
  636.8 2.3 copy.47
  639.1 0.8 copy.48
  639.9 0.8 copy.49
  640.7 0.8 copy.50
  641.5 0.8 copy.51
  642.2 2.1 copy.52
  644.4 1.6 copy-done.1
  646.0 2.1 copy.53
  648.1 1.6 copy-done
  649.7 2.0 copy.54
  (36 shorter events, 5.6 us)
Async XLA Ops:
  5.4 135.1 %copy-start.7 = (f32[4096]{0:T(1024)}, f32[4096]{0:T(1024)S(1)}, u32[]{:S(2)}) copy-start(f32[4096]{0:T(1024)S(1)} %convert_element_type.21) | copy-start | bytes 49156
  632.9 6.1 copy-start.6
  632.9 6.9 %copy-start.5 = (f32[64,2048]{1,0:T(8,128)S(1)}, f32[64,2048]{1,0:T(8,128)}, u32[]{:S(2)}) copy-start(f32[64,2048]{1,0:T(8,128)} %get-tuple-element.115) | copy-start | bytes 1572868
  633.0 7.7 %copy-start.4 = (f32[64,2048]{1,0:T(8,128)S(1)}, f32[64,2048]{1,0:T(8,128)}, u32[]{:S(2)}) copy-start(f32[64,2048]{1,0:T(8,128)} %get-tuple-element.116) | copy-start | bytes 1572868
  633.0 8.5 %copy-start.3 = (f32[64,2048]{1,0:T(8,128)S(1)}, f32[64,2048]{1,0:T(8,128)}, u32[]{:S(2)}) copy-start(f32[64,2048]{1,0:T(8,128)} %get-tuple-element.117) | copy-start | bytes 1572868
  634.3 7.9 %copy-start.2 = (f32[1024,1024]{1,0:T(8,128)S(1)}, f32[1024,1024]{1,0:T(8,128)}, u32[]{:S(2)}) copy-start(f32[1024,1024]{1,0:T(8,128)} %get-tuple-element.121) | copy-start | bytes 12582916
  642.2 3.7 copy-start.1
  646.0 3.7 copy-start

commit v7 on v6

--- a/solution.py
+++ b/solution.py
@@ -1081,6 +1081,62 @@
     pl.semaphore_wait(bar, count - 1)
 
 
+def weight_tiles(partner, plan, load, turn, right, left, ob, gt, fs, other, osem, ors, fsem, gsem, out):
+    side = fs.shape[2]
+
+    def sent(k):
+        return remote(ob(k), other.at[k], osem.at[k], ors.at[k], partner)
+
+    def tile_at(i):
+        kind, k = plan[i]
+        if load is not None and i + 1 < len(plan):
+            load(i + 1).start()
+        if kind == "o":
+            if k >= 2:
+                sent(k - 2).wait_send()
+        else:
+            landed(other.at[k], ors.at[k])
+            fetch = pltpu.make_async_copy(other.at[k], gt, gsem)
+            fetch.start()
+        if load is not None:
+            load(i).wait()
+        turn(i)
+        if kind == "w":
+            fetch.wait()
+        for h in (0, 1):
+            if kind == "w" and k > 0:
+                landed(fs.at[h], fsem.at[h])
+            for n in (0, 1):
+                made = dot(left[...], right(h, n), ((1,), (0,)))
+                cols = slice(h * side + n * 512, h * side + (n + 1) * 512)
+                if kind == "o":
+                    ob(k)[:, cols] = made.astype(BF)
+                else:
+                    fs[h, :, n * 512 : (n + 1) * 512] = made + wide(gt[:, cols])
+            if kind == "w":
+                pltpu.make_async_copy(fs.at[h], out(k, h), fsem.at[h]).start()
+        if kind == "o":
+            sent(k).start()
+
+    def finish():
+        count = len(plan) // 2
+        for k in (count - 2, count - 1):
+            sent(k).wait_send()
+        for h in (0, 1):
+            landed(fs.at[h], fsem.at[h])
+
+    return tile_at, finish
+
+
+def turned_into(left, flat, cols, tile=256):
+    def one(b, _):
+        sl = pl.ds(pl.multiple_of(b * tile, tile), tile)
+        left[:, sl] = flat[sl, cols].T
+        return 0
+
+    lax.fori_loop(0, flat.shape[0] // tile, one, 0)
+
+
 def qkv_kernel(cut, x_ref, wq, wk, wv, block, cot, n1_o, lin_o, wf_o, tot, sw, C, X, lin, wf, nb, gain, sums, sums_all, lsem, nsem, msem, ssem, csem, *gs):
     net = Net(ssem)
     u, z, c = net.u, net.z, net.c
@@ -1243,8 +1299,8 @@
     return jnp.where(g == 0, 3, jnp.where(g == 1, 0, jnp.where(g == 2, 2, 1)))
 
 
-def expert_kernel(cut, n2, cot_a, cot_b, share_rows, gate, up, down, d_n2, p_out, n2_o, other, dg_o, du_o, dd_o,
-                  X, C, GU, W, A, hid, pb, fs, share, lsem, wsem, wrs, psem, tsem, osem, ors, fsem, sa, sr, *scr):
+def expert_kernel(cut, n2, cot_a, cot_b, share_rows, gate, up, down, d_n2, p_out, n2_o, a_o, other, dd_o,
+                  X, C, GU, W, A, hid, pb, fs, share, lsem, wsem, wrs, psem, osem, tsem, ors, fsem, sa, sr, *scr):
     ga_sems, rs_bufs = scr[:7], scr[7:]
     na, nr = Net(sa), Net(sr)
     u, z, c = na.u, na.z, na.c
@@ -1308,6 +1364,7 @@
             return 0
 
         lax.fori_loop(0, ff // span, inner, 0)
+        pltpu.make_async_copy(A.at[:, zz], a_o.at[:, zz], psem.at[2]).start()
         weight = share[:, zz]
 
         def flushed(n):
@@ -1395,7 +1452,7 @@
     def at_turns(table):
         return {t: steps_of(sc, words) for t, words in table.items()}
 
-    steps = at_turns({1: "m3 f3 d3", 3: "m0 f0 d0", 5: "m2 f2 d2 M3", 6: "b31", 7: "m1 f1 d1 M0 b02"})
+    steps = at_turns({1: "m3 f3 d3", 3: "m0 f0 d0", 4: "M3", 5: "m2 f2 d2 b31", 6: "M0", 7: "m1 f1 d1 b02 b32"})
 
     def turn(t, _):
         backward(t)
@@ -1404,131 +1461,38 @@
 
     lax.fori_loop(0, 8, turn, 0)
 
-    GU4 = GU.reshape(4, 4, rows, width)
     left = W.at[pl.ds(0, tile), :]
 
-    def tile_load(k, which):
-        slot = lax.rem(k, 2)
-        cols = pl.ds(pl.multiple_of((which * 4 + k) * tile, tile), tile)
-        return pltpu.make_async_copy(
-            n2_o.at[:, :, :, cols], GU4.at[:, :, :, pl.ds(pl.multiple_of(slot * tile, tile), tile)], tsem.at[slot])
-
-    def left_tokens(k):
-        cols = pl.ds(pl.multiple_of(lax.rem(k, 2) * tile, tile), tile)
-
-        def one(b, _):
-            sl = pl.ds(pl.multiple_of(b * tile, tile), tile)
-            left[:, sl] = GU[sl, cols].T
-            return 0
-
-        lax.fori_loop(0, tokens // tile, one, 0)
-
-    def left_hidden(k, which):
-        cols = pl.ds(pl.multiple_of((which * 2 + k) * tile, tile), tile)
-        flat = hid.reshape(tokens, ff)
-
-        def one(b, _):
-            sl = pl.ds(pl.multiple_of(b * tile, tile), tile)
-            left[:, sl] = flat[sl, cols].T
-            return 0
-
-        lax.fori_loop(0, tokens // tile, one, 0)
-
-    def products(right, store):
-        flat = right.reshape(tokens, width)
-
-        def one(n, _):
-            cols = pl.ds(pl.multiple_of(n * 512, 512), 512)
-            store(cols, n, dot(left[...], flat[:, cols], ((1,), (0,))))
-            return 0
-
-        lax.fori_loop(0, width // 512, one, 0)
-
-    def sent(k):
-        slot = W.at[pl.ds(pl.multiple_of(tile + lax.rem(k, 2) * tile, tile), tile), :]
-        return slot, remote(slot, other.at[k], osem.at[k], ors.at[k], partner)
-
-    tile_load(0, 1 - c).start()
-
-    def other_tile(k, _):
-        slot, copy = sent(k)
-
-        @pl.when(k >= 2)
-        def _():
-            sent(k - 2)[1].wait_send()
-
-        def store(cols, n, v):
-            slot[:, cols] = v.astype(BF)
-
-        @pl.when(k < 4)
-        def _():
-            pl.when(k < 3)(lambda: tile_load(k + 1, 1 - c).start())
-            tile_load(k, 1 - c).wait()
-            left_tokens(k)
-            products(A, store)
-
-        @pl.when(k >= 4)
-        def _():
-            left_hidden(k - 4, 1 - c)
-            products(C, store)
-
-        copy.start()
-        acts(at_turns({0: "M2", 1: "h30 b32 b21", 2: "M1 h03 b01", 3: "h31 b12", 4: "h02 h20", 5: "h32 h23"}), k)
-        return 0
-
-    lax.fori_loop(0, 6, other_tile, 0)
+    def left_hidden(i):
+        kind, k = plan[i]
+        which = 1 - c if kind == "o" else c
+        turned_into(left, hid.reshape(tokens, ff), pl.ds(pl.multiple_of((which * 2 + k) * tile, tile), tile))
+
+    plan = [("o", 0), ("o", 1), ("w", 0), ("w", 1)]
+    made = C.reshape(tokens, width)
+    dw, dw_end = weight_tiles(
+        partner, plan, None, left_hidden, lambda h, n: made[:, h * side + n * 512 : h * side + (n + 1) * 512], left,
+        lambda k: W.at[pl.ds((1 + k % 2) * tile, tile), :], W.at[pl.ds(3 * tile, tile), :], fs, other, tsem, ors, fsem,
+        lsem.at[0], lambda k, h: dd_o.at[pl.ds(k * tile, tile), pl.ds(h * side, side)])
+
+    def go(words):
+        run_steps(steps_of(sc, words))
+
+    dw(0)
+    go("M2 b21")
+    dw(1)
+    go("h30 M1 b01 b12 h03")
+    dw(2)
+    go("h31 h02 h20 h23")
+    dw(3)
+    go("h32 h01 h10 h13 Q h21 h12 q")
 
     def store_out(sl, v):
         d_n2[sl, :] = v
 
-    tile_load(0, c).start()
-    got = W.at[pl.ds(3 * tile, tile), :]
-
-    def flush(k, h):
-        i = pl.ds(pl.multiple_of(lax.rem(k, 4) * tile, tile), tile)
-
-        def go(dst):
-            pltpu.make_async_copy(fs.at[h], dst, fsem.at[h]).start()
-
-        pl.when(k < 4)(lambda: go((dg_o, du_o)[h].at[i, :]))
-        pl.when(k >= 4)(lambda: go(dd_o.at[i, pl.ds(h * 1024, 1024)]))
-
-    def own_tile(k, _):
-        fetch = pltpu.make_async_copy(other.at[k], got, lsem.at[0])
-        landed(other.at[k], ors.at[k])
-        fetch.start()
-
-        def finish(right):
-            flat = right.reshape(tokens, width)
-            fetch.wait()
-            for h in (0, 1):
-                pl.when(k > 0)(lambda: landed(fs.at[h], fsem.at[h]))
-                for n in (0, 1):
-                    cols = pl.ds(h * 1024 + n * 512, 512)
-                    fs[h, :, n * 512 : (n + 1) * 512] = dot(left[...], flat[:, cols], ((1,), (0,))) + wide(got[:, cols])
-                flush(k, h)
-
-        @pl.when(k < 4)
-        def _():
-            pl.when(k < 3)(lambda: tile_load(k + 1, c).start())
-            tile_load(k, c).wait()
-            left_tokens(k)
-            finish(A)
-
-        @pl.when(k >= 4)
-        def _():
-            left_hidden(k - 4, c)
-            finish(C)
-
-        acts(at_turns({0: "h01 h10", 1: "Q h21", 2: "h13", 4: "h12", 5: "q"}), k)
-        return 0
-
-    lax.fori_loop(0, 6, own_tile, 0)
     sc.last(store_out)
-    for h in (0, 1):
-        landed(fs.at[h], fsem.at[h])
-    for k in (4, 5):
-        sent(k)[1].wait_send()
+    landed(A, psem.at[2])
+    dw_end()
     nr.finish()
 
 
@@ -1542,13 +1506,13 @@
     M = pl.BlockSpec(memory_space=pltpu.VMEM)
     return pl.pallas_call(
         functools.partial(expert_kernel, cut),
-        out_shape=(S((R, D), F32), S((4, 4, R, D), BF), S((4, 4, R, D), BF), S((6, 256, D), BF),
-                   S((half, ff), F32), S((half, ff), F32), S(down.shape, F32)),
+        out_shape=(S((R, D), F32), S((4, 4, R, D), BF), S((4, 4, R, D), BF), S((4, 4, R, 2 * ff), BF),
+                   S((2, 256, D), BF), S(down.shape, F32)),
         in_specs=[A, A, A, M, A, A, A],
-        out_specs=(M,) + (A,) * 6,
+        out_specs=(M,) + (A,) * 5,
         scratch_shapes=[V(4, 4, R, D), V(4, 4, R, D), V(D, 2 * ff), V(ff, D), V(4, 4, R, 2 * ff), V(4, 4, R, ff),
-                        V(2, 4, R, 512), pltpu.VMEM((2, 256, 1024), F32), pltpu.VMEM((4, 4, R, 1), F32),
-                        DMA((6,)), DMA((3,)), DMA((3,)), DMA((2,)), DMA((2,)), DMA((6,)), DMA((6,)), DMA((2,)),
+                        V(2, 4, R, 512), pltpu.VMEM((2, 256, D // 2), F32), pltpu.VMEM((4, 4, R, 1), F32),
+                        DMA((6,)), DMA((3,)), DMA((3,)), DMA((3,)), DMA((2,)), DMA((2,)), DMA((2,)), DMA((2,)),
                         DMA((64,)), DMA((96,))] + ag_sems() + rs_scratch(cut, R, D),
         compiler_params=pltpu.CompilerParams(collective_id=cid, has_side_effects=True, vmem_limit_bytes=63 * 2**20),
         name="expert",
@@ -1650,25 +1614,28 @@
             keep[2 * k + i] = jnp.where(c == 0, first, second)
             give[2 * k + i] = jnp.where(c == 0, second, first).astype(BF)
 
+    one("f2 f1")
+    join()
+    two("m3 m0 m2 m1 f3 f0")
     one("d3 d0")
     grads(0)
+    one("M3 M0")
+    one("d2 d1")
     grads(1)
-    one("f2 f1 d2 d1")
-    join()
-    two("m3 m0 m2 m1 f3 f0")
+    one("M2 M1")
+    two("d3 d0 d2 d1 f2 f1")
     grads(2)
+    one("b31 b02")
+    two("M3 M0 M2 M1")
     grads(3)
-    one("M3 M0 M2 M1")
-    two("d3 d0 d2 d1 f2 f1")
+    one("h30 h03 b21 b12")
     grads(4)
     grads(5)
-    one("b31 b02")
+    one("b32 b01")
     grads(6)
     grads(7)
     across = remote(give, got, msem.at[0], msem.at[1], partner)
     across.start()
-    two("M3 M0 M2 M1")
-    one("b21 b12 b32 b01 h30 h03")
     landed(got, msem.at[1])
 
     def total(e, _):
@@ -1937,8 +1904,9 @@
     )(lin, tot, near, far, gq, gk, q_seg, segments, w_own, x_in, gain, cot)
 
 
-def attend_back_kernel(scale, pads, cut, d_n2, cot, gain, wo_h, p_out, residual, q_rot, kv, q_seg, segments, lse, o_ref, lin, tot, near, far, gq, gk,
-                       d_lin, d_gains, output, d_residual, d_gain, d_res, k_seg, P, wo, d_mine, d_out, d_q, d_k, d_v, other, got, d_un, sums, sums_all, inner,
+def attend_back_kernel(scale, pads, cut, d_n2, cot, gain, wo_h, p_out, residual, q_rot, kv, q_seg, segments, lse, o_ref, lin, tot, near, far, gq, gk, n2, a_h,
+                       d_lin, d_gains, output, d_residual, d_gain, other_w, dg_o, du_o,
+                       nt, left, ob, gt, fs, tsem, osem, ors, fsem, gsem, d_res, k_seg, P, wo, d_mine, d_out, d_q, d_k, d_v, other, got, d_un, sums, sums_all, inner,
                        lsem, msem, ssem, *bufs):
     net = Net(ssem)
     sc = Scatter(net, cut, P, bufs)
@@ -1991,6 +1959,27 @@
 
     lax.fori_loop(0, 8, send, 0)
     d_out[me] = d_mine[me]
+    A = wo.reshape(16, rows, width)
+    load_a = pltpu.make_async_copy(a_h, A, lsem.at[0])
+    load_a.start()
+    plan = [("o", 0), ("o", 1), ("o", 2), ("o", 3), ("w", 0), ("w", 1), ("w", 2), ("w", 3)]
+    tile = 256
+
+    def left_load(i):
+        kind, k = plan[i]
+        which = 1 - c if kind == "o" else c
+        cols = pl.ds(pl.multiple_of((which * 4 + k) * tile, tile), tile)
+        return pltpu.make_async_copy(n2.at[:, :, cols], nt.at[i % 2], tsem.at[i % 2])
+
+    def left_turn(i):
+        turned_into(left, nt.at[i % 2].reshape(16 * rows, tile), slice(None))
+
+    left_load(0).start()
+    made = A.reshape(16 * rows, width)
+    dw, dw_end = weight_tiles(
+        partner, plan, left_load, left_turn, lambda h, n: made[:, h * 1024 + n * 512 : h * 1024 + (n + 1) * 512], left,
+        lambda k: ob.at[k % 2], gt, fs, other_w, osem, ors, fsem, gsem.at[0],
+        lambda k, h: (dg_o, du_o)[h].at[pl.ds(k * tile, tile), :])
     d_k[...] = jnp.zeros_like(d_k)
     d_v[...] = jnp.zeros_like(d_v)
     landed(d_out.at[pl.ds(0, 15)], msem.at[1])
@@ -2066,14 +2055,28 @@
         return 0
 
     lax.fori_loop(0, 16, finish, 0)
-    go("h31 h02 h20 h13 Q h32 h01 h10 h23 h21 h12 q")
+    load_a.wait()
+    go("h31 h02")
+    dw(0)
+    dw(1)
+    go("h20 h13 Q")
+    dw(2)
+    go("h32 h01")
+    dw(3)
+    dw(4)
+    go("h10 h23")
+    dw(5)
+    go("h21 h12 q")
+    dw(6)
+    dw(7)
     sc.last(store)
+    dw_end()
     landed(d_out.at[pl.ds(0, 15)], msem.at[0])
     landed(other, msem.at[2])
     net.finish()
 
 
-def run_attend_back(scale, pads, d_n2, cot, gain, wo, p_out, residual, q_rot, kv, q_seg, segments, lse, o, lin, tot, near, far, gq, gk, cid, cut=96):
+def run_attend_back(scale, pads, d_n2, cot, gain, wo, p_out, residual, q_rot, kv, q_seg, segments, lse, o, lin, tot, near, far, gq, gk, n2, a_h, half, cid, cut=96):
     R, D = d_n2.shape
     DMA = pltpu.SemaphoreType.DMA
     S = jax.ShapeDtypeStruct
@@ -2083,16 +2086,18 @@
     span = (pads + 16) * 2 * R
     return pl.pallas_call(
         functools.partial(attend_back_kernel, scale, pads, cut),
-        out_shape=(S((16, R, 384), BF), S((8, 128), F32), S((R, D), F32), S((R, D), F32), S((1, D), F32)),
-        in_specs=[M, M, M, A, A] + [M] * 13,
-        out_specs=(M,) * 5,
-        scratch_shapes=[V((R, D), BF), V((1, span), F32), V((4, 4, R, D), BF), V(wo.shape, BF), V((16, R, 128), BF), V((16, R, 128), BF), V((16, R, 128), BF),
+        out_shape=(S((16, R, 384), BF), S((8, 128), F32), S((R, D), F32), S((R, D), F32), S((1, D), F32),
+                   S((4, 256, D), BF), S(half, F32), S(half, F32)),
+        in_specs=[M, M, M, A, A] + [M] * 13 + [A, A],
+        out_specs=(M,) * 5 + (A,) * 3,
+        scratch_shapes=[V((2, 16, R, 256), BF), V((256, 16 * R), BF), V((2, 256, D), BF), V((256, D), BF), V((2, 256, 1024), F32),
+                        DMA((2,)), DMA((4,)), DMA((4,)), DMA((2,)), DMA((1,)), V((R, D), BF), V((1, span), F32), V((4, 4, R, D), BF), V(wo.shape, BF), V((16, R, 128), BF), V((16, R, 128), BF), V((16, R, 128), BF),
                         V((span, 128), F32), V((span, 128), F32), V((2, 16, R, 128), BF), V((2, 16, R, 128), BF),
                         V((2, 16, R, 128), F32), V((32, 128), F32), V((16, 32, 128), F32), V((32, 128), F32),
                         DMA((2,)), DMA((10,)), DMA((64,))] + rs_scratch(cut, R, D),
         compiler_params=pltpu.CompilerParams(collective_id=cid, has_side_effects=True, vmem_limit_bytes=63 * 2**20),
         name="attend_back",
-    )(d_n2, cot, gain, wo, p_out, residual, q_rot, kv, q_seg, segments, lse, o, lin, tot, near, far, gq, gk)
+    )(d_n2, cot, gain, wo, p_out, residual, q_rot, kv, q_seg, segments, lse, o, lin, tot, near, far, gq, gk, n2, a_h)
 def dot(a, b, dims):
     return lax.dot_general(a, b, (dims, ((), ())), preferred_element_type=jnp.float32)
 
@@ -2154,11 +2159,11 @@
     w_o, q_rot, kv, head_out, log_total, attended, residual, normed_two, cot_b = run_attend(
         scale, pads, lin, squares, near, far, gq, gk, q_seg, marks, w_output, inputs, gain_two, cotangent[:, side:], 4)
 
-    d_normed_two, mixed, _n2, _other, d_expert_gate, d_expert_up, d_expert_down = run_expert(
+    d_normed_two, mixed, n2_rows, d_pre, _other, d_expert_down = run_expert(
         normed_two, cot_a, cot_b, share, expert_gate, expert_up, expert_down, 6)
-    d_lin, d_qk_gains, output, d_residual, d_gain_two = run_attend_back(
+    d_lin, d_qk_gains, output, d_residual, d_gain_two, _other, d_expert_gate, d_expert_up = run_attend_back(
         scale, pads, d_normed_two, cotangent, gain_two, w_o, mixed, residual, q_rot, kv, q_seg, marks, log_total, head_out,
-        lin, squares, near, far, gq, gk, 7)
+        lin, squares, near, far, gq, gk, n2_rows.reshape(chips, rows, width), d_pre.reshape(chips, rows, -1), expert_gate.shape, 7)
     d_w_output, d_inputs, d_w_query, d_w_key, d_w_value, d_gains = run_finish(
         d_lin, w_qkv, n1_rows, attended, inputs, d_residual, gain_one, d_gain_two, d_qk_gains, 8)
     return (

time: 660 us -> 651 us (0.986)
  Pallas kernels: 619 us -> 611 us
    pallas_call x1, Pallas kernels: 180 us -> 164 us  [run_expert(): pl.pallas_call(functools.partial(expert_kernel, cut), out_shape=(S((R, D)...]
    pallas_call x1, Pallas kernels: 99 us -> 111 us  [run_attend_back(): pl.pallas_call(functools.partial(attend_back_kernel, scale, pads, cut), o...]
where the time goes in v7:
time: 651 us; the launch traced here: 643 us
  Pallas kernels  611 us (94%)
  local copies, waits for them, and re-layouts  22 us (3%)
  other arithmetic  8.47 us (1%)
    pallas_call x1, Pallas kernels, run_expert(): pl.pallas_call(functools.partial(expert_kernel, cut), out_shape=(S((R, D)...  164 us
    pallas_call x1, Pallas kernels, run_finish(): pl.pallas_call(functools.partial(finish_kernel, cut), out_shape=(own, S((...  127 us
    pallas_call x1, Pallas kernels, run_qkv(): pl.pallas_call(functools.partial(qkv_kernel, cut), out_shape=(S((16, R, D...  127 us
    pallas_call x1, Pallas kernels, run_attend_back(): pl.pallas_call(functools.partial(attend_back_kernel, scale, pads, cut), o...  111 us
    pallas_call x1, Pallas kernels, run_attend(): pl.pallas_call(functools.partial(attend_kernel, scale, pads, cut), out_sh...  81.3 us
    unnamed x25, local copies, waits for them, and re-layouts  17.4 us

profile of v7, /device:TPU:0, one launch (start us, length us, event | category | flops | bytes accessed | tf_op | source)
XLA Modules:
  0.0 643.3 jit_solution(3704183489010563251)
XLA Ops:
  0.8 0.7 maximum_convert_fusion
  2.3 0.9 convolution_select_fusion
  3.2 0.7 select_reduce_fusion
  4.7 0.7 convert_element_type.21
  7.0 1.9 fusion.9
  8.8 127.1 %project.1 = (bf16[16,128,2048]{2,1,0:T(8,128)(2,1)}, f32[16,128,384]{2,1,0:T(8,128)}, bf16[16,2,64,384]{3,2,1,0:T(8,128)(2,1)}, f32[32,128]{1,0:T(8,128)}, f32[...) custom-call(bf16[128,2048]{1,0:T(8,128)(2,1)} %x_in.3, bf16[64,2048]{1,0:T(8,128)(2,1)} %wq.1, bf16[64,2048]{1,0:T(8,128)(2,1)} %wk.1, ...), custom_call_target="tpu_custom_call" | custom-call | tf_op jit(solution)/shard_map/project/pallas_call | solution.py:1284
  135.9 1.3 fusion.5
  137.2 0.9 bitcast_reduce_fusion
  140.5 81.3 %attend.1 = (bf16[4,4,2,64,2048]{4,3,2,1,0:T(8,128)(2,1)}, bf16[16,128,128]{2,1,0:T(8,128)(2,1)}, bf16[2,20,2,128,128]{4,3,2,1,0:T(8,128)(2,1)}, bf16[16,128,128...) custom-call(f32[16,128,384]{2,1,0:T(8,128)} %get-tuple-element.46.li, ...), custom_call_target="tpu_custom_call" | custom-call | tf_op jit(solution)/shard_map/attend/pallas_call | solution.py:1893
  221.8 163.8 %expert.1 = (f32[128,2048]{1,0:T(8,128)}, bf16[4,4,128,2048]{3,2,1,0:T(8,128)(2,1)}, bf16[4,4,128,2048]{3,2,1,0:T(8,128)(2,1)}, bf16[4,4,128,2048]{3,2,1,0:T(8,1...) custom-call(bf16[128,2048]{1,0:T(8,128)(2,1)} %get-tuple-element.49.n2, ...), custom_call_target="tpu_custom_call" | custom-call | tf_op jit(solution)/shard_map/expert/pallas_call | solution.py:1507
  385.6 111.0 %attend_back.1 = (bf16[16,128,384]{2,1,0:T(8,128)(2,1)}, f32[8,128]{1,0:T(8,128)}, f32[128,2048]{1,0:T(8,128)}, f32[128,2048]{1,0:T(8,128)}, f32[1,2048]{1,0:T(1...) custom-call(f32[128,2048]{1,0:T(8,128)} %get-tuple-element.52.d_n2, ...), custom_call_target="tpu_custom_call" | custom-call | tf_op jit(solution)/shard_map/attend_back/pallas_call | solution.py:2087
  496.6 127.5 %finish.1 = (f32[64,2048]{1,0:T(8,128)}, f32[128,2048]{1,0:T(8,128)}, f32[64,2048]{1,0:T(8,128)}, f32[64,2048]{1,0:T(8,128)}, f32[64,2048]{1,0:T(8,128)}, /*index=5*/f32[8,64]{1,0:T(8,128)}) custom-call(bf16[16,128,384]{2,1,0:T(8,128)(2,1)} %get-tuple-element.63.d_lin, bf16[16,2,64,384]{3,2,1,0:T(8,128)(2,1)} %get-tuple-element.64.wf, ...), custom_call_target="tpu_custom_call" | custom-call | tf_op jit(solution)/shard_map/finish/pallas_call | solution.py:1717
  624.1 1.4 slice_bitcast_fusion.2
  625.5 2.4 copy.46
  627.9 2.3 copy.47
  630.2 0.8 copy.48
  631.0 0.8 copy.49
  631.8 0.8 copy.50
  632.6 0.8 copy.51
  633.4 2.1 copy.52
  635.5 1.6 copy-done.1
  637.1 2.1 copy.53
  639.2 1.6 copy-done
  640.8 2.0 copy.54
  (36 shorter events, 5.6 us)
Async XLA Ops:
  5.4 135.1 %copy-start.7 = (f32[4096]{0:T(1024)}, f32[4096]{0:T(1024)S(1)}, u32[]{:S(2)}) copy-start(f32[4096]{0:T(1024)S(1)} %convert_element_type.21) | copy-start | bytes 49156
  624.1 6.1 copy-start.6
  624.1 6.9 %copy-start.5 = (f32[64,2048]{1,0:T(8,128)S(1)}, f32[64,2048]{1,0:T(8,128)}, u32[]{:S(2)}) copy-start(f32[64,2048]{1,0:T(8,128)} %get-tuple-element.119) | copy-start | bytes 1572868
  624.1 7.7 %copy-start.4 = (f32[64,2048]{1,0:T(8,128)S(1)}, f32[64,2048]{1,0:T(8,128)}, u32[]{:S(2)}) copy-start(f32[64,2048]{1,0:T(8,128)} %get-tuple-element.120) | copy-start | bytes 1572868
  624.1 8.5 %copy-start.3 = (f32[64,2048]{1,0:T(8,128)S(1)}, f32[64,2048]{1,0:T(8,128)}, u32[]{:S(2)}) copy-start(f32[64,2048]{1,0:T(8,128)} %get-tuple-element.121) | copy-start | bytes 1572868
  625.5 7.9 %copy-start.2 = (f32[1024,1024]{1,0:T(8,128)S(1)}, f32[1024,1024]{1,0:T(8,128)}, u32[]{:S(2)}) copy-start(f32[1024,1024]{1,0:T(8,128)} %get-tuple-element.125) | copy-start | bytes 12582916
  633.4 3.7 copy-start.1
  637.1 3.7 copy-start

commit v8 on v7

--- a/solution.py
+++ b/solution.py
@@ -1053,12 +1053,14 @@
     return jnp.broadcast_to(row, (row.shape[1], row.shape[1])).T
 
 
-def share_sums(net, sums, sums_all, out, lsem, ssem, rsem):
+def share_sums(net, sums, sums_all, out, lsem, ssem, rsem, meanwhile=None):
     me = net.u * 4 + net.z
     own = pltpu.make_async_copy(sums, sums_all.at[me], lsem)
     own.start()
     each_chip(net, lambda t, dev: remote(sums, sums_all.at[me], ssem, rsem, dev).start())
     own.wait()
+    if meanwhile is not None:
+        meanwhile()
     part = sums_all.at[pl.ds(0, 15)]
     landed(part, rsem)
     total = sums_all[0]
@@ -1260,9 +1262,12 @@
     keep.start()
     landed(wf.at[pl.ds(0, 15), 0], msem.at[0])
     landed(wf.at[:, c], msem.at[2])
-    share_sums(net, sums, sums_all, tot, lsem.at[2], msem.at[4], msem.at[5])
-    gc.quads(3)
-    gc.cross(3)
+
+    def rest():
+        gc.quads(3)
+        gc.cross(3)
+
+    share_sums(net, sums, sums_all, tot, lsem.at[2], msem.at[4], msem.at[5], rest)
     for s in range(4):
         gc.settle(s)
     landed(sw.at[pl.ds(0, 31)], msem.at[6])
@@ -1324,8 +1329,6 @@
     own_w = [pltpu.make_async_copy(a, b, lsem.at[2 + i]) for i, (a, b) in enumerate(weights())]
     for one in first + own_w:
         one.start()
-    for k in range(16):
-        share[k // 4, k % 4] = column(share_rows[k : k + 1, :])[:, 0:1]
     na.barrier((partner,))
     first[0].wait()
 
@@ -1338,6 +1341,8 @@
     sent_w = [remote(a, b, wsem.at[i], wrs.at[i], partner) for i, (a, b) in enumerate(weights())]
     for one in sent_w:
         one.start()
+    for k in range(16):
+        share[k // 4, k % 4] = column(share_rows[k : k + 1, :])[:, 0:1]
 
     def forward(zz):
         pltpu.make_async_copy(X.at[:, zz], n2_o.at[:, zz], psem.at[1]).start()
@@ -1759,7 +1764,8 @@
     own_c.start()
     greet(net)
     own.wait()
-    ga = Gather(net, rows // 2, rows // 2, lambda uu, zz, lo, n: wo.at[uu, zz, c, pl.ds(lo, n), :], None, gs[:7])
+    ga = Gather(net, rows, cut, lambda uu, zz, lo, n: wo.at[uu, zz, c, :, pl.ds(lo * 16, n * 16)],
+                lambda zz, lo, n: wo.at[:, zz, c, :, pl.ds(lo * 16, n * 16)], gs[:7])
     netc = Net(csem)
     gc = Gather(netc, rows, cut, lambda uu, zz, lo, n: C.at[uu, zz, pl.ds(lo, n), :],
                 lambda zz, lo, n: C.at[:, zz, pl.ds(lo, n), :], gs[7:])
@@ -1790,7 +1796,9 @@
     mine = kv.at[:, pl.ds(pads, 16), c]
     to_partner = remote(mine, mine, msem.at[0], msem.at[1], partner)
     to_partner.start()
+    ga.begin2()
     ga.along(1)
+    ga.quads(0)
     ga.cross(0)
     own_c.wait()
     gc.begin()
@@ -1818,17 +1826,20 @@
 
     lax.fori_loop(0, 5, block, 0)
     ga.along(2)
+    ga.quads(1)
     ga.cross(1)
     halves(0)
     gc.begin2()
     lax.fori_loop(5, 10, block, 0)
     ga.along(3)
+    ga.quads(2)
     ga.cross(2)
     halves(1)
     gc.along(1)
     gc.quads(0)
     gc.cross(0)
     lax.fori_loop(10, 16, block, 0)
+    ga.quads(3)
     ga.cross(3)
     halves(2)
     gc.along(2)
@@ -1982,6 +1993,9 @@
         lambda k, h: (dg_o, du_o)[h].at[pl.ds(k * tile, tile), :])
     d_k[...] = jnp.zeros_like(d_k)
     d_v[...] = jnp.zeros_like(d_v)
+    load_a.wait()
+    dw(0)
+    dw(1)
     landed(d_out.at[pl.ds(0, 15)], msem.at[1])
     count = (pads + 16) * 2 * rows
 
@@ -2042,8 +2056,13 @@
         return 0
 
     lax.fori_loop(0, 16, undo, 0)
-    go("b21 b12 b32 b01")
-    share_sums(net, sums, sums_all, inner, lsem.at[1], msem.at[4], msem.at[5])
+
+    def meanwhile():
+        go("b21 b12 b32 b01")
+        dw(2)
+        dw(3)
+
+    share_sums(net, sums, sums_all, inner, lsem.at[1], msem.at[4], msem.at[5], meanwhile)
 
     def finish(i, _):
         both = lin[i]
@@ -2055,20 +2074,15 @@
         return 0
 
     lax.fori_loop(0, 16, finish, 0)
-    load_a.wait()
     go("h31 h02")
-    dw(0)
-    dw(1)
+    dw(4)
     go("h20 h13 Q")
-    dw(2)
+    dw(5)
     go("h32 h01")
-    dw(3)
-    dw(4)
+    dw(6)
     go("h10 h23")
-    dw(5)
+    dw(7)
     go("h21 h12 q")
-    dw(6)
-    dw(7)
     sc.last(store)
     dw_end()
     landed(d_out.at[pl.ds(0, 15)], msem.at[0])

time: 651 us -> 639 us (0.982)
  Pallas kernels: 611 us -> 598 us
    pallas_call x1, Pallas kernels: 111 us -> 100 us  [run_attend_back(): pl.pallas_call(functools.partial(attend_back_kernel, scale, pads, cut), o...]
where the time goes in v8:
time: 639 us; the launch traced here: 631 us
  Pallas kernels  598 us (94%)
  local copies, waits for them, and re-layouts  22 us (3%)
  other arithmetic  8.47 us (1%)
    pallas_call x1, Pallas kernels, run_expert(): pl.pallas_call(functools.partial(expert_kernel, cut), out_shape=(S((R, D)...  163 us
    pallas_call x1, Pallas kernels, run_finish(): pl.pallas_call(functools.partial(finish_kernel, cut), out_shape=(own, S((...  132 us
    pallas_call x1, Pallas kernels, run_qkv(): pl.pallas_call(functools.partial(qkv_kernel, cut), out_shape=(S((16, R, D...  123 us
    pallas_call x1, Pallas kernels, run_attend_back(): pl.pallas_call(functools.partial(attend_back_kernel, scale, pads, cut), o...  100 us
    pallas_call x1, Pallas kernels, run_attend(): pl.pallas_call(functools.partial(attend_kernel, scale, pads, cut), out_sh...  80 us
    unnamed x25, local copies, waits for them, and re-layouts  17.4 us

profile of v8, /device:TPU:0, one launch (start us, length us, event | category | flops | bytes accessed | tf_op | source)
XLA Modules:
  0.0 631.0 jit_solution(14934174713514995749)
XLA Ops:
  0.8 0.7 maximum_convert_fusion
  2.3 0.9 convolution_select_fusion
  3.2 0.7 select_reduce_fusion
  4.7 0.7 convert_element_type.21
  7.0 1.9 fusion.9
  8.8 122.9 %project.1 = (bf16[16,128,2048]{2,1,0:T(8,128)(2,1)}, f32[16,128,384]{2,1,0:T(8,128)}, bf16[16,2,64,384]{3,2,1,0:T(8,128)(2,1)}, f32[32,128]{1,0:T(8,128)}, f32[...) custom-call(bf16[128,2048]{1,0:T(8,128)(2,1)} %x_in.3, bf16[64,2048]{1,0:T(8,128)(2,1)} %wq.1, bf16[64,2048]{1,0:T(8,128)(2,1)} %wk.1, ...), custom_call_target="tpu_custom_call" | custom-call | tf_op jit(solution)/shard_map/project/pallas_call | solution.py:1289
  131.7 1.3 fusion.5
  133.0 0.9 bitcast_reduce_fusion
  136.3 80.0 %attend.1 = (bf16[4,4,2,64,2048]{4,3,2,1,0:T(8,128)(2,1)}, bf16[16,128,128]{2,1,0:T(8,128)(2,1)}, bf16[2,20,2,128,128]{4,3,2,1,0:T(8,128)(2,1)}, bf16[16,128,128...) custom-call(f32[16,128,384]{2,1,0:T(8,128)} %get-tuple-element.46.li, ...), custom_call_target="tpu_custom_call" | custom-call | tf_op jit(solution)/shard_map/attend/pallas_call | solution.py:1904
  216.3 163.3 %expert.1 = (f32[128,2048]{1,0:T(8,128)}, bf16[4,4,128,2048]{3,2,1,0:T(8,128)(2,1)}, bf16[4,4,128,2048]{3,2,1,0:T(8,128)(2,1)}, bf16[4,4,128,2048]{3,2,1,0:T(8,1...) custom-call(bf16[128,2048]{1,0:T(8,128)(2,1)} %get-tuple-element.49.n2, ...), custom_call_target="tpu_custom_call" | custom-call | tf_op jit(solution)/shard_map/expert/pallas_call | solution.py:1512
  379.6 100.2 %attend_back.1 = (bf16[16,128,384]{2,1,0:T(8,128)(2,1)}, f32[8,128]{1,0:T(8,128)}, f32[128,2048]{1,0:T(8,128)}, f32[128,2048]{1,0:T(8,128)}, f32[1,2048]{1,0:T(1...) custom-call(f32[128,2048]{1,0:T(8,128)} %get-tuple-element.52.d_n2, ...), custom_call_target="tpu_custom_call" | custom-call | tf_op jit(solution)/shard_map/attend_back/pallas_call | solution.py:2101
  479.9 131.9 %finish.1 = (f32[64,2048]{1,0:T(8,128)}, f32[128,2048]{1,0:T(8,128)}, f32[64,2048]{1,0:T(8,128)}, f32[64,2048]{1,0:T(8,128)}, f32[64,2048]{1,0:T(8,128)}, /*index=5*/f32[8,64]{1,0:T(8,128)}) custom-call(bf16[16,128,384]{2,1,0:T(8,128)(2,1)} %get-tuple-element.63.d_lin, bf16[16,2,64,384]{3,2,1,0:T(8,128)(2,1)} %get-tuple-element.64.wf, ...), custom_call_target="tpu_custom_call" | custom-call | tf_op jit(solution)/shard_map/finish/pallas_call | solution.py:1722
  611.9 1.4 slice_bitcast_fusion.2
  613.2 2.4 copy.46
  615.7 2.3 copy.47
  618.0 0.8 copy.48
  618.8 0.8 copy.49
  619.6 0.8 copy.50
  620.4 0.8 copy.51
  621.2 2.1 copy.52
  623.3 1.6 copy-done.1
  624.9 2.1 copy.53
  627.0 1.6 copy-done
  628.6 2.0 copy.54
  (36 shorter events, 5.6 us)
Async XLA Ops:
  5.4 131.0 %copy-start.7 = (f32[4096]{0:T(1024)}, f32[4096]{0:T(1024)S(1)}, u32[]{:S(2)}) copy-start(f32[4096]{0:T(1024)S(1)} %convert_element_type.21) | copy-start | bytes 49156
  611.8 6.1 copy-start.6
  611.8 6.9 %copy-start.5 = (f32[64,2048]{1,0:T(8,128)S(1)}, f32[64,2048]{1,0:T(8,128)}, u32[]{:S(2)}) copy-start(f32[64,2048]{1,0:T(8,128)} %get-tuple-element.119) | copy-start | bytes 1572868
  611.8 7.7 %copy-start.4 = (f32[64,2048]{1,0:T(8,128)S(1)}, f32[64,2048]{1,0:T(8,128)}, u32[]{:S(2)}) copy-start(f32[64,2048]{1,0:T(8,128)} %get-tuple-element.120) | copy-start | bytes 1572868
  611.9 8.5 %copy-start.3 = (f32[64,2048]{1,0:T(8,128)S(1)}, f32[64,2048]{1,0:T(8,128)}, u32[]{:S(2)}) copy-start(f32[64,2048]{1,0:T(8,128)} %get-tuple-element.121) | copy-start | bytes 1572868
  613.2 7.9 %copy-start.2 = (f32[1024,1024]{1,0:T(8,128)S(1)}, f32[1024,1024]{1,0:T(8,128)}, u32[]{:S(2)}) copy-start(f32[1024,1024]{1,0:T(8,128)} %get-tuple-element.125) | copy-start | bytes 12582916
  621.2 3.7 copy-start.1
  624.9 3.7 copy-start

commit v9 on v8

--- a/solution.py
+++ b/solution.py
@@ -862,7 +862,13 @@
 
 def steps_of(sc, text):
     names = {"m": sc.mid_send, "f": sc.bfirst, "d": sc.direct, "M": sc.mids, "h": sc.hop, "b": sc.bhop, "Q": sc.bquad, "q": sc.bquad2}
-    return [functools.partial(names[word[0]], *[int(digit) for digit in word[1:]]) for word in text.split()]
+    words = []
+    for letter in text:
+        if letter in names:
+            words.append((letter, []))
+        else:
+            words[-1][1].append(int(letter))
+    return [functools.partial(names[name], *digits) for name, digits in words]
 
 
 def run_steps(steps):
@@ -1457,7 +1463,7 @@
     def at_turns(table):
         return {t: steps_of(sc, words) for t, words in table.items()}
 
-    steps = at_turns({1: "m3 f3 d3", 3: "m0 f0 d0", 4: "M3", 5: "m2 f2 d2 b31", 6: "M0", 7: "m1 f1 d1 b02 b32"})
+    steps = at_turns({1: "m3f3d3", 3: "m0f0d0", 4: "M3", 5: "m2f2d2b31", 6: "M0", 7: "m1f1d1b02b32"})
 
     def turn(t, _):
         backward(t)
@@ -1484,13 +1490,13 @@
         run_steps(steps_of(sc, words))
 
     dw(0)
-    go("M2 b21")
+    go("M2b21")
     dw(1)
-    go("h30 M1 b01 b12 h03")
+    go("h30M1b01b12h03")
     dw(2)
-    go("h31 h02 h20 h23")
+    go("h31h02h20h23")
     dw(3)
-    go("h32 h01 h10 h13 Q h21 h12 q")
+    go("h32h01h10h13Qh21h12q")
 
     def store_out(sl, v):
         d_n2[sl, :] = v
@@ -1564,7 +1570,7 @@
 
     for zd in (3, 0, 2, 1):
         group(zd)
-        one(f"m{zd}" + (f" f{zd}" if zd in (3, 0) else ""))
+        one(f"m{zd}" + (f"f{zd}" if zd in (3, 0) else ""))
 
     side = width // 2
     own_cols = pl.ds(pl.multiple_of(c * side, side), side)
@@ -1619,24 +1625,24 @@
             keep[2 * k + i] = jnp.where(c == 0, first, second)
             give[2 * k + i] = jnp.where(c == 0, second, first).astype(BF)
 
-    one("f2 f1")
+    one("f2f1")
     join()
-    two("m3 m0 m2 m1 f3 f0")
-    one("d3 d0")
+    two("m3m0m2m1f3f0")
+    one("d3d0")
     grads(0)
-    one("M3 M0")
-    one("d2 d1")
+    one("M3M0")
+    one("d2d1")
     grads(1)
-    one("M2 M1")
-    two("d3 d0 d2 d1 f2 f1")
+    one("M2M1")
+    two("d3d0d2d1f2f1")
     grads(2)
-    one("b31 b02")
-    two("M3 M0 M2 M1")
+    one("b31b02")
+    two("M3M0M2M1")
     grads(3)
-    one("h30 h03 b21 b12")
+    one("h30h03b21b12")
     grads(4)
     grads(5)
-    one("b32 b01")
+    one("b32b01")
     grads(6)
     grads(7)
     across = remote(give, got, msem.at[0], msem.at[1], partner)
@@ -1650,12 +1656,12 @@
     lax.fori_loop(0, 16, total, 0)
     each_chip(net, lambda t, dev: remote(send.at[t], recv.at[me], msem.at[2], msem.at[3], dev).start())
     recv[me] = send[me]
-    two("b31 b02 b21 b12 b32 b01")
-    one("h31 h02 h20 h13 Q")
-    two("h30 h03 h20 h13 Q")
-    one("h32 h01 h10 h23")
-    two("h31 h02 h10 h23")
-    one("h21 h12 q")
+    two("b31b02b21b12b32b01")
+    one("h31h02h20h13Q")
+    two("h30h03h20h13Q")
+    one("h32h01h10h23")
+    two("h31h02h10h23")
+    one("h21h12q")
     sc1.last(store1)
     d_gain[...] = jnp.zeros_like(d_gain)
 
@@ -1684,7 +1690,7 @@
 
     lax.fori_loop(1, 32, tell, 0)
     gr[dev_me] = gb[me]
-    two("h32 h01 h21 h12 q")
+    two("h32h01h21h12q")
     landed(recv.at[pl.ds(0, 15)], msem.at[3])
     for e in range(16):
         piece = wide(recv[e])
@@ -1936,7 +1942,7 @@
         run_steps(steps_of(sc, words))
 
     load_p.wait()
-    go("m3 m0 m2 m1")
+    go("m3m0m2m1")
     d_gain[...] = jnp.zeros_like(d_gain)
 
     def norm_back(i, _):
@@ -2016,9 +2022,9 @@
     def store(sl, v):
         output[sl, :] = residual[sl, :] + v
 
-    go("f3 f0 d3 d0")
+    go("f3f0d3d0")
     done = 0
-    for upto, words in ((3, "M3 M0 M2 M1 d2 d1"), (6, "f2 f1"), (11, "b31 b02"), (16, "")):
+    for upto, words in ((3, "M3M0M2M1d2d1"), (6, "f2f1"), (11, "b31b02"), (16, "")):
         lax.fori_loop(done, upto, block, 0)
         go(words)
         done = upto
@@ -2031,7 +2037,7 @@
 
     lax.fori_loop(0, 16, pack, 0)
     remote(other, got, msem.at[2], msem.at[3], partner).start()
-    go("h30 h03")
+    go("h30h03")
     landed(got, msem.at[3])
     d_gains[...] = jnp.zeros_like(d_gains)
 
@@ -2058,7 +2064,7 @@
     lax.fori_loop(0, 16, undo, 0)
 
     def meanwhile():
-        go("b21 b12 b32 b01")
+        go("b21b12b32b01")
         dw(2)
         dw(3)
 
@@ -2074,15 +2080,15 @@
         return 0
 
     lax.fori_loop(0, 16, finish, 0)
-    go("h31 h02")
+    go("h31h02")
     dw(4)
-    go("h20 h13 Q")
+    go("h20h13Q")
     dw(5)
-    go("h32 h01")
+    go("h32h01")
     dw(6)
-    go("h10 h23")
+    go("h10h23")
     dw(7)
-    go("h21 h12 q")
+    go("h21h12q")
     sc.last(store)
     dw_end()
     landed(d_out.at[pl.ds(0, 15)], msem.at[0])

time: 639 us -> 639 us (level)
  no operation moved by 1% of the time
where the time goes in v9:
time: 639 us; the launch traced here: 631 us
  Pallas kernels  598 us (94%)
  local copies, waits for them, and re-layouts  22 us (3%)
  other arithmetic  8.47 us (1%)
    pallas_call x1, Pallas kernels, run_expert(): pl.pallas_call(functools.partial(expert_kernel, cut), out_shape=(S((R, D)...  163 us
    pallas_call x1, Pallas kernels, run_finish(): pl.pallas_call(functools.partial(finish_kernel, cut), out_shape=(own, S((...  132 us
    pallas_call x1, Pallas kernels, run_qkv(): pl.pallas_call(functools.partial(qkv_kernel, cut), out_shape=(S((16, R, D...  123 us
    pallas_call x1, Pallas kernels, run_attend_back(): pl.pallas_call(functools.partial(attend_back_kernel, scale, pads, cut), o...  100 us
    pallas_call x1, Pallas kernels, run_attend(): pl.pallas_call(functools.partial(attend_kernel, scale, pads, cut), out_sh...  80 us
    unnamed x25, local copies, waits for them, and re-layouts  17.4 us

profile of v9, /device:TPU:0, one launch (start us, length us, event | category | flops | bytes accessed | tf_op | source)
XLA Modules:
  0.0 631.0 jit_solution(14934174713514995749)
XLA Ops:
  0.8 0.7 maximum_convert_fusion
  2.3 0.9 convolution_select_fusion
  3.2 0.7 select_reduce_fusion
  4.7 0.7 convert_element_type.21
  7.0 1.9 fusion.9
  8.8 122.9 %project.1 = (bf16[16,128,2048]{2,1,0:T(8,128)(2,1)}, f32[16,128,384]{2,1,0:T(8,128)}, bf16[16,2,64,384]{3,2,1,0:T(8,128)(2,1)}, f32[32,128]{1,0:T(8,128)}, f32[...) custom-call(bf16[128,2048]{1,0:T(8,128)(2,1)} %x_in.3, bf16[64,2048]{1,0:T(8,128)(2,1)} %wq.1, bf16[64,2048]{1,0:T(8,128)(2,1)} %wk.1, ...), custom_call_target="tpu_custom_call" | custom-call | tf_op jit(solution)/shard_map/project/pallas_call | solution.py:1295
  131.7 1.3 fusion.5
  133.0 0.9 bitcast_reduce_fusion
  136.3 80.0 %attend.1 = (bf16[4,4,2,64,2048]{4,3,2,1,0:T(8,128)(2,1)}, bf16[16,128,128]{2,1,0:T(8,128)(2,1)}, bf16[2,20,2,128,128]{4,3,2,1,0:T(8,128)(2,1)}, bf16[16,128,128...) custom-call(f32[16,128,384]{2,1,0:T(8,128)} %get-tuple-element.46.li, ...), custom_call_target="tpu_custom_call" | custom-call | tf_op jit(solution)/shard_map/attend/pallas_call | solution.py:1910
  216.3 163.3 %expert.1 = (f32[128,2048]{1,0:T(8,128)}, bf16[4,4,128,2048]{3,2,1,0:T(8,128)(2,1)}, bf16[4,4,128,2048]{3,2,1,0:T(8,128)(2,1)}, bf16[4,4,128,2048]{3,2,1,0:T(8,1...) custom-call(bf16[128,2048]{1,0:T(8,128)(2,1)} %get-tuple-element.49.n2, ...), custom_call_target="tpu_custom_call" | custom-call | tf_op jit(solution)/shard_map/expert/pallas_call | solution.py:1518
  379.6 100.2 %attend_back.1 = (bf16[16,128,384]{2,1,0:T(8,128)(2,1)}, f32[8,128]{1,0:T(8,128)}, f32[128,2048]{1,0:T(8,128)}, f32[128,2048]{1,0:T(8,128)}, f32[1,2048]{1,0:T(1...) custom-call(f32[128,2048]{1,0:T(8,128)} %get-tuple-element.52.d_n2, ...), custom_call_target="tpu_custom_call" | custom-call | tf_op jit(solution)/shard_map/attend_back/pallas_call | solution.py:2107
  479.9 131.9 %finish.1 = (f32[64,2048]{1,0:T(8,128)}, f32[128,2048]{1,0:T(8,128)}, f32[64,2048]{1,0:T(8,128)}, f32[64,2048]{1,0:T(8,128)}, f32[64,2048]{1,0:T(8,128)}, /*index=5*/f32[8,64]{1,0:T(8,128)}) custom-call(bf16[16,128,384]{2,1,0:T(8,128)(2,1)} %get-tuple-element.63.d_lin, bf16[16,2,64,384]{3,2,1,0:T(8,128)(2,1)} %get-tuple-element.64.wf, ...), custom_call_target="tpu_custom_call" | custom-call | tf_op jit(solution)/shard_map/finish/pallas_call | solution.py:1728
  611.9 1.4 slice_bitcast_fusion.2
  613.2 2.4 copy.46
  615.7 2.3 copy.47
  618.0 0.8 copy.48
  618.8 0.8 copy.49
  619.6 0.8 copy.50
  620.4 0.8 copy.51
  621.2 2.1 copy.52
  623.3 1.6 copy-done.1
  624.9 2.1 copy.53
  627.0 1.6 copy-done
  628.6 2.0 copy.54
  (36 shorter events, 5.6 us)
Async XLA Ops:
  5.4 131.0 %copy-start.7 = (f32[4096]{0:T(1024)}, f32[4096]{0:T(1024)S(1)}, u32[]{:S(2)}) copy-start(f32[4096]{0:T(1024)S(1)} %convert_element_type.21) | copy-start | bytes 49156
  611.8 6.1 copy-start.6
  611.8 6.9 %copy-start.5 = (f32[64,2048]{1,0:T(8,128)S(1)}, f32[64,2048]{1,0:T(8,128)}, u32[]{:S(2)}) copy-start(f32[64,2048]{1,0:T(8,128)} %get-tuple-element.119) | copy-start | bytes 1572868
  611.8 7.7 %copy-start.4 = (f32[64,2048]{1,0:T(8,128)S(1)}, f32[64,2048]{1,0:T(8,128)}, u32[]{:S(2)}) copy-start(f32[64,2048]{1,0:T(8,128)} %get-tuple-element.120) | copy-start | bytes 1572868
  611.9 8.5 %copy-start.3 = (f32[64,2048]{1,0:T(8,128)S(1)}, f32[64,2048]{1,0:T(8,128)}, u32[]{:S(2)}) copy-start(f32[64,2048]{1,0:T(8,128)} %get-tuple-element.121) | copy-start | bytes 1572868
  613.2 7.9 %copy-start.2 = (f32[1024,1024]{1,0:T(8,128)S(1)}, f32[1024,1024]{1,0:T(8,128)}, u32[]{:S(2)}) copy-start(f32[1024,1024]{1,0:T(8,128)} %get-tuple-element.125) | copy-start | bytes 12582916
  621.2 3.7 copy-start.1
  624.9 3.7 copy-start
